TPU v7x, 32 devices: a whole 2x2x4 slice. The times are simulated.
32 devices in a mesh: seq: 4 (over y, x), expert: 8 (over z, core).
Axes of the slice: x: 2, y: 2, z: 4, core: 2. Of those that a mesh axis runs over, the one named last changes fastest.
Arguments:
- tokens: bfloat16 [512, 4096], P('seq'), may hold values from -8 to 8
- norm_gain: float32 [4096], replicated, may hold values from 0.25 to 1.75
- in_weight: bfloat16 [4096, 2, 8192], P('seq', None, 'expert'), may hold values from -0.09375 to 0.09375
- conv_weight: float32 [4, 8192], P(None, 'expert'), may hold values from -0.5 to 0.5
- conv_bias: float32 [8192], P('expert'), may hold values from -0.5 to 0.5
- proj_weight: bfloat16 [8192, 288], P('expert'), may hold values from -0.0625 to 0.0625
- step_weight: bfloat16 [256, 8192], P(None, 'expert'), may hold values from -1 to 1
- step_bias: float32 [8192], P('expert'), may hold values from -5 to -1
- decay_log: float32 [8192, 16], P('expert'), may hold values from -6 to 2.7
- skip_gain: float32 [8192], P('expert'), may hold values from 0.5 to 1.5
- out_weight: bfloat16 [8192, 4096], P('expert', 'seq'), may hold values from -0.0625 to 0.0625
- moe_gain: float32 [4096], replicated, may hold values from 0.25 to 1.75
- router_weight: bfloat16 [4096, 8], replicated, may hold values from -0.09375 to 0.09375
- routes: int32 [512, 2], P(('seq', 'expert')), may hold values from 0 to 7, all different within a row; in each aligned block of 16 rows (0 to 15, 16 to 31, ...) at most 6 rows name the same one
- gate_weight: bfloat16 [8, 4096, 7168], P('expert', None, 'seq'), may hold values from -0.09375 to 0.09375
- up_weight: bfloat16 [8, 4096, 7168], P('expert', None, 'seq'), may hold values from -0.09375 to 0.09375
- down_weight: bfloat16 [8, 7168, 4096], P('expert', 'seq'), may hold values from -0.0625 to 0.0625
Outputs:
- mixed: bfloat16 [512, 4096], P(('seq', 'expert'))
Inputs may be any that keep to these rules, and one draw needn't show every extreme that they name: `routes`: each row names two different experts; within each aligned block of 16 rows no expert is named by more than 6 rows, and that number is reached in some blocks.
All inputs are finite; a program needn't handle non-finite values.
Results may differ from a plain program's by a relative error of at most 0.013.
Values may be sent and summed in bfloat16 or wider, within the bound.
No kernel may reach another device: no remote copies, remote signals or barrier semaphores. Data moves between devices by JAX's collectives and lax.ppermute only.
A program may use at most 128 MiB of HBM per device.

v0:
```python
import jax
import jax.numpy as jnp
from jax import lax
from jax.sharding import PartitionSpec as P

EPSILON = 1e-06
SCAN_ROWS = 16


def shifted(block, axis, distance):
    devices = range(lax.axis_size(axis))
    route = [(i - distance, i) for i in devices if i - distance in devices]
    return lax.ppermute(block, axis, route)


def rms_norm(values_in, gain_row):
    as_float = values_in.astype(jnp.float32)
    inverse = lax.rsqrt(jnp.mean(as_float * as_float, axis=-1, keepdims=True) + EPSILON)
    return (as_float * inverse * gain_row).astype(jnp.bfloat16)


def scan_pairs(former, latter):
    return (former[0] * latter[0], latter[0] * former[1] + latter[1])


def route_tables(routes, logits, experts, block_rows, most_slots):
    expert_ids = lax.broadcasted_iota(jnp.int32, (1, 1, experts), 2)
    matches = routes[:, :, None] == expert_ids
    picked = jnp.sum(jnp.where(matches, logits[:, None, :], 0.0), axis=2)
    first_share = jax.nn.sigmoid(picked[:, 0] - picked[:, 1])
    shares = jnp.stack([first_share, 1.0 - first_share], axis=1)
    weight_table = jnp.sum(jnp.where(matches, shares[:, :, None], 0.0), axis=1)
    counts = jnp.sum(matches.astype(jnp.int32), axis=1)
    blocked = counts.reshape(-1, block_rows, experts)
    before = jnp.cumsum(blocked, axis=1) - blocked
    slot_ids = lax.broadcasted_iota(jnp.int32, (1, 1, 1, most_slots), 3)
    chosen = (blocked[..., None] > 0) & (before[..., None] == slot_ids)
    slot_table = jnp.where(chosen, 1.0, 0.0).astype(jnp.float32)
    return (slot_table, weight_table.reshape(-1, block_rows, experts))


def expert_terms(pieces, gate_weight, up_weight, down_weight):
    local_count = pieces.shape[0]
    model_width = pieces.shape[-1]
    flat_rows = pieces.reshape(local_count, -1, model_width)
    gate_act = jnp.einsum(
        "erd,edf->erf", flat_rows, gate_weight, preferred_element_type=jnp.float32
    )
    up_act = jnp.einsum("erd,edf->erf", flat_rows, up_weight, preferred_element_type=jnp.float32)
    hidden = (jax.nn.silu(gate_act) * up_act).astype(jnp.bfloat16)
    result = jnp.einsum("erf,efd->erd", hidden, down_weight, preferred_element_type=jnp.float32)
    return result.reshape(pieces.shape)


def local(
    tokens,
    norm_gain,
    in_weight,
    conv_weight,
    conv_bias,
    proj_weight,
    step_weight,
    step_bias,
    decay_log,
    skip_gain,
    out_weight,
    moe_gain,
    router_weight,
    routes,
    gate_weight,
    up_weight,
    down_weight,
):
    length = tokens.shape[0]
    model_width = tokens.shape[1]
    channels = in_weight.shape[2]
    rank_width = step_weight.shape[0]
    state_width = decay_log.shape[1]
    tap_count = conv_weight.shape[0]
    normed = rms_norm(tokens, norm_gain)
    pieces = lax.all_gather(in_weight, "seq", axis=0, tiled=True)
    projected = jnp.dot(
        normed, pieces.reshape(pieces.shape[0], 2 * channels), preferred_element_type=jnp.float32
    ).astype(jnp.bfloat16)
    mixer_in = projected[:, :channels]
    gate_in = projected[:, channels:].astype(jnp.float32)
    previous = shifted(mixer_in[length - tap_count + 1 :], "seq", 1)
    padded = jnp.concatenate([previous, mixer_in], axis=0).astype(jnp.float32)
    convolved = conv_bias + jnp.zeros((length, channels), jnp.float32)
    for tap_index in range(tap_count):
        convolved = convolved + conv_weight[tap_index] * padded[tap_index : tap_index + length]
    activated = jax.nn.silu(convolved).astype(jnp.bfloat16)
    features = jnp.dot(activated, proj_weight, preferred_element_type=jnp.float32)
    low_rank, state_maps = lax.psum((features[:, :rank_width], features[:, rank_width:]), "expert")
    input_map = state_maps[:, :state_width]
    output_map = state_maps[:, state_width:]
    step_size = jax.nn.softplus(
        jnp.dot(low_rank.astype(jnp.bfloat16), step_weight, preferred_element_type=jnp.float32)
        + step_bias
    )
    decay_rate = -jnp.exp(jnp.transpose(decay_log))
    drive_in = activated.astype(jnp.float32)
    block_count = length // SCAN_ROWS
    step_blocks = step_size.reshape(block_count, SCAN_ROWS, channels)
    drive_blocks = drive_in.reshape(block_count, SCAN_ROWS, channels)
    input_blocks = input_map.reshape(block_count, SCAN_ROWS, state_width)
    output_blocks = output_map.reshape(block_count, SCAN_ROWS, state_width)

    def advance(carried, block_in):
        step_block, drive_block, input_block, output_block = block_in
        decay_step = jnp.exp(step_block[:, None, :] * decay_rate[None])
        inject = input_block[:, :, None] * (step_block * drive_block)[:, None, :]
        cumulated, local_state = lax.associative_scan(scan_pairs, (decay_step, inject), axis=0)
        states = local_state + cumulated * carried[None]
        return (states[-1], jnp.einsum("tnc,tn->tc", states, output_block))

    start_state = jnp.zeros((state_width, channels), jnp.float32)
    final_local, local_out = lax.scan(
        advance, start_state, (step_blocks, drive_blocks, input_blocks, output_blocks)
    )
    local_out = local_out.reshape(length, channels)
    total_decay = jnp.exp(decay_rate * jnp.sum(step_size, axis=0)[None, :])
    summary = (total_decay, final_local)
    stacked = (
        lax.all_gather(summary[0][None], "seq", axis=0, tiled=True),
        lax.all_gather(summary[1][None], "seq", axis=0, tiled=True),
    )
    inclusive = lax.associative_scan(scan_pairs, stacked, axis=0)
    position = lax.axis_index("seq")
    earlier_state = lax.dynamic_index_in_dim(
        inclusive[1], jnp.maximum(position - 1, 0), 0, keepdims=False
    )
    incoming = jnp.where(position > 0, earlier_state, 0.0)
    running_steps = jnp.cumsum(step_size, axis=0).reshape(block_count, SCAN_ROWS, channels)

    def correct(unused, block_in):
        steps_block, output_block = block_in
        carried_decay = jnp.exp(steps_block[:, None, :] * decay_rate[None]) * incoming[None]
        return (unused, jnp.einsum("tnc,tn->tc", carried_decay, output_block))

    unused_carry, carried_out = lax.scan(
        correct, jnp.zeros((), jnp.float32), (running_steps, output_blocks)
    )
    scanned = local_out + carried_out.reshape(length, channels)
    gated_out = ((scanned + skip_gain * drive_in) * jax.nn.silu(gate_in)).astype(jnp.bfloat16)
    partials = jnp.dot(
        gated_out,
        lax.all_gather(out_weight, "seq", axis=1, tiled=True),
        preferred_element_type=jnp.float32,
    )
    mamba_out = lax.psum_scatter(partials, "expert", scatter_dimension=0, tiled=True)
    own_rows = routes.shape[0]
    own_tokens = lax.dynamic_slice_in_dim(tokens, lax.axis_index("expert") * own_rows, own_rows, 0)
    hidden_state = (own_tokens.astype(jnp.float32) + mamba_out).astype(jnp.bfloat16)
    moe_in = rms_norm(hidden_state, moe_gain)
    logits = jnp.dot(moe_in, router_weight, preferred_element_type=jnp.float32)
    experts = router_weight.shape[1]
    local_experts = gate_weight.shape[0]
    block_rows = own_rows // local_experts
    most_slots = max(2, 3 * block_rows // experts)
    slot_table, weight_table = route_tables(routes, logits, experts, block_rows, most_slots)
    outgoing = jnp.einsum(
        "btem,btd->ebmd",
        slot_table.astype(jnp.bfloat16),
        moe_in.reshape(-1, block_rows, model_width),
        preferred_element_type=jnp.float32,
    ).astype(jnp.bfloat16)
    seq_count = lax.axis_size("seq")
    arrived = lax.all_to_all(outgoing, "expert", split_axis=0, concat_axis=1, tiled=True)
    produced = expert_terms(
        lax.all_gather(arrived, "seq", axis=1, tiled=True), gate_weight, up_weight, down_weight
    )
    shaped = produced.reshape(local_experts, seq_count, -1, model_width)
    summed = lax.psum_scatter(shaped.astype(jnp.bfloat16), "seq", scatter_dimension=1, tiled=True)
    expert_out = summed.reshape(local_experts, -1, most_slots, model_width)
    returned = lax.all_to_all(expert_out, "expert", split_axis=1, concat_axis=0, tiled=True)
    mixed_weights = slot_table * weight_table[..., None]
    moe_out = jnp.einsum("btem,ebmd->btd", mixed_weights, returned.astype(jnp.float32)).reshape(
        own_rows, model_width
    )
    return (hidden_state.astype(jnp.float32) + moe_out).astype(jnp.bfloat16)


def solution(mesh):
    in_specs = (
        P("seq", None),
        P(),
        P("seq", None, "expert"),
        P(None, "expert"),
        P("expert"),
        P("expert", None),
        P(None, "expert"),
        P("expert"),
        P("expert", None),
        P("expert"),
        P("expert", "seq"),
        P(),
        P(),
        P(("seq", "expert"), None),
        P("expert", None, "seq"),
        P("expert", None, "seq"),
        P("expert", "seq", None),
    )
    out_specs = P(("seq", "expert"), None)
    return jax.shard_map(local, mesh=mesh, in_specs=in_specs, out_specs=out_specs, check_vma=False)
```

profile of v0, /device:TPU:0, one launch (start us, length us, event | category | flops | bytes accessed | tf_op | source)
XLA Modules:
  0.0 935.7 jit_solution(10611997397364357656)
XLA Ops:
  9.4 159.9 %all-gather.7.cloned.1.call-done = bf16[4096,2,1024]{2,1,0:T(2,128)(2,1)} async-done(((bf16[1024,2,1024]{2,1,0:T(2,128)(2,1)}), bf16[4096,2,1024]{2,1,0:T(2,128)(2,1)}) %all-gather.7.cloned.1.call-update) | async-done | bytes 16777232 | tf_op jit(solution)/shard_map/all_gather | solution.py:81
  169.4 12.2 %copy.78 = bf16[512,8,2,1024]{3,1,2,0:T(8,128)(2,1)S(1)} copy(bf16[512,8,2,1024]{3,2,1,0:T(2,128)(2,1)} %bitcast.152) | data formatting | bytes 33554432
  190.5 29.7 %all-reduce.23 = (f32[128,32]{0,1:T(8,128)S(1)}, bf16[128,256]{0,1:T(8,128)(2,1)S(1)}) all-reduce(f32[128,32]{0,1:T(8,128)S(1)} %slice.266, f32[128,256]{0,1:T(8,128)S(1)} %slice.268), channel_id=1, replica_groups=mesh['seq'=4,'expert'=8] {'expert'}, use_global_device_ids=true, to_apply=%region_2.3 | all-reduce | flops 36864 | bytes 229376 | tf_op jit(solution)/shard_map/psum | solution.py:94
  225.1 497.8 %while.22 = (s32[]{:T(128)}, f32[16,1024]{1,0:T(8,128)}, f32[8,16,1024]{2,1,0:T(8,128)}, f32[8,16,16]{2,1,0:T(8,128)}, f32[8,16,1024]{2,1,0:T(8,128)}, /*index=5...) while((s32[]{:T(128)}, f32[16,1024]{1,0:T(8,128)}, ...), condition=%wide.region_4.5_spmd, body=%wide.region_3.4_spmd.sunk | while | flops 4669442 | bytes 61479868 | solution.py:118
  248.8 5.7 pad.195
  257.0 3.7 pad.191
  262.4 3.7 pad.190
  268.4 3.5 pad.194
  272.7 5.7 pad.193
  279.6 3.5 pad.192
  311.0 5.7 pad.195
  319.2 3.7 pad.191
  324.6 3.7 pad.190
  330.6 3.5 pad.194
  334.9 5.7 pad.193
  341.8 3.5 pad.192
  373.2 5.7 pad.195
  381.4 3.7 pad.191
  386.9 3.7 pad.190
  392.8 3.5 pad.194
  397.2 5.7 pad.193
  404.0 3.5 pad.192
  435.5 5.7 pad.195
  443.7 3.7 pad.191
  449.1 3.7 pad.190
  455.0 3.5 pad.194
  459.4 5.7 pad.193
  466.3 3.5 pad.192
  497.7 5.7 pad.195
  505.9 3.7 pad.191
  511.3 3.7 pad.190
  517.3 3.5 pad.194
  521.6 5.7 pad.193
  528.5 3.5 pad.192
  559.9 5.7 pad.195
  568.1 3.7 pad.191
  573.5 3.7 pad.190
  579.5 3.5 pad.194
  583.9 5.7 pad.193
  590.7 3.5 pad.192
  622.2 5.7 pad.195
  630.4 3.7 pad.191
  635.8 3.7 pad.190
  646.1 5.7 pad.193
  653.0 3.5 pad.192
  684.4 5.7 pad.195
  692.6 3.7 pad.191
  698.0 3.7 pad.190
  704.0 3.5 pad.194
  708.3 5.7 pad.193
  715.2 3.5 pad.192
  724.5 10.6 %all-gather = f32[64,1024]{1,0:T(8,128)S(1)} all-gather(f32[16,1024]{1,0:T(8,128)} %get-tuple-element.81), channel_id=2, replica_groups=mesh['seq'=4,'expert'=8] {'seq'}, dimensions={0}, use_global_device_ids=true | all-gather | bytes 327680 | tf_op jit(solution)/shard_map/all_gather | solution.py:126
  736.0 8.5 all-gather.1
  744.8 15.1 %while.23 = (s32[]{:T(128)}, f32[8,16,1024]{2,1,0:T(8,128)S(1)}, f32[8,16,1024]{2,1,0:T(8,128)S(1)}, f32[16,1024]{1,0:T(8,128)}, f32[16,1024]{1,0:T(8,128)S(1)}, /*index=5*/f32[8,16,16]{2,1,0:T(8,128)}, s32[]{:T(128)}) while((s32[]{:T(128)}, f32[8,16,1024]{2,1,0:T(8,128)S(1)}, f32[8,16,1024]{2,1,0:T(8,128)S(1)}, f32[16,1024]{1,0:T(8,128)}, ...), condition=%wide.region_8.9_spmd, body=%wide.region_7.8_spmd.sunk | while | flops 1048578 | bytes 527449 | solution.py:141
  761.5 6.0 fusion.89
  768.4 32.3 %reduce-scatter.8.cloned.1.call-done = f32[16,4096]{1,0:T(8,128)} async-done(((f32[128,4096]{1,0:T(8,128)}), f32[16,4096]{1,0:T(8,128)}) %reduce-scatter.8.cloned.1.call-update) | async-done | bytes 262160 | tf_op jit(solution)/shard_map/reduce_scatter | solution.py:151
  802.4 17.8 %all_to_all.21 = bf16[8,1,6,4096]{3,2,1,0:T(8,128)(2,1)S(1)} all-to-all(bf16[8,1,6,4096]{3,2,1,0:T(8,128)(2,1)S(1)} %copy.65), channel_id=1, replica_groups=mesh['seq'=4,'expert'=8] {'expert'}, dimensions={0} | all-to-all | bytes 786432 | tf_op jit(solution)/shard_map/all_to_all | solution.py:169
  821.2 29.9 %all-gather.11.cloned.1.call-done = bf16[32,1,6,4096]{3,0,2,1:T(8,128)(2,1)} async-done(((bf16[8,1,6,4096]{3,0,2,1:T(8,128)(2,1)}), bf16[32,1,6,4096]{3,0,2,1:T(8,128)(2,1)}) %all-gather.11.cloned.1.call-update) | async-done | bytes 1572880 | tf_op jit(solution)/shard_map/all_gather | solution.py:171
  854.9 7.6 fusion.18
  862.5 8.5 fusion.32
  871.0 4.1 fusion.23
  875.2 31.1 %reduce-scatter.10.cloned.1.call-done = bf16[1,1,48,4096]{3,2,1,0:T(8,128)(2,1)} async-done(((bf16[1,4,48,4096]{3,2,1,0:T(8,128)(2,1)}), bf16[1,1,48,4096]{3,2,1,0:T(8,128)(2,1)}) %reduce-scatter.10.cloned.1.call-update) | async-done | bytes 393232
  908.2 4.6 all-to-all-start.1
  913.1 15.1 %all-to-all-done.1 = bf16[1,8,6,4096]{3,2,0,1:T(8,128)(2,1)S(1)} async-done(((bf16[1,8,6,4096]{3,2,0,1:T(8,128)(2,1)}), bf16[1,8,6,4096]{3,2,0,1:T(8,128)(2,1)S(1)}, u32[]{:S(2)}, u32[]{:S(2)}) %all-to-all-start.1) | async-done | bytes 393248 | tf_op jit(solution)/shard_map/all_to_all | solution.py:176
  (612 shorter events, 338.8 us)
Async XLA Ops:
  6.5 183.6 %copy-start = (bf16[1024,288]{0,1:T(8,128)(2,1)S(1)}, bf16[1024,288]{0,1:T(8,128)(2,1)}, u32[]{:S(2)}) copy-start(bf16[1024,288]{0,1:T(8,128)(2,1)} %param.26) | copy-start | bytes 1769476
  6.5 162.8 %all-gather.7.cloned.1.call-start = ((), (), s32[]{:S(2)}) async-start(), calls=%async_computation.4 | async-start | bytes 20971520 | tf_op jit(solution)/shard_map/all_gather | solution.py:81
  7.3 754.2 %all-gather.9.cloned.1.call-start = ((), (), s32[]{:S(2)}) async-start(), calls=%async_computation.5 | async-start | bytes 10485760 | tf_op jit(solution)/shard_map/all_gather | solution.py:148
  8.0 792.7 %reduce-scatter.8.cloned.1.call-start = ((), (), s32[]{:S(2)}) async-start(), calls=%async_computation.6 | async-start | bytes 2359296 | tf_op jit(solution)/shard_map/reduce_scatter | solution.py:151
  169.4 12.2 %copy-start.20 = (f32[4096]{0:T(1024)S(1)}, f32[4096]{0:T(1024)}, u32[]{:S(2)}) copy-start(f32[4096]{0:T(1024)} %param.22) | copy-start | bytes 49156
  181.6 6.0 copy-start.24
  181.6 8.2 copy-start.21
  184.1 6.4 copy-start.13
  184.2 4.7 collective-permute-start
  189.8 32.0 %copy-start.27 = (bf16[256,1024]{1,0:T(8,128)(2,1)S(1)}, bf16[256,1024]{1,0:T(8,128)(2,1)}, u32[]{:S(2)}) copy-start(bf16[256,1024]{1,0:T(8,128)(2,1)} %param.27) | copy-start | bytes 1572868
  189.8 32.0 %copy-start.29 = (f32[1024]{0:T(1024)S(1)}, f32[1024]{0:T(1024)}, u32[]{:S(2)}) copy-start(f32[1024]{0:T(1024)} %param.28) | copy-start | bytes 12292
  229.6 12.8 %copy-start.6 = (f32[8,16,1024]{2,1,0:T(8,128)}, f32[8,16,1024]{2,1,0:T(8,128)S(1)}, u32[]{:S(2)}) copy-start(f32[8,16,1024]{2,1,0:T(8,128)S(1)} %get-tuple-element.323) | copy-start | bytes 1572868 | tf_op jit(solution)/shard_map/while
  272.7 10.4 %copy-start.4 = (f32[16,16,1024]{2,1,0:T(8,128)S(1)}, f32[16,16,1024]{2,1,0:T(8,128)}, u32[]{:S(2)}) copy-start(f32[16,16,1024]{2,1,0:T(8,128)} %pad.195) | copy-start | bytes 3145732 | tf_op jit(solution)/shard_map/while
  272.7 10.4 %copy-start.12 = (f32[16,1024]{1,0:T(8,128)S(1)}, f32[16,1024]{1,0:T(8,128)}, u32[]{:S(2)}) copy-start(f32[16,1024]{1,0:T(8,128)} %get-tuple-element.357) | copy-start | bytes 196612 | tf_op jit(solution)/shard_map/while
  278.4 4.7 copy-start.5
  283.1 4.2 copy-start.18
  291.9 12.8 %copy-start.6 = (f32[8,16,1024]{2,1,0:T(8,128)}, f32[8,16,1024]{2,1,0:T(8,128)S(1)}, u32[]{:S(2)}) copy-start(f32[8,16,1024]{2,1,0:T(8,128)S(1)} %get-tuple-element.323) | copy-start | bytes 1572868 | tf_op jit(solution)/shard_map/while
  334.9 10.4 %copy-start.4 = (f32[16,16,1024]{2,1,0:T(8,128)S(1)}, f32[16,16,1024]{2,1,0:T(8,128)}, u32[]{:S(2)}) copy-start(f32[16,16,1024]{2,1,0:T(8,128)} %pad.195) | copy-start | bytes 3145732 | tf_op jit(solution)/shard_map/while
  334.9 10.4 %copy-start.12 = (f32[16,1024]{1,0:T(8,128)S(1)}, f32[16,1024]{1,0:T(8,128)}, u32[]{:S(2)}) copy-start(f32[16,1024]{1,0:T(8,128)} %get-tuple-element.357) | copy-start | bytes 196612 | tf_op jit(solution)/shard_map/while
  340.7 4.7 copy-start.5
  354.1 12.8 %copy-start.6 = (f32[8,16,1024]{2,1,0:T(8,128)}, f32[8,16,1024]{2,1,0:T(8,128)S(1)}, u32[]{:S(2)}) copy-start(f32[8,16,1024]{2,1,0:T(8,128)S(1)} %get-tuple-element.323) | copy-start | bytes 1572868 | tf_op jit(solution)/shard_map/while
  397.2 10.4 %copy-start.4 = (f32[16,16,1024]{2,1,0:T(8,128)S(1)}, f32[16,16,1024]{2,1,0:T(8,128)}, u32[]{:S(2)}) copy-start(f32[16,16,1024]{2,1,0:T(8,128)} %pad.195) | copy-start | bytes 3145732 | tf_op jit(solution)/shard_map/while
  397.2 10.4 %copy-start.12 = (f32[16,1024]{1,0:T(8,128)S(1)}, f32[16,1024]{1,0:T(8,128)}, u32[]{:S(2)}) copy-start(f32[16,1024]{1,0:T(8,128)} %get-tuple-element.357) | copy-start | bytes 196612 | tf_op jit(solution)/shard_map/while
  402.9 4.7 copy-start.5
  407.6 4.2 copy-start.18
  416.3 12.8 %copy-start.6 = (f32[8,16,1024]{2,1,0:T(8,128)}, f32[8,16,1024]{2,1,0:T(8,128)S(1)}, u32[]{:S(2)}) copy-start(f32[8,16,1024]{2,1,0:T(8,128)S(1)} %get-tuple-element.323) | copy-start | bytes 1572868 | tf_op jit(solution)/shard_map/while
  459.4 10.4 %copy-start.4 = (f32[16,16,1024]{2,1,0:T(8,128)S(1)}, f32[16,16,1024]{2,1,0:T(8,128)}, u32[]{:S(2)}) copy-start(f32[16,16,1024]{2,1,0:T(8,128)} %pad.195) | copy-start | bytes 3145732 | tf_op jit(solution)/shard_map/while
  459.4 10.4 %copy-start.12 = (f32[16,1024]{1,0:T(8,128)S(1)}, f32[16,1024]{1,0:T(8,128)}, u32[]{:S(2)}) copy-start(f32[16,1024]{1,0:T(8,128)} %get-tuple-element.357) | copy-start | bytes 196612 | tf_op jit(solution)/shard_map/while
  465.1 4.7 copy-start.5
  469.8 4.2 copy-start.18
  478.5 12.8 %copy-start.6 = (f32[8,16,1024]{2,1,0:T(8,128)}, f32[8,16,1024]{2,1,0:T(8,128)S(1)}, u32[]{:S(2)}) copy-start(f32[8,16,1024]{2,1,0:T(8,128)S(1)} %get-tuple-element.323) | copy-start | bytes 1572868 | tf_op jit(solution)/shard_map/while
  521.6 10.4 %copy-start.4 = (f32[16,16,1024]{2,1,0:T(8,128)S(1)}, f32[16,16,1024]{2,1,0:T(8,128)}, u32[]{:S(2)}) copy-start(f32[16,16,1024]{2,1,0:T(8,128)} %pad.195) | copy-start | bytes 3145732 | tf_op jit(solution)/shard_map/while
  521.6 10.4 %copy-start.12 = (f32[16,1024]{1,0:T(8,128)S(1)}, f32[16,1024]{1,0:T(8,128)}, u32[]{:S(2)}) copy-start(f32[16,1024]{1,0:T(8,128)} %get-tuple-element.357) | copy-start | bytes 196612 | tf_op jit(solution)/shard_map/while
  527.3 4.7 copy-start.5
  532.1 4.2 copy-start.18
  540.8 12.8 %copy-start.6 = (f32[8,16,1024]{2,1,0:T(8,128)}, f32[8,16,1024]{2,1,0:T(8,128)S(1)}, u32[]{:S(2)}) copy-start(f32[8,16,1024]{2,1,0:T(8,128)S(1)} %get-tuple-element.323) | copy-start | bytes 1572868 | tf_op jit(solution)/shard_map/while
  583.9 10.4 %copy-start.4 = (f32[16,16,1024]{2,1,0:T(8,128)S(1)}, f32[16,16,1024]{2,1,0:T(8,128)}, u32[]{:S(2)}) copy-start(f32[16,16,1024]{2,1,0:T(8,128)} %pad.195) | copy-start | bytes 3145732 | tf_op jit(solution)/shard_map/while
  583.9 10.4 %copy-start.12 = (f32[16,1024]{1,0:T(8,128)S(1)}, f32[16,1024]{1,0:T(8,128)}, u32[]{:S(2)}) copy-start(f32[16,1024]{1,0:T(8,128)} %get-tuple-element.357) | copy-start | bytes 196612 | tf_op jit(solution)/shard_map/while
  589.6 4.7 copy-start.5
  594.3 4.2 copy-start.18
  603.0 12.8 %copy-start.6 = (f32[8,16,1024]{2,1,0:T(8,128)}, f32[8,16,1024]{2,1,0:T(8,128)S(1)}, u32[]{:S(2)}) copy-start(f32[8,16,1024]{2,1,0:T(8,128)S(1)} %get-tuple-element.323) | copy-start | bytes 1572868 | tf_op jit(solution)/shard_map/while
  646.1 10.4 %copy-start.4 = (f32[16,16,1024]{2,1,0:T(8,128)S(1)}, f32[16,16,1024]{2,1,0:T(8,128)}, u32[]{:S(2)}) copy-start(f32[16,16,1024]{2,1,0:T(8,128)} %pad.195) | copy-start | bytes 3145732 | tf_op jit(solution)/shard_map/while
  646.1 10.4 %copy-start.12 = (f32[16,1024]{1,0:T(8,128)S(1)}, f32[16,1024]{1,0:T(8,128)}, u32[]{:S(2)}) copy-start(f32[16,1024]{1,0:T(8,128)} %get-tuple-element.357) | copy-start | bytes 196612 | tf_op jit(solution)/shard_map/while
  651.8 4.7 copy-start.5
  656.5 4.2 copy-start.18
  665.2 12.8 %copy-start.6 = (f32[8,16,1024]{2,1,0:T(8,128)}, f32[8,16,1024]{2,1,0:T(8,128)S(1)}, u32[]{:S(2)}) copy-start(f32[8,16,1024]{2,1,0:T(8,128)S(1)} %get-tuple-element.323) | copy-start | bytes 1572868 | tf_op jit(solution)/shard_map/while
  708.3 10.4 %copy-start.4 = (f32[16,16,1024]{2,1,0:T(8,128)S(1)}, f32[16,16,1024]{2,1,0:T(8,128)}, u32[]{:S(2)}) copy-start(f32[16,16,1024]{2,1,0:T(8,128)} %pad.195) | copy-start | bytes 3145732 | tf_op jit(solution)/shard_map/while
  708.3 10.4 %copy-start.12 = (f32[16,1024]{1,0:T(8,128)S(1)}, f32[16,1024]{1,0:T(8,128)}, u32[]{:S(2)}) copy-start(f32[16,1024]{1,0:T(8,128)} %get-tuple-element.357) | copy-start | bytes 196612 | tf_op jit(solution)/shard_map/while
  714.0 4.7 copy-start.5
  744.8 15.2 %copy-start.15 = (f32[8,16,1024]{2,1,0:T(8,128)S(1)}, f32[8,16,1024]{2,1,0:T(8,128)}, u32[]{:S(2)}) copy-start(f32[8,16,1024]{2,1,0:T(8,128)} %get-tuple-element.80) | copy-start | bytes 1572868
  744.8 15.2 %copy-start.14 = (bf16[128,2048]{1,0:T(8,128)(2,1)S(1)}, bf16[128,2048]{1,0:T(8,128)(2,1)}, u32[]{:S(2)}) copy-start(bf16[128,2048]{1,0:T(8,128)(2,1)} %copy-done.13) | copy-start | bytes 1572868
  744.8 15.2 %copy-start.22 = (f32[1024]{0:T(1024)S(1)}, f32[1024]{0:T(1024)}, u32[]{:S(2)}) copy-start(f32[1024]{0:T(1024)} %param.25) | copy-start | bytes 12292
  744.8 15.2 %copy-start.26 = (f32[1024]{0:T(1024)S(1)}, f32[1024]{0:T(1024)}, u32[]{:S(2)}) copy-start(f32[1024]{0:T(1024)} %param.30) | copy-start | bytes 12292
  767.5 34.3 %copy-start.23 = (f32[4096]{0:T(1024)S(1)}, f32[4096]{0:T(1024)}, u32[]{:S(2)}) copy-start(f32[4096]{0:T(1024)} %param.32) | copy-start | bytes 49156
  767.6 83.6 %all-gather.11.cloned.1.call-start = ((), (), s32[]{:S(2)}) async-start(), calls=%async_computation.7 | async-start | bytes 1966080 | tf_op jit(solution)/shard_map/all_gather | solution.py:171
  821.2 85.1 %reduce-scatter.10.cloned.1.call-start = ((), (), s32[]{:S(2)}) async-start(), calls=%async_computation.8 | async-start | bytes 1966080
  854.9 7.6 copy-start.16
  854.9 16.1 %slice-start = ((s8[14680064]{0:T(1024)(128)(4,1)}), s8[4194304]{0:T(1024)(128)(4,1)S(1)}, s32[]{:S(2)}) async-start(s8[14680064]{0:T(1024)(128)(4,1)} %bitcast.168), calls=%async_computation.9 | async-start | bytes 8388608
  854.9 16.1 %slice-start.1 = ((s8[14680064]{0:T(1024)(128)(4,1)}), s8[4194304]{0:T(1024)(128)(4,1)S(1)}, s32[]{:S(2)}) async-start(s8[14680064]{0:T(1024)(128)(4,1)} %bitcast.168), calls=%async_computation.10 | async-start | bytes 8388608
  862.5 8.5 slice-start.2
  862.5 8.5 slice-start.3
  875.1 37.6 %copy-start.28 = (bf16[4096,8]{0,1:T(8,128)(2,1)S(1)}, bf16[4096,8]{0,1:T(8,128)(2,1)}, u32[]{:S(2)}) copy-start(bf16[4096,8]{0,1:T(8,128)(2,1)} %param.33) | copy-start | bytes 196612
  875.1 54.0 %copy-start.1 = (bf16[1024,288]{0,1:T(8,128)(2,1)S(1)}, bf16[1024,288]{0,1:T(8,128)(2,1)}, u32[]{:S(2)}) copy-start(bf16[1024,288]{0,1:T(8,128)(2,1)} %param.26) | copy-start | bytes 1769476
  908.2 20.0 %all-to-all-start.1 = ((bf16[1,8,6,4096]{3,2,0,1:T(8,128)(2,1)}), bf16[1,8,6,4096]{3,2,0,1:T(8,128)(2,1)S(1)}, u32[]{:S(2)}, u32[]{:S(2)}) async-start(bf16[1,8,6,4096]{3,2,0,1:T(8,128)(2,1)} %bitcast.40), calls=%async_computation.2 | async-start | bytes 1048576 | tf_op jit(solution)/shard_map/all_to_all | solution.py:176
  (47 other events, 89.1 us)
Sparse Core Ops, SparseCore 0:
  9.2 160.1 all-gather.6
  171.2 87.5 all-gather.8
  767.7 32.9 reduce-scatter.7
  821.3 29.7 all-gather.10
  875.3 30.9 reduce-scatter.9
where the time goes:
time: 950 us; the launch traced here: 936 us
  local copies, waits for them, and re-layouts  355 us (37%)
  waiting for transfers between devices  271 us (29%)
  other arithmetic  177 us (19%)
  blocking collectives  66.6 us (7%)
  matrix products  43 us (5%)
  between operations  13.7 us (1%)
    pad x96, local copies, waits for them, and re-layouts, advance(): lax.associative_scan(scan_pairs, (decay_step, inject), axis=0)  282 us
    all_gather x1, waiting for transfers between devices, local(): pieces = lax.all_gather(in_weight, 'seq', axis=0, tiled=True)  160 us
    add x48, other arithmetic, advance(): lax.associative_scan(scan_pairs, (decay_step, inject), axis=0)  58.8 us
    concatenate x48, other arithmetic, advance(): lax.associative_scan(scan_pairs, (decay_step, inject), axis=0)  40.5 us
    add x42, other arithmetic, scan_pairs(): return (former[0] * latter[0], latter[0] * former[1] + latter[1])  34.3 us
    unnamed x6, waiting for transfers between devices  32.6 us
    reduce_scatter x1, waiting for transfers between devices, local(): lax.psum_scatter(partials, 'expert', scatter_dimension=0, tiled=True)  32.3 us
    all_gather x1, waiting for transfers between devices, local(): lax.all_gather(arrived, 'seq', axis=1, tiled=True)  29.9 us
  transfers between devices with their start and end apart: 7, of which 6 were waited for; matrix products, arithmetic and copies ran while one was open for 57% of the time, Pallas kernels for 0%

commit v1 on v0

v1 whole, which is shorter than its diff:
```python
import functools

import jax
import jax.numpy as jnp
from jax import lax
from jax.experimental import pallas as pl
from jax.experimental.pallas import tpu as pltpu
from jax.sharding import PartitionSpec as P

EPSILON = 1e-06
HALO = 16
MIB = 1 << 20
BF16 = jnp.bfloat16
F32 = jnp.float32

VMEM = pl.BlockSpec(memory_space=pltpu.VMEM)
SMEM = pl.BlockSpec(memory_space=pltpu.SMEM)


def partner(block, axis, mask):
    size = lax.axis_size(axis)
    return lax.ppermute(block, axis, [(i, i ^ mask) for i in range(size)])


def later_partner(block, axis, mask):
    size = lax.axis_size(axis)
    return lax.ppermute(block, axis, [(i, i ^ mask) for i in range(size) if i < i ^ mask])


def after(values, *done):
    flat, tree = jax.tree.flatten(values)
    held = lax.optimization_barrier((*flat, *done))
    return jax.tree.unflatten(tree, held[: len(flat)])


def shape(dims, dtype):
    return jax.ShapeDtypeStruct(tuple(dims), dtype)


def kernel_call(body, outs, in_specs, scratch=(), flops=0, moved=0, limit=32):
    return pl.pallas_call(
        body,
        out_shape=outs,
        in_specs=in_specs,
        out_specs=jax.tree.map(lambda _: VMEM, outs),
        scratch_shapes=list(scratch),
        compiler_params=pltpu.CompilerParams(vmem_limit_bytes=limit * MIB),
        cost_estimate=pl.CostEstimate(flops=flops, bytes_accessed=moved, transcendentals=0),
    )


def dot(left, right):
    return jnp.dot(left, right, preferred_element_type=F32)


def silu(v):
    return v / (1.0 + jnp.exp(-v))


def norm_body(seq, place, tokens, gain, own, *sends):
    values = tokens[...].astype(F32)
    inverse = lax.rsqrt(jnp.mean(values * values, axis=-1, keepdims=True) + EPSILON)
    own_width = own.shape[1]
    half = own_width // 2
    me, core = place[0], place[1]

    def columns(start, width):
        start = pl.multiple_of(start, 128)
        part = tokens[:, pl.ds(start, width)].astype(F32)
        return (part * inverse * gain[:, pl.ds(start, width)]).astype(BF16)

    own[...] = columns(me * own_width, own_width)
    for mask in range(1, seq):
        sends[mask - 1][...] = columns((me ^ mask) * own_width + core * half, half)


def project(x_own, x_mine, x_other, weight, core):
    half = weight.shape[0] // 2
    yield dot(x_own[...], weight[...])
    first = weight[pl.ds(pl.multiple_of(core * half, half), half), :]
    second = weight[pl.ds(pl.multiple_of((1 - core) * half, half), half), :]
    for mine, other in zip(x_mine, x_other):
        yield dot(mine[...], first) + dot(other[...], second)


def mixer_project_body(seq, place, x_own, *refs):
    x_mine, x_other = refs[: seq - 1], refs[seq - 1 : 2 * seq - 2]
    weight = refs[2 * seq - 2]
    outs = refs[2 * seq - 1 : 3 * seq - 1]
    tails = refs[3 * seq - 1]
    me, core = place[0], place[1]
    length = x_own.shape[0]
    for index, product in enumerate(project(x_own, x_mine, x_other, weight, core)):
        outs[index][HALO:, :] = product.astype(outs[index].dtype)
        tails[index] = product[length - HALO :, :]
    for mask in range(seq):
        shard = me ^ mask
        source = me ^ jnp.maximum(shard - 1, 0)
        before = jnp.where(shard > 0, tails[source], 0.0)
        outs[mask][:HALO, :] = before.astype(outs[mask].dtype)


def gate_project_body(seq, place, x_own, *refs):
    x_mine, x_other = refs[: seq - 1], refs[seq - 1 : 2 * seq - 2]
    weight = refs[2 * seq - 2]
    outs = refs[2 * seq - 1 :]
    for index, product in enumerate(project(x_own, x_mine, x_other, weight, place[1])):
        outs[index][...] = product.astype(outs[index].dtype)


def conv_body(seq, *refs):
    terms = refs[:seq]
    taps, bias, proj, activated, features = refs[seq:]
    total = terms[0][...]
    for term in terms[1:]:
        total = total + term[...].astype(F32)
    padded = total.astype(BF16).astype(F32)
    length = activated.shape[0]
    count = taps.shape[0]
    convolved = bias[...]
    for tap in range(count):
        start = HALO - count + 1 + tap
        convolved = convolved + taps[tap : tap + 1, :] * padded[start : start + length]
    rounded = silu(convolved).astype(BF16)
    activated[...] = rounded
    features[...] = dot(rounded, proj[...])


def scan_body(maps, low_rank, activated, step_weight, step_bias, rate, y, cumulated, final, steps, drive):
    length, groups, lanes = y.shape
    states = rate.shape[0]
    raw = dot(low_rank[...], step_weight[...]) + step_bias[...]
    step_size = jnp.maximum(raw, 0.0) + jnp.log1p(jnp.exp(-jnp.abs(raw)))
    driven = step_size * activated[...].astype(F32)
    for group in range(groups):
        part = slice(group * lanes, (group + 1) * lanes)
        steps[:, group, :] = step_size[:, part]
        drive[:, group, :] = driven[:, part]
    rates = [rate[n] for n in range(states)]

    def advance(t, carry):
        state, running = carry
        step, push = steps[t], drive[t]
        running = running + step
        fresh = []
        out = jnp.zeros_like(step)
        for n in range(states):
            value = jnp.exp(step * rates[n]) * state[n] + push * maps[t, n]
            out = out + value * maps[t, states + n]
            fresh.append(value)
        y[t] = out
        cumulated[t] = running
        return tuple(fresh), running

    zero = jnp.zeros((groups, lanes), F32)
    state, running = lax.fori_loop(0, length, advance, ((zero,) * states, zero), unroll=4)
    for n in range(states):
        final[n] = state[n]
    final[states] = running


def gated_body(seq, own_rows, place, maps, *refs):
    arrived = refs[: seq - 1]
    y, cumulated, rate, activated, skip_gain = refs[seq - 1 : seq + 4]
    gates = refs[seq + 4 : 2 * seq + 4]
    gated, scanned, result = refs[2 * seq + 4 :]
    length, groups, lanes = y.shape
    states = rate.shape[0]
    me, expert = place[0], place[2]
    zero = jnp.zeros((groups, lanes), F32)
    incoming = [zero] * states
    for mask in range(1, seq):
        shard = me ^ mask
        between = zero
        for other in range(1, seq):
            middle = me ^ other
            inside = (shard < middle) & (middle < me)
            between = between + jnp.where(inside, arrived[other - 1][states], 0.0)
        for n in range(states):
            term = jnp.exp(rate[n] * between) * arrived[mask - 1][n]
            incoming[n] = incoming[n] + jnp.where(shard < me, term, 0.0)
    rates = [rate[n] for n in range(states)]

    def correct(t, carry):
        steps = cumulated[t]
        out = y[t]
        for n in range(states):
            out = out + (jnp.exp(steps * rates[n]) * incoming[n]) * maps[t, states + n]
        scanned[t] = out
        return carry

    lax.fori_loop(0, length, correct, 0, unroll=4)
    for group in range(groups):
        part = slice(group * lanes, (group + 1) * lanes)
        gate = gates[0][:, part]
        for term in gates[1:]:
            gate = gate + term[:, part].astype(F32)
        gate = gate.astype(BF16).astype(F32)
        drive = activated[:, part].astype(F32)
        result[:, part] = (scanned[:, group, :] + skip_gain[:, part] * drive) * silu(gate)
    blocks = length // own_rows
    moved = [
        result[pl.ds(pl.multiple_of((expert ^ k) * own_rows, own_rows), own_rows), :]
        for k in range(blocks)
    ]
    gated[...] = jnp.concatenate(moved, axis=0).astype(BF16)


def out_project_body(seq, own_rows, *refs):
    blocks = refs[:seq]
    weight, keep, send = refs[seq:]
    for shard in range(seq):
        product = dot(blocks[shard][...], weight[...])
        for owner in range(product.shape[0] // own_rows):
            rows = product[owner * own_rows : (owner + 1) * own_rows]
            place = (owner // 2, pl.ds(shard * own_rows, own_rows))
            if owner % 2 == 0:
                keep[place[0], place[1], :] = rows
            else:
                send[place[0], place[1], :] = rows.astype(BF16)


def core_sum_body(keep, arrived, own, *sends):
    own[...] = keep[0] + arrived[0].astype(F32)
    for w in range(1, keep.shape[0]):
        sends[w - 1][...] = (keep[w] + arrived[w].astype(F32)).astype(BF16)


def hidden_body(chips, own, *refs):
    terms = refs[: chips - 1]
    residual, choose, hidden = refs[chips - 1 : chips + 2]
    outs = refs[chips + 2 :]
    total = own[...]
    for term in terms:
        total = total + term[...].astype(F32)
    rounded = (residual[...].astype(F32) + total).astype(BF16)
    hidden[...] = rounded
    slots = dot(choose[...], rounded).astype(BF16)
    rows = slots.shape[0] // chips
    for w in range(chips):
        outs[w][...] = slots[w * rows : (w + 1) * rows]


def expert_body(seq, place, *refs):
    pieces = refs[:seq]
    gain, gate, up, hidden, rows = refs[seq:]
    width = pieces[0].shape[1]

    @pl.when(pl.program_id(0) == 0)
    def _():
        square = jnp.zeros((pieces[0].shape[0], 1), F32)
        for piece in pieces:
            values = piece[...].astype(F32)
            square = square + jnp.sum(values * values, axis=-1, keepdims=True)
        inverse = lax.rsqrt(square / (seq * width) + EPSILON)
        for mask in range(seq):
            start = pl.multiple_of((place[0] ^ mask) * width, 128)
            scaled = pieces[mask][...].astype(F32) * inverse * gain[:, pl.ds(start, width)]
            rows[:, pl.ds(start, width)] = scaled.astype(BF16)

    gate_act = dot(rows[...], gate[...])
    up_act = dot(rows[...], up[...])
    hidden[...] = (silu(gate_act) * up_act).astype(BF16)


def down_body(place, hidden, down, out):
    out[...] = dot(hidden[...], down[...]).astype(BF16)


def expert_sum_body(seq, *refs):
    terms, outs = refs[:seq], refs[seq:]
    total = terms[0][...].astype(F32)
    for term in terms[1:]:
        total = total + term[...].astype(F32)
    rounded = total.astype(BF16)
    rows = rounded.shape[0] // len(outs)
    for w, out in enumerate(outs):
        out[...] = rounded[w * rows : (w + 1) * rows]


def combine_body(chips, seq, *refs):
    direct = refs[:chips]
    crossed, hidden, first, second, shares = refs[chips : chips + 5]
    outs = refs[chips + 5 :]
    half = crossed.shape[1]
    table = jnp.concatenate(
        [block for w in range(chips) for block in (direct[w][:half, :], crossed[w])], axis=0
    )
    picked = shares[:, 0:1] * dot(first[...], table) + shares[:, 1:2] * dot(second[...], table)
    mixed = (hidden[...].astype(F32) + picked).astype(BF16)
    rows = mixed.shape[0] // seq
    for d, out in enumerate(outs):
        out[...] = mixed[d * rows : (d + 1) * rows]


def place_body(place, *refs):
    pieces, out = refs[:-1], refs[-1]
    width = pieces[0].shape[1]
    for mask, piece in enumerate(pieces):
        out[:, pl.ds(pl.multiple_of((place[0] ^ mask) * width, 128), width)] = piece[...]


def tile_of(total, most):
    for width in range(most, 0, -128):
        if total % width == 0:
            return width
    return total


def local(
    tokens,
    norm_gain,
    in_weight,
    conv_weight,
    conv_bias,
    proj_weight,
    step_weight,
    step_bias,
    decay_log,
    skip_gain,
    out_weight,
    moe_gain,
    router_weight,
    routes,
    gate_weight,
    up_weight,
    down_weight,
):
    seq, groups = lax.axis_size("seq"), lax.axis_size("expert")
    chips = groups // 2
    me, expert = lax.axis_index("seq"), lax.axis_index("expert")
    core = expert % 2
    place = jnp.stack([me, core, expert]).astype(jnp.int32)
    masks = range(1, seq)
    length, model_width = tokens.shape
    width = model_width // seq
    half = width // 2
    channels = in_weight.shape[2]
    rank_width = step_weight.shape[0]
    state_width = decay_log.shape[1]
    lanes = 128
    tiles = channels // lanes
    own_rows = routes.shape[0]
    experts = router_weight.shape[1]
    most_slots = max(2, 3 * own_rows // experts)
    window = seq * own_rows

    x_own, *x_send = kernel_call(
        functools.partial(norm_body, seq),
        [shape((length, width), BF16)] + [shape((length, half), BF16)] * (seq - 1),
        [SMEM, VMEM, VMEM],
        flops=8 * length * model_width,
        moved=4 * length * model_width,
    )(place, tokens, norm_gain[None])
    x_mine = [partner(block, "seq", mask) for mask, block in zip(masks, x_send)]
    x_other = [partner(block, "expert", 1) for block in x_mine]
    mixer_weight, side_weight = in_weight[:, 0, :], in_weight[:, 1, :]
    in_specs = [SMEM] + [VMEM] * (2 * seq)
    cost = dict(flops=2 * seq * length * width * channels, moved=2 * width * channels)
    mixer_own, *mixer_send = kernel_call(
        functools.partial(mixer_project_body, seq),
        [shape((HALO + length, channels), F32)] + [shape((HALO + length, channels), BF16)] * (seq - 1),
        in_specs,
        [pltpu.VMEM((seq, HALO, channels), F32)],
        **cost,
    )(place, x_own, *x_mine, *x_other, mixer_weight)
    mixer_terms = [partner(block, "seq", mask) for mask, block in zip(masks, mixer_send)]
    side_own, *side_send = kernel_call(
        functools.partial(gate_project_body, seq),
        [shape((length, channels), F32)] + [shape((length, channels), BF16)] * (seq - 1),
        in_specs,
        **cost,
    )(place, x_own, *x_mine, *x_other, side_weight)
    side_send = after(side_send, *mixer_terms)
    side_terms = [partner(block, "seq", mask) for mask, block in zip(masks, side_send)]

    activated, features = kernel_call(
        functools.partial(conv_body, seq),
        [shape((length, channels), BF16), shape((length, proj_weight.shape[1]), F32)],
        [VMEM] * (seq + 3),
        flops=2 * length * channels * proj_weight.shape[1] + 16 * length * channels,
        moved=2 * channels * proj_weight.shape[1] + 10 * length * channels,
    )(mixer_own, *mixer_terms, conv_weight, conv_bias[None], proj_weight)
    features = features + partner(features, "expert", 1)
    sent = features.astype(BF16)
    for w in range(1, chips):
        features = features + partner(sent, "expert", 2 * w).astype(F32)
    low_rank, maps = features[:, :rank_width].astype(BF16), features[:, rank_width:]

    rate = -jnp.exp(jnp.transpose(decay_log)).reshape(state_width, tiles, lanes)
    tiled = shape((length, tiles, lanes), F32)
    y, cumulated, final = kernel_call(
        scan_body,
        [tiled, tiled, shape((state_width + 1, tiles, lanes), F32)],
        [SMEM] + [VMEM] * 5,
        [pltpu.VMEM(tiled.shape, F32)] * 2,
        flops=8 * length * channels * state_width,
        moved=12 * length * channels,
    )(maps, low_rank, activated, step_weight, step_bias[None], rate)
    arrived = [later_partner(final, "seq", mask) for mask in masks]
    gated = kernel_call(
        functools.partial(gated_body, seq, own_rows),
        shape((length, channels), BF16),
        [SMEM, SMEM] + [VMEM] * (2 * seq + 4),
        [pltpu.VMEM(tiled.shape, F32), pltpu.VMEM((length, channels), F32)],
        flops=8 * length * channels * state_width,
        moved=16 * length * channels,
    )(place, maps, *arrived, y, cumulated, rate, activated, skip_gain[None], side_own, *side_terms)

    others = after((routes, tokens), *side_terms)
    near_routes = jnp.stack(
        [others[0]] + [partner(others[0], "seq", mask) for mask in masks]
    )
    own_tokens = lax.dynamic_slice_in_dim(others[1], expert * own_rows, own_rows, 0)
    residual = jnp.concatenate(
        [lax.dynamic_slice_in_dim(own_tokens, me * width, width, 1)]
        + [
            partner(lax.dynamic_slice_in_dim(own_tokens, (me ^ mask) * width, width, 1), "seq", mask)
            for mask in masks
        ],
        axis=0,
    )
    ids = expert ^ jnp.arange(groups, dtype=jnp.int32)
    named = near_routes[None] == ids[:, None, None, None]
    either = named[..., 0] | named[..., 1]
    earlier = jnp.arange(own_rows)[:, None] > jnp.arange(own_rows)[None, :]
    before = jnp.sum((either[:, :, None, :] & earlier).astype(jnp.int32), axis=-1)
    shards = me ^ jnp.arange(seq, dtype=jnp.int32)
    slot = jnp.arange(most_slots, dtype=jnp.int32)
    fits = (
        (jnp.arange(seq)[None, :, None, None, None] == shards[None, None, None, :, None])
        & (before[:, None, None] == slot[None, None, :, None, None])
    )
    slots = groups * seq * most_slots
    choose = (fits & either[:, None, None]).reshape(slots, window).astype(BF16)
    first = (fits & named[:, None, None, :, :, 0]).reshape(slots, window).astype(BF16).T
    second = (fits & named[:, None, None, :, :, 1]).reshape(slots, window).astype(BF16).T

    blocks = [gated] + [partner(gated, "seq", mask) for mask in masks]
    keep, send = kernel_call(
        functools.partial(out_project_body, seq, own_rows),
        [shape((chips, window, width), F32), shape((chips, window, width), BF16)],
        [VMEM] * (seq + 1),
        flops=2 * seq * length * channels * width,
        moved=2 * channels * width + 8 * seq * length * width,
    )(*blocks, out_weight)
    crossing = partner(send, "expert", 1)
    own_sum, *chip_sends = kernel_call(
        core_sum_body,
        [shape((window, width), F32)] + [shape((window, width), BF16)] * (chips - 1),
        [VMEM] * 2,
        flops=chips * window * width,
        moved=10 * chips * window * width,
    )(keep, crossing)
    chip_terms = [partner(block, "expert", 2 * w) for w, block in zip(range(1, chips), chip_sends)]
    per_chip = slots // chips
    per_group = slots // groups
    hidden_state, *outgoing = kernel_call(
        functools.partial(hidden_body, chips),
        [shape((window, width), BF16)] + [shape((per_chip, width), BF16)] * chips,
        [VMEM] * (chips + 2),
        flops=2 * slots * window * width,
        moved=10 * window * width,
    )(own_sum, *chip_terms, residual, choose)

    came = [outgoing[0]] + [
        partner(block, "expert", 2 * w) for w, block in zip(range(1, chips), outgoing[1:])
    ]
    crossed = partner(jnp.stack([block[per_group:] for block in came]), "expert", 1)
    rows = jnp.concatenate(
        [piece for w in range(chips) for piece in (came[w][:per_group], crossed[w])], axis=0
    )
    pieces = [rows] + [partner(rows, "seq", mask) for mask in masks]

    hidden_units = gate_weight.shape[2]
    tile = tile_of(hidden_units, 256)
    hidden = pl.pallas_call(
        functools.partial(expert_body, seq),
        out_shape=shape((slots, hidden_units), BF16),
        grid=(hidden_units // tile,),
        in_specs=[SMEM]
        + [pl.BlockSpec((slots, width), lambda i: (0, 0))] * seq
        + [pl.BlockSpec((1, model_width), lambda i: (0, 0))]
        + [pl.BlockSpec((None, model_width, tile), lambda i: (0, 0, i))] * 2,
        out_specs=pl.BlockSpec((slots, tile), lambda i: (0, i)),
        scratch_shapes=[pltpu.VMEM((slots, model_width), BF16)],
        compiler_params=pltpu.CompilerParams(vmem_limit_bytes=40 * MIB),
        cost_estimate=pl.CostEstimate(
            flops=4 * slots * model_width * hidden_units,
            bytes_accessed=4 * model_width * hidden_units,
            transcendentals=0,
        ),
    )(place, *pieces, moe_gain[None], gate_weight, up_weight)
    expert_out = pl.pallas_call(
        down_body,
        out_shape=shape((seq, slots, width), BF16),
        grid_spec=pltpu.PrefetchScalarGridSpec(
            num_scalar_prefetch=1,
            grid=(seq,),
            in_specs=[
                pl.BlockSpec((slots, hidden_units), lambda i, place: (0, 0)),
                pl.BlockSpec((None, hidden_units, width), lambda i, place: (0, 0, place[0] ^ i)),
            ],
            out_specs=pl.BlockSpec((None, slots, width), lambda i, place: (i, 0, 0)),
        ),
        compiler_params=pltpu.CompilerParams(vmem_limit_bytes=32 * MIB),
        cost_estimate=pl.CostEstimate(
            flops=2 * slots * model_width * hidden_units,
            bytes_accessed=2 * model_width * hidden_units,
            transcendentals=0,
        ),
    )(place, hidden, down_weight)
    terms = [expert_out[0]] + [partner(expert_out[mask], "seq", mask) for mask in masks]
    answers = kernel_call(
        functools.partial(expert_sum_body, seq),
        [shape((per_chip, width), BF16)] * chips,
        [VMEM] * seq,
        flops=seq * slots * width,
        moved=10 * slots * width,
    )(*terms)
    answers = [answers[0]] + [
        partner(block, "expert", 2 * w) for w, block in zip(range(1, chips), answers[1:])
    ]
    crossed_back = partner(jnp.stack([block[per_group:] for block in answers]), "expert", 1)

    values = hidden_state.astype(F32)
    square = jnp.sum(values * values, axis=-1)
    square = seq_sum_by_shard(square.reshape(seq, own_rows), masks, me)
    inverse = lax.rsqrt(square / model_width + EPSILON).reshape(window, 1)
    own_gain = lax.dynamic_slice_in_dim(moe_gain, me * width, width, 0)
    moe_in = (values * inverse * own_gain).astype(BF16)
    own_router = lax.dynamic_slice_in_dim(router_weight, me * width, width, 0)
    logits = dot(moe_in, own_router).reshape(seq, own_rows, experts)
    logits = seq_sum_by_shard(logits, masks, me)
    matches = near_routes[..., None] == jnp.arange(experts, dtype=jnp.int32)
    picked = jnp.sum(jnp.where(matches, logits[:, :, None, :], 0.0), axis=-1)
    first_share = jax.nn.sigmoid(picked[..., 0] - picked[..., 1])
    shares = jnp.stack([first_share, 1.0 - first_share], axis=-1).reshape(window, 2)

    mixed_own, *mixed_send = kernel_call(
        functools.partial(combine_body, chips, seq),
        [shape((own_rows, width), BF16)] * seq,
        [VMEM] * (chips + 5),
        flops=4 * slots * window * width,
        moved=8 * slots * width,
    )(*answers, crossed_back, hidden_state, first, second, shares)
    mixed = [mixed_own] + [partner(block, "seq", mask) for mask, block in zip(masks, mixed_send)]
    return kernel_call(
        place_body,
        shape((own_rows, model_width), BF16),
        [SMEM] + [VMEM] * seq,
        flops=0,
        moved=4 * own_rows * model_width,
    )(place, *mixed)


def seq_sum_by_shard(blocks, masks, me):
    total = blocks
    for mask in masks:
        other = partner(blocks, "seq", mask)
        total = total + jnp.stack([other[d ^ mask] for d in range(blocks.shape[0])])
    return total


def solution(mesh):
    in_specs = (
        P("seq", None),
        P(),
        P("seq", None, "expert"),
        P(None, "expert"),
        P("expert"),
        P("expert", None),
        P(None, "expert"),
        P("expert"),
        P("expert", None),
        P("expert"),
        P("expert", "seq"),
        P(),
        P(),
        P(("seq", "expert"), None),
        P("expert", None, "seq"),
        P("expert", None, "seq"),
        P("expert", "seq", None),
    )
    out_specs = P(("seq", "expert"), None)
    return jax.shard_map(local, mesh=mesh, in_specs=in_specs, out_specs=out_specs, check_vma=False)
```

time: 950 us -> 227 us (0.24); the launches traced: 936 us -> 226 us
  local copies, waits for them, and re-layouts: 355 us -> 29.8 us
  waiting for transfers between devices: 271 us -> 84.5 us
  other arithmetic: 177 us -> 5.45 us
  blocking collectives: 66.6 us -> 0 us
  starting transfers between devices: 8.16 us -> 65.9 us
  matrix products: 43 us -> 0.22 us
  Pallas kernels: 0 us -> 39.8 us
  between operations: 13.7 us -> 0.75 us
    pad x98 -> x0, local copies, waits for them, and re-layouts: 282 us -> none  [the longest x96 282 us: advance(): lax.associative_scan(scan_pairs, (decay_step, inject), axis=0)]
    all_gather x3 -> x0, waiting for transfers between devices: 190 us -> none  [the longest x1 160 us: local(): pieces = lax.all_gather(in_weight, 'seq', axis=0, tiled=True)]
    add x100 -> x2, other arithmetic: 109 us -> 1.09 us  [the longest x1 1.03 us: local(): features = features + partner(sent, 'expert', 2 * w).astype(F32)]
    ppermute x1 -> x55, waiting for transfers between devices: 1.28 us -> 84.5 us  [the longest x52 84.4 us: partner(): return lax.ppermute(block, axis, [(i, i ^ mask) for i in range(size)])]
    ppermute x1 -> x55, starting transfers between devices: 3.39 us -> 65.9 us  [the longest x52 58.6 us: partner(): return lax.ppermute(block, axis, [(i, i ^ mask) for i in range(size)])]
    dot_general x26 -> x1, matrix products: 43 us -> 0.22 us  [dot(): return jnp.dot(left, right, preferred_element_type=F32)]
    concatenate x49 -> x1, other arithmetic: 40.5 us -> 0.01 us  [local(): jnp.concatenate([lax.dynamic_slice_in_dim(own_tokens, me * width, width,...]
    pallas_call x0 -> x14, Pallas kernels: none -> 39.8 us  [the longest x1 14.2 us: local(): pl.pallas_call(functools.partial(expert_body, seq), out_shape=shape((slot...]
  transfers between devices with their start and end apart: 7 -> 55, of which waited for: 6 -> 25; matrix products, arithmetic and copies ran while one was open for 57% -> 10% of each run, Pallas kernels for 0% -> 15%
where the time goes in v1:
time: 227 us; the launch traced here: 226 us
  waiting for transfers between devices  84.5 us (37%)
  starting transfers between devices  65.9 us (29%)
  Pallas kernels  39.8 us (18%)
  local copies, waits for them, and re-layouts  29.8 us (13%)
  other arithmetic  5.45 us (2%)
    ppermute x52, waiting for transfers between devices, partner(): return lax.ppermute(block, axis, [(i, i ^ mask) for i in range(size)])  84.4 us
    ppermute x52, starting transfers between devices, partner(): return lax.ppermute(block, axis, [(i, i ^ mask) for i in range(size)])  58.6 us
    unnamed x48, local copies, waits for them, and re-layouts  14.9 us
    pallas_call x1, Pallas kernels, local(): pl.pallas_call(functools.partial(expert_body, seq), out_shape=shape((slot...  14.2 us
    slice x1, local copies, waits for them, and re-layouts, local(): mixer_weight, side_weight = (in_weight[:, 0, :], in_weight[:, 1, :])  8.87 us
    ppermute x3, starting transfers between devices, later_partner(): lax.ppermute(block, axis, [(i, i ^ mask) for i in range(size) if i < i ^...  7.35 us
    pallas_call x1, Pallas kernels, local(): kernel_call(scan_body, [tiled, tiled, shape((state_width + 1, tiles, lane...  5.65 us
    pallas_call x1, Pallas kernels, local(): pl.pallas_call(down_body, out_shape=shape((seq, slots, width), BF16), gri...  5.16 us
  transfers between devices with their start and end apart: 55, of which 25 were waited for; matrix products, arithmetic and copies ran while one was open for 10% of the time, Pallas kernels for 15%

profile of v1, /device:TPU:0, one launch (start us, length us, event | category | flops | bytes accessed | tf_op | source)
XLA Modules:
  0.0 226.4 jit_solution(5131984054745670183)
XLA Ops:
  0.1 1.2 copy-done.4
  3.0 3.0 %collective-permute-start = (bf16[128,512]{1,0:T(8,128)(2,1)S(1)}, bf16[128,512]{1,0:T(8,128)(2,1)S(1)}, u32[]{:S(2)}, u32[]{:S(2)}) collective-permute-start(bf16[128,512]{1,0:T(8,128)(2,1)S(1)} %get-tuple-element.47), channel_id=1, source_target_pairs={{0,8},{8,0},{16,24},{24,16},{1,9},{9,1},{17,25},{25,17},{2,10},{10... | collective-permute-start | bytes 393224 | tf_op jit(solution)/shard_map/ppermute | solution.py:22
  6.0 1.5 collective-permute-start.1
  7.5 8.9 %fusion.22 = (bf16[1024,1,1024]{2,1,0:T(2,128)(2,1)S(1)}, bf16[1024,1,1024]{2,1,0:T(2,128)(2,1)S(1)}) fusion(bf16[1024,2,1024]{2,1,0:T(2,128)(2,1)} %param.19), kind=kLoop, calls=%fused_computation.76 | loop fusion | bytes 8388608 | tf_op jit(solution)/shard_map/slice | solution.py:357
  17.1 3.0 %copy_bitcast_fusion = (bf16[1024,1024]{1,0:T(8,128)(2,1)S(1)}, bf16[1024,1024]{1,0:T(8,128)(2,1)}) fusion(bf16[1024,1,1024]{2,1,0:T(2,128)(2,1)S(1)} %get-tuple-element.91, bf16[1024,1,1024]{2,1,0:T(2,128)(2,1)S(1)} %get-tuple-element.92), kind=kLoop, calls=%fused_computation | loop fusion | bytes 8388608 | tf_op jit(solution)/shard_map/squeeze | solution.py:357
  20.1 1.4 copy.48.refs_6_
  21.7 1.6 copy-done.3
  23.2 2.4 %shard_map.164 = (f32[144,1024]{1,0:T(8,128)S(1)}, bf16[144,1024]{1,0:T(8,128)(2,1)S(1)}, bf16[144,1024]{1,0:T(8,128)(2,1)S(1)}, bf16[144,1024]{1,0:T(8,128)(2,1)S(1)}) custom-call(s32[3]{0:T(128)S(1)} %pad_add_fusion.1.place, bf16[128,1024]{1,0:T(8,128)(2,1)S(1)} %get-tuple-element.46.x_own, bf16[128,512]{1,0:T(8,128)(2,1)S(1)} %collective-permute-done.refs_0_, ...), custom_call_target="tpu_custom_call" | custom-call | flops 1073741824 | bytes 2097152 | tf_op jit(solution)/shard_map/pallas_call | solution.py:360
  25.7 2.0 collective-permute-start.6
  27.7 1.5 collective-permute-start.7
  29.2 1.5 negate_bitcast_fusion
  30.7 4.8 %collective-permute-done.6.refs_1_ = bf16[144,1024]{1,0:T(8,128)(2,1)S(1)} collective-permute-done((bf16[144,1024]{1,0:T(8,128)(2,1)S(1)}, bf16[144,1024]{1,0:T(8,128)(2,1)S(1)}, u32[]{:S(2)}, u32[]{:S(2)}) %collective-permute-start.6) | collective-permute-done | bytes 294944 | tf_op jit(solution)/shard_map/ppermute | solution.py:22
  35.5 7.5 %collective-permute-done.7.refs_2_ = bf16[144,1024]{1,0:T(8,128)(2,1)S(1)} collective-permute-done((bf16[144,1024]{1,0:T(8,128)(2,1)S(1)}, bf16[144,1024]{1,0:T(8,128)(2,1)S(1)}, u32[]{:S(2)}, u32[]{:S(2)}) %collective-permute-start.7) | collective-permute-done | bytes 294944 | tf_op jit(solution)/shard_map/ppermute | solution.py:22
  44.0 1.4 collective-permute-done.9
  46.1 1.6 collective-permute-start.10
  50.5 2.8 %shard_map.167 = (f32[128,1024]{1,0:T(8,128)S(1)}, bf16[128,1024]{1,0:T(8,128)(2,1)}, bf16[128,1024]{1,0:T(8,128)(2,1)}, bf16[128,1024]{1,0:T(8,128)(2,1)S(1)}) custom-call(s32[3]{0:T(128)S(1)} %pad_add_fusion.1.place, bf16[128,1024]{1,0:T(8,128)(2,1)S(1)} %copy-done.14, bf16[128,512]{1,0:T(8,128)(2,1)S(1)} %copy-done.16, bf16[128,512]{1,0:T(8,128)(2,1)S(1)} %copy-done.18, ...), custom_call_target="tpu_custom_call" | custom-call | flops 1073741824 | bytes 2097152 | tf_op jit(solution)/shard_map/pallas_call | solution.py:368
  53.3 1.2 collective-permute-start.16
  55.3 1.4 collective-permute-start.18
  56.8 2.6 %collective-permute-start.11 = (bf16[128,288]{1,0:T(8,128)(2,1)}, bf16[128,288]{1,0:T(8,128)(2,1)S(1)}, u32[]{:S(2)}, u32[]{:S(2)}) collective-permute-start(bf16[128,288]{1,0:T(8,128)(2,1)} %get-tuple-element.89), channel_id=1, source_target_pairs={{0,4},{1,5},{2,6},{3,7},{4,0},{5,1},{6,2},{7,3},{8,12},{9,13},{10,... | collective-permute-start | bytes 221192 | tf_op jit(solution)/shard_map/ppermute | solution.py:22
  60.4 6.3 %collective-permute-done.11 = bf16[128,288]{1,0:T(8,128)(2,1)S(1)} collective-permute-done((bf16[128,288]{1,0:T(8,128)(2,1)}, bf16[128,288]{1,0:T(8,128)(2,1)S(1)}, u32[]{:S(2)}, u32[]{:S(2)}) %collective-permute-start.11) | collective-permute-done | bytes 73760 | tf_op jit(solution)/shard_map/ppermute | solution.py:22
  68.9 5.6 %shard_map.166 = (f32[128,8,128]{2,1,0:T(8,128)S(1)}, f32[128,8,128]{2,1,0:T(8,128)S(1)}, f32[17,8,128]{2,1,0:T(8,128)S(1)}) custom-call(f32[128,32]{1,0:T(8,128)S(1)} %slice.203.maps, bf16[128,256]{1,0:T(8,128)(2,1)S(1)} %slice.279.low_rank, bf16[128,1024]{1,0:T(8,128)(2,1)S(1)} %get-tuple-element.55.activated.refs_6_, bf16[256,1024]{1,0:T(8,128)(2,1)S(1)} %copy-done.5, ...), custom_call_target="tpu_custom_call" | custom-call | flops 16777216 | bytes 1572864 | tf_op jit(solution)/shard_map/pallas_call | solution.py:392
  74.5 3.1 %collective-permute-start.13 = (f32[17,8,128]{2,1,0:T(8,128)S(1)}, f32[17,8,128]{2,1,0:T(8,128)S(1)}, u32[]{:S(2)}, u32[]{:S(2)}) collective-permute-start(f32[17,8,128]{2,1,0:T(8,128)S(1)} %get-tuple-element.56), channel_id=1, source_target_pairs={{0,8},{16,24},{1,9},{17,25},{2,10},{18,26},{3,11},{19,27},{4,12},{... | collective-permute-start | bytes 208904 | tf_op jit(solution)/shard_map/ppermute | solution.py:27
  77.7 2.8 %collective-permute-start.14 = (f32[17,8,128]{2,1,0:T(8,128)S(1)}, f32[17,8,128]{2,1,0:T(8,128)S(1)}, u32[]{:S(2)}, u32[]{:S(2)}) collective-permute-start(f32[17,8,128]{2,1,0:T(8,128)S(1)} %get-tuple-element.56), channel_id=1, source_target_pairs={{0,16},{8,24},{1,17},{9,25},{2,18},{10,26},{3,19},{11,27},{4,20},{... | collective-permute-start | bytes 208904 | tf_op jit(solution)/shard_map/ppermute | solution.py:27
  80.4 1.5 collective-permute-start.15
  81.9 1.5 collective-permute-start.29
  84.5 1.2 collective-permute-done.29
  88.0 2.1 collective-permute-done.31
  91.1 4.6 %shard_map.168.refs_0_ = bf16[128,1024]{1,0:T(8,128)(2,1)S(1)} custom-call(s32[3]{0:T(128)S(1)} %pad_add_fusion.1.place, f32[128,32]{1,0:T(8,128)S(1)} %slice.203.maps, f32[17,8,128]{2,1,0:T(8,128)S(1)} %collective-permute-done.13.refs_0_, f32[17,8,128]{2,1,0:T(8,128)S(1)} %collective-permute-done.14.refs_1_, ...), custom_call_target="tpu_custom_call" | custom-call | flops 16777216 | bytes 2097152 | tf_op jit(solution)/shard_map/pallas_call | solution.py:401
  96.3 1.9 collective-permute-start.20
  99.4 2.8 %collective-permute-done.19.refs_1_ = bf16[128,1024]{1,0:T(8,128)(2,1)S(1)} collective-permute-done((bf16[128,1024]{1,0:T(8,128)(2,1)S(1)}, bf16[128,1024]{1,0:T(8,128)(2,1)S(1)}, u32[]{:S(2)}, u32[]{:S(2)}) %collective-permute-start.19) | collective-permute-done | bytes 262176 | tf_op jit(solution)/shard_map/ppermute | solution.py:22
  102.2 1.9 collective-permute-start.28
  105.5 1.3 shard_map.169
  107.6 1.2 collective-permute-done.22.arrived
  108.9 2.9 %collective-permute-start.23 = (bf16[64,1024]{1,0:T(8,128)(2,1)S(1)}, bf16[64,1024]{1,0:T(8,128)(2,1)S(1)}, u32[]{:S(2)}, u32[]{:S(2)}) collective-permute-start(bf16[64,1024]{1,0:T(8,128)(2,1)S(1)} %get-tuple-element.69), channel_id=1, source_target_pairs={{0,2},{1,3},{2,0},{3,1},{4,6},{5,7},{6,4},{7,5},{8,10},{9,11},{10,... | collective-permute-start | bytes 393224 | tf_op jit(solution)/shard_map/ppermute | solution.py:22
  112.9 1.4 collective-permute-start.25
  115.3 2.2 collective-permute-done.23.refs_0_
  117.5 7.2 %collective-permute-done.24.refs_1_ = bf16[64,1024]{1,0:T(8,128)(2,1)S(1)} collective-permute-done((bf16[64,1024]{1,0:T(8,128)(2,1)S(1)}, bf16[64,1024]{1,0:T(8,128)(2,1)S(1)}, u32[]{:S(2)}, u32[]{:S(2)}) %collective-permute-start.24) | collective-permute-done | bytes 131104 | tf_op jit(solution)/shard_map/ppermute | solution.py:22
  125.2 1.5 collective-permute-start.46
  127.5 1.2 collective-permute-start.48
  128.7 2.3 %collective-permute-start.34 = (bf16[48,1024]{1,0:T(8,128)(2,1)S(1)}, bf16[48,1024]{1,0:T(8,128)(2,1)S(1)}, u32[]{:S(2)}, u32[]{:S(2)}) collective-permute-start(bf16[48,1024]{1,0:T(8,128)(2,1)S(1)} %get-tuple-element.77), channel_id=1, source_target_pairs={{0,6},{1,7},{2,4},{3,5},{4,2},{5,3},{6,0},{7,1},{8,14},{9,15},{10,... | collective-permute-start | bytes 294920 | tf_op jit(solution)/shard_map/ppermute | solution.py:22
  131.0 1.5 collective-permute-start.33
  133.5 2.7 %collective-permute-done.34 = bf16[48,1024]{1,0:T(8,128)(2,1)S(1)} collective-permute-done((bf16[48,1024]{1,0:T(8,128)(2,1)S(1)}, bf16[48,1024]{1,0:T(8,128)(2,1)S(1)}, u32[]{:S(2)}, u32[]{:S(2)}) %collective-permute-start.34) | collective-permute-done | bytes 98336 | tf_op jit(solution)/shard_map/ppermute | solution.py:22
  136.2 2.6 %collective-permute-done.33 = bf16[48,1024]{1,0:T(8,128)(2,1)S(1)} collective-permute-done((bf16[48,1024]{1,0:T(8,128)(2,1)S(1)}, bf16[48,1024]{1,0:T(8,128)(2,1)S(1)}, u32[]{:S(2)}, u32[]{:S(2)}) %collective-permute-start.33) | collective-permute-done | bytes 98336 | tf_op jit(solution)/shard_map/ppermute | solution.py:22
  139.3 1.7 collective-permute-start.51
  141.0 1.2 collective-permute-start.50
  142.9 1.5 collective-permute-start.36
  145.2 1.2 collective-permute-start.38
  146.5 8.5 %collective-permute-done.36.refs_1_ = bf16[192,1024]{1,0:T(8,128)(2,1)S(1)} collective-permute-done((bf16[192,1024]{1,0:T(8,128)(2,1)S(1)}, bf16[192,1024]{1,0:T(8,128)(2,1)S(1)}, u32[]{:S(2)}, u32[]{:S(2)}) %collective-permute-start.36) | collective-permute-done | bytes 393248 | tf_op jit(solution)/shard_map/ppermute | solution.py:22
  155.0 6.6 %collective-permute-done.37.refs_2_ = bf16[192,1024]{1,0:T(8,128)(2,1)S(1)} collective-permute-done((bf16[192,1024]{1,0:T(8,128)(2,1)S(1)}, bf16[192,1024]{1,0:T(8,128)(2,1)S(1)}, u32[]{:S(2)}, u32[]{:S(2)}) %collective-permute-start.37) | collective-permute-done | bytes 393248 | tf_op jit(solution)/shard_map/ppermute | solution.py:22
  161.5 1.6 collective-permute-done.38.refs_3_
  163.2 14.2 %shard_map.172.hidden = bf16[192,1792]{1,0:T(8,128)(2,1)S(1)} custom-call(s32[3]{0:T(128)S(1)} %pad_add_fusion.1.place, bf16[192,1024]{1,0:T(8,128)(2,1)S(1)} %fusion.10.refs_0_, bf16[192,1024]{1,0:T(8,128)(2,1)S(1)} %collective-permute-done.36.refs_1_, bf16[192,1024]{1,0:T(8,128)(2,1)S(1)} %collective-permute-done.37.refs_2_, ...), custom_call_target="tpu_custom_call" | custom-call | flops 5637144576 | bytes 29360128 | tf_op jit(solution)/shard_map/pallas_call | solution.py:477
  177.4 5.2 %copy-done.2 = bf16[1,1792,4096]{2,1,0:T(8,128)(2,1)S(1)} copy-done((bf16[1,1792,4096]{2,1,0:T(8,128)(2,1)S(1)}, bf16[1,1792,4096]{2,1,0:T(8,128)(2,1)}, u32[]{:S(2)}) %copy-start.2) | copy-done | bytes 14680088
  182.5 5.2 %shard_map.173 = bf16[4,192,1024]{2,1,0:T(8,128)(2,1)S(1)} custom-call(s32[3]{0:T(128)S(1)} %pad_add_fusion.1.place, bf16[192,1792]{1,0:T(8,128)(2,1)S(1)} %shard_map.172.hidden, bf16[1,1792,4096]{2,1,0:T(8,128)(2,1)S(1)} %copy-done.2), custom_call_target="tpu_custom_call" | custom-call | flops 2818572288 | bytes 14680064 | tf_op jit(solution)/shard_map/pallas_call | solution.py:494
  188.6 1.6 collective-permute-start.40
  190.2 1.2 collective-permute-start.41
  191.5 8.4 %collective-permute-done.39.refs_1_ = bf16[192,1024]{1,0:T(8,128)(2,1)S(1)} collective-permute-done((bf16[192,1024]{1,0:T(8,128)(2,1)S(1)}, bf16[192,1024]{1,0:T(8,128)(2,1)S(1)}, u32[]{:S(2)}, u32[]{:S(2)}) %collective-permute-start.39) | collective-permute-done | bytes 393248 | tf_op jit(solution)/shard_map/ppermute | solution.py:22
  199.9 6.7 %collective-permute-done.40.refs_2_ = bf16[192,1024]{1,0:T(8,128)(2,1)S(1)} collective-permute-done((bf16[192,1024]{1,0:T(8,128)(2,1)S(1)}, bf16[192,1024]{1,0:T(8,128)(2,1)S(1)}, u32[]{:S(2)}, u32[]{:S(2)}) %collective-permute-start.40) | collective-permute-done | bytes 393248 | tf_op jit(solution)/shard_map/ppermute | solution.py:22
  206.9 2.5 %collective-permute-start.44 = (bf16[48,1024]{1,0:T(8,128)(2,1)S(1)}, bf16[48,1024]{1,0:T(8,128)(2,1)S(1)}, u32[]{:S(2)}, u32[]{:S(2)}) collective-permute-start(bf16[48,1024]{1,0:T(8,128)(2,1)S(1)} %get-tuple-element.81), channel_id=1, source_target_pairs={{0,6},{1,7},{2,4},{3,5},{4,2},{5,3},{6,0},{7,1},{8,14},{9,15},{10,... | collective-permute-start | bytes 294920 | tf_op jit(solution)/shard_map/ppermute | solution.py:22
  209.4 1.9 collective-permute-start.42
  211.3 2.2 collective-permute-done.44.refs_3_
  213.5 2.4 %collective-permute-done.43.refs_2_ = bf16[48,1024]{1,0:T(8,128)(2,1)S(1)} collective-permute-done((bf16[48,1024]{1,0:T(8,128)(2,1)S(1)}, bf16[48,1024]{1,0:T(8,128)(2,1)S(1)}, u32[]{:S(2)}, u32[]{:S(2)}) %collective-permute-start.43) | collective-permute-done | bytes 98336 | tf_op jit(solution)/shard_map/ppermute | solution.py:22
  218.6 1.8 collective-permute-start.53
  222.5 2.7 %collective-permute-done.54.refs_3_ = bf16[16,1024]{1,0:T(8,128)(2,1)S(1)} collective-permute-done((bf16[16,1024]{1,0:T(8,128)(2,1)S(1)}, bf16[16,1024]{1,0:T(8,128)(2,1)S(1)}, u32[]{:S(2)}, u32[]{:S(2)}) %collective-permute-start.54) | collective-permute-done | bytes 32800 | tf_op jit(solution)/shard_map/ppermute | solution.py:22
  225.2 1.2 shard_map.176
  (175 shorter events, 31.3 us)
Async XLA Ops:
  0.0 139.0 %copy-start = (bf16[4096,8]{0,1:T(8,128)(2,1)S(1)}, bf16[4096,8]{0,1:T(8,128)(2,1)}, u32[]{:S(2)}) copy-start(bf16[4096,8]{0,1:T(8,128)(2,1)} %param.29) | copy-start | bytes 196612
  3.0 13.4 %collective-permute-start = (bf16[128,512]{1,0:T(8,128)(2,1)S(1)}, bf16[128,512]{1,0:T(8,128)(2,1)S(1)}, u32[]{:S(2)}, u32[]{:S(2)}) collective-permute-start(bf16[128,512]{1,0:T(8,128)(2,1)S(1)} %get-tuple-element.47), channel_id=1, source_target_pairs={{0,8},{8,0},{16,24},{24,16},{1,9},{9,1},{17,25},{25,17},{2,10},{10... | collective-permute-start | bytes 393224 | tf_op jit(solution)/shard_map/ppermute | solution.py:22
  6.0 10.5 %collective-permute-start.1 = (bf16[128,512]{1,0:T(8,128)(2,1)S(1)}, bf16[128,512]{1,0:T(8,128)(2,1)S(1)}, u32[]{:S(2)}, u32[]{:S(2)}) collective-permute-start(bf16[128,512]{1,0:T(8,128)(2,1)S(1)} %get-tuple-element.48), channel_id=1, source_target_pairs={{0,16},{8,24},{16,0},{24,8},{1,17},{9,25},{17,1},{25,9},{2,18},{10... | collective-permute-start | bytes 393224 | tf_op jit(solution)/shard_map/ppermute | solution.py:22
  7.5 9.5 %collective-permute-start.2 = (bf16[128,512]{1,0:T(8,128)(2,1)S(1)}, bf16[128,512]{1,0:T(8,128)(2,1)}, u32[]{:S(2)}, u32[]{:S(2)}) collective-permute-start(bf16[128,512]{1,0:T(8,128)(2,1)S(1)} %get-tuple-element.49), channel_id=1, source_target_pairs={{0,24},{8,16},{16,8},{24,0},{1,25},{9,17},{17,9},{25,1},{2,26},{10... | collective-permute-start | bytes 393224 | tf_op jit(solution)/shard_map/ppermute | solution.py:22
  16.4 5.1 %collective-permute-start.3 = (bf16[128,512]{1,0:T(8,128)(2,1)S(1)}, bf16[128,512]{1,0:T(8,128)(2,1)}, u32[]{:S(2)}, u32[]{:S(2)}) collective-permute-start(bf16[128,512]{1,0:T(8,128)(2,1)S(1)} %collective-permute-done.refs_0_), channel_id=1, source_target_pairs={{0,1},{1,0},{2,3},{3,2},{4,5},{5,4},{6,7},{7,6},{8,9},{9,8},{10,11... | collective-permute-start | bytes 393224 | tf_op jit(solution)/shard_map/ppermute | solution.py:22
  16.5 5.1 %collective-permute-start.4 = (bf16[128,512]{1,0:T(8,128)(2,1)S(1)}, bf16[128,512]{1,0:T(8,128)(2,1)}, u32[]{:S(2)}, u32[]{:S(2)}) collective-permute-start(bf16[128,512]{1,0:T(8,128)(2,1)S(1)} %collective-permute-done.1.refs_1_), channel_id=1, source_target_pairs={{0,1},{1,0},{2,3},{3,2},{4,5},{5,4},{6,7},{7,6},{8,9},{9,8},{10,11... | collective-permute-start | bytes 393224 | tf_op jit(solution)/shard_map/ppermute | solution.py:22
  17.0 4.6 %collective-permute-start.5 = (bf16[128,512]{1,0:T(8,128)(2,1)}, bf16[128,512]{1,0:T(8,128)(2,1)}, u32[]{:S(2)}, u32[]{:S(2)}) collective-permute-start(bf16[128,512]{1,0:T(8,128)(2,1)} %collective-permute-done.2.refs_2_), channel_id=1, source_target_pairs={{0,1},{1,0},{2,3},{3,2},{4,5},{5,4},{6,7},{7,6},{8,9},{9,8},{10,11... | collective-permute-start | bytes 393224 | tf_op jit(solution)/shard_map/ppermute | solution.py:22
  20.1 22.9 %copy-start.9 = (f32[1024]{0:T(1024)S(1)}, f32[1024]{0:T(1024)}, u32[]{:S(2)}) copy-start(f32[1024]{0:T(1024)} %param.21) | copy-start | bytes 12292
  25.6 42.2 %copy-start.10 = (f32[1024]{0:T(1024)S(1)}, f32[1024]{0:T(1024)}, u32[]{:S(2)}) copy-start(f32[1024]{0:T(1024)} %param.24) | copy-start | bytes 12292
  25.7 9.9 %collective-permute-start.6 = (bf16[144,1024]{1,0:T(8,128)(2,1)S(1)}, bf16[144,1024]{1,0:T(8,128)(2,1)S(1)}, u32[]{:S(2)}, u32[]{:S(2)}) collective-permute-start(bf16[144,1024]{1,0:T(8,128)(2,1)S(1)} %get-tuple-element.51), channel_id=1, source_target_pairs={{0,8},{8,0},{16,24},{24,16},{1,9},{9,1},{17,25},{25,17},{2,10},{10... | collective-permute-start | bytes 884744 | tf_op jit(solution)/shard_map/ppermute | solution.py:22
  27.7 15.4 %collective-permute-start.7 = (bf16[144,1024]{1,0:T(8,128)(2,1)S(1)}, bf16[144,1024]{1,0:T(8,128)(2,1)S(1)}, u32[]{:S(2)}, u32[]{:S(2)}) collective-permute-start(bf16[144,1024]{1,0:T(8,128)(2,1)S(1)} %get-tuple-element.52), channel_id=1, source_target_pairs={{0,16},{8,24},{16,0},{24,8},{1,17},{9,25},{17,1},{25,9},{2,18},{10... | collective-permute-start | bytes 884744 | tf_op jit(solution)/shard_map/ppermute | solution.py:22
  29.2 13.9 %collective-permute-start.8 = (bf16[144,1024]{1,0:T(8,128)(2,1)S(1)}, bf16[144,1024]{1,0:T(8,128)(2,1)S(1)}, u32[]{:S(2)}, u32[]{:S(2)}) collective-permute-start(bf16[144,1024]{1,0:T(8,128)(2,1)S(1)} %get-tuple-element.53), channel_id=1, source_target_pairs={{0,24},{8,16},{16,8},{24,0},{1,25},{9,17},{17,9},{25,1},{2,26},{10... | collective-permute-start | bytes 884744 | tf_op jit(solution)/shard_map/ppermute | solution.py:22
  43.1 38.9 %copy-start.19 = (s32[16,2]{0,1:T(2,128)S(1)}, s32[16,2]{0,1:T(2,128)}, u32[]{:S(2)}) copy-start(s32[16,2]{0,1:T(2,128)} %param.30) | copy-start | bytes 388
  43.1 48.0 %copy-start.11 = (f32[1024]{0:T(1024)S(1)}, f32[1024]{0:T(1024)}, u32[]{:S(2)}) copy-start(f32[1024]{0:T(1024)} %param.26) | copy-start | bytes 12292
  43.9 1.5 collective-permute-start.9
  46.1 13.2 %collective-permute-start.10 = (bf16[128,288]{1,0:T(8,128)(2,1)}, bf16[128,288]{1,0:T(8,128)(2,1)}, u32[]{:S(2)}, u32[]{:S(2)}) collective-permute-start(bf16[128,288]{1,0:T(8,128)(2,1)} %get-tuple-element.89), channel_id=1, source_target_pairs={{0,2},{1,3},{2,0},{3,1},{4,6},{5,7},{6,4},{7,5},{8,10},{9,11},{10,... | collective-permute-start | bytes 221192 | tf_op jit(solution)/shard_map/ppermute | solution.py:22
  53.3 27.1 %collective-permute-start.16 = (bf16[128,1024]{1,0:T(8,128)(2,1)}, bf16[128,1024]{1,0:T(8,128)(2,1)S(1)}, u32[]{:S(2)}, u32[]{:S(2)}) collective-permute-start(bf16[128,1024]{1,0:T(8,128)(2,1)} %get-tuple-element.63), channel_id=1, source_target_pairs={{0,8},{8,0},{16,24},{24,16},{1,9},{9,1},{17,25},{25,17},{2,10},{10... | collective-permute-start | bytes 786440 | tf_op jit(solution)/shard_map/ppermute | solution.py:22
  54.5 27.4 %collective-permute-start.17 = (bf16[128,1024]{1,0:T(8,128)(2,1)}, bf16[128,1024]{1,0:T(8,128)(2,1)S(1)}, u32[]{:S(2)}, u32[]{:S(2)}) collective-permute-start(bf16[128,1024]{1,0:T(8,128)(2,1)} %get-tuple-element.64), channel_id=1, source_target_pairs={{0,16},{8,24},{16,0},{24,8},{1,17},{9,25},{17,1},{25,9},{2,18},{10... | collective-permute-start | bytes 786440 | tf_op jit(solution)/shard_map/ppermute | solution.py:22
  55.3 26.6 %collective-permute-start.18 = (bf16[128,1024]{1,0:T(8,128)(2,1)S(1)}, bf16[128,1024]{1,0:T(8,128)(2,1)S(1)}, u32[]{:S(2)}, u32[]{:S(2)}) collective-permute-start(bf16[128,1024]{1,0:T(8,128)(2,1)S(1)} %get-tuple-element.65), channel_id=1, source_target_pairs={{0,24},{8,16},{16,8},{24,0},{1,25},{9,17},{17,9},{25,1},{2,26},{10... | collective-permute-start | bytes 786440 | tf_op jit(solution)/shard_map/ppermute | solution.py:22
  56.8 10.0 %collective-permute-start.11 = (bf16[128,288]{1,0:T(8,128)(2,1)}, bf16[128,288]{1,0:T(8,128)(2,1)S(1)}, u32[]{:S(2)}, u32[]{:S(2)}) collective-permute-start(bf16[128,288]{1,0:T(8,128)(2,1)} %get-tuple-element.89), channel_id=1, source_target_pairs={{0,4},{1,5},{2,6},{3,7},{4,0},{5,1},{6,2},{7,3},{8,12},{9,13},{10,... | collective-permute-start | bytes 221192 | tf_op jit(solution)/shard_map/ppermute | solution.py:22
  59.4 7.4 %collective-permute-start.12 = (bf16[128,288]{1,0:T(8,128)(2,1)}, bf16[128,288]{1,0:T(8,128)(2,1)S(1)}, u32[]{:S(2)}, u32[]{:S(2)}) collective-permute-start(bf16[128,288]{1,0:T(8,128)(2,1)} %get-tuple-element.89), channel_id=1, source_target_pairs={{0,6},{1,7},{2,4},{3,5},{4,2},{5,3},{6,0},{7,1},{8,14},{9,15},{10,... | collective-permute-start | bytes 221192 | tf_op jit(solution)/shard_map/ppermute | solution.py:22
  68.9 36.7 %copy-start.12 = (bf16[1024,1024]{1,0:T(8,128)(2,1)S(1)}, bf16[1024,1024]{1,0:T(8,128)(2,1)}, u32[]{:S(2)}) copy-start(bf16[1024,1024]{1,0:T(8,128)(2,1)} %refs_4_.3) | copy-start | bytes 6291460
  74.5 16.5 %collective-permute-start.13 = (f32[17,8,128]{2,1,0:T(8,128)S(1)}, f32[17,8,128]{2,1,0:T(8,128)S(1)}, u32[]{:S(2)}, u32[]{:S(2)}) collective-permute-start(f32[17,8,128]{2,1,0:T(8,128)S(1)} %get-tuple-element.56), channel_id=1, source_target_pairs={{0,8},{16,24},{1,9},{17,25},{2,10},{18,26},{3,11},{19,27},{4,12},{... | collective-permute-start | bytes 208904 | tf_op jit(solution)/shard_map/ppermute | solution.py:27
  77.7 13.4 %collective-permute-start.14 = (f32[17,8,128]{2,1,0:T(8,128)S(1)}, f32[17,8,128]{2,1,0:T(8,128)S(1)}, u32[]{:S(2)}, u32[]{:S(2)}) collective-permute-start(f32[17,8,128]{2,1,0:T(8,128)S(1)} %get-tuple-element.56), channel_id=1, source_target_pairs={{0,16},{8,24},{1,17},{9,25},{2,18},{10,26},{3,19},{11,27},{4,20},{... | collective-permute-start | bytes 208904 | tf_op jit(solution)/shard_map/ppermute | solution.py:27
  80.4 10.6 %collective-permute-start.15 = (f32[17,8,128]{2,1,0:T(8,128)S(1)}, f32[17,8,128]{2,1,0:T(8,128)S(1)}, u32[]{:S(2)}, u32[]{:S(2)}) collective-permute-start(f32[17,8,128]{2,1,0:T(8,128)S(1)} %get-tuple-element.56), channel_id=1, source_target_pairs={{0,24},{8,16},{1,25},{9,17},{2,26},{10,18},{3,27},{11,19},{4,28},{... | collective-permute-start | bytes 208904 | tf_op jit(solution)/shard_map/ppermute | solution.py:27
  81.9 3.8 %collective-permute-start.29 = (s32[16,2]{0,1:T(2,128)S(1)}, s32[16,2]{0,1:T(2,128)S(1)}, u32[]{:S(2)}, u32[]{:S(2)}) collective-permute-start(s32[16,2]{0,1:T(2,128)S(1)} %copy-done.19), channel_id=1, source_target_pairs={{0,8},{8,0},{16,24},{24,16},{1,9},{9,1},{17,25},{25,17},{2,10},{10... | collective-permute-start | bytes 392 | tf_op jit(solution)/shard_map/ppermute | solution.py:22
  83.5 3.6 %collective-permute-start.30 = (s32[16,2]{0,1:T(2,128)S(1)}, s32[16,2]{0,1:T(2,128)S(1)}, u32[]{:S(2)}, u32[]{:S(2)}) collective-permute-start(s32[16,2]{0,1:T(2,128)S(1)} %copy-done.19), channel_id=1, source_target_pairs={{0,16},{8,24},{16,0},{24,8},{1,17},{9,25},{17,1},{25,9},{2,18},{10... | collective-permute-start | bytes 392 | tf_op jit(solution)/shard_map/ppermute | solution.py:22
  85.7 4.5 %collective-permute-start.31 = (s32[16,2]{0,1:T(2,128)S(1)}, s32[16,2]{0,1:T(2,128)S(1)}, u32[]{:S(2)}, u32[]{:S(2)}) collective-permute-start(s32[16,2]{0,1:T(2,128)S(1)} %copy-done.19), channel_id=1, source_target_pairs={{0,24},{8,16},{16,8},{24,0},{1,25},{9,17},{17,9},{25,1},{2,26},{10... | collective-permute-start | bytes 392 | tf_op jit(solution)/shard_map/ppermute | solution.py:22
  87.0 25.8 %collective-permute-start.26 = (bf16[16,1024]{1,0:T(8,128)(2,1)S(1)}, bf16[16,1024]{1,0:T(8,128)(2,1)S(1)}, u32[]{:S(2)}, u32[]{:S(2)}) collective-permute-start(bf16[16,1024]{1,0:T(8,128)(2,1)S(1)} %get-tuple-element.100), channel_id=1, source_target_pairs={{0,8},{8,0},{16,24},{24,16},{1,9},{9,1},{17,25},{25,17},{2,10},{10... | collective-permute-start | bytes 98312 | tf_op jit(solution)/shard_map/ppermute | solution.py:22
  90.2 25.1 %collective-permute-start.27 = (bf16[16,1024]{1,0:T(8,128)(2,1)S(1)}, bf16[16,1024]{1,0:T(8,128)(2,1)S(1)}, u32[]{:S(2)}, u32[]{:S(2)}) collective-permute-start(bf16[16,1024]{1,0:T(8,128)(2,1)S(1)} %get-tuple-element.99), channel_id=1, source_target_pairs={{0,16},{8,24},{16,0},{24,8},{1,17},{9,25},{17,1},{25,9},{2,18},{10... | collective-permute-start | bytes 98312 | tf_op jit(solution)/shard_map/ppermute | solution.py:22
  95.7 6.4 %collective-permute-start.19 = (bf16[128,1024]{1,0:T(8,128)(2,1)S(1)}, bf16[128,1024]{1,0:T(8,128)(2,1)S(1)}, u32[]{:S(2)}, u32[]{:S(2)}) collective-permute-start(bf16[128,1024]{1,0:T(8,128)(2,1)S(1)} %shard_map.168.refs_0_), channel_id=1, source_target_pairs={{0,8},{8,0},{16,24},{24,16},{1,9},{9,1},{17,25},{25,17},{2,10},{10... | collective-permute-start | bytes 786440 | tf_op jit(solution)/shard_map/ppermute | solution.py:22
  96.3 8.6 %collective-permute-start.20 = (bf16[128,1024]{1,0:T(8,128)(2,1)S(1)}, bf16[128,1024]{1,0:T(8,128)(2,1)S(1)}, u32[]{:S(2)}, u32[]{:S(2)}) collective-permute-start(bf16[128,1024]{1,0:T(8,128)(2,1)S(1)} %shard_map.168.refs_0_), channel_id=1, source_target_pairs={{0,16},{8,24},{16,0},{24,8},{1,17},{9,25},{17,1},{25,9},{2,18},{10... | collective-permute-start | bytes 786440 | tf_op jit(solution)/shard_map/ppermute | solution.py:22
  98.3 7.3 %collective-permute-start.21 = (bf16[128,1024]{1,0:T(8,128)(2,1)S(1)}, bf16[128,1024]{1,0:T(8,128)(2,1)S(1)}, u32[]{:S(2)}, u32[]{:S(2)}) collective-permute-start(bf16[128,1024]{1,0:T(8,128)(2,1)S(1)} %shard_map.168.refs_0_), channel_id=1, source_target_pairs={{0,24},{8,16},{16,8},{24,0},{1,25},{9,17},{17,9},{25,1},{2,26},{10... | collective-permute-start | bytes 786440 | tf_op jit(solution)/shard_map/ppermute | solution.py:22
  102.1 36.8 %dynamic-slice-start = ((f32[4096]{0:T(1024)}, s32[]{:T(128)}), f32[1024]{0:T(1024)S(1)}, s32[]{:S(2)}) async-start(f32[4096]{0:T(1024)} %param.28, s32[]{:T(128)} %select_n.41), calls=%async_computation | async-start | bytes 8704 | tf_op jit(solution)/shard_map/dynamic_slice | solution.py:530
  102.2 13.1 %collective-permute-start.28 = (bf16[16,1024]{1,0:T(8,128)(2,1)S(1)}, bf16[16,1024]{1,0:T(8,128)(2,1)S(1)}, u32[]{:S(2)}, u32[]{:S(2)}) collective-permute-start(bf16[16,1024]{1,0:T(8,128)(2,1)S(1)} %get-tuple-element.98), channel_id=1, source_target_pairs={{0,24},{8,16},{16,8},{24,0},{1,25},{9,17},{17,9},{25,1},{2,26},{10... | collective-permute-start | bytes 98312 | tf_op jit(solution)/shard_map/ppermute | solution.py:22
  106.8 56.4 %copy-start.6 = (f32[4096]{0:T(1024)S(1)}, f32[4096]{0:T(1024)}, u32[]{:S(2)}) copy-start(f32[4096]{0:T(1024)} %param.28) | copy-start | bytes 49156
  106.8 2.0 collective-permute-start.22
  108.9 8.6 %collective-permute-start.23 = (bf16[64,1024]{1,0:T(8,128)(2,1)S(1)}, bf16[64,1024]{1,0:T(8,128)(2,1)S(1)}, u32[]{:S(2)}, u32[]{:S(2)}) collective-permute-start(bf16[64,1024]{1,0:T(8,128)(2,1)S(1)} %get-tuple-element.69), channel_id=1, source_target_pairs={{0,2},{1,3},{2,0},{3,1},{4,6},{5,7},{6,4},{7,5},{8,10},{9,11},{10,... | collective-permute-start | bytes 393224 | tf_op jit(solution)/shard_map/ppermute | solution.py:22
  111.8 12.9 %collective-permute-start.24 = (bf16[64,1024]{1,0:T(8,128)(2,1)S(1)}, bf16[64,1024]{1,0:T(8,128)(2,1)S(1)}, u32[]{:S(2)}, u32[]{:S(2)}) collective-permute-start(bf16[64,1024]{1,0:T(8,128)(2,1)S(1)} %get-tuple-element.70), channel_id=1, source_target_pairs={{0,4},{1,5},{2,6},{3,7},{4,0},{5,1},{6,2},{7,3},{8,12},{9,13},{10,... | collective-permute-start | bytes 393224 | tf_op jit(solution)/shard_map/ppermute | solution.py:22
  112.9 11.8 %collective-permute-start.25 = (bf16[64,1024]{1,0:T(8,128)(2,1)S(1)}, bf16[64,1024]{1,0:T(8,128)(2,1)S(1)}, u32[]{:S(2)}, u32[]{:S(2)}) collective-permute-start(bf16[64,1024]{1,0:T(8,128)(2,1)S(1)} %get-tuple-element.71), channel_id=1, source_target_pairs={{0,6},{1,7},{2,4},{3,5},{4,2},{5,3},{6,0},{7,1},{8,14},{9,15},{10,... | collective-permute-start | bytes 393224 | tf_op jit(solution)/shard_map/ppermute | solution.py:22
  125.2 8.0 %collective-permute-start.46 = (f32[4,16]{1,0:T(4,128)S(1)}, f32[4,16]{1,0:T(4,128)S(1)}, u32[]{:S(2)}, u32[]{:S(2)}) collective-permute-start(f32[4,16]{1,0:T(4,128)S(1)} %reshape.208), channel_id=1, source_target_pairs={{0,8},{8,0},{16,24},{24,16},{1,9},{9,1},{17,25},{25,17},{2,10},{10... | collective-permute-start | bytes 776 | tf_op jit(solution)/shard_map/ppermute | solution.py:22
  126.7 5.9 %collective-permute-start.47 = (f32[4,16]{1,0:T(4,128)S(1)}, f32[4,16]{1,0:T(4,128)S(1)}, u32[]{:S(2)}, u32[]{:S(2)}) collective-permute-start(f32[4,16]{1,0:T(4,128)S(1)} %reshape.208), channel_id=1, source_target_pairs={{0,16},{8,24},{16,0},{24,8},{1,17},{9,25},{17,1},{25,9},{2,18},{10... | collective-permute-start | bytes 776 | tf_op jit(solution)/shard_map/ppermute | solution.py:22
  127.5 5.9 %collective-permute-start.48 = (f32[4,16]{1,0:T(4,128)S(1)}, f32[4,16]{1,0:T(4,128)S(1)}, u32[]{:S(2)}, u32[]{:S(2)}) collective-permute-start(f32[4,16]{1,0:T(4,128)S(1)} %reshape.208), channel_id=1, source_target_pairs={{0,24},{8,16},{16,8},{24,0},{1,25},{9,17},{17,9},{25,1},{2,26},{10... | collective-permute-start | bytes 776 | tf_op jit(solution)/shard_map/ppermute | solution.py:22
  128.7 7.5 %collective-permute-start.34 = (bf16[48,1024]{1,0:T(8,128)(2,1)S(1)}, bf16[48,1024]{1,0:T(8,128)(2,1)S(1)}, u32[]{:S(2)}, u32[]{:S(2)}) collective-permute-start(bf16[48,1024]{1,0:T(8,128)(2,1)S(1)} %get-tuple-element.77), channel_id=1, source_target_pairs={{0,6},{1,7},{2,4},{3,5},{4,2},{5,3},{6,0},{7,1},{8,14},{9,15},{10,... | collective-permute-start | bytes 294920 | tf_op jit(solution)/shard_map/ppermute | solution.py:22
  131.0 7.8 %collective-permute-start.33 = (bf16[48,1024]{1,0:T(8,128)(2,1)S(1)}, bf16[48,1024]{1,0:T(8,128)(2,1)S(1)}, u32[]{:S(2)}, u32[]{:S(2)}) collective-permute-start(bf16[48,1024]{1,0:T(8,128)(2,1)S(1)} %get-tuple-element.76), channel_id=1, source_target_pairs={{0,4},{1,5},{2,6},{3,7},{4,0},{5,1},{6,2},{7,3},{8,12},{9,13},{10,... | collective-permute-start | bytes 294920 | tf_op jit(solution)/shard_map/ppermute | solution.py:22
  132.5 6.3 %collective-permute-start.32 = (bf16[48,1024]{1,0:T(8,128)(2,1)S(1)}, bf16[48,1024]{1,0:T(8,128)(2,1)S(1)}, u32[]{:S(2)}, u32[]{:S(2)}) collective-permute-start(bf16[48,1024]{1,0:T(8,128)(2,1)S(1)} %get-tuple-element.75), channel_id=1, source_target_pairs={{0,2},{1,3},{2,0},{3,1},{4,6},{5,7},{6,4},{7,5},{8,10},{9,11},{10,... | collective-permute-start | bytes 294920 | tf_op jit(solution)/shard_map/ppermute | solution.py:22
  138.9 3.9 %collective-permute-start.35 = (bf16[4,24,1024]{2,1,0:T(8,128)(2,1)S(1)}, bf16[4,24,1024]{2,1,0:T(8,128)(2,1)S(1)}, u32[]{:S(2)}, u32[]{:S(2)}) collective-permute-start(bf16[4,24,1024]{2,1,0:T(8,128)(2,1)S(1)} %pad_maximum_fusion), channel_id=1, source_target_pairs={{0,1},{1,0},{2,3},{3,2},{4,5},{5,4},{6,7},{7,6},{8,9},{9,8},{10,11... | collective-permute-start | bytes 589832 | tf_op jit(solution)/shard_map/ppermute | solution.py:22
  139.3 5.9 %collective-permute-start.51 = (f32[4,16,8]{1,0,2:T(4,128)S(1)}, f32[4,16,8]{1,0,2:T(4,128)S(1)}, u32[]{:S(2)}, u32[]{:S(2)}) collective-permute-start(f32[4,16,8]{1,0,2:T(4,128)S(1)} %reshape.209), channel_id=1, source_target_pairs={{0,24},{8,16},{16,8},{24,0},{1,25},{9,17},{17,9},{25,1},{2,26},{10... | collective-permute-start | bytes 6152 | tf_op jit(solution)/shard_map/ppermute | solution.py:22
  141.0 5.5 %collective-permute-start.50 = (f32[4,16,8]{1,0,2:T(4,128)S(1)}, f32[4,16,8]{1,0,2:T(4,128)S(1)}, u32[]{:S(2)}, u32[]{:S(2)}) collective-permute-start(f32[4,16,8]{1,0,2:T(4,128)S(1)} %reshape.209), channel_id=1, source_target_pairs={{0,16},{8,24},{16,0},{24,8},{1,17},{9,25},{17,1},{25,9},{2,18},{10... | collective-permute-start | bytes 6152 | tf_op jit(solution)/shard_map/ppermute | solution.py:22
  142.2 49.2 %collective-permute-start.49 = (f32[4,16,8]{1,0,2:T(4,128)S(1)}, f32[4,16,8]{1,0,2:T(4,128)S(1)}, u32[]{:S(2)}, u32[]{:S(2)}) collective-permute-start(f32[4,16,8]{1,0,2:T(4,128)S(1)} %reshape.209), channel_id=1, source_target_pairs={{0,8},{8,0},{16,24},{24,16},{1,9},{9,1},{17,25},{25,17},{2,10},{10... | collective-permute-start | bytes 6152 | tf_op jit(solution)/shard_map/ppermute | solution.py:22
  142.9 12.1 %collective-permute-start.36 = (bf16[192,1024]{1,0:T(8,128)(2,1)S(1)}, bf16[192,1024]{1,0:T(8,128)(2,1)S(1)}, u32[]{:S(2)}, u32[]{:S(2)}) collective-permute-start(bf16[192,1024]{1,0:T(8,128)(2,1)S(1)} %fusion.10.refs_0_), channel_id=1, source_target_pairs={{0,8},{8,0},{16,24},{24,16},{1,9},{9,1},{17,25},{25,17},{2,10},{10... | collective-permute-start | bytes 1179656 | tf_op jit(solution)/shard_map/ppermute | solution.py:22
  144.4 17.1 %collective-permute-start.37 = (bf16[192,1024]{1,0:T(8,128)(2,1)S(1)}, bf16[192,1024]{1,0:T(8,128)(2,1)S(1)}, u32[]{:S(2)}, u32[]{:S(2)}) collective-permute-start(bf16[192,1024]{1,0:T(8,128)(2,1)S(1)} %fusion.10.refs_0_), channel_id=1, source_target_pairs={{0,16},{8,24},{16,0},{24,8},{1,17},{9,25},{17,1},{25,9},{2,18},{10... | collective-permute-start | bytes 1179656 | tf_op jit(solution)/shard_map/ppermute | solution.py:22
  145.2 18.0 %collective-permute-start.38 = (bf16[192,1024]{1,0:T(8,128)(2,1)S(1)}, bf16[192,1024]{1,0:T(8,128)(2,1)S(1)}, u32[]{:S(2)}, u32[]{:S(2)}) collective-permute-start(bf16[192,1024]{1,0:T(8,128)(2,1)S(1)} %fusion.10.refs_0_), channel_id=1, source_target_pairs={{0,24},{8,16},{16,8},{24,0},{1,25},{9,17},{17,9},{25,1},{2,26},{10... | collective-permute-start | bytes 1179656 | tf_op jit(solution)/shard_map/ppermute | solution.py:22
  182.5 43.9 %copy-start.1 = (bf16[4096,8]{0,1:T(8,128)(2,1)S(1)}, bf16[4096,8]{0,1:T(8,128)(2,1)}, u32[]{:S(2)}) copy-start(bf16[4096,8]{0,1:T(8,128)(2,1)} %param.29) | copy-start | bytes 196612
  187.8 12.1 %collective-permute-start.39 = (bf16[192,1024]{1,0:T(8,128)(2,1)S(1)}, bf16[192,1024]{1,0:T(8,128)(2,1)S(1)}, u32[]{:S(2)}, u32[]{:S(2)}) collective-permute-start(bf16[192,1024]{1,0:T(8,128)(2,1)S(1)} %get-tuple-element.95), channel_id=1, source_target_pairs={{0,8},{8,0},{16,24},{24,16},{1,9},{9,1},{17,25},{25,17},{2,10},{10... | collective-permute-start | bytes 1179656 | tf_op jit(solution)/shard_map/ppermute | solution.py:22
  188.6 18.1 %collective-permute-start.40 = (bf16[192,1024]{1,0:T(8,128)(2,1)S(1)}, bf16[192,1024]{1,0:T(8,128)(2,1)S(1)}, u32[]{:S(2)}, u32[]{:S(2)}) collective-permute-start(bf16[192,1024]{1,0:T(8,128)(2,1)S(1)} %get-tuple-element.94), channel_id=1, source_target_pairs={{0,16},{8,24},{16,0},{24,8},{1,17},{9,25},{17,1},{25,9},{2,18},{10... | collective-permute-start | bytes 1179656 | tf_op jit(solution)/shard_map/ppermute | solution.py:22
  190.2 16.5 %collective-permute-start.41 = (bf16[192,1024]{1,0:T(8,128)(2,1)S(1)}, bf16[192,1024]{1,0:T(8,128)(2,1)S(1)}, u32[]{:S(2)}, u32[]{:S(2)}) collective-permute-start(bf16[192,1024]{1,0:T(8,128)(2,1)S(1)} %get-tuple-element.93), channel_id=1, source_target_pairs={{0,24},{8,16},{16,8},{24,0},{1,25},{9,17},{17,9},{25,1},{2,26},{10... | collective-permute-start | bytes 1179656 | tf_op jit(solution)/shard_map/ppermute | solution.py:22
  206.9 6.6 %collective-permute-start.44 = (bf16[48,1024]{1,0:T(8,128)(2,1)S(1)}, bf16[48,1024]{1,0:T(8,128)(2,1)S(1)}, u32[]{:S(2)}, u32[]{:S(2)}) collective-permute-start(bf16[48,1024]{1,0:T(8,128)(2,1)S(1)} %get-tuple-element.81), channel_id=1, source_target_pairs={{0,6},{1,7},{2,4},{3,5},{4,2},{5,3},{6,0},{7,1},{8,14},{9,15},{10,... | collective-permute-start | bytes 294920 | tf_op jit(solution)/shard_map/ppermute | solution.py:22
  209.4 6.6 %collective-permute-start.43 = (bf16[48,1024]{1,0:T(8,128)(2,1)S(1)}, bf16[48,1024]{1,0:T(8,128)(2,1)S(1)}, u32[]{:S(2)}, u32[]{:S(2)}) collective-permute-start(bf16[48,1024]{1,0:T(8,128)(2,1)S(1)} %get-tuple-element.80), channel_id=1, source_target_pairs={{0,4},{1,5},{2,6},{3,7},{4,0},{5,1},{6,2},{7,3},{8,12},{9,13},{10,... | collective-permute-start | bytes 294920 | tf_op jit(solution)/shard_map/ppermute | solution.py:22
  209.4 6.6 %collective-permute-start.42 = (bf16[48,1024]{1,0:T(8,128)(2,1)S(1)}, bf16[48,1024]{1,0:T(8,128)(2,1)S(1)}, u32[]{:S(2)}, u32[]{:S(2)}) collective-permute-start(bf16[48,1024]{1,0:T(8,128)(2,1)S(1)} %get-tuple-element.79), channel_id=1, source_target_pairs={{0,2},{1,3},{2,0},{3,1},{4,6},{5,7},{6,4},{7,5},{8,10},{9,11},{10,... | collective-permute-start | bytes 294920 | tf_op jit(solution)/shard_map/ppermute | solution.py:22
  216.0 1.6 collective-permute-start.45
  217.8 4.0 %collective-permute-start.52 = (bf16[16,1024]{1,0:T(8,128)(2,1)S(1)}, bf16[16,1024]{1,0:T(8,128)(2,1)S(1)}, u32[]{:S(2)}, u32[]{:S(2)}) collective-permute-start(bf16[16,1024]{1,0:T(8,128)(2,1)S(1)} %get-tuple-element.84), channel_id=1, source_target_pairs={{0,8},{8,0},{16,24},{24,16},{1,9},{9,1},{17,25},{25,17},{2,10},{10... | collective-permute-start | bytes 98312 | tf_op jit(solution)/shard_map/ppermute | solution.py:22
  218.6 3.9 %collective-permute-start.53 = (bf16[16,1024]{1,0:T(8,128)(2,1)S(1)}, bf16[16,1024]{1,0:T(8,128)(2,1)S(1)}, u32[]{:S(2)}, u32[]{:S(2)}) collective-permute-start(bf16[16,1024]{1,0:T(8,128)(2,1)S(1)} %get-tuple-element.85), channel_id=1, source_target_pairs={{0,16},{8,24},{16,0},{24,8},{1,17},{9,25},{17,1},{25,9},{2,18},{10... | collective-permute-start | bytes 98312 | tf_op jit(solution)/shard_map/ppermute | solution.py:22
  220.4 4.8 %collective-permute-start.54 = (bf16[16,1024]{1,0:T(8,128)(2,1)S(1)}, bf16[16,1024]{1,0:T(8,128)(2,1)S(1)}, u32[]{:S(2)}, u32[]{:S(2)}) collective-permute-start(bf16[16,1024]{1,0:T(8,128)(2,1)S(1)} %get-tuple-element.86), channel_id=1, source_target_pairs={{0,24},{8,16},{16,8},{24,0},{1,25},{9,17},{17,9},{25,1},{2,26},{10... | collective-permute-start | bytes 98312 | tf_op jit(solution)/shard_map/ppermute | solution.py:22
  (12 other events, 64.4 us)

commit v2 on v1

v2 whole, which is shorter than its diff:
```python
import functools

import jax
import jax.numpy as jnp
from jax import lax
from jax.experimental import pallas as pl
from jax.experimental.pallas import tpu as pltpu
from jax.sharding import PartitionSpec as P

EPSILON = 1e-06
HALO = 16
ROUTE_ROWS = 2
LOG2_E = 1.4426950408889634
MIB = 1 << 20
BF16 = jnp.bfloat16
F32 = jnp.float32

VMEM = pl.BlockSpec(memory_space=pltpu.VMEM)
SMEM = pl.BlockSpec(memory_space=pltpu.SMEM)


def partner(block, axis, mask):
    size = lax.axis_size(axis)
    return lax.ppermute(block, axis, [(i, i ^ mask) for i in range(size)])


def later_partner(block, axis, mask):
    size = lax.axis_size(axis)
    return lax.ppermute(block, axis, [(i, i ^ mask) for i in range(size) if i < i ^ mask])


def after(values, *done):
    flat, tree = jax.tree.flatten(values)
    held = lax.optimization_barrier((*flat, *done))
    return jax.tree.unflatten(tree, held[: len(flat)])


def shape(dims, dtype):
    return jax.ShapeDtypeStruct(tuple(dims), dtype)


def kernel_call(body, outs, in_specs, scratch=(), flops=0, moved=0, limit=8, deps=()):
    deps = list(deps)
    count = len(in_specs)

    def with_deps(*refs):
        body(*refs[:count], *refs[count + len(deps) :])

    call = pl.pallas_call(
        with_deps,
        out_shape=outs,
        in_specs=list(in_specs) + [pl.BlockSpec(memory_space=pl.ANY)] * len(deps),
        out_specs=jax.tree.map(lambda _: VMEM, outs),
        scratch_shapes=list(scratch),
        compiler_params=pltpu.CompilerParams(vmem_limit_bytes=limit * MIB),
        cost_estimate=pl.CostEstimate(flops=flops, bytes_accessed=moved, transcendentals=0),
    )
    return lambda *operands: call(*operands, *deps)


def dot(left, right):
    return jnp.dot(left, right, preferred_element_type=F32)


def silu(v):
    return v / (1.0 + jnp.exp(-v))


def norm_body(seq, place, tokens, gain, own, *sends):
    values = tokens[...].astype(F32)
    inverse = lax.rsqrt(jnp.mean(values * values, axis=-1, keepdims=True) + EPSILON)
    own_width = own.shape[1]
    half = own_width // 2
    me, core = place[0], place[1]

    def columns(start, width):
        start = pl.multiple_of(start, 128)
        part = tokens[:, pl.ds(start, width)].astype(F32)
        return (part * inverse * gain[:, pl.ds(start, width)]).astype(BF16)

    own[...] = columns(me * own_width, own_width)
    for mask in range(1, seq):
        sends[mask - 1][...] = columns((me ^ mask) * own_width + core * half, half)


def project(x_own, x_mine, x_other, weight, core, branch):
    half = weight.shape[0] // 2
    channels = weight.shape[1] // 2
    part = slice(branch * channels, (branch + 1) * channels)
    yield dot(x_own[...], weight[:, part])
    first = weight[pl.ds(pl.multiple_of(core * half, half), half), part]
    second = weight[pl.ds(pl.multiple_of((1 - core) * half, half), half), part]
    for mine, other in zip(x_mine, x_other):
        yield dot(mine[...], first) + dot(other[...], second)


def mixer_project_body(seq, place, x_own, *refs):
    x_mine, x_other = refs[: seq - 1], refs[seq - 1 : 2 * seq - 2]
    weight, routes = refs[2 * seq - 2 : 2 * seq]
    outs = refs[2 * seq : 3 * seq]
    tails = refs[3 * seq]
    me, core = place[0], place[1]
    length = x_own.shape[0]
    for index, product in enumerate(project(x_own, x_mine, x_other, weight, core, 0)):
        outs[index][HALO:, :] = product.astype(outs[index].dtype)
        tails[index] = product[length - HALO :, :]
    for mask in range(seq):
        shard = me ^ mask
        source = me ^ jnp.maximum(shard - 1, 0)
        before = jnp.where(shard > 0, tails[source], 0.0)
        row = lax.broadcasted_iota(jnp.int32, before.shape, 0)
        before = jnp.where(row < ROUTE_ROWS, routes[mask], before)
        outs[mask][:HALO, :] = before.astype(outs[mask].dtype)


def gate_project_body(seq, place, x_own, *refs):
    x_mine, x_other = refs[: seq - 1], refs[seq - 1 : 2 * seq - 2]
    weight, own_tokens = refs[2 * seq - 2 : 2 * seq]
    outs = refs[2 * seq :]
    length, width = x_own.shape
    for index, product in enumerate(project(x_own, x_mine, x_other, weight, place[1], 1)):
        outs[index][:length, :] = product.astype(outs[index].dtype)
        if index:
            start = pl.multiple_of((place[0] ^ index) * width, 128)
            rows = own_tokens[:, pl.ds(start, width)]
            spare = outs[index].shape[1] - width
            if spare:
                rows = jnp.concatenate([rows, jnp.zeros((rows.shape[0], spare), rows.dtype)], axis=1)
            outs[index][length:, :] = rows


def conv_body(seq, *refs):
    terms = refs[:seq]
    taps, bias, proj, activated, features = refs[seq:]
    total = terms[0][...]
    for term in terms[1:]:
        total = total + term[...].astype(F32)
    padded = total.astype(BF16).astype(F32)
    length = activated.shape[0]
    count = taps.shape[0]
    convolved = bias[...]
    for tap in range(count):
        start = HALO - count + 1 + tap
        convolved = convolved + taps[tap : tap + 1, :] * padded[start : start + length]
    rounded = silu(convolved).astype(BF16)
    activated[...] = rounded
    features[...] = lax.dot_general(
        rounded, proj[...], (((1,), (1,)), ((), ())), preferred_element_type=F32
    )


def scan_body(maps, low_rank, activated, step_weight, step_bias, rate, y, cumulated, final, steps, drive):
    length, groups, lanes = y.shape
    states = rate.shape[0]
    raw = dot(low_rank[...], step_weight[...]) + step_bias[...]
    step_size = jnp.maximum(raw, 0.0) + jnp.log1p(jnp.exp(-jnp.abs(raw)))
    driven = step_size * activated[...].astype(F32)
    for group in range(groups):
        part = slice(group * lanes, (group + 1) * lanes)
        steps[:, group, :] = step_size[:, part]
        drive[:, group, :] = driven[:, part]
    rates = [rate[n] for n in range(states)]

    def advance(t, carry):
        state, running = carry
        step, push = steps[t], drive[t]
        running = running + step
        fresh = []
        out = jnp.zeros_like(step)
        for n in range(states):
            value = jnp.exp2(step * rates[n]) * state[n] + push * maps[t, n]
            out = out + value * maps[t, states + n]
            fresh.append(value)
        y[t] = out
        cumulated[t] = running
        return tuple(fresh), running

    zero = jnp.zeros((groups, lanes), F32)
    state, running = lax.fori_loop(0, length, advance, ((zero,) * states, zero), unroll=4)
    for n in range(states):
        final[n] = state[n]
    final[states] = running


def gated_body(seq, own_rows, place, maps, *refs):
    arrived = refs[: seq - 1]
    y, cumulated, rate, activated, skip_gain = refs[seq - 1 : seq + 4]
    gates = refs[seq + 4 : 2 * seq + 4]
    gated, scanned, result = refs[2 * seq + 4 :]
    length, groups, lanes = y.shape
    states = rate.shape[0]
    me, expert = place[0], place[2]
    zero = jnp.zeros((groups, lanes), F32)
    incoming = [zero] * states
    for mask in range(1, seq):
        shard = me ^ mask
        between = zero
        for other in range(1, seq):
            middle = me ^ other
            inside = (shard < middle) & (middle < me)
            between = between + jnp.where(inside, arrived[other - 1][states], 0.0)
        for n in range(states):
            term = jnp.exp2(rate[n] * between) * arrived[mask - 1][n]
            incoming[n] = incoming[n] + jnp.where(shard < me, term, 0.0)
    rates = [rate[n] for n in range(states)]

    def correct(t, carry):
        steps = cumulated[t]
        out = y[t]
        for n in range(states):
            out = out + (jnp.exp2(steps * rates[n]) * incoming[n]) * maps[t, states + n]
        scanned[t] = out
        return carry

    lax.fori_loop(0, length, correct, 0, unroll=4)
    for group in range(groups):
        part = slice(group * lanes, (group + 1) * lanes)
        gate = gates[0][:, part]
        for term in gates[1:]:
            gate = gate + term[:length, part].astype(F32)
        gate = gate.astype(BF16).astype(F32)
        drive = activated[:, part].astype(F32)
        result[:, part] = (scanned[:, group, :] + skip_gain[:, part] * drive) * silu(gate)
    blocks = length // own_rows
    moved = [
        result[pl.ds(pl.multiple_of((expert ^ k) * own_rows, own_rows), own_rows), :]
        for k in range(blocks)
    ]
    gated[...] = jnp.concatenate(moved, axis=0).astype(BF16)


def out_project_body(seq, own_rows, *refs):
    blocks = refs[:seq]
    weight, keep, send = refs[seq:]
    for shard in range(seq):
        product = dot(blocks[shard][...], weight[...])
        for owner in range(product.shape[0] // own_rows):
            rows = product[owner * own_rows : (owner + 1) * own_rows]
            place = (owner // 2, pl.ds(shard * own_rows, own_rows))
            if owner % 2 == 0:
                keep[place[0], place[1], :] = rows
            else:
                send[place[0], place[1], :] = rows.astype(BF16)


def core_sum_body(keep, arrived, own, *sends):
    own[...] = keep[0] + arrived[0].astype(F32)
    for w in range(1, keep.shape[0]):
        sends[w - 1][...] = (keep[w] + arrived[w].astype(F32)).astype(BF16)


def tables_body(seq, own_rows, most_slots, place, routes, *refs):
    terms, outs = refs[: seq - 1], refs[seq - 1 :]
    choose, first, second, named = outs
    slots, window = choose.shape
    near = routes[:8, :window]
    for term in terms:
        near = near + term[:16, :window].astype(F32)[:8]
    row = lax.broadcasted_iota(jnp.int32, (slots, window), 0)
    column = lax.broadcasted_iota(jnp.int32, (slots, window), 1)
    wanted = (place[2] ^ (row // (seq * most_slots))).astype(F32)
    shard = (row // most_slots) % seq
    hits = [jnp.where(near[i : i + 1, :] == wanted, 1.0, 0.0) for i in range(2)]
    source = lax.broadcasted_iota(jnp.int32, (window, window), 0)
    target = lax.broadcasted_iota(jnp.int32, (window, window), 1)
    earlier = (source // own_rows == target // own_rows) & (source < target)
    before = dot((hits[0] + hits[1]).astype(BF16), jnp.where(earlier, 1.0, 0.0).astype(BF16))
    here = (before == (row % most_slots).astype(F32)) & (shard == (place[0] ^ (column // own_rows)))
    fits = jnp.where(here, 1.0, 0.0)
    choose[...] = (fits * (hits[0] + hits[1])).astype(BF16)
    first[...] = (fits * hits[0]).astype(BF16)
    second[...] = (fits * hits[1]).astype(BF16)
    same = jnp.where(source == target, 1.0, 0.0).astype(BF16)
    named[...] = lax.dot_general(
        same, near.astype(BF16), (((1,), (1,)), ((), ())), preferred_element_type=F32
    )


def hidden_body(chips, seq, place, own, *refs):
    terms, refs = refs[: chips - 1], refs[chips - 1 :]
    own_tokens, refs = refs[0], refs[1:]
    payloads, refs = refs[: seq - 1], refs[seq - 1 :]
    choose, hidden = refs[:2]
    outs = refs[2:]
    total = own[...]
    for term in terms:
        total = total + term[...].astype(F32)
    width = own.shape[1]
    rows = own_tokens.shape[0]
    start = pl.multiple_of(place[0] * width, 128)
    residual = [own_tokens[:, pl.ds(start, width)].astype(F32)]
    for payload in payloads:
        residual.append(payload[payload.shape[0] - rows :, :width].astype(F32))
    rounded = (jnp.concatenate(residual, axis=0) + total).astype(BF16)
    hidden[...] = rounded
    slots = dot(choose[...], rounded).astype(BF16)
    rows = slots.shape[0] // chips
    for w in range(chips):
        outs[w][...] = slots[w * rows : (w + 1) * rows]


def start_copies(jobs, place, sources, outs, sems):
    copies = []
    for index, (source, mask, axis) in enumerate(jobs):
        size = outs[index].shape[axis]
        start = pl.multiple_of((place[0] ^ mask) * size, 128 if axis else 16)
        where = (0, slice(None), pl.ds(start, size)) if axis else (0, pl.ds(start, size))
        copies.append(pltpu.make_async_copy(sources[source].at[where], outs[index], sems.at[index]))
    for copy in copies:
        copy.start()
    return copies


def in_hbm(sources):
    return [pltpu.with_memory_space_constraint(source, pltpu.HBM) for source in sources]


def fetched_shapes(jobs, sources, width):
    blocks = []
    for source, _, axis in jobs:
        rows, columns = sources[source].shape[1:]
        blocks.append(pltpu.VMEM((rows, width) if axis else (width, columns), BF16))
    return blocks


def fetch_body(jobs, count, place, *refs):
    sources, outs, sems = refs[:count], refs[count:-1], refs[-1]
    for copy in start_copies(jobs, place, sources, outs, sems):
        copy.wait()


def fetch(place, jobs, width, sources, deps):
    return kernel_call(
        functools.partial(fetch_body, jobs, len(sources)),
        fetched_shapes(jobs, sources, width),
        [SMEM] + [pl.BlockSpec(memory_space=pltpu.HBM)] * len(sources),
        [pltpu.SemaphoreType.DMA((len(jobs),))],
        moved=2 * len(jobs) * width * sources[0].shape[2],
        deps=deps,
    )(place, *in_hbm(sources))


def expert_body(mask, first, last, model_width, jobs, count, place, piece, gain, gate, up, *refs):
    before, refs = ([], refs) if first else (refs[:3], refs[3:])
    sources, refs = refs[:count], refs[count:]
    outs, refs = (refs[:1], refs[1:]) if last else (refs[:3], refs[3:])
    copies = start_copies(jobs, place, sources, refs[:-1], refs[-1]) if jobs else []
    width = piece.shape[1]
    values = piece[...].astype(F32)
    square = jnp.sum(values * values, axis=-1, keepdims=True)
    if not first:
        square = square + before[2][:, 0:1]
    start = pl.multiple_of((place[0] ^ mask) * width, 128)
    rows = (values * gain[:, pl.ds(start, width)]).astype(BF16)
    inverse = lax.rsqrt(square / model_width + EPSILON)
    if not last:
        outs[2][...] = jnp.broadcast_to(square, outs[2].shape)
    hidden_units = gate.shape[1]
    tile = tile_of(hidden_units, 512)
    for step in range(hidden_units // tile):
        part = slice(step * tile, (step + 1) * tile)
        gate_act = dot(rows, gate[:, part])
        up_act = dot(rows, up[:, part])
        if not first:
            gate_act = gate_act + before[0][:, part]
            up_act = up_act + before[1][:, part]
        if last:
            outs[0][:, part] = (silu(gate_act * inverse) * (up_act * inverse)).astype(BF16)
        else:
            outs[0][:, part] = gate_act
            outs[1][:, part] = up_act
    for copy in copies:
        copy.wait()


def expert_chunk(mask, first, last, place, piece, gain, gate, up, before, jobs, sources):
    slots, width = piece.shape
    model_width, hidden_units = gain.shape[1], gate.shape[1]
    total = shape((slots, hidden_units), F32)
    outs = [total, total, shape((slots, 128), F32)]
    if last:
        outs = [shape((slots, hidden_units), BF16)]
    sources = sources if jobs else []
    far = pl.BlockSpec(memory_space=pltpu.HBM)
    results = kernel_call(
        functools.partial(expert_body, mask, first, last, model_width, jobs, len(sources)),
        outs + fetched_shapes(jobs, sources, width),
        [SMEM] + [VMEM] * (4 + len(before)) + [far] * len(sources),
        [pltpu.SemaphoreType.DMA((len(jobs),))] if jobs else [],
        flops=4 * slots * width * hidden_units,
        moved=4 * width * hidden_units,
        limit=12,
    )(place, piece, gain, gate, up, *before, *in_hbm(sources))
    return results[: len(outs)], results[len(outs) :]


def down_body(hidden, down, out):
    width = out.shape[1]
    tile = tile_of(width, 512)
    for step in range(width // tile):
        part = slice(step * tile, (step + 1) * tile)
        out[:, part] = dot(hidden[...], down[:, part]).astype(BF16)


def down_chunk(hidden, down):
    slots, hidden_units = hidden.shape
    width = down.shape[1]
    return kernel_call(
        down_body,
        shape((slots, width), BF16),
        [VMEM] * 2,
        flops=2 * slots * width * hidden_units,
        moved=2 * width * hidden_units,
        limit=16,
    )(hidden, down)


def expert_sum_body(seq, *refs):
    terms, outs = refs[:seq], refs[seq:]
    total = terms[0][...].astype(F32)
    for term in terms[1:]:
        total = total + term[...].astype(F32)
    rounded = total.astype(BF16)
    rows = rounded.shape[0] // len(outs)
    for w, out in enumerate(outs):
        out[...] = rounded[w * rows : (w + 1) * rows]


def scores_body(experts, hidden, gain, router, scores):
    values = hidden[...].astype(F32)
    part = dot((values * gain[...]).astype(BF16), router[...])
    square = jnp.sum(values * values, axis=-1, keepdims=True)
    lane = lax.broadcasted_iota(jnp.int32, part.shape, 1)
    scores[...] = jnp.where(lane < experts, part, square)


def halves_body(*refs):
    blocks, out = refs[:-1], refs[-1]
    for w, block in enumerate(blocks):
        out[w] = block[out.shape[1] :, :]


def second_halves(blocks, deps=()):
    rows, width = blocks[0].shape
    return kernel_call(
        halves_body,
        shape((len(blocks), rows // 2, width), BF16),
        [VMEM] * len(blocks),
        moved=2 * len(blocks) * rows * width,
        deps=deps,
    )(*blocks)


def rows_body(chips, *refs):
    direct, crossed, out = refs[:chips], refs[chips], refs[chips + 1]
    half = crossed.shape[1]
    out[...] = jnp.concatenate(
        [block for w in range(chips) for block in (direct[w][:half, :], crossed[w])], axis=0
    )


def combine_body(chips, seq, experts, model_width, *refs):
    direct = refs[:chips]
    crossed, hidden, first, second, routes = refs[chips : chips + 5]
    scores = refs[chips + 5 : chips + 5 + seq]
    outs = refs[chips + 5 + seq :]
    rows = outs[0].shape[0]
    total = scores[0][...]
    for mask in range(1, seq):
        other = scores[mask][...]
        total = total + jnp.concatenate(
            [other[(d ^ mask) * rows : ((d ^ mask) + 1) * rows] for d in range(seq)], axis=0
        )
    logits = total * lax.rsqrt(total[:, experts : experts + 1] / model_width + EPSILON)
    lane = lax.broadcasted_iota(jnp.int32, logits.shape, 1).astype(F32)
    picked = [
        jnp.sum(jnp.where(lane == routes[:, i : i + 1], logits, 0.0), axis=-1, keepdims=True)
        for i in range(2)
    ]
    first_share = 1.0 / (1.0 + jnp.exp(picked[1] - picked[0]))
    half = crossed.shape[1]
    table = jnp.concatenate(
        [block for w in range(chips) for block in (direct[w][:half, :], crossed[w])], axis=0
    )

    def rows_of(choice):
        return lax.dot_general(
            choice[...], table, (((0,), (0,)), ((), ())), preferred_element_type=F32
        )

    sent = first_share * rows_of(first) + (1.0 - first_share) * rows_of(second)
    mixed = (hidden[...].astype(F32) + sent).astype(BF16)
    for d, out in enumerate(outs):
        out[...] = mixed[d * rows : (d + 1) * rows]


def place_body(place, *refs):
    pieces, out = refs[:-1], refs[-1]
    width = pieces[0].shape[1]
    for mask, piece in enumerate(pieces):
        out[:, pl.ds(pl.multiple_of((place[0] ^ mask) * width, 128), width)] = piece[...]


def tile_of(total, most):
    for width in range(most, 0, -128):
        if total % width == 0:
            return width
    return total


def local(
    tokens,
    norm_gain,
    in_weight,
    conv_weight,
    conv_bias,
    proj_weight,
    step_weight,
    step_bias,
    decay_log,
    skip_gain,
    out_weight,
    moe_gain,
    router_weight,
    routes,
    gate_weight,
    up_weight,
    down_weight,
):
    seq, groups = lax.axis_size("seq"), lax.axis_size("expert")
    chips = groups // 2
    me, expert = lax.axis_index("seq"), lax.axis_index("expert")
    core = expert % 2
    place = jnp.stack([me, core, expert]).astype(jnp.int32)
    masks = range(1, seq)
    length, model_width = tokens.shape
    width = model_width // seq
    half = width // 2
    channels = in_weight.shape[2]
    rank_width = step_weight.shape[0]
    state_width = decay_log.shape[1]
    lanes = 128
    tiles = channels // lanes
    own_rows = routes.shape[0]
    experts = router_weight.shape[1]
    most_slots = max(2, 3 * own_rows // experts)
    window = seq * own_rows

    x_own, *x_send = kernel_call(
        functools.partial(norm_body, seq),
        [shape((length, width), BF16)] + [shape((length, half), BF16)] * (seq - 1),
        [SMEM, VMEM, VMEM],
        flops=8 * length * model_width,
        moved=4 * length * model_width,
        limit=24,
    )(place, tokens, norm_gain[None])
    x_mine = [partner(block, "seq", mask) for mask, block in zip(masks, x_send)]
    weight = after(in_weight, x_own).reshape(width, 2 * channels)
    x_mine = after(x_mine, weight)
    x_other = [partner(block, "expert", 1) for block in x_mine]
    lane_routes = jnp.transpose(routes).astype(F32)
    spread_routes = jnp.stack(
        [
            jnp.pad(lane_routes, ((0, HALO - ROUTE_ROWS), (d * own_rows, channels - (d + 1) * own_rows)))
            for d in range(seq)
        ]
    )
    in_specs = [SMEM] + [VMEM] * (2 * seq)
    cost = dict(flops=2 * seq * length * width * channels, moved=2 * width * channels, limit=24)
    mixer_own, *mixer_send = kernel_call(
        functools.partial(mixer_project_body, seq),
        [shape((HALO + length, channels), F32)] + [shape((HALO + length, channels), BF16)] * (seq - 1),
        in_specs + [VMEM],
        [pltpu.VMEM((seq, HALO, channels), F32)],
        **cost,
    )(place, x_own, *x_mine, *x_other, weight, spread_routes)
    mixer_terms = [partner(block, "seq", mask) for mask, block in zip(masks, mixer_send)]
    assert width <= channels and window <= channels
    own_tokens = lax.dynamic_slice_in_dim(tokens, expert * own_rows, own_rows, 0)
    side_own, *side_send = kernel_call(
        functools.partial(gate_project_body, seq),
        [shape((length, channels), F32)] + [shape((length + own_rows, channels), BF16)] * (seq - 1),
        in_specs + [VMEM],
        **cost,
    )(place, x_own, *x_mine, *x_other, weight, own_tokens)

    early = seq // 2
    mixer_own = after(mixer_own, side_own)
    activated, features = kernel_call(
        functools.partial(conv_body, seq),
        [shape((length, channels), BF16), shape((length, proj_weight.shape[1]), F32)],
        [VMEM] * (seq + 3),
        flops=2 * length * channels * proj_weight.shape[1] + 16 * length * channels,
        moved=2 * channels * proj_weight.shape[1] + 10 * length * channels,
        limit=16,
    )(mixer_own, *mixer_terms, conv_weight, conv_bias[None], jnp.transpose(proj_weight))
    features = features + partner(features, "expert", 1)
    sent = features.astype(BF16)
    features_came = [partner(sent, "expert", 2 * w) for w in range(1, chips)]
    side_send = after(side_send[:early], mixer_terms[early - 1]) + after(side_send[early:], features_came[0])
    side_terms = [partner(block, "seq", mask) for mask, block in zip(masks, side_send)]
    for term in features_came:
        features = features + term.astype(F32)
    low_rank, maps = features[:, :rank_width].astype(BF16), features[:, rank_width:]

    rate = -LOG2_E * jnp.exp(jnp.transpose(decay_log)).reshape(state_width, tiles, lanes)
    tiled = shape((length, tiles, lanes), F32)
    y, cumulated, final = kernel_call(
        scan_body,
        [tiled, tiled, shape((state_width + 1, tiles, lanes), F32)],
        [SMEM] + [VMEM] * 5,
        [pltpu.VMEM(tiled.shape, F32)] * 2,
        flops=8 * length * channels * state_width,
        moved=12 * length * channels,
        limit=24,
    )(maps, low_rank, activated, step_weight, step_bias[None], rate)
    arrived = [later_partner(final, "seq", mask) for mask in masks]
    gated = kernel_call(
        functools.partial(gated_body, seq, own_rows),
        shape((length, channels), BF16),
        [SMEM, SMEM] + [VMEM] * (2 * seq + 4),
        [pltpu.VMEM(tiled.shape, F32), pltpu.VMEM((length, channels), F32)],
        flops=8 * length * channels * state_width,
        moved=16 * length * channels,
        limit=24,
    )(place, maps, *arrived, y, cumulated, rate, activated, skip_gain[None], side_own, *side_terms)

    blocks = [gated] + [partner(gated, "seq", mask) for mask in masks]

    slots = groups * seq * most_slots
    per_chip = slots // chips
    per_group = slots // groups
    choose, first, second, named = kernel_call(
        functools.partial(tables_body, seq, own_rows, most_slots),
        [shape((slots, window), BF16)] * 3 + [shape((window, 8), F32)],
        [SMEM, VMEM] + [VMEM] * (seq - 1),
        flops=2 * slots * window * window,
        moved=8 * slots * window,
    )(place, spread_routes[0], *mixer_terms)

    keep, send = kernel_call(
        functools.partial(out_project_body, seq, own_rows),
        [shape((chips, window, width), F32), shape((chips, window, width), BF16)],
        [VMEM] * (seq + 1),
        flops=2 * seq * length * channels * width,
        moved=2 * channels * width + 8 * seq * length * width,
        limit=16,
    )(*blocks, out_weight)
    crossing = partner(send, "expert", 1)
    own_sum, *chip_sends = kernel_call(
        core_sum_body,
        [shape((window, width), F32)] + [shape((window, width), BF16)] * (chips - 1),
        [VMEM] * 2,
        flops=chips * window * width,
        moved=10 * chips * window * width,
    )(keep, crossing)
    chip_terms = [partner(block, "expert", 2 * w) for w, block in zip(range(1, chips), chip_sends)]

    hidden_state, *outgoing = kernel_call(
        functools.partial(hidden_body, chips, seq),
        [shape((window, width), BF16)] + [shape((per_chip, width), BF16)] * chips,
        [SMEM] + [VMEM] * (chips + seq + 1),
        flops=2 * slots * window * width,
        moved=10 * window * width,
    )(place, own_sum, *chip_terms, own_tokens, *side_terms, choose)

    came = [outgoing[0]] + [
        partner(block, "expert", 2 * w) for w, block in zip(range(1, chips), outgoing[1:])
    ]
    sources = [gate_weight, up_weight, down_weight]
    both = lambda mask: [(0, mask, 0), (1, mask, 0)]
    current = list(fetch(place, both(0) + both(1), width, sources[:2], [hidden_state]))
    crossed = partner(second_halves(came, current), "expert", 1)
    rows = kernel_call(
        functools.partial(rows_body, chips),
        shape((slots, width), BF16),
        [VMEM] * (chips + 1),
        moved=4 * slots * width,
    )(*came, crossed)
    pieces = [rows] + [partner(rows, "seq", mask) for mask in masks]

    before, waiting = [], current
    for mask in range(seq):
        jobs = both(mask + 2) if mask + 2 < seq else []
        if mask == max(0, seq - 4):
            jobs = jobs + (both(mask + 3) if mask + 3 < seq else [])
        elif mask == seq - 3:
            jobs = [(2, other, 1) for other in range(seq)]
        elif mask > seq - 3:
            jobs = []
        before, came_in = expert_chunk(
            mask, mask == 0, mask == seq - 1, place, pieces[mask], moe_gain[None], *waiting[:2], before, jobs, sources
        )
        waiting = waiting[2:] + list(came_in)
    downs = waiting
    hidden = before[0]
    sums = []
    for mask in reversed(range(seq)):
        sums = [down_chunk(hidden, downs[mask])] + sums
    terms = [sums[0]] + [partner(sums[mask], "seq", mask) for mask in masks]
    router = jnp.pad(
        lax.dynamic_slice_in_dim(router_weight, me * width, width, 0), ((0, 0), (0, lanes - experts))
    )
    scores = kernel_call(
        functools.partial(scores_body, experts),
        shape((window, lanes), F32),
        [VMEM] * 3,
        flops=2 * window * width * lanes,
        moved=4 * window * width,
        deps=[sums[0]],
    )(hidden_state, lax.dynamic_slice_in_dim(moe_gain, me * width, width, 0)[None], router)
    scores = [scores] + [partner(scores, "seq", mask) for mask in masks]

    answers = kernel_call(
        functools.partial(expert_sum_body, seq),
        [shape((per_chip, width), BF16)] * chips,
        [VMEM] * seq,
        flops=seq * slots * width,
        moved=10 * slots * width,
        deps=scores[1:],
    )(*terms)
    answers = [answers[0]] + [
        partner(block, "expert", 2 * w) for w, block in zip(range(1, chips), answers[1:])
    ]
    crossed_back = partner(second_halves(answers), "expert", 1)

    mixed_own, *mixed_send = kernel_call(
        functools.partial(combine_body, chips, seq, experts, model_width),
        [shape((own_rows, width), BF16)] * seq,
        [VMEM] * (chips + 5 + seq),
        flops=4 * slots * window * width,
        moved=8 * slots * width,
    )(*answers, crossed_back, hidden_state, first, second, named, *scores)
    mixed = [mixed_own] + [partner(block, "seq", mask) for mask, block in zip(masks, mixed_send)]
    return kernel_call(
        place_body,
        shape((own_rows, model_width), BF16),
        [SMEM] + [VMEM] * seq,
        flops=0,
        moved=4 * own_rows * model_width,
    )(place, *mixed)


def solution(mesh):
    in_specs = (
        P("seq", None),
        P(),
        P("seq", None, "expert"),
        P(None, "expert"),
        P("expert"),
        P("expert", None),
        P(None, "expert"),
        P("expert"),
        P("expert", None),
        P("expert"),
        P("expert", "seq"),
        P(),
        P(),
        P(("seq", "expert"), None),
        P("expert", None, "seq"),
        P("expert", None, "seq"),
        P("expert", "seq", None),
    )
    out_specs = P(("seq", "expert"), None)
    return jax.shard_map(local, mesh=mesh, in_specs=in_specs, out_specs=out_specs, check_vma=False)
```

time: 227 us -> 187 us (0.82)
  waiting for transfers between devices: 84.5 us -> 63 us
  local copies, waits for them, and re-layouts: 29.8 us -> 15 us
  Pallas kernels: 39.8 us -> 47.5 us
  other arithmetic: 5.45 us -> 0.19 us
  starting transfers between devices: 65.9 us -> 60.7 us
    ppermute x52 -> x43, waiting for transfers between devices: 84.4 us -> 61 us  [partner(): return lax.ppermute(block, axis, [(i, i ^ mask) for i in range(size)])]
    slice x7 -> x0, local copies, waits for them, and re-layouts: 8.92 us -> none  [the longest x1 8.87 us: local(): mixer_weight, side_weight = (in_weight[:, 0, :], in_weight[:, 1, :])]
    pallas_call x14 -> x26, Pallas kernels: 39.8 us -> 47.5 us  [kernel_call(): return lambda *operands: call(*operands, *deps)]
    ppermute x52 -> x43, starting transfers between devices: 58.6 us -> 51.1 us  [partner(): return lax.ppermute(block, axis, [(i, i ^ mask) for i in range(size)])]
    squeeze x3 -> x0, local copies, waits for them, and re-layouts: 3.14 us -> none  [the longest x1 3.01 us: local(): mixer_weight, side_weight = (in_weight[:, 0, :], in_weight[:, 1, :])]
    unnamed x48 -> x53, local copies, waits for them, and re-layouts: 14.9 us -> 13.3 us
  transfers between devices with their start and end apart: 55 -> 46, of which waited for: 25 -> 25; matrix products, arithmetic and copies ran while one was open for 10% -> 4% of each run, Pallas kernels for 15% -> 17%
where the time goes in v2:
time: 187 us
  waiting for transfers between devices  63 us (34%)
  starting transfers between devices  60.7 us (32%)
  Pallas kernels  47.5 us (25%)
  local copies, waits for them, and re-layouts  15 us (8%)
    ppermute x43, waiting for transfers between devices, partner(): return lax.ppermute(block, axis, [(i, i ^ mask) for i in range(size)])  61 us
    ppermute x43, starting transfers between devices, partner(): return lax.ppermute(block, axis, [(i, i ^ mask) for i in range(size)])  51.1 us
    pallas_call x26, Pallas kernels, kernel_call(): return lambda *operands: call(*operands, *deps)  47.5 us
    unnamed x53, local copies, waits for them, and re-layouts  13.3 us
    ppermute x3, starting transfers between devices, later_partner(): lax.ppermute(block, axis, [(i, i ^ mask) for i in range(size) if i < i ^...  9.6 us
  transfers between devices with their start and end apart: 46, of which 25 were waited for; matrix products, arithmetic and copies ran while one was open for 4% of the time, Pallas kernels for 17%

profile of v2, /device:TPU:0, one launch (start us, length us, event | category | flops | bytes accessed | tf_op | source)
XLA Modules:
  0.0 186.8 jit_solution(12288937612761687947)
XLA Ops:
  0.1 1.2 copy-done.4
  2.0 1.0 shard_map.163
  3.0 3.0 %collective-permute-start = (bf16[128,512]{1,0:T(8,128)(2,1)S(1)}, bf16[128,512]{1,0:T(8,128)(2,1)S(1)}, u32[]{:S(2)}, u32[]{:S(2)}) collective-permute-start(bf16[128,512]{1,0:T(8,128)(2,1)S(1)} %get-tuple-element.75), channel_id=1, source_target_pairs={{0,8},{8,0},{16,24},{24,16},{1,9},{9,1},{17,25},{25,17},{2,10},{10... | collective-permute-start | bytes 393224 | tf_op jit(solution)/shard_map/ppermute | solution.py:24
  6.0 1.5 collective-permute-start.1
  7.5 5.6 %copy.20 = bf16[128,8,2,1024]{3,1,2,0:T(8,128)(2,1)} copy(bf16[128,8,2,1024]{3,2,1,0:T(2,128)(2,1)} %bitcast.40) | data formatting | bytes 8388608
  15.6 2.2 %copy-done.1 = bf16[128,8,2,1024]{3,1,2,0:T(8,128)(2,1)S(1)} copy-done((bf16[128,8,2,1024]{3,1,2,0:T(8,128)(2,1)S(1)}, bf16[128,8,2,1024]{3,1,2,0:T(8,128)(2,1)}, u32[]{:S(2)}) %copy-start.1) | copy-done | bytes 4194328
  17.8 1.8 shard_map.164
  19.7 1.5 collective-permute-start.6
  21.2 1.5 collective-permute-start.7
  23.3 0.9 constant_dynamic-slice_fusion.1.refs_9_.refs_5_
  24.2 1.8 shard_map.165
  26.1 3.6 %collective-permute-done.6.refs_1_.refs_2_ = bf16[144,1024]{1,0:T(8,128)(2,1)S(1)} collective-permute-done((bf16[144,1024]{1,0:T(8,128)(2,1)S(1)}, bf16[144,1024]{1,0:T(8,128)(2,1)S(1)}, u32[]{:S(2)}, u32[]{:S(2)}) %collective-permute-start.6) | collective-permute-done | bytes 294944 | tf_op jit(solution)/shard_map/ppermute | solution.py:24
  29.6 6.7 %collective-permute-done.7.refs_2_.refs_3_ = bf16[144,1024]{1,0:T(8,128)(2,1)S(1)} collective-permute-done((bf16[144,1024]{1,0:T(8,128)(2,1)S(1)}, bf16[144,1024]{1,0:T(8,128)(2,1)S(1)}, u32[]{:S(2)}, u32[]{:S(2)}) %collective-permute-start.7) | collective-permute-done | bytes 294944 | tf_op jit(solution)/shard_map/ppermute | solution.py:24
  37.3 1.4 collective-permute-done.9
  38.8 1.6 collective-permute-start.10
  40.4 2.6 %collective-permute-start.11 = (bf16[128,288]{1,0:T(8,128)(2,1)S(1)}, bf16[128,288]{1,0:T(8,128)(2,1)S(1)}, u32[]{:S(2)}, u32[]{:S(2)}) collective-permute-start(bf16[128,288]{1,0:T(8,128)(2,1)S(1)} %get-tuple-element.143), channel_id=1, source_target_pairs={{0,4},{1,5},{2,6},{3,7},{4,0},{5,1},{6,2},{7,3},{8,12},{9,13},{10,... | collective-permute-start | bytes 221192 | tf_op jit(solution)/shard_map/ppermute | solution.py:24
  43.3 1.3 collective-permute-start.16
  45.4 1.4 collective-permute-start.18
  46.8 4.3 %collective-permute-done.11 = bf16[128,288]{1,0:T(8,128)(2,1)S(1)} collective-permute-done((bf16[128,288]{1,0:T(8,128)(2,1)S(1)}, bf16[128,288]{1,0:T(8,128)(2,1)S(1)}, u32[]{:S(2)}, u32[]{:S(2)}) %collective-permute-start.11) | collective-permute-done | bytes 73760 | tf_op jit(solution)/shard_map/ppermute | solution.py:24
  51.2 5.4 %shard_map.167 = (f32[128,8,128]{2,1,0:T(8,128)S(1)}, f32[128,8,128]{2,1,0:T(8,128)S(1)}, f32[17,8,128]{2,1,0:T(8,128)S(1)}) custom-call(f32[128,32]{1,0:T(8,128)S(1)} %slice.9.refs_0_.refs_1_, bf16[128,256]{1,0:T(8,128)(2,1)S(1)} %slice.12.refs_1_, bf16[128,1024]{1,0:T(8,128)(2,1)S(1)} %get-tuple-element.89.refs_2_.refs_8_, ...), custom_call_target="tpu_custom_call" | custom-call | flops 16777216 | bytes 1572864 | tf_op jit(solution)/shard_map/pallas_call | solution.py:58
  56.6 3.1 %collective-permute-start.13 = (f32[17,8,128]{2,1,0:T(8,128)S(1)}, f32[17,8,128]{2,1,0:T(8,128)S(1)}, u32[]{:S(2)}, u32[]{:S(2)}) collective-permute-start(f32[17,8,128]{2,1,0:T(8,128)S(1)} %get-tuple-element.90), channel_id=1, source_target_pairs={{0,8},{16,24},{1,9},{17,25},{2,10},{18,26},{3,11},{19,27},{4,12},{... | collective-permute-start | bytes 208904 | tf_op jit(solution)/shard_map/ppermute | solution.py:29
  59.8 2.8 %collective-permute-start.14 = (f32[17,8,128]{2,1,0:T(8,128)S(1)}, f32[17,8,128]{2,1,0:T(8,128)S(1)}, u32[]{:S(2)}, u32[]{:S(2)}) collective-permute-start(f32[17,8,128]{2,1,0:T(8,128)S(1)} %get-tuple-element.90), channel_id=1, source_target_pairs={{0,16},{8,24},{1,17},{9,25},{2,18},{10,26},{3,19},{11,27},{4,20},{... | collective-permute-start | bytes 208904 | tf_op jit(solution)/shard_map/ppermute | solution.py:29
  62.5 3.7 %collective-permute-start.15 = (f32[17,8,128]{2,1,0:T(8,128)S(1)}, f32[17,8,128]{2,1,0:T(8,128)S(1)}, u32[]{:S(2)}, u32[]{:S(2)}) collective-permute-start(f32[17,8,128]{2,1,0:T(8,128)S(1)} %get-tuple-element.90), channel_id=1, source_target_pairs={{0,24},{8,16},{1,25},{9,17},{2,26},{10,18},{3,27},{11,19},{4,28},{... | collective-permute-start | bytes 208904 | tf_op jit(solution)/shard_map/ppermute | solution.py:29
  66.2 1.9 %collective-permute-done.15.refs_4_ = f32[17,8,128]{2,1,0:T(8,128)S(1)} collective-permute-done((f32[17,8,128]{2,1,0:T(8,128)S(1)}, f32[17,8,128]{2,1,0:T(8,128)S(1)}, u32[]{:S(2)}, u32[]{:S(2)}) %collective-permute-start.15) | collective-permute-done | bytes 69664 | tf_op jit(solution)/shard_map/ppermute | solution.py:29
  68.2 4.5 %shard_map.168.refs_0_ = bf16[128,1024]{1,0:T(8,128)(2,1)S(1)} custom-call(s32[3]{0:T(128)S(1)} %pad_add_fusion.refs_0_, f32[128,32]{1,0:T(8,128)S(1)} %slice.9.refs_0_.refs_1_, f32[17,8,128]{2,1,0:T(8,128)S(1)} %collective-permute-done.13.refs_2_, f32[17,8,128]{2,1,0:T(8,128)S(1)} %collective-permute-done.14.refs_3_, ...), custom_call_target="tpu_custom_call" | custom-call | flops 16777216 | bytes 2097152 | tf_op jit(solution)/shard_map/pallas_call | solution.py:58
  72.7 3.8 %collective-permute-start.20 = (bf16[128,1024]{1,0:T(8,128)(2,1)S(1)}, bf16[128,1024]{1,0:T(8,128)(2,1)S(1)}, u32[]{:S(2)}, u32[]{:S(2)}) collective-permute-start(bf16[128,1024]{1,0:T(8,128)(2,1)S(1)} %shard_map.168.refs_0_), channel_id=1, source_target_pairs={{0,16},{8,24},{16,0},{24,8},{1,17},{9,25},{17,1},{25,9},{2,18},{10... | collective-permute-start | bytes 786440 | tf_op jit(solution)/shard_map/ppermute | solution.py:24
  76.5 3.4 %collective-permute-done.19.refs_1_ = bf16[128,1024]{1,0:T(8,128)(2,1)S(1)} collective-permute-done((bf16[128,1024]{1,0:T(8,128)(2,1)S(1)}, bf16[128,1024]{1,0:T(8,128)(2,1)S(1)}, u32[]{:S(2)}, u32[]{:S(2)}) %collective-permute-start.19) | collective-permute-done | bytes 262176 | tf_op jit(solution)/shard_map/ppermute | solution.py:24
  79.9 4.3 %collective-permute-done.20.refs_2_ = bf16[128,1024]{1,0:T(8,128)(2,1)S(1)} collective-permute-done((bf16[128,1024]{1,0:T(8,128)(2,1)S(1)}, bf16[128,1024]{1,0:T(8,128)(2,1)S(1)}, u32[]{:S(2)}, u32[]{:S(2)}) %collective-permute-start.20) | collective-permute-done | bytes 262176 | tf_op jit(solution)/shard_map/ppermute | solution.py:24
  84.2 1.3 shard_map.169
  85.6 1.9 %collective-permute-done.22.refs_1_ = bf16[4,64,1024]{2,1,0:T(8,128)(2,1)S(1)} collective-permute-done((bf16[4,64,1024]{2,1,0:T(8,128)(2,1)S(1)}, bf16[4,64,1024]{2,1,0:T(8,128)(2,1)S(1)}, u32[]{:S(2)}, u32[]{:S(2)}) %collective-permute-start.22) | collective-permute-done | bytes 524320 | tf_op jit(solution)/shard_map/ppermute | solution.py:24
  87.6 2.8 %collective-permute-start.23 = (bf16[64,1024]{1,0:T(8,128)(2,1)S(1)}, bf16[64,1024]{1,0:T(8,128)(2,1)S(1)}, u32[]{:S(2)}, u32[]{:S(2)}) collective-permute-start(bf16[64,1024]{1,0:T(8,128)(2,1)S(1)} %get-tuple-element.102), channel_id=1, source_target_pairs={{0,2},{1,3},{2,0},{3,1},{4,6},{5,7},{6,4},{7,5},{8,10},{9,11},{10,... | collective-permute-start | bytes 393224 | tf_op jit(solution)/shard_map/ppermute | solution.py:24
  90.4 1.0 collective-permute-start.24
  91.3 1.5 collective-permute-start.25
  94.7 1.2 collective-permute-done.23.refs_2_
  96.0 7.3 %collective-permute-done.24.refs_3_ = bf16[64,1024]{1,0:T(8,128)(2,1)S(1)} collective-permute-done((bf16[64,1024]{1,0:T(8,128)(2,1)S(1)}, bf16[64,1024]{1,0:T(8,128)(2,1)S(1)}, u32[]{:S(2)}, u32[]{:S(2)}) %collective-permute-start.24) | collective-permute-done | bytes 131104 | tf_op jit(solution)/shard_map/ppermute | solution.py:24
  104.1 2.4 %collective-permute-start.26 = (bf16[48,1024]{1,0:T(8,128)(2,1)S(1)}, bf16[48,1024]{1,0:T(8,128)(2,1)S(1)}, u32[]{:S(2)}, u32[]{:S(2)}) collective-permute-start(bf16[48,1024]{1,0:T(8,128)(2,1)S(1)} %get-tuple-element.107), channel_id=1, source_target_pairs={{0,2},{1,3},{2,0},{3,1},{4,6},{5,7},{6,4},{7,5},{8,10},{9,11},{10,... | collective-permute-start | bytes 294920 | tf_op jit(solution)/shard_map/ppermute | solution.py:24
  106.4 0.9 collective-permute-start.27
  107.4 1.5 collective-permute-start.28
  108.9 5.8 %shard_map.173 = (bf16[1024,1792]{1,0:T(8,128)(2,1)S(1)}, bf16[1024,1792]{1,0:T(8,128)(2,1)S(1)}, bf16[1024,1792]{1,0:T(8,128)(2,1)S(1)}, bf16[1024,1792]{1,0:T(8,128)(2,1)S(1)}) custom-call(s32[3]{0:T(128)S(1)} %pad_add_fusion.refs_0_, bf16[1,4096,1792]{2,1,0:T(8,128)(2,1)} %refs_8_.1, bf16[1,4096,1792]{2,1,0:T(8,128)(2,1)} %refs_9_.1, ...), custom_call_target="tpu_custom_call" | custom-call | bytes 14680064 | tf_op jit(solution)/shard_map/pallas_call | solution.py:58
  114.7 1.3 collective-permute-done.27.refs_2_
  116.2 1.4 collective-permute-done.29.refs_4_
  117.6 1.5 collective-permute-start.32
  119.8 1.4 collective-permute-start.30
  121.2 6.1 %shard_map.176 = (f32[192,1792]{1,0:T(8,128)S(1)}, f32[192,1792]{1,0:T(8,128)S(1)}, f32[192,128]{1,0:T(8,128)S(1)}, bf16[1024,1792]{1,0:T(8,128)(2,1)S(1)}, bf16...) custom-call(s32[3]{0:T(128)S(1)} %pad_add_fusion.refs_0_, ...), custom_call_target="tpu_custom_call" | custom-call | flops 1409286144 | bytes 7340032 | tf_op jit(solution)/shard_map/pallas_call | solution.py:58
  127.3 2.4 %collective-permute-done.32.refs_1_ = bf16[192,1024]{1,0:T(8,128)(2,1)S(1)} collective-permute-done((bf16[192,1024]{1,0:T(8,128)(2,1)S(1)}, bf16[192,1024]{1,0:T(8,128)(2,1)S(1)}, u32[]{:S(2)}, u32[]{:S(2)}) %collective-permute-start.32) | collective-permute-done | bytes 393248 | tf_op jit(solution)/shard_map/ppermute | solution.py:24
  129.6 7.4 %shard_map.177 = (f32[192,1792]{1,0:T(8,128)S(1)}, f32[192,1792]{1,0:T(8,128)S(1)}, f32[192,128]{1,0:T(8,128)S(1)}, bf16[1792,1024]{1,0:T(8,128)(2,1)S(1)}, bf16...) custom-call(s32[3]{0:T(128)S(1)} %pad_add_fusion.refs_0_, ...), custom_call_target="tpu_custom_call" | custom-call | flops 1409286144 | bytes 7340032 | tf_op jit(solution)/shard_map/pallas_call | solution.py:58
  137.0 2.2 %shard_map.178 = (f32[192,1792]{1,0:T(8,128)S(1)}, f32[192,1792]{1,0:T(8,128)S(1)}, f32[192,128]{1,0:T(8,128)S(1)}) custom-call(s32[3]{0:T(128)S(1)} %pad_add_fusion.refs_0_, bf16[192,1024]{1,0:T(8,128)(2,1)S(1)} %collective-permute-done.31.refs_1_, f32[1,4096]{1,0:T(1,128)S(1)} %bitcast.33, bf16[1024,1792]{1,0:T(8,128)(2,1)S(1)} %get-tuple-element.117.refs_3_, ...), custom_call_target="tpu_custom_call" | custom-call | flops 1409286144 | bytes 7340032 | tf_op jit(solution)/shard_map/pallas_call | solution.py:58
  139.3 2.3 %shard_map.179.refs_0_ = bf16[192,1792]{1,0:T(8,128)(2,1)S(1)} custom-call(s32[3]{0:T(128)S(1)} %pad_add_fusion.refs_0_, bf16[192,1024]{1,0:T(8,128)(2,1)S(1)} %collective-permute-done.30.refs_1_, f32[1,4096]{1,0:T(1,128)S(1)} %bitcast.34, bf16[1024,1792]{1,0:T(8,128)(2,1)S(1)} %get-tuple-element.115.refs_3_, ...), custom_call_target="tpu_custom_call" | custom-call | flops 1409286144 | bytes 7340032 | tf_op jit(solution)/shard_map/pallas_call | solution.py:58
  142.5 3.2 %collective-permute-start.35 = (bf16[192,1024]{1,0:T(8,128)(2,1)S(1)}, bf16[192,1024]{1,0:T(8,128)(2,1)S(1)}, u32[]{:S(2)}, u32[]{:S(2)}) collective-permute-start(bf16[192,1024]{1,0:T(8,128)(2,1)S(1)} %shard_map.183), channel_id=1, source_target_pairs={{0,24},{8,16},{16,8},{24,0},{1,25},{9,17},{17,9},{25,1},{2,26},{10... | collective-permute-start | bytes 1179656 | tf_op jit(solution)/shard_map/ppermute | solution.py:24
  147.0 0.9 shard_map.181
  149.1 2.0 %copy-done.3 = bf16[1792,1024]{1,0:T(8,128)(2,1)S(1)} copy-done((bf16[1792,1024]{1,0:T(8,128)(2,1)S(1)}, bf16[1792,1024]{1,0:T(8,128)(2,1)}, u32[]{:S(2)}) %copy-start.3) | copy-done | bytes 3670040
  152.2 1.8 collective-permute-start.36
  154.0 1.7 collective-permute-start.37
  155.8 7.0 %collective-permute-done.36.refs_4_.refs_10_ = f32[64,128]{1,0:T(8,128)S(1)} collective-permute-done((f32[64,128]{1,0:T(8,128)S(1)}, f32[64,128]{1,0:T(8,128)S(1)}, u32[]{:S(2)}, u32[]{:S(2)}) %collective-permute-start.36) | collective-permute-done | bytes 32800 | tf_op jit(solution)/shard_map/ppermute | solution.py:24
  162.7 1.3 collective-permute-start.38
  164.0 3.5 %collective-permute-done.38.refs_6_.refs_12_ = f32[64,128]{1,0:T(8,128)S(1)} collective-permute-done((f32[64,128]{1,0:T(8,128)S(1)}, f32[64,128]{1,0:T(8,128)S(1)}, u32[]{:S(2)}, u32[]{:S(2)}) %collective-permute-start.38) | collective-permute-done | bytes 32800 | tf_op jit(solution)/shard_map/ppermute | solution.py:24
  167.8 1.7 collective-permute-start.39
  170.3 1.9 %collective-permute-start.41 = (bf16[48,1024]{1,0:T(8,128)(2,1)S(1)}, bf16[48,1024]{1,0:T(8,128)(2,1)S(1)}, u32[]{:S(2)}, u32[]{:S(2)}) collective-permute-start(bf16[48,1024]{1,0:T(8,128)(2,1)S(1)} %get-tuple-element.135), channel_id=1, source_target_pairs={{0,6},{1,7},{2,4},{3,5},{4,2},{5,3},{6,0},{7,1},{8,14},{9,15},{10,... | collective-permute-start | bytes 294920 | tf_op jit(solution)/shard_map/ppermute | solution.py:24
  172.8 4.3 %collective-permute-done.40.refs_2_ = bf16[48,1024]{1,0:T(8,128)(2,1)S(1)} collective-permute-done((bf16[48,1024]{1,0:T(8,128)(2,1)S(1)}, bf16[48,1024]{1,0:T(8,128)(2,1)S(1)}, u32[]{:S(2)}, u32[]{:S(2)}) %collective-permute-start.40) | collective-permute-done | bytes 98336 | tf_op jit(solution)/shard_map/ppermute | solution.py:24
  177.2 1.4 collective-permute-done.42.refs_4_
  179.1 1.7 collective-permute-start.44
  180.8 1.7 collective-permute-start.45
  183.0 2.6 %collective-permute-done.45.refs_4_ = bf16[16,1024]{1,0:T(8,128)(2,1)S(1)} collective-permute-done((bf16[16,1024]{1,0:T(8,128)(2,1)S(1)}, bf16[16,1024]{1,0:T(8,128)(2,1)S(1)}, u32[]{:S(2)}, u32[]{:S(2)}) %collective-permute-start.45) | collective-permute-done | bytes 32800 | tf_op jit(solution)/shard_map/ppermute | solution.py:24
  185.6 1.2 shard_map.188
  (120 shorter events, 16.8 us)
Async XLA Ops:
  0.0 148.8 %copy-start = (bf16[4096,8]{0,1:T(8,128)(2,1)S(1)}, bf16[4096,8]{0,1:T(8,128)(2,1)}, u32[]{:S(2)}) copy-start(bf16[4096,8]{0,1:T(8,128)(2,1)} %param.29) | copy-start | bytes 196612
  0.1 139.2 %copy-start.8 = (s32[3]{0:T(128)}, s32[3]{0:T(128)S(1)}, u32[]{:S(2)}) copy-start(s32[3]{0:T(128)S(1)} %pad_add_fusion.refs_0_) | copy-start | bytes 40
  3.0 10.2 %collective-permute-start = (bf16[128,512]{1,0:T(8,128)(2,1)S(1)}, bf16[128,512]{1,0:T(8,128)(2,1)S(1)}, u32[]{:S(2)}, u32[]{:S(2)}) collective-permute-start(bf16[128,512]{1,0:T(8,128)(2,1)S(1)} %get-tuple-element.75), channel_id=1, source_target_pairs={{0,8},{8,0},{16,24},{24,16},{1,9},{9,1},{17,25},{25,17},{2,10},{10... | collective-permute-start | bytes 393224 | tf_op jit(solution)/shard_map/ppermute | solution.py:24
  6.0 7.8 %collective-permute-start.1 = (bf16[128,512]{1,0:T(8,128)(2,1)S(1)}, bf16[128,512]{1,0:T(8,128)(2,1)S(1)}, u32[]{:S(2)}, u32[]{:S(2)}) collective-permute-start(bf16[128,512]{1,0:T(8,128)(2,1)S(1)} %get-tuple-element.76), channel_id=1, source_target_pairs={{0,16},{8,24},{16,0},{24,8},{1,17},{9,25},{17,1},{25,9},{2,18},{10... | collective-permute-start | bytes 393224 | tf_op jit(solution)/shard_map/ppermute | solution.py:24
  7.5 6.3 %collective-permute-start.2 = (bf16[128,512]{1,0:T(8,128)(2,1)S(1)}, bf16[128,512]{1,0:T(8,128)(2,1)S(1)}, u32[]{:S(2)}, u32[]{:S(2)}) collective-permute-start(bf16[128,512]{1,0:T(8,128)(2,1)S(1)} %get-tuple-element.77), channel_id=1, source_target_pairs={{0,24},{8,16},{16,8},{24,0},{1,25},{9,17},{17,9},{25,1},{2,26},{10... | collective-permute-start | bytes 393224 | tf_op jit(solution)/shard_map/ppermute | solution.py:24
  7.5 5.6 %copy-start.24 = (s32[16,2]{0,1:T(2,128)S(1)}, s32[16,2]{0,1:T(2,128)}, u32[]{:S(2)}) copy-start(s32[16,2]{0,1:T(2,128)} %param.30) | copy-start | bytes 388
  13.8 1.3 collective-permute-start.3
  13.8 1.5 collective-permute-start.4
  14.3 1.3 collective-permute-start.5
  19.7 16.7 %copy-start.5 = (bf16[1024,288]{0,1:T(8,128)(2,1)S(1)}, bf16[1024,288]{0,1:T(8,128)(2,1)}, u32[]{:S(2)}) copy-start(bf16[1024,288]{0,1:T(8,128)(2,1)} %param.22) | copy-start | bytes 1769476
  19.7 16.7 %copy-start.17 = (f32[4,1024]{1,0:T(4,128)S(1)}, f32[4,1024]{1,0:T(4,128)}, u32[]{:S(2)}) copy-start(f32[4,1024]{1,0:T(4,128)} %refs_4_.2) | copy-start | bytes 49156
  19.7 16.7 %copy-start.19 = (f32[1024]{0:T(1024)S(1)}, f32[1024]{0:T(1024)}, u32[]{:S(2)}) copy-start(f32[1024]{0:T(1024)} %param.21) | copy-start | bytes 12292
  19.7 9.9 %collective-permute-start.6 = (bf16[144,1024]{1,0:T(8,128)(2,1)S(1)}, bf16[144,1024]{1,0:T(8,128)(2,1)S(1)}, u32[]{:S(2)}, u32[]{:S(2)}) collective-permute-start(bf16[144,1024]{1,0:T(8,128)(2,1)S(1)} %get-tuple-element.85), channel_id=1, source_target_pairs={{0,8},{8,0},{16,24},{24,16},{1,9},{9,1},{17,25},{25,17},{2,10},{10... | collective-permute-start | bytes 884744 | tf_op jit(solution)/shard_map/ppermute | solution.py:24
  21.2 15.1 %collective-permute-start.7 = (bf16[144,1024]{1,0:T(8,128)(2,1)S(1)}, bf16[144,1024]{1,0:T(8,128)(2,1)S(1)}, u32[]{:S(2)}, u32[]{:S(2)}) collective-permute-start(bf16[144,1024]{1,0:T(8,128)(2,1)S(1)} %get-tuple-element.86), channel_id=1, source_target_pairs={{0,16},{8,24},{16,0},{24,8},{1,17},{9,25},{17,1},{25,9},{2,18},{10... | collective-permute-start | bytes 884744 | tf_op jit(solution)/shard_map/ppermute | solution.py:24
  22.8 13.6 %collective-permute-start.8 = (bf16[144,1024]{1,0:T(8,128)(2,1)S(1)}, bf16[144,1024]{1,0:T(8,128)(2,1)S(1)}, u32[]{:S(2)}, u32[]{:S(2)}) collective-permute-start(bf16[144,1024]{1,0:T(8,128)(2,1)S(1)} %get-tuple-element.87), channel_id=1, source_target_pairs={{0,24},{8,16},{16,8},{24,0},{1,25},{9,17},{17,9},{25,1},{2,26},{10... | collective-permute-start | bytes 884744 | tf_op jit(solution)/shard_map/ppermute | solution.py:24
  24.2 19.1 %copy-start.23 = (f32[1024,16]{0,1:T(8,128)S(1)}, f32[1024,16]{0,1:T(8,128)}, u32[]{:S(2)}) copy-start(f32[1024,16]{0,1:T(8,128)} %param.25) | copy-start | bytes 196612
  24.2 27.0 %copy-start.6 = (bf16[256,1024]{1,0:T(8,128)(2,1)S(1)}, bf16[256,1024]{1,0:T(8,128)(2,1)}, u32[]{:S(2)}) copy-start(bf16[256,1024]{1,0:T(8,128)(2,1)} %refs_3_.1) | copy-start | bytes 1572868
  24.2 27.0 %copy-start.20 = (f32[1024]{0:T(1024)S(1)}, f32[1024]{0:T(1024)}, u32[]{:S(2)}) copy-start(f32[1024]{0:T(1024)} %param.24) | copy-start | bytes 12292
  26.0 42.1 %copy-start.21 = (f32[1024]{0:T(1024)S(1)}, f32[1024]{0:T(1024)}, u32[]{:S(2)}) copy-start(f32[1024]{0:T(1024)} %param.26) | copy-start | bytes 12292
  36.4 47.8 %copy-start.22 = (bf16[1024,1024]{1,0:T(8,128)(2,1)S(1)}, bf16[1024,1024]{1,0:T(8,128)(2,1)}, u32[]{:S(2)}) copy-start(bf16[1024,1024]{1,0:T(8,128)(2,1)} %refs_4_.3) | copy-start | bytes 6291460
  37.3 1.5 collective-permute-start.9
  38.8 6.7 %collective-permute-start.10 = (bf16[128,288]{1,0:T(8,128)(2,1)S(1)}, bf16[128,288]{1,0:T(8,128)(2,1)S(1)}, u32[]{:S(2)}, u32[]{:S(2)}) collective-permute-start(bf16[128,288]{1,0:T(8,128)(2,1)S(1)} %get-tuple-element.143), channel_id=1, source_target_pairs={{0,2},{1,3},{2,0},{3,1},{4,6},{5,7},{6,4},{7,5},{8,10},{9,11},{10,... | collective-permute-start | bytes 221192 | tf_op jit(solution)/shard_map/ppermute | solution.py:24
  40.4 10.7 %collective-permute-start.11 = (bf16[128,288]{1,0:T(8,128)(2,1)S(1)}, bf16[128,288]{1,0:T(8,128)(2,1)S(1)}, u32[]{:S(2)}, u32[]{:S(2)}) collective-permute-start(bf16[128,288]{1,0:T(8,128)(2,1)S(1)} %get-tuple-element.143), channel_id=1, source_target_pairs={{0,4},{1,5},{2,6},{3,7},{4,0},{5,1},{6,2},{7,3},{8,12},{9,13},{10,... | collective-permute-start | bytes 221192 | tf_op jit(solution)/shard_map/ppermute | solution.py:24
  43.0 8.1 %collective-permute-start.12 = (bf16[128,288]{1,0:T(8,128)(2,1)S(1)}, bf16[128,288]{1,0:T(8,128)(2,1)S(1)}, u32[]{:S(2)}, u32[]{:S(2)}) collective-permute-start(bf16[128,288]{1,0:T(8,128)(2,1)S(1)} %get-tuple-element.143), channel_id=1, source_target_pairs={{0,6},{1,7},{2,4},{3,5},{4,2},{5,3},{6,0},{7,1},{8,14},{9,15},{10,... | collective-permute-start | bytes 221192 | tf_op jit(solution)/shard_map/ppermute | solution.py:24
  43.3 24.9 %collective-permute-start.16 = (bf16[144,1024]{1,0:T(8,128)(2,1)S(1)}, bf16[144,1024]{1,0:T(8,128)(2,1)S(1)}, u32[]{:S(2)}, u32[]{:S(2)}) collective-permute-start(bf16[144,1024]{1,0:T(8,128)(2,1)S(1)} %get-tuple-element.95), channel_id=1, source_target_pairs={{0,8},{8,0},{16,24},{24,16},{1,9},{9,1},{17,25},{25,17},{2,10},{10... | collective-permute-start | bytes 884744 | tf_op jit(solution)/shard_map/ppermute | solution.py:24
  44.6 23.6 %collective-permute-start.17 = (bf16[144,1024]{1,0:T(8,128)(2,1)S(1)}, bf16[144,1024]{1,0:T(8,128)(2,1)S(1)}, u32[]{:S(2)}, u32[]{:S(2)}) collective-permute-start(bf16[144,1024]{1,0:T(8,128)(2,1)S(1)} %get-tuple-element.96), channel_id=1, source_target_pairs={{0,16},{8,24},{16,0},{24,8},{1,17},{9,25},{17,1},{25,9},{2,18},{10... | collective-permute-start | bytes 884744 | tf_op jit(solution)/shard_map/ppermute | solution.py:24
  45.4 22.7 %collective-permute-start.18 = (bf16[144,1024]{1,0:T(8,128)(2,1)S(1)}, bf16[144,1024]{1,0:T(8,128)(2,1)S(1)}, u32[]{:S(2)}, u32[]{:S(2)}) collective-permute-start(bf16[144,1024]{1,0:T(8,128)(2,1)S(1)} %get-tuple-element.98), channel_id=1, source_target_pairs={{0,24},{8,16},{16,8},{24,0},{1,25},{9,17},{17,9},{25,1},{2,26},{10... | collective-permute-start | bytes 884744 | tf_op jit(solution)/shard_map/ppermute | solution.py:24
  56.6 5.9 %collective-permute-start.13 = (f32[17,8,128]{2,1,0:T(8,128)S(1)}, f32[17,8,128]{2,1,0:T(8,128)S(1)}, u32[]{:S(2)}, u32[]{:S(2)}) collective-permute-start(f32[17,8,128]{2,1,0:T(8,128)S(1)} %get-tuple-element.90), channel_id=1, source_target_pairs={{0,8},{16,24},{1,9},{17,25},{2,10},{18,26},{3,11},{19,27},{4,12},{... | collective-permute-start | bytes 208904 | tf_op jit(solution)/shard_map/ppermute | solution.py:29
  59.8 6.5 %collective-permute-start.14 = (f32[17,8,128]{2,1,0:T(8,128)S(1)}, f32[17,8,128]{2,1,0:T(8,128)S(1)}, u32[]{:S(2)}, u32[]{:S(2)}) collective-permute-start(f32[17,8,128]{2,1,0:T(8,128)S(1)} %get-tuple-element.90), channel_id=1, source_target_pairs={{0,16},{8,24},{1,17},{9,25},{2,18},{10,26},{3,19},{11,27},{4,20},{... | collective-permute-start | bytes 208904 | tf_op jit(solution)/shard_map/ppermute | solution.py:29
  62.5 5.6 %collective-permute-start.15 = (f32[17,8,128]{2,1,0:T(8,128)S(1)}, f32[17,8,128]{2,1,0:T(8,128)S(1)}, u32[]{:S(2)}, u32[]{:S(2)}) collective-permute-start(f32[17,8,128]{2,1,0:T(8,128)S(1)} %get-tuple-element.90), channel_id=1, source_target_pairs={{0,24},{8,16},{1,25},{9,17},{2,26},{10,18},{3,27},{11,19},{4,28},{... | collective-permute-start | bytes 208904 | tf_op jit(solution)/shard_map/ppermute | solution.py:29
  72.6 7.3 %collective-permute-start.19 = (bf16[128,1024]{1,0:T(8,128)(2,1)S(1)}, bf16[128,1024]{1,0:T(8,128)(2,1)S(1)}, u32[]{:S(2)}, u32[]{:S(2)}) collective-permute-start(bf16[128,1024]{1,0:T(8,128)(2,1)S(1)} %shard_map.168.refs_0_), channel_id=1, source_target_pairs={{0,8},{8,0},{16,24},{24,16},{1,9},{9,1},{17,25},{25,17},{2,10},{10... | collective-permute-start | bytes 786440 | tf_op jit(solution)/shard_map/ppermute | solution.py:24
  72.7 11.5 %collective-permute-start.20 = (bf16[128,1024]{1,0:T(8,128)(2,1)S(1)}, bf16[128,1024]{1,0:T(8,128)(2,1)S(1)}, u32[]{:S(2)}, u32[]{:S(2)}) collective-permute-start(bf16[128,1024]{1,0:T(8,128)(2,1)S(1)} %shard_map.168.refs_0_), channel_id=1, source_target_pairs={{0,16},{8,24},{16,0},{24,8},{1,17},{9,25},{17,1},{25,9},{2,18},{10... | collective-permute-start | bytes 786440 | tf_op jit(solution)/shard_map/ppermute | solution.py:24
  76.5 7.7 %collective-permute-start.21 = (bf16[128,1024]{1,0:T(8,128)(2,1)S(1)}, bf16[128,1024]{1,0:T(8,128)(2,1)S(1)}, u32[]{:S(2)}, u32[]{:S(2)}) collective-permute-start(bf16[128,1024]{1,0:T(8,128)(2,1)S(1)} %shard_map.168.refs_0_), channel_id=1, source_target_pairs={{0,24},{8,16},{16,8},{24,0},{1,25},{9,17},{17,9},{25,1},{2,26},{10... | collective-permute-start | bytes 786440 | tf_op jit(solution)/shard_map/ppermute | solution.py:24
  85.5 2.0 %collective-permute-start.22 = (bf16[4,64,1024]{2,1,0:T(8,128)(2,1)S(1)}, bf16[4,64,1024]{2,1,0:T(8,128)(2,1)S(1)}, u32[]{:S(2)}, u32[]{:S(2)}) collective-permute-start(bf16[4,64,1024]{2,1,0:T(8,128)(2,1)S(1)} %get-tuple-element.100), channel_id=1, source_target_pairs={{0,1},{1,0},{2,3},{3,2},{4,5},{5,4},{6,7},{7,6},{8,9},{9,8},{10,11... | collective-permute-start | bytes 1572872 | tf_op jit(solution)/shard_map/ppermute | solution.py:24
  87.6 8.4 %collective-permute-start.23 = (bf16[64,1024]{1,0:T(8,128)(2,1)S(1)}, bf16[64,1024]{1,0:T(8,128)(2,1)S(1)}, u32[]{:S(2)}, u32[]{:S(2)}) collective-permute-start(bf16[64,1024]{1,0:T(8,128)(2,1)S(1)} %get-tuple-element.102), channel_id=1, source_target_pairs={{0,2},{1,3},{2,0},{3,1},{4,6},{5,7},{6,4},{7,5},{8,10},{9,11},{10,... | collective-permute-start | bytes 393224 | tf_op jit(solution)/shard_map/ppermute | solution.py:24
  90.4 12.9 %collective-permute-start.24 = (bf16[64,1024]{1,0:T(8,128)(2,1)S(1)}, bf16[64,1024]{1,0:T(8,128)(2,1)S(1)}, u32[]{:S(2)}, u32[]{:S(2)}) collective-permute-start(bf16[64,1024]{1,0:T(8,128)(2,1)S(1)} %get-tuple-element.103), channel_id=1, source_target_pairs={{0,4},{1,5},{2,6},{3,7},{4,0},{5,1},{6,2},{7,3},{8,12},{9,13},{10,... | collective-permute-start | bytes 393224 | tf_op jit(solution)/shard_map/ppermute | solution.py:24
  91.3 11.9 %collective-permute-start.25 = (bf16[64,1024]{1,0:T(8,128)(2,1)S(1)}, bf16[64,1024]{1,0:T(8,128)(2,1)S(1)}, u32[]{:S(2)}, u32[]{:S(2)}) collective-permute-start(bf16[64,1024]{1,0:T(8,128)(2,1)S(1)} %get-tuple-element.104), channel_id=1, source_target_pairs={{0,6},{1,7},{2,4},{3,5},{4,2},{5,3},{6,0},{7,1},{8,14},{9,15},{10,... | collective-permute-start | bytes 393224 | tf_op jit(solution)/shard_map/ppermute | solution.py:24
  94.7 20.0 %copy-start.10 = (bf16[192,64]{1,0:T(8,128)(2,1)}, bf16[192,64]{1,0:T(8,128)(2,1)S(1)}, u32[]{:S(2)}) copy-start(bf16[192,64]{1,0:T(8,128)(2,1)S(1)} %get-tuple-element.136.refs_6_) | copy-start | bytes 73732
  104.1 10.6 %collective-permute-start.26 = (bf16[48,1024]{1,0:T(8,128)(2,1)S(1)}, bf16[48,1024]{1,0:T(8,128)(2,1)S(1)}, u32[]{:S(2)}, u32[]{:S(2)}) collective-permute-start(bf16[48,1024]{1,0:T(8,128)(2,1)S(1)} %get-tuple-element.107), channel_id=1, source_target_pairs={{0,2},{1,3},{2,0},{3,1},{4,6},{5,7},{6,4},{7,5},{8,10},{9,11},{10,... | collective-permute-start | bytes 294920 | tf_op jit(solution)/shard_map/ppermute | solution.py:24
  106.4 9.6 %collective-permute-start.27 = (bf16[48,1024]{1,0:T(8,128)(2,1)S(1)}, bf16[48,1024]{1,0:T(8,128)(2,1)S(1)}, u32[]{:S(2)}, u32[]{:S(2)}) collective-permute-start(bf16[48,1024]{1,0:T(8,128)(2,1)S(1)} %get-tuple-element.108), channel_id=1, source_target_pairs={{0,4},{1,5},{2,6},{3,7},{4,0},{5,1},{6,2},{7,3},{8,12},{9,13},{10,... | collective-permute-start | bytes 294920 | tf_op jit(solution)/shard_map/ppermute | solution.py:24
  107.4 8.7 %collective-permute-start.28 = (bf16[48,1024]{1,0:T(8,128)(2,1)S(1)}, bf16[48,1024]{1,0:T(8,128)(2,1)S(1)}, u32[]{:S(2)}, u32[]{:S(2)}) collective-permute-start(bf16[48,1024]{1,0:T(8,128)(2,1)S(1)} %get-tuple-element.109), channel_id=1, source_target_pairs={{0,6},{1,7},{2,4},{3,5},{4,2},{5,3},{6,0},{7,1},{8,14},{9,15},{10,... | collective-permute-start | bytes 294920 | tf_op jit(solution)/shard_map/ppermute | solution.py:24
  116.1 5.1 %copy-start.7 = (f32[4096]{0:T(1024)S(1)}, f32[4096]{0:T(1024)}, u32[]{:S(2)}) copy-start(f32[4096]{0:T(1024)} %param.28) | copy-start | bytes 49156
  116.1 1.5 collective-permute-start.29
  117.6 12.0 %collective-permute-start.32 = (bf16[192,1024]{1,0:T(8,128)(2,1)S(1)}, bf16[192,1024]{1,0:T(8,128)(2,1)S(1)}, u32[]{:S(2)}, u32[]{:S(2)}) collective-permute-start(bf16[192,1024]{1,0:T(8,128)(2,1)S(1)} %shard_map.175.refs_1_), channel_id=1, source_target_pairs={{0,8},{8,0},{16,24},{24,16},{1,9},{9,1},{17,25},{25,17},{2,10},{10... | collective-permute-start | bytes 1179656 | tf_op jit(solution)/shard_map/ppermute | solution.py:24
  119.1 17.9 %collective-permute-start.31 = (bf16[192,1024]{1,0:T(8,128)(2,1)S(1)}, bf16[192,1024]{1,0:T(8,128)(2,1)S(1)}, u32[]{:S(2)}, u32[]{:S(2)}) collective-permute-start(bf16[192,1024]{1,0:T(8,128)(2,1)S(1)} %shard_map.175.refs_1_), channel_id=1, source_target_pairs={{0,16},{8,24},{16,0},{24,8},{1,17},{9,25},{17,1},{25,9},{2,18},{10... | collective-permute-start | bytes 1179656 | tf_op jit(solution)/shard_map/ppermute | solution.py:24
  119.8 19.5 %collective-permute-start.30 = (bf16[192,1024]{1,0:T(8,128)(2,1)S(1)}, bf16[192,1024]{1,0:T(8,128)(2,1)S(1)}, u32[]{:S(2)}, u32[]{:S(2)}) collective-permute-start(bf16[192,1024]{1,0:T(8,128)(2,1)S(1)} %shard_map.175.refs_1_), channel_id=1, source_target_pairs={{0,24},{8,16},{16,8},{24,0},{1,25},{9,17},{17,9},{25,1},{2,26},{10... | collective-permute-start | bytes 1179656 | tf_op jit(solution)/shard_map/ppermute | solution.py:24
  142.5 25.0 %collective-permute-start.35 = (bf16[192,1024]{1,0:T(8,128)(2,1)S(1)}, bf16[192,1024]{1,0:T(8,128)(2,1)S(1)}, u32[]{:S(2)}, u32[]{:S(2)}) collective-permute-start(bf16[192,1024]{1,0:T(8,128)(2,1)S(1)} %shard_map.183), channel_id=1, source_target_pairs={{0,24},{8,16},{16,8},{24,0},{1,25},{9,17},{17,9},{25,1},{2,26},{10... | collective-permute-start | bytes 1179656 | tf_op jit(solution)/shard_map/ppermute | solution.py:24
  146.6 20.9 %collective-permute-start.34 = (bf16[192,1024]{1,0:T(8,128)(2,1)S(1)}, bf16[192,1024]{1,0:T(8,128)(2,1)S(1)}, u32[]{:S(2)}, u32[]{:S(2)}) collective-permute-start(bf16[192,1024]{1,0:T(8,128)(2,1)S(1)} %shard_map.182), channel_id=1, source_target_pairs={{0,16},{8,24},{16,0},{24,8},{1,17},{9,25},{17,1},{25,9},{2,18},{10... | collective-permute-start | bytes 1179656 | tf_op jit(solution)/shard_map/ppermute | solution.py:24
  147.9 19.7 %collective-permute-start.33 = (bf16[192,1024]{1,0:T(8,128)(2,1)S(1)}, bf16[192,1024]{1,0:T(8,128)(2,1)S(1)}, u32[]{:S(2)}, u32[]{:S(2)}) collective-permute-start(bf16[192,1024]{1,0:T(8,128)(2,1)S(1)} %shard_map.181), channel_id=1, source_target_pairs={{0,8},{8,0},{16,24},{24,16},{1,9},{9,1},{17,25},{25,17},{2,10},{10... | collective-permute-start | bytes 1179656 | tf_op jit(solution)/shard_map/ppermute | solution.py:24
  148.8 3.2 %copy-start.18 = (f32[1024]{0:T(1024)S(1)}, f32[1024]{0:T(1024)}, u32[]{:S(2)}) copy-start(f32[1024]{0:T(1024)} %dynamic_slice.10) | copy-start | bytes 12292
  151.1 27.5 %copy-start.11 = (bf16[192,64]{1,0:T(8,128)(2,1)S(1)}, bf16[192,64]{1,0:T(8,128)(2,1)}, u32[]{:S(2)}) copy-start(bf16[192,64]{1,0:T(8,128)(2,1)} %copy-done.10) | copy-start | bytes 73732
  151.1 27.5 %copy-start.13 = (bf16[192,64]{1,0:T(8,128)(2,1)S(1)}, bf16[192,64]{1,0:T(8,128)(2,1)}, u32[]{:S(2)}) copy-start(bf16[192,64]{1,0:T(8,128)(2,1)} %copy-done.12) | copy-start | bytes 73732
  151.1 27.5 %copy-start.15 = (f32[64,8]{1,0:T(8,128)S(1)}, f32[64,8]{1,0:T(8,128)}, u32[]{:S(2)}) copy-start(f32[64,8]{1,0:T(8,128)} %copy-done.14) | copy-start | bytes 6148
  151.1 34.5 %copy-start.9 = (s32[3]{0:T(128)S(1)}, s32[3]{0:T(128)}, u32[]{:S(2)}) copy-start(s32[3]{0:T(128)} %copy-done.8) | copy-start | bytes 40
  152.2 10.5 %collective-permute-start.36 = (f32[64,128]{1,0:T(8,128)S(1)}, f32[64,128]{1,0:T(8,128)S(1)}, u32[]{:S(2)}, u32[]{:S(2)}) collective-permute-start(f32[64,128]{1,0:T(8,128)S(1)} %shard_map.184.refs_9_), channel_id=1, source_target_pairs={{0,8},{8,0},{16,24},{24,16},{1,9},{9,1},{17,25},{25,17},{2,10},{10... | collective-permute-start | bytes 98312 | tf_op jit(solution)/shard_map/ppermute | solution.py:24
  154.0 10.0 %collective-permute-start.37 = (f32[64,128]{1,0:T(8,128)S(1)}, f32[64,128]{1,0:T(8,128)S(1)}, u32[]{:S(2)}, u32[]{:S(2)}) collective-permute-start(f32[64,128]{1,0:T(8,128)S(1)} %shard_map.184.refs_9_), channel_id=1, source_target_pairs={{0,16},{8,24},{16,0},{24,8},{1,17},{9,25},{17,1},{25,9},{2,18},{10... | collective-permute-start | bytes 98312 | tf_op jit(solution)/shard_map/ppermute | solution.py:24
  162.7 4.8 %collective-permute-start.38 = (f32[64,128]{1,0:T(8,128)S(1)}, f32[64,128]{1,0:T(8,128)S(1)}, u32[]{:S(2)}, u32[]{:S(2)}) collective-permute-start(f32[64,128]{1,0:T(8,128)S(1)} %shard_map.184.refs_9_), channel_id=1, source_target_pairs={{0,24},{8,16},{16,8},{24,0},{1,25},{9,17},{17,9},{25,1},{2,26},{10... | collective-permute-start | bytes 98312 | tf_op jit(solution)/shard_map/ppermute | solution.py:24
  167.8 5.0 %collective-permute-start.39 = (bf16[48,1024]{1,0:T(8,128)(2,1)S(1)}, bf16[48,1024]{1,0:T(8,128)(2,1)S(1)}, u32[]{:S(2)}, u32[]{:S(2)}) collective-permute-start(bf16[48,1024]{1,0:T(8,128)(2,1)S(1)} %get-tuple-element.133), channel_id=1, source_target_pairs={{0,2},{1,3},{2,0},{3,1},{4,6},{5,7},{6,4},{7,5},{8,10},{9,11},{10,... | collective-permute-start | bytes 294920 | tf_op jit(solution)/shard_map/ppermute | solution.py:24
  169.4 7.6 %collective-permute-start.40 = (bf16[48,1024]{1,0:T(8,128)(2,1)S(1)}, bf16[48,1024]{1,0:T(8,128)(2,1)S(1)}, u32[]{:S(2)}, u32[]{:S(2)}) collective-permute-start(bf16[48,1024]{1,0:T(8,128)(2,1)S(1)} %get-tuple-element.134), channel_id=1, source_target_pairs={{0,4},{1,5},{2,6},{3,7},{4,0},{5,1},{6,2},{7,3},{8,12},{9,13},{10,... | collective-permute-start | bytes 294920 | tf_op jit(solution)/shard_map/ppermute | solution.py:24
  170.3 6.8 %collective-permute-start.41 = (bf16[48,1024]{1,0:T(8,128)(2,1)S(1)}, bf16[48,1024]{1,0:T(8,128)(2,1)S(1)}, u32[]{:S(2)}, u32[]{:S(2)}) collective-permute-start(bf16[48,1024]{1,0:T(8,128)(2,1)S(1)} %get-tuple-element.135), channel_id=1, source_target_pairs={{0,6},{1,7},{2,4},{3,5},{4,2},{5,3},{6,0},{7,1},{8,14},{9,15},{10,... | collective-permute-start | bytes 294920 | tf_op jit(solution)/shard_map/ppermute | solution.py:24
  177.1 1.5 collective-permute-start.42
  178.9 4.0 %collective-permute-start.43 = (bf16[16,1024]{1,0:T(8,128)(2,1)S(1)}, bf16[16,1024]{1,0:T(8,128)(2,1)S(1)}, u32[]{:S(2)}, u32[]{:S(2)}) collective-permute-start(bf16[16,1024]{1,0:T(8,128)(2,1)S(1)} %get-tuple-element.140), channel_id=1, source_target_pairs={{0,8},{8,0},{16,24},{24,16},{1,9},{9,1},{17,25},{25,17},{2,10},{10... | collective-permute-start | bytes 98312 | tf_op jit(solution)/shard_map/ppermute | solution.py:24
  179.1 3.9 %collective-permute-start.44 = (bf16[16,1024]{1,0:T(8,128)(2,1)S(1)}, bf16[16,1024]{1,0:T(8,128)(2,1)S(1)}, u32[]{:S(2)}, u32[]{:S(2)}) collective-permute-start(bf16[16,1024]{1,0:T(8,128)(2,1)S(1)} %get-tuple-element.141), channel_id=1, source_target_pairs={{0,16},{8,24},{16,0},{24,8},{1,17},{9,25},{17,1},{25,9},{2,18},{10... | collective-permute-start | bytes 98312 | tf_op jit(solution)/shard_map/ppermute | solution.py:24
  180.8 4.8 %collective-permute-start.45 = (bf16[16,1024]{1,0:T(8,128)(2,1)S(1)}, bf16[16,1024]{1,0:T(8,128)(2,1)S(1)}, u32[]{:S(2)}, u32[]{:S(2)}) collective-permute-start(bf16[16,1024]{1,0:T(8,128)(2,1)S(1)} %get-tuple-element.142), channel_id=1, source_target_pairs={{0,24},{8,16},{16,8},{24,0},{1,25},{9,17},{17,9},{25,1},{2,26},{10... | collective-permute-start | bytes 98312 | tf_op jit(solution)/shard_map/ppermute | solution.py:24
  (7 other events, 9.7 us)

commit v3 on v2

--- a/solution.py
+++ b/solution.py
@@ -74,34 +74,48 @@
     me, core = place[0], place[1]
 
     def columns(start, width):
-        start = pl.multiple_of(start, 128)
-        part = tokens[:, pl.ds(start, width)].astype(F32)
-        return (part * inverse * gain[:, pl.ds(start, width)]).astype(BF16)
+        part = pl.ds(pl.multiple_of(start, 128), width)
+        return (tokens[:, part].astype(F32) * inverse * gain[:, part]).astype(BF16)
 
     own[...] = columns(me * own_width, own_width)
     for mask in range(1, seq):
         sends[mask - 1][...] = columns((me ^ mask) * own_width + core * half, half)
 
 
-def project(x_own, x_mine, x_other, weight, core, branch):
-    half = weight.shape[0] // 2
-    channels = weight.shape[1] // 2
-    part = slice(branch * channels, (branch + 1) * channels)
-    yield dot(x_own[...], weight[:, part])
-    first = weight[pl.ds(pl.multiple_of(core * half, half), half), part]
-    second = weight[pl.ds(pl.multiple_of((1 - core) * half, half), half), part]
-    for mine, other in zip(x_mine, x_other):
-        yield dot(mine[...], first) + dot(other[...], second)
-
-
-def mixer_project_body(seq, place, x_own, *refs):
-    x_mine, x_other = refs[: seq - 1], refs[seq - 1 : 2 * seq - 2]
-    weight, routes = refs[2 * seq - 2 : 2 * seq]
-    outs = refs[2 * seq : 3 * seq]
-    tails = refs[3 * seq]
-    me, core = place[0], place[1]
-    length = x_own.shape[0]
-    for index, product in enumerate(project(x_own, x_mine, x_other, weight, core, 0)):
+def pass_body(*refs):
+    for block, out in zip(refs[: len(refs) // 2], refs[len(refs) // 2 :]):
+        out[...] = block[...]
+
+
+def project(core, own, mine, other, source, branch, weight, sems):
+    depth, channels = weight.shape
+    parts = sems.shape[0]
+    copies = []
+    for i in range(parts):
+        rows = pl.ds(i * (depth // parts), depth // parts)
+        part = source.at[rows, pl.ds(branch * channels, channels)]
+        copies.append((rows, pltpu.make_async_copy(part, weight.at[rows], sems.at[i])))
+    for _, copy in copies:
+        copy.start()
+    first = 0.0
+    for rows, copy in copies:
+        copy.wait()
+        first = first + dot(own[:, rows], weight[rows, :])
+    yield first
+    half = depth // 2
+    near = weight[pl.ds(pl.multiple_of(core * half, half), half), :]
+    far = weight[pl.ds(pl.multiple_of((1 - core) * half, half), half), :]
+    for left, right in zip(mine, other):
+        yield dot(left[...], near) + dot(right[...], far)
+
+
+def mixer_project_body(seq, place, *refs):
+    own, mine, other = refs[0], refs[1:seq], refs[seq : 2 * seq - 1]
+    refs = refs[2 * seq - 1 :]
+    (weight, routes), outs, (tails, held, sems) = refs[:2], refs[2 : seq + 2], refs[seq + 2 :]
+    me = place[0]
+    length = own.shape[0]
+    for index, product in enumerate(project(place[1], own, mine, other, weight, 0, held, sems)):
         outs[index][HALO:, :] = product.astype(outs[index].dtype)
         tails[index] = product[length - HALO :, :]
     for mask in range(seq):
@@ -113,12 +127,12 @@
         outs[mask][:HALO, :] = before.astype(outs[mask].dtype)
 
 
-def gate_project_body(seq, place, x_own, *refs):
-    x_mine, x_other = refs[: seq - 1], refs[seq - 1 : 2 * seq - 2]
-    weight, own_tokens = refs[2 * seq - 2 : 2 * seq]
-    outs = refs[2 * seq :]
-    length, width = x_own.shape
-    for index, product in enumerate(project(x_own, x_mine, x_other, weight, place[1], 1)):
+def gate_project_body(seq, place, *refs):
+    own, mine, other = refs[0], refs[1:seq], refs[seq : 2 * seq - 1]
+    refs = refs[2 * seq - 1 :]
+    (weight, own_tokens), outs, (held, sems) = refs[:2], refs[2 : seq + 2], refs[seq + 2 :]
+    length, width = own.shape
+    for index, product in enumerate(project(place[1], own, mine, other, weight, 1, held, sems)):
         outs[index][:length, :] = product.astype(outs[index].dtype)
         if index:
             start = pl.multiple_of((place[0] ^ index) * width, 128)
@@ -178,8 +192,10 @@
     zero = jnp.zeros((groups, lanes), F32)
     state, running = lax.fori_loop(0, length, advance, ((zero,) * states, zero), unroll=4)
     for n in range(states):
-        final[n] = state[n]
-    final[states] = running
+        final[n] = state[n].astype(BF16)
+    upper = running.astype(BF16)
+    final[states] = upper
+    final[states + 1] = (running - upper.astype(F32)).astype(BF16)
 
 
 def gated_body(seq, own_rows, place, maps, *refs):
@@ -192,15 +208,16 @@
     me, expert = place[0], place[2]
     zero = jnp.zeros((groups, lanes), F32)
     incoming = [zero] * states
+    sums = [block[states].astype(F32) + block[states + 1].astype(F32) for block in arrived]
     for mask in range(1, seq):
         shard = me ^ mask
         between = zero
         for other in range(1, seq):
             middle = me ^ other
             inside = (shard < middle) & (middle < me)
-            between = between + jnp.where(inside, arrived[other - 1][states], 0.0)
+            between = between + jnp.where(inside, sums[other - 1], 0.0)
         for n in range(states):
-            term = jnp.exp2(rate[n] * between) * arrived[mask - 1][n]
+            term = jnp.exp2(rate[n] * between) * arrived[mask - 1][n].astype(F32)
             incoming[n] = incoming[n] + jnp.where(shard < me, term, 0.0)
     rates = [rate[n] for n in range(states)]
 
@@ -265,23 +282,33 @@
     target = lax.broadcasted_iota(jnp.int32, (window, window), 1)
     earlier = (source // own_rows == target // own_rows) & (source < target)
     before = dot((hits[0] + hits[1]).astype(BF16), jnp.where(earlier, 1.0, 0.0).astype(BF16))
-    here = (before == (row % most_slots).astype(F32)) & (shard == (place[0] ^ (column // own_rows)))
-    fits = jnp.where(here, 1.0, 0.0)
-    choose[...] = (fits * (hits[0] + hits[1])).astype(BF16)
-    first[...] = (fits * hits[0]).astype(BF16)
-    second[...] = (fits * hits[1]).astype(BF16)
+    numbered = jnp.where(before == (row % most_slots).astype(F32), 1.0, 0.0)
+    here = jnp.where(shard == (place[0] ^ (column // own_rows)), numbered, 0.0)
+    choose[...] = (here * (hits[0] + hits[1])).astype(BF16)
+    first[...] = (numbered * hits[0])[:, :own_rows]
+    second[...] = (numbered * hits[1])[:, :own_rows]
     same = jnp.where(source == target, 1.0, 0.0).astype(BF16)
-    named[...] = lax.dot_general(
+    columns = lax.dot_general(
         same, near.astype(BF16), (((1,), (1,)), ((), ())), preferred_element_type=F32
     )
+    named[...] = columns[:own_rows]
+
+
+def reordered(table, outer, inner, count):
+    rows = table.shape[0]
+    row = lax.broadcasted_iota(jnp.int32, (rows, rows), 0)
+    column = lax.broadcasted_iota(jnp.int32, (rows, rows), 1)
+    big, small, number = row // (inner * count), (row // count) % inner, row % count
+    choice = jnp.where(column == small * (outer * count) + big * count + number, 1.0, 0.0).astype(BF16)
+    return dot(choice, table).astype(BF16)
 
 
 def hidden_body(chips, seq, place, own, *refs):
     terms, refs = refs[: chips - 1], refs[chips - 1 :]
     own_tokens, refs = refs[0], refs[1:]
     payloads, refs = refs[: seq - 1], refs[seq - 1 :]
-    choose, hidden = refs[:2]
-    outs = refs[2:]
+    choose, hidden = refs[0], refs[1 : 1 + seq]
+    outs = refs[1 + seq :]
     total = own[...]
     for term in terms:
         total = total + term[...].astype(F32)
@@ -292,7 +319,8 @@
     for payload in payloads:
         residual.append(payload[payload.shape[0] - rows :, :width].astype(F32))
     rounded = (jnp.concatenate(residual, axis=0) + total).astype(BF16)
-    hidden[...] = rounded
+    for d, out in enumerate(hidden):
+        out[...] = rounded[d * rows : (d + 1) * rows]
     slots = dot(choose[...], rounded).astype(BF16)
     rows = slots.shape[0] // chips
     for w in range(chips):
@@ -303,8 +331,10 @@
     copies = []
     for index, (source, mask, axis) in enumerate(jobs):
         size = outs[index].shape[axis]
-        start = pl.multiple_of((place[0] ^ mask) * size, 128 if axis else 16)
-        where = (0, slice(None), pl.ds(start, size)) if axis else (0, pl.ds(start, size))
+        if axis:
+            where = (0, slice(None), pl.ds(mask * size, size))
+        else:
+            where = (0, pl.ds(pl.multiple_of((place[0] ^ mask) * size, 16), size))
         copies.append(pltpu.make_async_copy(sources[source].at[where], outs[index], sems.at[index]))
     for copy in copies:
         copy.start()
@@ -394,44 +424,53 @@
     return results[: len(outs)], results[len(outs) :]
 
 
-def down_body(hidden, down, out):
-    width = out.shape[1]
+def down_body(seq, place, hidden, *refs):
+    downs, outs, product = refs[:seq], refs[seq:-1], refs[-1]
+    width = downs[0].shape[1]
     tile = tile_of(width, 512)
-    for step in range(width // tile):
-        part = slice(step * tile, (step + 1) * tile)
-        out[:, part] = dot(hidden[...], down[:, part]).astype(BF16)
-
-
-def down_chunk(hidden, down):
-    slots, hidden_units = hidden.shape
-    width = down.shape[1]
-    return kernel_call(
-        down_body,
-        shape((slots, width), BF16),
-        [VMEM] * 2,
-        flops=2 * slots * width * hidden_units,
-        moved=2 * width * hidden_units,
-        limit=16,
-    )(hidden, down)
-
-
-def expert_sum_body(seq, *refs):
+    for block, down in enumerate(downs):
+        for step in range(width // tile):
+            part = slice(step * tile, (step + 1) * tile)
+            to = slice(block * width + step * tile, block * width + (step + 1) * tile)
+            product[:, to] = dot(hidden[...], down[:, part]).astype(BF16)
+    for mask, out in enumerate(outs):
+        rows = out.shape[0]
+        out[...] = product[pl.ds(pl.multiple_of((place[0] ^ mask) * rows, 16), rows), :]
+
+
+def expert_sum_body(seq, groups, most_slots, *refs):
     terms, outs = refs[:seq], refs[seq:]
     total = terms[0][...].astype(F32)
     for term in terms[1:]:
         total = total + term[...].astype(F32)
     rounded = total.astype(BF16)
-    rows = rounded.shape[0] // len(outs)
+    width = outs[0].shape[1]
+    pieces = jnp.concatenate([rounded[:, q * width : (q + 1) * width] for q in range(seq)], axis=0)
+    pieces = reordered(pieces, groups, seq, most_slots)
+    rows = pieces.shape[0] // len(outs)
     for w, out in enumerate(outs):
-        out[...] = rounded[w * rows : (w + 1) * rows]
-
-
-def scores_body(experts, hidden, gain, router, scores):
-    values = hidden[...].astype(F32)
-    part = dot((values * gain[...]).astype(BF16), router[...])
-    square = jnp.sum(values * values, axis=-1, keepdims=True)
-    lane = lax.broadcasted_iota(jnp.int32, part.shape, 1)
-    scores[...] = jnp.where(lane < experts, part, square)
+        out[...] = pieces[w * rows : (w + 1) * rows]
+
+
+def shares_body(seq, place, gain, router, named, *refs):
+    pieces, rows, shares = refs[:seq], refs[seq], refs[seq + 1]
+    width = pieces[0].shape[1]
+    for mask, piece in enumerate(pieces):
+        start = pl.multiple_of((place[0] ^ mask) * width, 128)
+        rows[:, pl.ds(start, width)] = piece[...].astype(F32)
+    values = rows[...]
+    inverse = lax.rsqrt(jnp.mean(values * values, axis=-1, keepdims=True) + EPSILON)
+    moe_in = (values * inverse * gain[...]).astype(BF16)
+    logits = lax.dot_general(
+        moe_in, router[...], (((1,), (1,)), ((), ())), preferred_element_type=F32
+    )
+    lane = lax.broadcasted_iota(jnp.int32, logits.shape, 1).astype(F32)
+    picked = [
+        jnp.sum(jnp.where(lane == named[:, i : i + 1], logits, 0.0), axis=-1, keepdims=True)
+        for i in range(2)
+    ]
+    first_share = 1.0 / (1.0 + jnp.exp(picked[1] - picked[0]))
+    shares[...] = jnp.broadcast_to(first_share, shares.shape)
 
 
 def halves_body(*refs):
@@ -451,54 +490,37 @@
     )(*blocks)
 
 
-def rows_body(chips, *refs):
+def rows_body(chips, seq, groups, most_slots, *refs):
     direct, crossed, out = refs[:chips], refs[chips], refs[chips + 1]
-    half = crossed.shape[1]
-    out[...] = jnp.concatenate(
-        [block for w in range(chips) for block in (direct[w][:half, :], crossed[w])], axis=0
-    )
-
-
-def combine_body(chips, seq, experts, model_width, *refs):
-    direct = refs[:chips]
-    crossed, hidden, first, second, routes = refs[chips : chips + 5]
-    scores = refs[chips + 5 : chips + 5 + seq]
-    outs = refs[chips + 5 + seq :]
-    rows = outs[0].shape[0]
-    total = scores[0][...]
-    for mask in range(1, seq):
-        other = scores[mask][...]
-        total = total + jnp.concatenate(
-            [other[(d ^ mask) * rows : ((d ^ mask) + 1) * rows] for d in range(seq)], axis=0
-        )
-    logits = total * lax.rsqrt(total[:, experts : experts + 1] / model_width + EPSILON)
-    lane = lax.broadcasted_iota(jnp.int32, logits.shape, 1).astype(F32)
-    picked = [
-        jnp.sum(jnp.where(lane == routes[:, i : i + 1], logits, 0.0), axis=-1, keepdims=True)
-        for i in range(2)
-    ]
-    first_share = 1.0 / (1.0 + jnp.exp(picked[1] - picked[0]))
     half = crossed.shape[1]
     table = jnp.concatenate(
         [block for w in range(chips) for block in (direct[w][:half, :], crossed[w])], axis=0
     )
-
-    def rows_of(choice):
-        return lax.dot_general(
-            choice[...], table, (((0,), (0,)), ((), ())), preferred_element_type=F32
-        )
-
-    sent = first_share * rows_of(first) + (1.0 - first_share) * rows_of(second)
-    mixed = (hidden[...].astype(F32) + sent).astype(BF16)
-    for d, out in enumerate(outs):
-        out[...] = mixed[d * rows : (d + 1) * rows]
-
-
-def place_body(place, *refs):
-    pieces, out = refs[:-1], refs[-1]
-    width = pieces[0].shape[1]
-    for mask, piece in enumerate(pieces):
-        out[:, pl.ds(pl.multiple_of((place[0] ^ mask) * width, 128), width)] = piece[...]
+    out[...] = reordered(table, seq, groups, most_slots)
+
+
+def combine_body(chips, seq, most_slots, *refs):
+    direct = refs[:chips]
+    crossed, first, second, rows, shares, out = refs[chips:]
+    half = crossed.shape[1]
+    table = jnp.concatenate(
+        [block for w in range(chips) for block in (direct[w][:half, :], crossed[w])], axis=0
+    )
+    width = table.shape[1]
+    row = lax.broadcasted_iota(jnp.int32, first.shape, 0)
+    piece = (row // most_slots) % seq
+    first_share = shares[:, 0:1]
+    for q in range(seq):
+
+        def rows_of(choice):
+            chosen = jnp.where(piece == q, choice[...], 0.0).astype(BF16)
+            return lax.dot_general(
+                chosen, table, (((0,), (0,)), ((), ())), preferred_element_type=F32
+            )
+
+        part = slice(q * width, (q + 1) * width)
+        sent = first_share * rows_of(first) + (1.0 - first_share) * rows_of(second)
+        out[:, part] = (rows[:, part] + sent).astype(BF16)
 
 
 def tile_of(total, most):
@@ -535,7 +557,6 @@
     masks = range(1, seq)
     length, model_width = tokens.shape
     width = model_width // seq
-    half = width // 2
     channels = in_weight.shape[2]
     rank_width = step_weight.shape[0]
     state_width = decay_log.shape[1]
@@ -548,16 +569,22 @@
 
     x_own, *x_send = kernel_call(
         functools.partial(norm_body, seq),
-        [shape((length, width), BF16)] + [shape((length, half), BF16)] * (seq - 1),
+        [shape((length, width), BF16)] + [shape((length, width // 2), BF16)] * (seq - 1),
         [SMEM, VMEM, VMEM],
         flops=8 * length * model_width,
         moved=4 * length * model_width,
         limit=24,
     )(place, tokens, norm_gain[None])
     x_mine = [partner(block, "seq", mask) for mask, block in zip(masks, x_send)]
-    weight = after(in_weight, x_own).reshape(width, 2 * channels)
-    x_mine = after(x_mine, weight)
-    x_other = [partner(block, "expert", 1) for block in x_mine]
+    weight = in_hbm([in_weight.reshape(width, 2 * channels)])[0]
+    x_passed = kernel_call(
+        pass_body,
+        [shape((length, width // 2), BF16)] * (seq - 1),
+        [VMEM] * (seq - 1),
+        deps=[weight],
+    )(*x_mine)
+    x_other = [partner(block, "expert", 1) for block in x_passed]
+    x = [x_own, *x_mine, *x_other]
     lane_routes = jnp.transpose(routes).astype(F32)
     spread_routes = jnp.stack(
         [
@@ -565,40 +592,39 @@
             for d in range(seq)
         ]
     )
-    in_specs = [SMEM] + [VMEM] * (2 * seq)
+    in_specs = [SMEM] + [VMEM] * (2 * seq - 1) + [pl.BlockSpec(memory_space=pltpu.HBM), VMEM]
+    scratch = [pltpu.VMEM((width, channels), BF16), pltpu.SemaphoreType.DMA((4,))]
     cost = dict(flops=2 * seq * length * width * channels, moved=2 * width * channels, limit=24)
     mixer_own, *mixer_send = kernel_call(
         functools.partial(mixer_project_body, seq),
         [shape((HALO + length, channels), F32)] + [shape((HALO + length, channels), BF16)] * (seq - 1),
-        in_specs + [VMEM],
-        [pltpu.VMEM((seq, HALO, channels), F32)],
+        in_specs,
+        [pltpu.VMEM((seq, HALO, channels), F32)] + scratch,
         **cost,
-    )(place, x_own, *x_mine, *x_other, weight, spread_routes)
+    )(place, *x, weight, spread_routes)
     mixer_terms = [partner(block, "seq", mask) for mask, block in zip(masks, mixer_send)]
     assert width <= channels and window <= channels
     own_tokens = lax.dynamic_slice_in_dim(tokens, expert * own_rows, own_rows, 0)
     side_own, *side_send = kernel_call(
         functools.partial(gate_project_body, seq),
         [shape((length, channels), F32)] + [shape((length + own_rows, channels), BF16)] * (seq - 1),
-        in_specs + [VMEM],
+        in_specs,
+        scratch,
+        deps=[mixer_terms[seq // 2 - 1]],
         **cost,
-    )(place, x_own, *x_mine, *x_other, weight, own_tokens)
-
-    early = seq // 2
-    mixer_own = after(mixer_own, side_own)
+    )(place, *x, weight, own_tokens)
+
+    side_terms = [partner(block, "seq", mask) for mask, block in zip(masks, side_send)]
     activated, features = kernel_call(
         functools.partial(conv_body, seq),
         [shape((length, channels), BF16), shape((length, proj_weight.shape[1]), F32)],
         [VMEM] * (seq + 3),
-        flops=2 * length * channels * proj_weight.shape[1] + 16 * length * channels,
-        moved=2 * channels * proj_weight.shape[1] + 10 * length * channels,
         limit=16,
+        deps=[side_own],
     )(mixer_own, *mixer_terms, conv_weight, conv_bias[None], jnp.transpose(proj_weight))
     features = features + partner(features, "expert", 1)
     sent = features.astype(BF16)
     features_came = [partner(sent, "expert", 2 * w) for w in range(1, chips)]
-    side_send = after(side_send[:early], mixer_terms[early - 1]) + after(side_send[early:], features_came[0])
-    side_terms = [partner(block, "seq", mask) for mask, block in zip(masks, side_send)]
     for term in features_came:
         features = features + term.astype(F32)
     low_rank, maps = features[:, :rank_width].astype(BF16), features[:, rank_width:]
@@ -607,11 +633,9 @@
     tiled = shape((length, tiles, lanes), F32)
     y, cumulated, final = kernel_call(
         scan_body,
-        [tiled, tiled, shape((state_width + 1, tiles, lanes), F32)],
+        [tiled, tiled, shape((state_width + 2, tiles, lanes), BF16)],
         [SMEM] + [VMEM] * 5,
         [pltpu.VMEM(tiled.shape, F32)] * 2,
-        flops=8 * length * channels * state_width,
-        moved=12 * length * channels,
         limit=24,
     )(maps, low_rank, activated, step_weight, step_bias[None], rate)
     arrived = [later_partner(final, "seq", mask) for mask in masks]
@@ -620,8 +644,6 @@
         shape((length, channels), BF16),
         [SMEM, SMEM] + [VMEM] * (2 * seq + 4),
         [pltpu.VMEM(tiled.shape, F32), pltpu.VMEM((length, channels), F32)],
-        flops=8 * length * channels * state_width,
-        moved=16 * length * channels,
         limit=24,
     )(place, maps, *arrived, y, cumulated, rate, activated, skip_gain[None], side_own, *side_terms)
 
@@ -632,7 +654,7 @@
     per_group = slots // groups
     choose, first, second, named = kernel_call(
         functools.partial(tables_body, seq, own_rows, most_slots),
-        [shape((slots, window), BF16)] * 3 + [shape((window, 8), F32)],
+        [shape((slots, window), BF16)] + [shape((slots, own_rows), F32)] * 2 + [shape((own_rows, 8), F32)],
         [SMEM, VMEM] + [VMEM] * (seq - 1),
         flops=2 * slots * window * window,
         moved=8 * slots * window,
@@ -656,89 +678,87 @@
     )(keep, crossing)
     chip_terms = [partner(block, "expert", 2 * w) for w, block in zip(range(1, chips), chip_sends)]
 
-    hidden_state, *outgoing = kernel_call(
+    sources = [gate_weight, up_weight, down_weight]
+    both = lambda mask: [(0, mask, 0), (1, mask, 0)]
+    current = list(fetch(place, both(0) + both(1), width, sources[:2], [own_sum]))
+    near_hidden = kernel_call(
         functools.partial(hidden_body, chips, seq),
-        [shape((window, width), BF16)] + [shape((per_chip, width), BF16)] * chips,
+        [shape((own_rows, width), BF16)] * seq + [shape((per_chip, width), BF16)] * chips,
         [SMEM] + [VMEM] * (chips + seq + 1),
         flops=2 * slots * window * width,
         moved=10 * window * width,
+        deps=current,
     )(place, own_sum, *chip_terms, own_tokens, *side_terms, choose)
+    near_hidden, outgoing = near_hidden[:seq], near_hidden[seq:]
 
     came = [outgoing[0]] + [
         partner(block, "expert", 2 * w) for w, block in zip(range(1, chips), outgoing[1:])
     ]
-    sources = [gate_weight, up_weight, down_weight]
-    both = lambda mask: [(0, mask, 0), (1, mask, 0)]
-    current = list(fetch(place, both(0) + both(1), width, sources[:2], [hidden_state]))
-    crossed = partner(second_halves(came, current), "expert", 1)
+    whole = [near_hidden[0]] + [partner(near_hidden[mask], "seq", mask) for mask in masks]
+    crossed = partner(second_halves(came, whole[1:]), "expert", 1)
     rows = kernel_call(
-        functools.partial(rows_body, chips),
+        functools.partial(rows_body, chips, seq, groups, most_slots),
         shape((slots, width), BF16),
         [VMEM] * (chips + 1),
         moved=4 * slots * width,
     )(*came, crossed)
     pieces = [rows] + [partner(rows, "seq", mask) for mask in masks]
 
-    before, waiting = [], current
+    before, waiting, downs = [], current, []
     for mask in range(seq):
         jobs = both(mask + 2) if mask + 2 < seq else []
-        if mask == max(0, seq - 4):
-            jobs = jobs + (both(mask + 3) if mask + 3 < seq else [])
+        if mask == seq - 4:
+            jobs = both(mask + 2) + both(mask + 3)
         elif mask == seq - 3:
-            jobs = [(2, other, 1) for other in range(seq)]
-        elif mask > seq - 3:
-            jobs = []
+            jobs = [(2, block, 1) for block in range(seq)]
         before, came_in = expert_chunk(
             mask, mask == 0, mask == seq - 1, place, pieces[mask], moe_gain[None], *waiting[:2], before, jobs, sources
         )
-        waiting = waiting[2:] + list(came_in)
-    downs = waiting
+        waiting = waiting[2:]
+        if mask == seq - 3:
+            downs = list(came_in)
+        else:
+            waiting = waiting + list(came_in)
     hidden = before[0]
-    sums = []
-    for mask in reversed(range(seq)):
-        sums = [down_chunk(hidden, downs[mask])] + sums
+    back = groups * most_slots
+    sums = kernel_call(
+        functools.partial(down_body, seq),
+        [shape((back, model_width), BF16)] * seq,
+        [SMEM] + [VMEM] * (seq + 1),
+        [pltpu.VMEM((slots, model_width), BF16)],
+        flops=2 * slots * model_width * gate_weight.shape[2],
+        moved=2 * model_width * gate_weight.shape[2],
+        limit=16,
+    )(place, hidden, *downs)
     terms = [sums[0]] + [partner(sums[mask], "seq", mask) for mask in masks]
-    router = jnp.pad(
-        lax.dynamic_slice_in_dim(router_weight, me * width, width, 0), ((0, 0), (0, lanes - experts))
-    )
-    scores = kernel_call(
-        functools.partial(scores_body, experts),
-        shape((window, lanes), F32),
-        [VMEM] * 3,
-        flops=2 * window * width * lanes,
-        moved=4 * window * width,
+
+    own_hidden, shares = kernel_call(
+        functools.partial(shares_body, seq),
+        [shape((own_rows, model_width), F32), shape((own_rows, lanes), F32)],
+        [SMEM] + [VMEM] * (seq + 3),
+        flops=2 * own_rows * model_width * lanes,
+        moved=16 * own_rows * model_width,
         deps=[sums[0]],
-    )(hidden_state, lax.dynamic_slice_in_dim(moe_gain, me * width, width, 0)[None], router)
-    scores = [scores] + [partner(scores, "seq", mask) for mask in masks]
-
+    )(place, moe_gain[None], jnp.transpose(router_weight), named, *whole)
     answers = kernel_call(
-        functools.partial(expert_sum_body, seq),
+        functools.partial(expert_sum_body, seq, groups, most_slots),
         [shape((per_chip, width), BF16)] * chips,
         [VMEM] * seq,
         flops=seq * slots * width,
         moved=10 * slots * width,
-        deps=scores[1:],
+        deps=[shares],
     )(*terms)
     answers = [answers[0]] + [
         partner(block, "expert", 2 * w) for w, block in zip(range(1, chips), answers[1:])
     ]
     crossed_back = partner(second_halves(answers), "expert", 1)
-
-    mixed_own, *mixed_send = kernel_call(
-        functools.partial(combine_body, chips, seq, experts, model_width),
-        [shape((own_rows, width), BF16)] * seq,
-        [VMEM] * (chips + 5 + seq),
-        flops=4 * slots * window * width,
+    return kernel_call(
+        functools.partial(combine_body, chips, seq, most_slots),
+        shape((own_rows, model_width), BF16),
+        [VMEM] * (chips + 5),
+        flops=4 * slots * own_rows * model_width,
         moved=8 * slots * width,
-    )(*answers, crossed_back, hidden_state, first, second, named, *scores)
-    mixed = [mixed_own] + [partner(block, "seq", mask) for mask, block in zip(masks, mixed_send)]
-    return kernel_call(
-        place_body,
-        shape((own_rows, model_width), BF16),
-        [SMEM] + [VMEM] * seq,
-        flops=0,
-        moved=4 * own_rows * model_width,
-    )(place, *mixed)
+    )(*answers, crossed_back, first, second, own_hidden, shares)
 
 
 def solution(mesh):

time: 187 us -> 179 us (0.957)
  local copies, waits for them, and re-layouts: 15 us -> 8.63 us
  starting transfers between devices: 60.7 us -> 56.5 us
  Pallas kernels: 47.5 us -> 51.6 us
    unnamed x53 -> x28, local copies, waits for them, and re-layouts: 13.3 us -> 7.63 us
    ppermute x43 -> x40, starting transfers between devices: 51.1 us -> 46.4 us  [partner(): return lax.ppermute(block, axis, [(i, i ^ mask) for i in range(size)])]
    pallas_call x26 -> x23, Pallas kernels: 47.5 us -> 51.6 us  [kernel_call(): return lambda *operands: call(*operands, *deps)]
    ppermute x43 -> x40, waiting for transfers between devices: 61 us -> 59.8 us  [partner(): return lax.ppermute(block, axis, [(i, i ^ mask) for i in range(size)])]
  transfers between devices with their start and end apart: 46 -> 43, of which waited for: 25 -> 25; matrix products, arithmetic and copies ran while one was open for 4% -> 4% of each run, Pallas kernels for 17% -> 18%
where the time goes in v3:
time: 179 us
  waiting for transfers between devices  61.4 us (34%)
  starting transfers between devices  56.5 us (32%)
  Pallas kernels  51.6 us (29%)
  local copies, waits for them, and re-layouts  8.63 us (5%)
    ppermute x40, waiting for transfers between devices, partner(): return lax.ppermute(block, axis, [(i, i ^ mask) for i in range(size)])  59.8 us
    pallas_call x23, Pallas kernels, kernel_call(): return lambda *operands: call(*operands, *deps)  51.6 us
    ppermute x40, starting transfers between devices, partner(): return lax.ppermute(block, axis, [(i, i ^ mask) for i in range(size)])  46.4 us
    ppermute x3, starting transfers between devices, later_partner(): lax.ppermute(block, axis, [(i, i ^ mask) for i in range(size) if i < i ^...  10 us
    unnamed x28, local copies, waits for them, and re-layouts  7.63 us
  transfers between devices with their start and end apart: 43, of which 25 were waited for; matrix products, arithmetic and copies ran while one was open for 4% of the time, Pallas kernels for 18%

profile of v3, /device:TPU:0, one launch (start us, length us, event | category | flops | bytes accessed | tf_op | source)
XLA Modules:
  0.0 178.7 jit_solution(5587653975271534778)
XLA Ops:
  0.1 1.2 copy-done
  2.0 1.0 shard_map.163
  3.0 3.0 %collective-permute-start = (bf16[128,512]{1,0:T(8,128)(2,1)S(1)}, bf16[128,512]{1,0:T(8,128)(2,1)S(1)}, u32[]{:S(2)}, u32[]{:S(2)}) collective-permute-start(bf16[128,512]{1,0:T(8,128)(2,1)S(1)} %get-tuple-element.75), channel_id=1, source_target_pairs={{0,8},{8,0},{16,24},{24,16},{1,9},{9,1},{17,25},{25,17},{2,10},{10... | collective-permute-start | bytes 393224 | tf_op jit(solution)/shard_map/ppermute | solution.py:24
  6.0 1.5 collective-permute-start.1
  7.5 5.6 %copy.18 = bf16[128,8,2,1024]{3,1,2,0:T(8,128)(2,1)} copy(bf16[128,8,2,1024]{3,2,1,0:T(2,128)(2,1)} %bitcast.42) | data formatting | bytes 8388608
  15.7 3.2 %shard_map.165 = (f32[144,1024]{1,0:T(8,128)S(1)}, bf16[144,1024]{1,0:T(8,128)(2,1)S(1)}, bf16[144,1024]{1,0:T(8,128)(2,1)S(1)}, bf16[144,1024]{1,0:T(8,128)(2,1)S(1)}) custom-call(s32[3]{0:T(128)S(1)} %pad_add_fusion.refs_0_, bf16[128,1024]{1,0:T(8,128)(2,1)S(1)} %get-tuple-element.74.refs_1_, bf16[128,512]{1,0:T(8,128)(2,1)S(1)} %collective-permute-done.refs_0_.refs_2_, ...), custom_call_target="tpu_custom_call" | custom-call | flops 1073741824 | bytes 2097152 | tf_op jit(solution)/shard_map/pallas_call | solution.py:58
  19.0 1.6 collective-permute-start.7
  20.5 1.4 collective-permute-start.6
  22.5 0.9 constant_dynamic-slice_fusion.refs_9_.refs_5_
  23.5 4.7 %collective-permute-done.7.refs_10_.refs_2_.refs_3_ = bf16[144,1024]{1,0:T(8,128)(2,1)S(1)} collective-permute-done((bf16[144,1024]{1,0:T(8,128)(2,1)S(1)}, bf16[144,1024]{1,0:T(8,128)(2,1)S(1)}, u32[]{:S(2)}, u32[]{:S(2)}) %collective-permute-start.7) | collective-permute-done | bytes 294944 | tf_op jit(solution)/shard_map/ppermute | solution.py:24
  28.1 3.2 %shard_map.166 = (f32[128,1024]{1,0:T(8,128)S(1)}, bf16[144,1024]{1,0:T(8,128)(2,1)S(1)}, bf16[144,1024]{1,0:T(8,128)(2,1)S(1)}, bf16[144,1024]{1,0:T(8,128)(2,1)S(1)}) custom-call(s32[3]{0:T(128)S(1)} %pad_add_fusion.refs_0_, bf16[128,1024]{1,0:T(8,128)(2,1)S(1)} %get-tuple-element.74.refs_1_, bf16[128,512]{1,0:T(8,128)(2,1)S(1)} %collective-permute-done.refs_0_.refs_2_, ...), custom_call_target="tpu_custom_call" | custom-call | flops 1073741824 | bytes 2097152 | tf_op jit(solution)/shard_map/pallas_call | solution.py:58
  31.4 4.3 %collective-permute-done.8.refs_3_.refs_4_ = bf16[144,1024]{1,0:T(8,128)(2,1)S(1)} collective-permute-done((bf16[144,1024]{1,0:T(8,128)(2,1)S(1)}, bf16[144,1024]{1,0:T(8,128)(2,1)S(1)}, u32[]{:S(2)}, u32[]{:S(2)}) %collective-permute-start.8) | collective-permute-done | bytes 294944 | tf_op jit(solution)/shard_map/ppermute | solution.py:24
  36.6 1.4 collective-permute-done.9
  38.0 1.6 collective-permute-start.10
  39.7 2.6 %collective-permute-start.11 = (bf16[128,288]{1,0:T(8,128)(2,1)S(1)}, bf16[128,288]{1,0:T(8,128)(2,1)S(1)}, u32[]{:S(2)}, u32[]{:S(2)}) collective-permute-start(bf16[128,288]{1,0:T(8,128)(2,1)S(1)} %get-tuple-element.143), channel_id=1, source_target_pairs={{0,4},{1,5},{2,6},{3,7},{4,0},{5,1},{6,2},{7,3},{8,12},{9,13},{10,... | collective-permute-start | bytes 221192 | tf_op jit(solution)/shard_map/ppermute | solution.py:24
  42.5 1.4 collective-permute-start.16
  44.0 1.5 collective-permute-start.17
  46.1 4.3 %collective-permute-done.11 = bf16[128,288]{1,0:T(8,128)(2,1)S(1)} collective-permute-done((bf16[128,288]{1,0:T(8,128)(2,1)S(1)}, bf16[128,288]{1,0:T(8,128)(2,1)S(1)}, u32[]{:S(2)}, u32[]{:S(2)}) %collective-permute-start.11) | collective-permute-done | bytes 73760 | tf_op jit(solution)/shard_map/ppermute | solution.py:24
  50.5 5.4 %shard_map.168 = (f32[128,8,128]{2,1,0:T(8,128)S(1)}, f32[128,8,128]{2,1,0:T(8,128)S(1)}, bf16[18,8,128]{2,1,0:T(8,128)(2,1)S(1)}) custom-call(f32[128,32]{1,0:T(8,128)S(1)} %slice.9.refs_0_.refs_1_, bf16[128,256]{1,0:T(8,128)(2,1)S(1)} %slice.12.refs_1_, bf16[128,1024]{1,0:T(8,128)(2,1)S(1)} %get-tuple-element.87.refs_2_.refs_8_, ...), custom_call_target="tpu_custom_call" | custom-call | tf_op jit(solution)/shard_map/pallas_call | solution.py:58
  55.8 3.3 %collective-permute-start.13 = (bf16[18,8,128]{2,1,0:T(8,128)(2,1)S(1)}, bf16[18,8,128]{2,1,0:T(8,128)(2,1)S(1)}, u32[]{:S(2)}, u32[]{:S(2)}) collective-permute-start(bf16[18,8,128]{2,1,0:T(8,128)(2,1)S(1)} %get-tuple-element.88), channel_id=1, source_target_pairs={{0,8},{16,24},{1,9},{17,25},{2,10},{18,26},{3,11},{19,27},{4,12},{... | collective-permute-start | bytes 110600 | tf_op jit(solution)/shard_map/ppermute | solution.py:29
  59.1 3.4 %collective-permute-start.14 = (bf16[18,8,128]{2,1,0:T(8,128)(2,1)S(1)}, bf16[18,8,128]{2,1,0:T(8,128)(2,1)S(1)}, u32[]{:S(2)}, u32[]{:S(2)}) collective-permute-start(bf16[18,8,128]{2,1,0:T(8,128)(2,1)S(1)} %get-tuple-element.88), channel_id=1, source_target_pairs={{0,16},{8,24},{1,17},{9,25},{2,18},{10,26},{3,19},{11,27},{4,20},{... | collective-permute-start | bytes 110600 | tf_op jit(solution)/shard_map/ppermute | solution.py:29
  62.6 3.3 %collective-permute-start.15 = (bf16[18,8,128]{2,1,0:T(8,128)(2,1)S(1)}, bf16[18,8,128]{2,1,0:T(8,128)(2,1)S(1)}, u32[]{:S(2)}, u32[]{:S(2)}) collective-permute-start(bf16[18,8,128]{2,1,0:T(8,128)(2,1)S(1)} %get-tuple-element.88), channel_id=1, source_target_pairs={{0,24},{8,16},{1,25},{9,17},{2,26},{10,18},{3,27},{11,19},{4,28},{... | collective-permute-start | bytes 110600 | tf_op jit(solution)/shard_map/ppermute | solution.py:29
  65.9 1.6 collective-permute-done.15.refs_4_
  67.6 4.5 %shard_map.169.refs_0_ = bf16[128,1024]{1,0:T(8,128)(2,1)S(1)} custom-call(s32[3]{0:T(128)S(1)} %pad_add_fusion.refs_0_, f32[128,32]{1,0:T(8,128)S(1)} %slice.9.refs_0_.refs_1_, bf16[18,8,128]{2,1,0:T(8,128)(2,1)S(1)} %collective-permute-done.13.refs_2_, bf16[18,8,128]{2,1,0:T(8,128)(2,1)S(1)} %collective-permute-done.14.refs_3_, ...), custom_call_target="tpu_custom_call" | custom-call | tf_op jit(solution)/shard_map/pallas_call | solution.py:58
  72.1 3.8 %collective-permute-start.20 = (bf16[128,1024]{1,0:T(8,128)(2,1)S(1)}, bf16[128,1024]{1,0:T(8,128)(2,1)S(1)}, u32[]{:S(2)}, u32[]{:S(2)}) collective-permute-start(bf16[128,1024]{1,0:T(8,128)(2,1)S(1)} %shard_map.169.refs_0_), channel_id=1, source_target_pairs={{0,16},{8,24},{16,0},{24,8},{1,17},{9,25},{17,1},{25,9},{2,18},{10... | collective-permute-start | bytes 786440 | tf_op jit(solution)/shard_map/ppermute | solution.py:24
  75.9 3.4 %collective-permute-done.19.refs_1_ = bf16[128,1024]{1,0:T(8,128)(2,1)S(1)} collective-permute-done((bf16[128,1024]{1,0:T(8,128)(2,1)S(1)}, bf16[128,1024]{1,0:T(8,128)(2,1)S(1)}, u32[]{:S(2)}, u32[]{:S(2)}) %collective-permute-start.19) | collective-permute-done | bytes 262176 | tf_op jit(solution)/shard_map/ppermute | solution.py:24
  79.3 4.2 %collective-permute-done.20.refs_2_ = bf16[128,1024]{1,0:T(8,128)(2,1)S(1)} collective-permute-done((bf16[128,1024]{1,0:T(8,128)(2,1)S(1)}, bf16[128,1024]{1,0:T(8,128)(2,1)S(1)}, u32[]{:S(2)}, u32[]{:S(2)}) %collective-permute-start.20) | collective-permute-done | bytes 262176 | tf_op jit(solution)/shard_map/ppermute | solution.py:24
  83.6 1.3 shard_map.170
  84.9 1.9 %collective-permute-done.22.refs_1_ = bf16[4,64,1024]{2,1,0:T(8,128)(2,1)S(1)} collective-permute-done((bf16[4,64,1024]{2,1,0:T(8,128)(2,1)S(1)}, bf16[4,64,1024]{2,1,0:T(8,128)(2,1)S(1)}, u32[]{:S(2)}, u32[]{:S(2)}) %collective-permute-start.22) | collective-permute-done | bytes 524320 | tf_op jit(solution)/shard_map/ppermute | solution.py:24
  87.0 2.8 %collective-permute-start.23 = (bf16[64,1024]{1,0:T(8,128)(2,1)S(1)}, bf16[64,1024]{1,0:T(8,128)(2,1)S(1)}, u32[]{:S(2)}, u32[]{:S(2)}) collective-permute-start(bf16[64,1024]{1,0:T(8,128)(2,1)S(1)} %get-tuple-element.97), channel_id=1, source_target_pairs={{0,2},{1,3},{2,0},{3,1},{4,6},{5,7},{6,4},{7,5},{8,10},{9,11},{10,... | collective-permute-start | bytes 393224 | tf_op jit(solution)/shard_map/ppermute | solution.py:24
  89.8 0.9 collective-permute-start.24
  90.7 1.5 collective-permute-start.25
  93.0 5.8 %shard_map.173 = (bf16[1024,1792]{1,0:T(8,128)(2,1)S(1)}, bf16[1024,1792]{1,0:T(8,128)(2,1)S(1)}, bf16[1024,1792]{1,0:T(8,128)(2,1)S(1)}, bf16[1024,1792]{1,0:T(8,128)(2,1)S(1)}) custom-call(s32[3]{0:T(128)S(1)} %pad_add_fusion.refs_0_, bf16[1,4096,1792]{2,1,0:T(8,128)(2,1)} %refs_8_.1, bf16[1,4096,1792]{2,1,0:T(8,128)(2,1)} %refs_9_.1, ...), custom_call_target="tpu_custom_call" | custom-call | bytes 14680064 | tf_op jit(solution)/shard_map/pallas_call | solution.py:58
  98.8 3.9 %collective-permute-done.24.refs_3_ = bf16[64,1024]{1,0:T(8,128)(2,1)S(1)} collective-permute-done((bf16[64,1024]{1,0:T(8,128)(2,1)S(1)}, bf16[64,1024]{1,0:T(8,128)(2,1)S(1)}, u32[]{:S(2)}, u32[]{:S(2)}) %collective-permute-start.24) | collective-permute-done | bytes 131104 | tf_op jit(solution)/shard_map/ppermute | solution.py:24
  103.6 2.4 %collective-permute-start.26 = (bf16[48,1024]{1,0:T(8,128)(2,1)S(1)}, bf16[48,1024]{1,0:T(8,128)(2,1)S(1)}, u32[]{:S(2)}, u32[]{:S(2)}) collective-permute-start(bf16[48,1024]{1,0:T(8,128)(2,1)S(1)} %get-tuple-element.106), channel_id=1, source_target_pairs={{0,2},{1,3},{2,0},{3,1},{4,6},{5,7},{6,4},{7,5},{8,10},{9,11},{10,... | collective-permute-start | bytes 294920 | tf_op jit(solution)/shard_map/ppermute | solution.py:24
  105.9 0.9 collective-permute-start.27
  106.8 1.6 collective-permute-start.28
  108.4 1.4 collective-permute-start.29
  110.4 1.9 %collective-permute-done.29.refs_4_.refs_5_ = bf16[16,1024]{1,0:T(8,128)(2,1)S(1)} collective-permute-done((bf16[16,1024]{1,0:T(8,128)(2,1)S(1)}, bf16[16,1024]{1,0:T(8,128)(2,1)S(1)}, u32[]{:S(2)}, u32[]{:S(2)}) %collective-permute-start.29) | collective-permute-done | bytes 32800 | tf_op jit(solution)/shard_map/ppermute | solution.py:24
  112.3 1.5 collective-permute-start.31
  113.9 3.2 %collective-permute-done.31.refs_6_.refs_7_ = bf16[16,1024]{1,0:T(8,128)(2,1)S(1)} collective-permute-done((bf16[16,1024]{1,0:T(8,128)(2,1)S(1)}, bf16[16,1024]{1,0:T(8,128)(2,1)S(1)}, u32[]{:S(2)}, u32[]{:S(2)}) %collective-permute-start.31) | collective-permute-done | bytes 32800 | tf_op jit(solution)/shard_map/ppermute | solution.py:24
  117.2 1.4 collective-permute-done.32.refs_4_
  119.0 1.4 collective-permute-start.35
  121.1 1.4 collective-permute-start.33
  122.5 6.1 %shard_map.177 = (f32[192,1792]{1,0:T(8,128)S(1)}, f32[192,1792]{1,0:T(8,128)S(1)}, f32[192,128]{1,0:T(8,128)S(1)}, bf16[1024,1792]{1,0:T(8,128)(2,1)S(1)}, bf16...) custom-call(s32[3]{0:T(128)S(1)} %pad_add_fusion.refs_0_, ...), custom_call_target="tpu_custom_call" | custom-call | flops 1409286144 | bytes 7340032 | tf_op jit(solution)/shard_map/pallas_call | solution.py:58
  128.6 2.4 %collective-permute-done.35.refs_1_ = bf16[192,1024]{1,0:T(8,128)(2,1)S(1)} collective-permute-done((bf16[192,1024]{1,0:T(8,128)(2,1)S(1)}, bf16[192,1024]{1,0:T(8,128)(2,1)S(1)}, u32[]{:S(2)}, u32[]{:S(2)}) %collective-permute-start.35) | collective-permute-done | bytes 393248 | tf_op jit(solution)/shard_map/ppermute | solution.py:24
  131.0 7.4 %shard_map.178 = (f32[192,1792]{1,0:T(8,128)S(1)}, f32[192,1792]{1,0:T(8,128)S(1)}, f32[192,128]{1,0:T(8,128)S(1)}, bf16[1792,1024]{1,0:T(8,128)(2,1)S(1)}, bf16...) custom-call(s32[3]{0:T(128)S(1)} %pad_add_fusion.refs_0_, ...), custom_call_target="tpu_custom_call" | custom-call | flops 1409286144 | bytes 7340032 | tf_op jit(solution)/shard_map/pallas_call | solution.py:58
  138.4 2.2 %shard_map.179 = (f32[192,1792]{1,0:T(8,128)S(1)}, f32[192,1792]{1,0:T(8,128)S(1)}, f32[192,128]{1,0:T(8,128)S(1)}) custom-call(s32[3]{0:T(128)S(1)} %pad_add_fusion.refs_0_, bf16[192,1024]{1,0:T(8,128)(2,1)S(1)} %collective-permute-done.34.refs_1_, f32[1,4096]{1,0:T(1,128)S(1)} %bitcast.31, bf16[1024,1792]{1,0:T(8,128)(2,1)S(1)} %get-tuple-element.114.refs_3_, ...), custom_call_target="tpu_custom_call" | custom-call | flops 1409286144 | bytes 7340032 | tf_op jit(solution)/shard_map/pallas_call | solution.py:58
  140.6 2.3 %shard_map.180.refs_1_ = bf16[192,1792]{1,0:T(8,128)(2,1)S(1)} custom-call(s32[3]{0:T(128)S(1)} %pad_add_fusion.refs_0_, bf16[192,1024]{1,0:T(8,128)(2,1)S(1)} %collective-permute-done.33.refs_1_, f32[1,4096]{1,0:T(1,128)S(1)} %bitcast.32, bf16[1024,1792]{1,0:T(8,128)(2,1)S(1)} %get-tuple-element.112.refs_3_, ...), custom_call_target="tpu_custom_call" | custom-call | flops 1409286144 | bytes 7340032 | tf_op jit(solution)/shard_map/pallas_call | solution.py:58
  143.0 3.7 %shard_map.181 = (bf16[48,4096]{1,0:T(8,128)(2,1)S(1)}, bf16[48,4096]{1,0:T(8,128)(2,1)S(1)}, bf16[48,4096]{1,0:T(8,128)(2,1)S(1)}, bf16[48,4096]{1,0:T(8,128)(2,1)S(1)}) custom-call(s32[3]{0:T(128)S(1)} %pad_add_fusion.refs_0_, bf16[192,1792]{1,0:T(8,128)(2,1)S(1)} %shard_map.180.refs_1_, bf16[1792,1024]{1,0:T(8,128)(2,1)S(1)} %get-tuple-element.125.refs_2_, ...), custom_call_target="tpu_custom_call" | custom-call | flops 2818572288 | bytes 14680064 | tf_op jit(solution)/shard_map/pallas_call | solution.py:58
  146.6 2.2 %collective-permute-start.36 = (bf16[48,4096]{1,0:T(8,128)(2,1)S(1)}, bf16[48,4096]{1,0:T(8,128)(2,1)S(1)}, u32[]{:S(2)}, u32[]{:S(2)}) collective-permute-start(bf16[48,4096]{1,0:T(8,128)(2,1)S(1)} %get-tuple-element.130), channel_id=1, source_target_pairs={{0,8},{8,0},{16,24},{24,16},{1,9},{9,1},{17,25},{25,17},{2,10},{10... | collective-permute-start | bytes 1179656 | tf_op jit(solution)/shard_map/ppermute | solution.py:24
  148.9 1.7 collective-permute-start.37
  150.6 1.0 shard_map.182
  151.6 7.3 %collective-permute-done.36.refs_1_ = bf16[48,4096]{1,0:T(8,128)(2,1)S(1)} collective-permute-done((bf16[48,4096]{1,0:T(8,128)(2,1)S(1)}, bf16[48,4096]{1,0:T(8,128)(2,1)S(1)}, u32[]{:S(2)}, u32[]{:S(2)}) %collective-permute-start.36) | collective-permute-done | bytes 393248 | tf_op jit(solution)/shard_map/ppermute | solution.py:24
  158.9 5.5 %collective-permute-done.37.refs_2_ = bf16[48,4096]{1,0:T(8,128)(2,1)S(1)} collective-permute-done((bf16[48,4096]{1,0:T(8,128)(2,1)S(1)}, bf16[48,4096]{1,0:T(8,128)(2,1)S(1)}, u32[]{:S(2)}, u32[]{:S(2)}) %collective-permute-start.37) | collective-permute-done | bytes 393248 | tf_op jit(solution)/shard_map/ppermute | solution.py:24
  164.4 1.7 collective-permute-done.38.refs_3_
  166.5 1.1 collective-permute-start.39
  167.6 1.8 %collective-permute-start.40 = (bf16[48,1024]{1,0:T(8,128)(2,1)S(1)}, bf16[48,1024]{1,0:T(8,128)(2,1)S(1)}, u32[]{:S(2)}, u32[]{:S(2)}) collective-permute-start(bf16[48,1024]{1,0:T(8,128)(2,1)S(1)} %get-tuple-element.138), channel_id=1, source_target_pairs={{0,4},{1,5},{2,6},{3,7},{4,0},{5,1},{6,2},{7,3},{8,12},{9,13},{10,... | collective-permute-start | bytes 294920 | tf_op jit(solution)/shard_map/ppermute | solution.py:24
  169.4 1.5 collective-permute-start.41
  171.0 1.5 collective-permute-done.39.refs_1_
  172.5 1.9 %collective-permute-done.40.refs_2_ = bf16[48,1024]{1,0:T(8,128)(2,1)S(1)} collective-permute-done((bf16[48,1024]{1,0:T(8,128)(2,1)S(1)}, bf16[48,1024]{1,0:T(8,128)(2,1)S(1)}, u32[]{:S(2)}, u32[]{:S(2)}) %collective-permute-start.40) | collective-permute-done | bytes 98336 | tf_op jit(solution)/shard_map/ppermute | solution.py:24
  174.4 1.5 collective-permute-done.41.refs_3_
  176.0 1.4 collective-permute-done.42.refs_4_
  177.5 1.3 shard_map.185
  (83 shorter events, 10.2 us)
Async XLA Ops:
  0.1 1.2 copy-start
  1.3 0.7 copy-start.5
  3.0 10.2 %collective-permute-start = (bf16[128,512]{1,0:T(8,128)(2,1)S(1)}, bf16[128,512]{1,0:T(8,128)(2,1)S(1)}, u32[]{:S(2)}, u32[]{:S(2)}) collective-permute-start(bf16[128,512]{1,0:T(8,128)(2,1)S(1)} %get-tuple-element.75), channel_id=1, source_target_pairs={{0,8},{8,0},{16,24},{24,16},{1,9},{9,1},{17,25},{25,17},{2,10},{10... | collective-permute-start | bytes 393224 | tf_op jit(solution)/shard_map/ppermute | solution.py:24
  6.0 7.8 %collective-permute-start.1 = (bf16[128,512]{1,0:T(8,128)(2,1)S(1)}, bf16[128,512]{1,0:T(8,128)(2,1)S(1)}, u32[]{:S(2)}, u32[]{:S(2)}) collective-permute-start(bf16[128,512]{1,0:T(8,128)(2,1)S(1)} %get-tuple-element.76), channel_id=1, source_target_pairs={{0,16},{8,24},{16,0},{24,8},{1,17},{9,25},{17,1},{25,9},{2,18},{10... | collective-permute-start | bytes 393224 | tf_op jit(solution)/shard_map/ppermute | solution.py:24
  7.5 6.3 %collective-permute-start.2 = (bf16[128,512]{1,0:T(8,128)(2,1)S(1)}, bf16[128,512]{1,0:T(8,128)(2,1)S(1)}, u32[]{:S(2)}, u32[]{:S(2)}) collective-permute-start(bf16[128,512]{1,0:T(8,128)(2,1)S(1)} %get-tuple-element.77), channel_id=1, source_target_pairs={{0,24},{8,16},{16,8},{24,0},{1,25},{9,17},{17,9},{25,1},{2,26},{10... | collective-permute-start | bytes 393224 | tf_op jit(solution)/shard_map/ppermute | solution.py:24
  7.5 5.6 %copy-start.12 = (s32[16,2]{0,1:T(2,128)S(1)}, s32[16,2]{0,1:T(2,128)}, u32[]{:S(2)}) copy-start(s32[16,2]{0,1:T(2,128)} %param.30) | copy-start | bytes 388
  13.8 1.4 collective-permute-start.3
  13.9 1.5 collective-permute-start.4
  14.4 1.3 collective-permute-start.5
  18.9 16.7 %copy-start.1 = (bf16[1024,288]{0,1:T(8,128)(2,1)S(1)}, bf16[1024,288]{0,1:T(8,128)(2,1)}, u32[]{:S(2)}) copy-start(bf16[1024,288]{0,1:T(8,128)(2,1)} %param.22) | copy-start | bytes 1769476
  18.9 16.7 %copy-start.6 = (f32[4,1024]{1,0:T(4,128)S(1)}, f32[4,1024]{1,0:T(4,128)}, u32[]{:S(2)}) copy-start(f32[4,1024]{1,0:T(4,128)} %refs_4_.2) | copy-start | bytes 49156
  19.0 16.7 %copy-start.7 = (f32[1024]{0:T(1024)S(1)}, f32[1024]{0:T(1024)}, u32[]{:S(2)}) copy-start(f32[1024]{0:T(1024)} %param.21) | copy-start | bytes 12292
  19.0 9.2 %collective-permute-start.7 = (bf16[144,1024]{1,0:T(8,128)(2,1)S(1)}, bf16[144,1024]{1,0:T(8,128)(2,1)S(1)}, u32[]{:S(2)}, u32[]{:S(2)}) collective-permute-start(bf16[144,1024]{1,0:T(8,128)(2,1)S(1)} %get-tuple-element.83), channel_id=1, source_target_pairs={{0,16},{8,24},{16,0},{24,8},{1,17},{9,25},{17,1},{25,9},{2,18},{10... | collective-permute-start | bytes 884744 | tf_op jit(solution)/shard_map/ppermute | solution.py:24
  20.5 10.8 %collective-permute-start.6 = (bf16[144,1024]{1,0:T(8,128)(2,1)S(1)}, bf16[144,1024]{1,0:T(8,128)(2,1)S(1)}, u32[]{:S(2)}, u32[]{:S(2)}) collective-permute-start(bf16[144,1024]{1,0:T(8,128)(2,1)S(1)} %get-tuple-element.82), channel_id=1, source_target_pairs={{0,8},{8,0},{16,24},{24,16},{1,9},{9,1},{17,25},{25,17},{2,10},{10... | collective-permute-start | bytes 884744 | tf_op jit(solution)/shard_map/ppermute | solution.py:24
  21.9 13.7 %collective-permute-start.8 = (bf16[144,1024]{1,0:T(8,128)(2,1)S(1)}, bf16[144,1024]{1,0:T(8,128)(2,1)S(1)}, u32[]{:S(2)}, u32[]{:S(2)}) collective-permute-start(bf16[144,1024]{1,0:T(8,128)(2,1)S(1)} %get-tuple-element.84), channel_id=1, source_target_pairs={{0,24},{8,16},{16,8},{24,0},{1,25},{9,17},{17,9},{25,1},{2,26},{10... | collective-permute-start | bytes 884744 | tf_op jit(solution)/shard_map/ppermute | solution.py:24
  23.4 19.0 %copy-start.11 = (f32[1024,16]{0,1:T(8,128)S(1)}, f32[1024,16]{0,1:T(8,128)}, u32[]{:S(2)}) copy-start(f32[1024,16]{0,1:T(8,128)} %param.25) | copy-start | bytes 196612
  31.3 19.1 %copy-start.2 = (bf16[256,1024]{1,0:T(8,128)(2,1)S(1)}, bf16[256,1024]{1,0:T(8,128)(2,1)}, u32[]{:S(2)}) copy-start(bf16[256,1024]{1,0:T(8,128)(2,1)} %refs_3_.1) | copy-start | bytes 1572868
  31.3 19.1 %copy-start.8 = (f32[1024]{0:T(1024)S(1)}, f32[1024]{0:T(1024)}, u32[]{:S(2)}) copy-start(f32[1024]{0:T(1024)} %param.24) | copy-start | bytes 12292
  31.3 36.2 %copy-start.9 = (f32[1024]{0:T(1024)S(1)}, f32[1024]{0:T(1024)}, u32[]{:S(2)}) copy-start(f32[1024]{0:T(1024)} %param.26) | copy-start | bytes 12292
  36.5 47.1 %copy-start.10 = (bf16[1024,1024]{1,0:T(8,128)(2,1)S(1)}, bf16[1024,1024]{1,0:T(8,128)(2,1)}, u32[]{:S(2)}) copy-start(bf16[1024,1024]{1,0:T(8,128)(2,1)} %refs_4_.3) | copy-start | bytes 6291460
  36.5 1.5 collective-permute-start.9
  38.0 7.5 %collective-permute-start.10 = (bf16[128,288]{1,0:T(8,128)(2,1)S(1)}, bf16[128,288]{1,0:T(8,128)(2,1)S(1)}, u32[]{:S(2)}, u32[]{:S(2)}) collective-permute-start(bf16[128,288]{1,0:T(8,128)(2,1)S(1)} %get-tuple-element.143), channel_id=1, source_target_pairs={{0,2},{1,3},{2,0},{3,1},{4,6},{5,7},{6,4},{7,5},{8,10},{9,11},{10,... | collective-permute-start | bytes 221192 | tf_op jit(solution)/shard_map/ppermute | solution.py:24
  39.7 10.7 %collective-permute-start.11 = (bf16[128,288]{1,0:T(8,128)(2,1)S(1)}, bf16[128,288]{1,0:T(8,128)(2,1)S(1)}, u32[]{:S(2)}, u32[]{:S(2)}) collective-permute-start(bf16[128,288]{1,0:T(8,128)(2,1)S(1)} %get-tuple-element.143), channel_id=1, source_target_pairs={{0,4},{1,5},{2,6},{3,7},{4,0},{5,1},{6,2},{7,3},{8,12},{9,13},{10,... | collective-permute-start | bytes 221192 | tf_op jit(solution)/shard_map/ppermute | solution.py:24
  42.3 8.1 %collective-permute-start.12 = (bf16[128,288]{1,0:T(8,128)(2,1)S(1)}, bf16[128,288]{1,0:T(8,128)(2,1)S(1)}, u32[]{:S(2)}, u32[]{:S(2)}) collective-permute-start(bf16[128,288]{1,0:T(8,128)(2,1)S(1)} %get-tuple-element.143), channel_id=1, source_target_pairs={{0,6},{1,7},{2,4},{3,5},{4,2},{5,3},{6,0},{7,1},{8,14},{9,15},{10,... | collective-permute-start | bytes 221192 | tf_op jit(solution)/shard_map/ppermute | solution.py:24
  42.5 25.0 %collective-permute-start.16 = (bf16[144,1024]{1,0:T(8,128)(2,1)S(1)}, bf16[144,1024]{1,0:T(8,128)(2,1)S(1)}, u32[]{:S(2)}, u32[]{:S(2)}) collective-permute-start(bf16[144,1024]{1,0:T(8,128)(2,1)S(1)} %get-tuple-element.91), channel_id=1, source_target_pairs={{0,8},{8,0},{16,24},{24,16},{1,9},{9,1},{17,25},{25,17},{2,10},{10... | collective-permute-start | bytes 884744 | tf_op jit(solution)/shard_map/ppermute | solution.py:24
  44.0 23.6 %collective-permute-start.17 = (bf16[144,1024]{1,0:T(8,128)(2,1)S(1)}, bf16[144,1024]{1,0:T(8,128)(2,1)S(1)}, u32[]{:S(2)}, u32[]{:S(2)}) collective-permute-start(bf16[144,1024]{1,0:T(8,128)(2,1)S(1)} %get-tuple-element.92), channel_id=1, source_target_pairs={{0,16},{8,24},{16,0},{24,8},{1,17},{9,25},{17,1},{25,9},{2,18},{10... | collective-permute-start | bytes 884744 | tf_op jit(solution)/shard_map/ppermute | solution.py:24
  45.5 22.1 %collective-permute-start.18 = (bf16[144,1024]{1,0:T(8,128)(2,1)S(1)}, bf16[144,1024]{1,0:T(8,128)(2,1)S(1)}, u32[]{:S(2)}, u32[]{:S(2)}) collective-permute-start(bf16[144,1024]{1,0:T(8,128)(2,1)S(1)} %get-tuple-element.93), channel_id=1, source_target_pairs={{0,24},{8,16},{16,8},{24,0},{1,25},{9,17},{17,9},{25,1},{2,26},{10... | collective-permute-start | bytes 884744 | tf_op jit(solution)/shard_map/ppermute | solution.py:24
  55.8 6.7 %collective-permute-start.13 = (bf16[18,8,128]{2,1,0:T(8,128)(2,1)S(1)}, bf16[18,8,128]{2,1,0:T(8,128)(2,1)S(1)}, u32[]{:S(2)}, u32[]{:S(2)}) collective-permute-start(bf16[18,8,128]{2,1,0:T(8,128)(2,1)S(1)} %get-tuple-element.88), channel_id=1, source_target_pairs={{0,8},{16,24},{1,9},{17,25},{2,10},{18,26},{3,11},{19,27},{4,12},{... | collective-permute-start | bytes 110600 | tf_op jit(solution)/shard_map/ppermute | solution.py:29
  59.1 6.8 %collective-permute-start.14 = (bf16[18,8,128]{2,1,0:T(8,128)(2,1)S(1)}, bf16[18,8,128]{2,1,0:T(8,128)(2,1)S(1)}, u32[]{:S(2)}, u32[]{:S(2)}) collective-permute-start(bf16[18,8,128]{2,1,0:T(8,128)(2,1)S(1)} %get-tuple-element.88), channel_id=1, source_target_pairs={{0,16},{8,24},{1,17},{9,25},{2,18},{10,26},{3,19},{11,27},{4,20},{... | collective-permute-start | bytes 110600 | tf_op jit(solution)/shard_map/ppermute | solution.py:29
  62.6 5.0 %collective-permute-start.15 = (bf16[18,8,128]{2,1,0:T(8,128)(2,1)S(1)}, bf16[18,8,128]{2,1,0:T(8,128)(2,1)S(1)}, u32[]{:S(2)}, u32[]{:S(2)}) collective-permute-start(bf16[18,8,128]{2,1,0:T(8,128)(2,1)S(1)} %get-tuple-element.88), channel_id=1, source_target_pairs={{0,24},{8,16},{1,25},{9,17},{2,26},{10,18},{3,27},{11,19},{4,28},{... | collective-permute-start | bytes 110600 | tf_op jit(solution)/shard_map/ppermute | solution.py:29
  72.0 7.3 %collective-permute-start.19 = (bf16[128,1024]{1,0:T(8,128)(2,1)S(1)}, bf16[128,1024]{1,0:T(8,128)(2,1)S(1)}, u32[]{:S(2)}, u32[]{:S(2)}) collective-permute-start(bf16[128,1024]{1,0:T(8,128)(2,1)S(1)} %shard_map.169.refs_0_), channel_id=1, source_target_pairs={{0,8},{8,0},{16,24},{24,16},{1,9},{9,1},{17,25},{25,17},{2,10},{10... | collective-permute-start | bytes 786440 | tf_op jit(solution)/shard_map/ppermute | solution.py:24
  72.1 11.5 %collective-permute-start.20 = (bf16[128,1024]{1,0:T(8,128)(2,1)S(1)}, bf16[128,1024]{1,0:T(8,128)(2,1)S(1)}, u32[]{:S(2)}, u32[]{:S(2)}) collective-permute-start(bf16[128,1024]{1,0:T(8,128)(2,1)S(1)} %shard_map.169.refs_0_), channel_id=1, source_target_pairs={{0,16},{8,24},{16,0},{24,8},{1,17},{9,25},{17,1},{25,9},{2,18},{10... | collective-permute-start | bytes 786440 | tf_op jit(solution)/shard_map/ppermute | solution.py:24
  75.9 7.7 %collective-permute-start.21 = (bf16[128,1024]{1,0:T(8,128)(2,1)S(1)}, bf16[128,1024]{1,0:T(8,128)(2,1)S(1)}, u32[]{:S(2)}, u32[]{:S(2)}) collective-permute-start(bf16[128,1024]{1,0:T(8,128)(2,1)S(1)} %shard_map.169.refs_0_), channel_id=1, source_target_pairs={{0,24},{8,16},{16,8},{24,0},{1,25},{9,17},{17,9},{25,1},{2,26},{10... | collective-permute-start | bytes 786440 | tf_op jit(solution)/shard_map/ppermute | solution.py:24
  84.9 2.0 %collective-permute-start.22 = (bf16[4,64,1024]{2,1,0:T(8,128)(2,1)S(1)}, bf16[4,64,1024]{2,1,0:T(8,128)(2,1)S(1)}, u32[]{:S(2)}, u32[]{:S(2)}) collective-permute-start(bf16[4,64,1024]{2,1,0:T(8,128)(2,1)S(1)} %get-tuple-element.95), channel_id=1, source_target_pairs={{0,1},{1,0},{2,3},{3,2},{4,5},{5,4},{6,7},{7,6},{8,9},{9,8},{10,11... | collective-permute-start | bytes 1572872 | tf_op jit(solution)/shard_map/ppermute | solution.py:24
  87.0 11.8 %collective-permute-start.23 = (bf16[64,1024]{1,0:T(8,128)(2,1)S(1)}, bf16[64,1024]{1,0:T(8,128)(2,1)S(1)}, u32[]{:S(2)}, u32[]{:S(2)}) collective-permute-start(bf16[64,1024]{1,0:T(8,128)(2,1)S(1)} %get-tuple-element.97), channel_id=1, source_target_pairs={{0,2},{1,3},{2,0},{3,1},{4,6},{5,7},{6,4},{7,5},{8,10},{9,11},{10,... | collective-permute-start | bytes 393224 | tf_op jit(solution)/shard_map/ppermute | solution.py:24
  89.8 12.9 %collective-permute-start.24 = (bf16[64,1024]{1,0:T(8,128)(2,1)S(1)}, bf16[64,1024]{1,0:T(8,128)(2,1)S(1)}, u32[]{:S(2)}, u32[]{:S(2)}) collective-permute-start(bf16[64,1024]{1,0:T(8,128)(2,1)S(1)} %get-tuple-element.98), channel_id=1, source_target_pairs={{0,4},{1,5},{2,6},{3,7},{4,0},{5,1},{6,2},{7,3},{8,12},{9,13},{10,... | collective-permute-start | bytes 393224 | tf_op jit(solution)/shard_map/ppermute | solution.py:24
  90.7 12.0 %collective-permute-start.25 = (bf16[64,1024]{1,0:T(8,128)(2,1)S(1)}, bf16[64,1024]{1,0:T(8,128)(2,1)S(1)}, u32[]{:S(2)}, u32[]{:S(2)}) collective-permute-start(bf16[64,1024]{1,0:T(8,128)(2,1)S(1)} %get-tuple-element.99), channel_id=1, source_target_pairs={{0,6},{1,7},{2,4},{3,5},{4,2},{5,3},{6,0},{7,1},{8,14},{9,15},{10,... | collective-permute-start | bytes 393224 | tf_op jit(solution)/shard_map/ppermute | solution.py:24
  102.7 19.8 %copy-start.3 = (f32[4096]{0:T(1024)S(1)}, f32[4096]{0:T(1024)}, u32[]{:S(2)}) copy-start(f32[4096]{0:T(1024)} %param.28) | copy-start | bytes 49156
  103.6 13.5 %collective-permute-start.26 = (bf16[48,1024]{1,0:T(8,128)(2,1)S(1)}, bf16[48,1024]{1,0:T(8,128)(2,1)S(1)}, u32[]{:S(2)}, u32[]{:S(2)}) collective-permute-start(bf16[48,1024]{1,0:T(8,128)(2,1)S(1)} %get-tuple-element.106), channel_id=1, source_target_pairs={{0,2},{1,3},{2,0},{3,1},{4,6},{5,7},{6,4},{7,5},{8,10},{9,11},{10,... | collective-permute-start | bytes 294920 | tf_op jit(solution)/shard_map/ppermute | solution.py:24
  105.9 11.2 %collective-permute-start.27 = (bf16[48,1024]{1,0:T(8,128)(2,1)S(1)}, bf16[48,1024]{1,0:T(8,128)(2,1)S(1)}, u32[]{:S(2)}, u32[]{:S(2)}) collective-permute-start(bf16[48,1024]{1,0:T(8,128)(2,1)S(1)} %get-tuple-element.107), channel_id=1, source_target_pairs={{0,4},{1,5},{2,6},{3,7},{4,0},{5,1},{6,2},{7,3},{8,12},{9,13},{10,... | collective-permute-start | bytes 294920 | tf_op jit(solution)/shard_map/ppermute | solution.py:24
  106.8 10.3 %collective-permute-start.28 = (bf16[48,1024]{1,0:T(8,128)(2,1)S(1)}, bf16[48,1024]{1,0:T(8,128)(2,1)S(1)}, u32[]{:S(2)}, u32[]{:S(2)}) collective-permute-start(bf16[48,1024]{1,0:T(8,128)(2,1)S(1)} %get-tuple-element.108), channel_id=1, source_target_pairs={{0,6},{1,7},{2,4},{3,5},{4,2},{5,3},{6,0},{7,1},{8,14},{9,15},{10,... | collective-permute-start | bytes 294920 | tf_op jit(solution)/shard_map/ppermute | solution.py:24
  108.4 3.9 %collective-permute-start.29 = (bf16[16,1024]{1,0:T(8,128)(2,1)S(1)}, bf16[16,1024]{1,0:T(8,128)(2,1)S(1)}, u32[]{:S(2)}, u32[]{:S(2)}) collective-permute-start(bf16[16,1024]{1,0:T(8,128)(2,1)S(1)} %get-tuple-element.109), channel_id=1, source_target_pairs={{0,8},{8,0},{16,24},{24,16},{1,9},{9,1},{17,25},{25,17},{2,10},{10... | collective-permute-start | bytes 98312 | tf_op jit(solution)/shard_map/ppermute | solution.py:24
  109.7 4.2 %collective-permute-start.30 = (bf16[16,1024]{1,0:T(8,128)(2,1)S(1)}, bf16[16,1024]{1,0:T(8,128)(2,1)S(1)}, u32[]{:S(2)}, u32[]{:S(2)}) collective-permute-start(bf16[16,1024]{1,0:T(8,128)(2,1)S(1)} %get-tuple-element.110), channel_id=1, source_target_pairs={{0,16},{8,24},{16,0},{24,8},{1,17},{9,25},{17,1},{25,9},{2,18},{10... | collective-permute-start | bytes 98312 | tf_op jit(solution)/shard_map/ppermute | solution.py:24
  112.3 4.8 %collective-permute-start.31 = (bf16[16,1024]{1,0:T(8,128)(2,1)S(1)}, bf16[16,1024]{1,0:T(8,128)(2,1)S(1)}, u32[]{:S(2)}, u32[]{:S(2)}) collective-permute-start(bf16[16,1024]{1,0:T(8,128)(2,1)S(1)} %get-tuple-element.111), channel_id=1, source_target_pairs={{0,24},{8,16},{16,8},{24,0},{1,25},{9,17},{17,9},{25,1},{2,26},{10... | collective-permute-start | bytes 98312 | tf_op jit(solution)/shard_map/ppermute | solution.py:24
  117.1 1.5 collective-permute-start.32
  119.0 12.0 %collective-permute-start.35 = (bf16[192,1024]{1,0:T(8,128)(2,1)S(1)}, bf16[192,1024]{1,0:T(8,128)(2,1)S(1)}, u32[]{:S(2)}, u32[]{:S(2)}) collective-permute-start(bf16[192,1024]{1,0:T(8,128)(2,1)S(1)} %shard_map.176.refs_1_), channel_id=1, source_target_pairs={{0,8},{8,0},{16,24},{24,16},{1,9},{9,1},{17,25},{25,17},{2,10},{10... | collective-permute-start | bytes 1179656 | tf_op jit(solution)/shard_map/ppermute | solution.py:24
  120.4 18.0 %collective-permute-start.34 = (bf16[192,1024]{1,0:T(8,128)(2,1)S(1)}, bf16[192,1024]{1,0:T(8,128)(2,1)S(1)}, u32[]{:S(2)}, u32[]{:S(2)}) collective-permute-start(bf16[192,1024]{1,0:T(8,128)(2,1)S(1)} %shard_map.176.refs_1_), channel_id=1, source_target_pairs={{0,16},{8,24},{16,0},{24,8},{1,17},{9,25},{17,1},{25,9},{2,18},{10... | collective-permute-start | bytes 1179656 | tf_op jit(solution)/shard_map/ppermute | solution.py:24
  121.1 19.6 %collective-permute-start.33 = (bf16[192,1024]{1,0:T(8,128)(2,1)S(1)}, bf16[192,1024]{1,0:T(8,128)(2,1)S(1)}, u32[]{:S(2)}, u32[]{:S(2)}) collective-permute-start(bf16[192,1024]{1,0:T(8,128)(2,1)S(1)} %shard_map.176.refs_1_), channel_id=1, source_target_pairs={{0,24},{8,16},{16,8},{24,0},{1,25},{9,17},{17,9},{25,1},{2,26},{10... | collective-permute-start | bytes 1179656 | tf_op jit(solution)/shard_map/ppermute | solution.py:24
  143.0 7.6 %copy-start.4 = (bf16[4096,8]{0,1:T(8,128)(2,1)S(1)}, bf16[4096,8]{0,1:T(8,128)(2,1)}, u32[]{:S(2)}) copy-start(bf16[4096,8]{0,1:T(8,128)(2,1)} %param.29) | copy-start | bytes 196612
  146.6 12.3 %collective-permute-start.36 = (bf16[48,4096]{1,0:T(8,128)(2,1)S(1)}, bf16[48,4096]{1,0:T(8,128)(2,1)S(1)}, u32[]{:S(2)}, u32[]{:S(2)}) collective-permute-start(bf16[48,4096]{1,0:T(8,128)(2,1)S(1)} %get-tuple-element.130), channel_id=1, source_target_pairs={{0,8},{8,0},{16,24},{24,16},{1,9},{9,1},{17,25},{25,17},{2,10},{10... | collective-permute-start | bytes 1179656 | tf_op jit(solution)/shard_map/ppermute | solution.py:24
  148.9 15.5 %collective-permute-start.37 = (bf16[48,4096]{1,0:T(8,128)(2,1)S(1)}, bf16[48,4096]{1,0:T(8,128)(2,1)S(1)}, u32[]{:S(2)}, u32[]{:S(2)}) collective-permute-start(bf16[48,4096]{1,0:T(8,128)(2,1)S(1)} %get-tuple-element.131), channel_id=1, source_target_pairs={{0,16},{8,24},{16,0},{24,8},{1,17},{9,25},{17,1},{25,9},{2,18},{10... | collective-permute-start | bytes 1179656 | tf_op jit(solution)/shard_map/ppermute | solution.py:24
  150.6 15.4 %collective-permute-start.38 = (bf16[48,4096]{1,0:T(8,128)(2,1)S(1)}, bf16[48,4096]{1,0:T(8,128)(2,1)S(1)}, u32[]{:S(2)}, u32[]{:S(2)}) collective-permute-start(bf16[48,4096]{1,0:T(8,128)(2,1)S(1)} %get-tuple-element.132), channel_id=1, source_target_pairs={{0,24},{8,16},{16,8},{24,0},{1,25},{9,17},{17,9},{25,1},{2,26},{10... | collective-permute-start | bytes 1179656 | tf_op jit(solution)/shard_map/ppermute | solution.py:24
  166.5 6.0 %collective-permute-start.39 = (bf16[48,1024]{1,0:T(8,128)(2,1)S(1)}, bf16[48,1024]{1,0:T(8,128)(2,1)S(1)}, u32[]{:S(2)}, u32[]{:S(2)}) collective-permute-start(bf16[48,1024]{1,0:T(8,128)(2,1)S(1)} %get-tuple-element.137), channel_id=1, source_target_pairs={{0,2},{1,3},{2,0},{3,1},{4,6},{5,7},{6,4},{7,5},{8,10},{9,11},{10,... | collective-permute-start | bytes 294920 | tf_op jit(solution)/shard_map/ppermute | solution.py:24
  167.6 6.8 %collective-permute-start.40 = (bf16[48,1024]{1,0:T(8,128)(2,1)S(1)}, bf16[48,1024]{1,0:T(8,128)(2,1)S(1)}, u32[]{:S(2)}, u32[]{:S(2)}) collective-permute-start(bf16[48,1024]{1,0:T(8,128)(2,1)S(1)} %get-tuple-element.138), channel_id=1, source_target_pairs={{0,4},{1,5},{2,6},{3,7},{4,0},{5,1},{6,2},{7,3},{8,12},{9,13},{10,... | collective-permute-start | bytes 294920 | tf_op jit(solution)/shard_map/ppermute | solution.py:24
  169.4 6.5 %collective-permute-start.41 = (bf16[48,1024]{1,0:T(8,128)(2,1)S(1)}, bf16[48,1024]{1,0:T(8,128)(2,1)S(1)}, u32[]{:S(2)}, u32[]{:S(2)}) collective-permute-start(bf16[48,1024]{1,0:T(8,128)(2,1)S(1)} %get-tuple-element.139), channel_id=1, source_target_pairs={{0,6},{1,7},{2,4},{3,5},{4,2},{5,3},{6,0},{7,1},{8,14},{9,15},{10,... | collective-permute-start | bytes 294920 | tf_op jit(solution)/shard_map/ppermute | solution.py:24
  176.0 1.5 collective-permute-start.42

commit v4 on v3

--- a/solution.py
+++ b/solution.py
@@ -370,13 +370,14 @@
     )(place, *in_hbm(sources))
 
 
-def expert_body(mask, first, last, model_width, jobs, count, place, piece, gain, gate, up, *refs):
+def expert_body(mask, first, last, model_width, jobs, count, parts, place, *refs):
+    pieces, (gain, gate, up), refs = refs[:parts], refs[parts : parts + 3], refs[parts + 3 :]
     before, refs = ([], refs) if first else (refs[:3], refs[3:])
     sources, refs = refs[:count], refs[count:]
     outs, refs = (refs[:1], refs[1:]) if last else (refs[:3], refs[3:])
     copies = start_copies(jobs, place, sources, refs[:-1], refs[-1]) if jobs else []
-    width = piece.shape[1]
-    values = piece[...].astype(F32)
+    width = pieces[0].shape[1]
+    values = jnp.concatenate([piece[...].astype(F32) for piece in pieces], axis=0)
     square = jnp.sum(values * values, axis=-1, keepdims=True)
     if not first:
         square = square + before[2][:, 0:1]
@@ -403,8 +404,8 @@
         copy.wait()
 
 
-def expert_chunk(mask, first, last, place, piece, gain, gate, up, before, jobs, sources):
-    slots, width = piece.shape
+def expert_chunk(mask, first, last, place, piece, gain, gate, up, before, jobs, sources, deps):
+    slots, width = sum(part.shape[0] for part in piece), piece[0].shape[1]
     model_width, hidden_units = gain.shape[1], gate.shape[1]
     total = shape((slots, hidden_units), F32)
     outs = [total, total, shape((slots, 128), F32)]
@@ -413,14 +414,15 @@
     sources = sources if jobs else []
     far = pl.BlockSpec(memory_space=pltpu.HBM)
     results = kernel_call(
-        functools.partial(expert_body, mask, first, last, model_width, jobs, len(sources)),
+        functools.partial(expert_body, mask, first, last, model_width, jobs, len(sources), len(piece)),
         outs + fetched_shapes(jobs, sources, width),
-        [SMEM] + [VMEM] * (4 + len(before)) + [far] * len(sources),
+        [SMEM] + [VMEM] * (3 + len(piece) + len(before)) + [far] * len(sources),
         [pltpu.SemaphoreType.DMA((len(jobs),))] if jobs else [],
         flops=4 * slots * width * hidden_units,
         moved=4 * width * hidden_units,
         limit=12,
-    )(place, piece, gain, gate, up, *before, *in_hbm(sources))
+        deps=deps,
+    )(place, *piece, gain, gate, up, *before, *in_hbm(sources))
     return results[: len(outs)], results[len(outs) :]
 
 
@@ -638,7 +640,7 @@
         [pltpu.VMEM(tiled.shape, F32)] * 2,
         limit=24,
     )(maps, low_rank, activated, step_weight, step_bias[None], rate)
-    arrived = [later_partner(final, "seq", mask) for mask in masks]
+    arrived = [partner(final, "seq", mask) for mask in masks]
     gated = kernel_call(
         functools.partial(gated_body, seq, own_rows),
         shape((length, channels), BF16),
@@ -680,7 +682,8 @@
 
     sources = [gate_weight, up_weight, down_weight]
     both = lambda mask: [(0, mask, 0), (1, mask, 0)]
-    current = list(fetch(place, both(0) + both(1), width, sources[:2], [own_sum]))
+    early = min(seq, 3)
+    current = list(fetch(place, sum([both(mask) for mask in range(early)], []), width, sources[:2], [own_sum]))
     near_hidden = kernel_call(
         functools.partial(hidden_body, chips, seq),
         [shape((own_rows, width), BF16)] * seq + [shape((per_chip, width), BF16)] * chips,
@@ -695,27 +698,33 @@
         partner(block, "expert", 2 * w) for w, block in zip(range(1, chips), outgoing[1:])
     ]
     whole = [near_hidden[0]] + [partner(near_hidden[mask], "seq", mask) for mask in masks]
-    crossed = partner(second_halves(came, whole[1:]), "expert", 1)
+    more = list(fetch(place, both(early), width, sources[:2], [outgoing[0]])) if early < seq else []
+    crossed = partner(second_halves(came, whole[1:] + more), "expert", 1)
     rows = kernel_call(
         functools.partial(rows_body, chips, seq, groups, most_slots),
         shape((slots, width), BF16),
         [VMEM] * (chips + 1),
         moved=4 * slots * width,
     )(*came, crossed)
-    pieces = [rows] + [partner(rows, "seq", mask) for mask in masks]
-
-    before, waiting, downs = [], current, []
+    if seq == 4:
+        pieces = [rows, partner(rows, "seq", 1), partner(rows, "seq", 2)]
+        half = slots // 2
+        pieces = [[piece] for piece in pieces] + [
+            [partner(pieces[1][:half], "seq", 2), partner(pieces[2][half:], "seq", 1)]
+        ]
+    else:
+        pieces = [[rows]] + [[partner(rows, "seq", mask)] for mask in masks]
+
+    before, waiting, downs = [], current + more, []
     for mask in range(seq):
-        jobs = both(mask + 2) if mask + 2 < seq else []
-        if mask == seq - 4:
-            jobs = both(mask + 2) + both(mask + 3)
-        elif mask == seq - 3:
+        jobs = both(mask + 4) if mask + 4 < seq else []
+        if mask == max(0, seq - 4):
             jobs = [(2, block, 1) for block in range(seq)]
         before, came_in = expert_chunk(
-            mask, mask == 0, mask == seq - 1, place, pieces[mask], moe_gain[None], *waiting[:2], before, jobs, sources
+            mask, mask == 0, mask == seq - 1, place, pieces[mask], moe_gain[None], *waiting[:2], before, jobs, sources, downs
         )
         waiting = waiting[2:]
-        if mask == seq - 3:
+        if mask == max(0, seq - 4):
             downs = list(came_in)
         else:
             waiting = waiting + list(came_in)

time: 179 us -> 172 us (0.961)
  starting transfers between devices: 56.5 us -> 50.9 us
  waiting for transfers between devices: 61.4 us -> 59.3 us
    ppermute x3 -> x0, starting transfers between devices: 10 us -> none  [later_partner(): lax.ppermute(block, axis, [(i, i ^ mask) for i in range(size) if i < i ^...]
    ppermute x40 -> x44, starting transfers between devices: 46.4 us -> 50.9 us  [partner(): return lax.ppermute(block, axis, [(i, i ^ mask) for i in range(size)])]
    pallas_call x23 -> x24, Pallas kernels: 51.6 us -> 52.3 us  [kernel_call(): return lambda *operands: call(*operands, *deps)]
    ppermute x40 -> x44, waiting for transfers between devices: 59.8 us -> 59.3 us  [partner(): return lax.ppermute(block, axis, [(i, i ^ mask) for i in range(size)])]
    unnamed x28 -> x32, local copies, waits for them, and re-layouts: 7.63 us -> 7.66 us
  transfers between devices with their start and end apart: 43 -> 44, of which waited for: 25 -> 24; matrix products, arithmetic and copies ran while one was open for 4% -> 4% of each run, Pallas kernels for 18% -> 19%
where the time goes in v4:
time: 172 us
  waiting for transfers between devices  59.3 us (34%)
  Pallas kernels  52.3 us (30%)
  starting transfers between devices  50.9 us (30%)
  local copies, waits for them, and re-layouts  8.69 us (5%)
    ppermute x44, waiting for transfers between devices, partner(): return lax.ppermute(block, axis, [(i, i ^ mask) for i in range(size)])  59.3 us
    pallas_call x24, Pallas kernels, kernel_call(): return lambda *operands: call(*operands, *deps)  52.3 us
    ppermute x44, starting transfers between devices, partner(): return lax.ppermute(block, axis, [(i, i ^ mask) for i in range(size)])  50.9 us
    unnamed x32, local copies, waits for them, and re-layouts  7.66 us
  transfers between devices with their start and end apart: 44, of which 24 were waited for; matrix products, arithmetic and copies ran while one was open for 4% of the time, Pallas kernels for 19%

profile of v4, /device:TPU:0, one launch (start us, length us, event | category | flops | bytes accessed | tf_op | source)
XLA Modules:
  0.0 171.9 jit_solution(13010414850300035200)
XLA Ops:
  0.1 1.2 copy-done.2
  2.0 1.0 shard_map.163
  3.0 3.0 %collective-permute-start = (bf16[128,512]{1,0:T(8,128)(2,1)S(1)}, bf16[128,512]{1,0:T(8,128)(2,1)S(1)}, u32[]{:S(2)}, u32[]{:S(2)}) collective-permute-start(bf16[128,512]{1,0:T(8,128)(2,1)S(1)} %get-tuple-element.75), channel_id=1, source_target_pairs={{0,8},{8,0},{16,24},{24,16},{1,9},{9,1},{17,25},{25,17},{2,10},{10... | collective-permute-start | bytes 393224 | tf_op jit(solution)/shard_map/ppermute | solution.py:24
  6.0 1.5 collective-permute-start.1
  7.5 5.6 %copy.18 = bf16[128,8,2,1024]{3,1,2,0:T(8,128)(2,1)} copy(bf16[128,8,2,1024]{3,2,1,0:T(2,128)(2,1)} %bitcast.42) | data formatting | bytes 8388608
  15.7 3.2 %shard_map.165 = (f32[144,1024]{1,0:T(8,128)S(1)}, bf16[144,1024]{1,0:T(8,128)(2,1)S(1)}, bf16[144,1024]{1,0:T(8,128)(2,1)S(1)}, bf16[144,1024]{1,0:T(8,128)(2,1)S(1)}) custom-call(s32[3]{0:T(128)S(1)} %pad_add_fusion.refs_0_, bf16[128,1024]{1,0:T(8,128)(2,1)S(1)} %get-tuple-element.74.refs_1_, bf16[128,512]{1,0:T(8,128)(2,1)S(1)} %collective-permute-done.refs_0_.refs_2_, ...), custom_call_target="tpu_custom_call" | custom-call | flops 1073741824 | bytes 2097152 | tf_op jit(solution)/shard_map/pallas_call | solution.py:58
  19.0 1.6 collective-permute-start.7
  20.5 1.4 collective-permute-start.6
  23.5 4.7 %collective-permute-done.7.refs_10_.refs_2_.refs_3_ = bf16[144,1024]{1,0:T(8,128)(2,1)S(1)} collective-permute-done((bf16[144,1024]{1,0:T(8,128)(2,1)S(1)}, bf16[144,1024]{1,0:T(8,128)(2,1)S(1)}, u32[]{:S(2)}, u32[]{:S(2)}) %collective-permute-start.7) | collective-permute-done | bytes 294944 | tf_op jit(solution)/shard_map/ppermute | solution.py:24
  28.1 3.2 %shard_map.166 = (f32[128,1024]{1,0:T(8,128)S(1)}, bf16[144,1024]{1,0:T(8,128)(2,1)S(1)}, bf16[144,1024]{1,0:T(8,128)(2,1)S(1)}, bf16[144,1024]{1,0:T(8,128)(2,1)S(1)}) custom-call(s32[3]{0:T(128)S(1)} %pad_add_fusion.refs_0_, bf16[128,1024]{1,0:T(8,128)(2,1)S(1)} %get-tuple-element.74.refs_1_, bf16[128,512]{1,0:T(8,128)(2,1)S(1)} %collective-permute-done.refs_0_.refs_2_, ...), custom_call_target="tpu_custom_call" | custom-call | flops 1073741824 | bytes 2097152 | tf_op jit(solution)/shard_map/pallas_call | solution.py:58
  31.4 4.3 %collective-permute-done.8.refs_3_.refs_4_ = bf16[144,1024]{1,0:T(8,128)(2,1)S(1)} collective-permute-done((bf16[144,1024]{1,0:T(8,128)(2,1)S(1)}, bf16[144,1024]{1,0:T(8,128)(2,1)S(1)}, u32[]{:S(2)}, u32[]{:S(2)}) %collective-permute-start.8) | collective-permute-done | bytes 294944 | tf_op jit(solution)/shard_map/ppermute | solution.py:24
  36.6 1.4 collective-permute-done.9
  38.0 1.6 collective-permute-start.10
  39.7 2.6 %collective-permute-start.11 = (bf16[128,288]{1,0:T(8,128)(2,1)S(1)}, bf16[128,288]{1,0:T(8,128)(2,1)S(1)}, u32[]{:S(2)}, u32[]{:S(2)}) collective-permute-start(bf16[128,288]{1,0:T(8,128)(2,1)S(1)} %get-tuple-element.143), channel_id=1, source_target_pairs={{0,4},{1,5},{2,6},{3,7},{4,0},{5,1},{6,2},{7,3},{8,12},{9,13},{10,... | collective-permute-start | bytes 221192 | tf_op jit(solution)/shard_map/ppermute | solution.py:24
  42.5 1.4 collective-permute-start.16
  44.0 1.5 collective-permute-start.17
  46.1 4.3 %collective-permute-done.11 = bf16[128,288]{1,0:T(8,128)(2,1)S(1)} collective-permute-done((bf16[128,288]{1,0:T(8,128)(2,1)S(1)}, bf16[128,288]{1,0:T(8,128)(2,1)S(1)}, u32[]{:S(2)}, u32[]{:S(2)}) %collective-permute-start.11) | collective-permute-done | bytes 73760 | tf_op jit(solution)/shard_map/ppermute | solution.py:24
  50.5 5.4 %shard_map.168 = (f32[128,8,128]{2,1,0:T(8,128)S(1)}, f32[128,8,128]{2,1,0:T(8,128)S(1)}, bf16[18,8,128]{2,1,0:T(8,128)(2,1)S(1)}) custom-call(f32[128,32]{1,0:T(8,128)S(1)} %slice.17.refs_0_.refs_1_, bf16[128,256]{1,0:T(8,128)(2,1)S(1)} %slice.22.refs_1_, bf16[128,1024]{1,0:T(8,128)(2,1)S(1)} %get-tuple-element.87.refs_2_.refs_8_, ...), custom_call_target="tpu_custom_call" | custom-call | tf_op jit(solution)/shard_map/pallas_call | solution.py:58
  55.8 1.4 collective-permute-start.13
  57.3 1.5 collective-permute-start.14
  58.8 1.1 collective-permute-done.13.refs_2_
  59.9 2.3 %collective-permute-start.15 = (bf16[18,8,128]{2,1,0:T(8,128)(2,1)S(1)}, bf16[18,8,128]{2,1,0:T(8,128)(2,1)S(1)}, u32[]{:S(2)}, u32[]{:S(2)}) collective-permute-start(bf16[18,8,128]{2,1,0:T(8,128)(2,1)S(1)} %get-tuple-element.88), channel_id=1, source_target_pairs={{0,24},{8,16},{16,8},{24,0},{1,25},{9,17},{17,9},{25,1},{2,26},{10... | collective-permute-start | bytes 110600 | tf_op jit(solution)/shard_map/ppermute | solution.py:24
  62.2 2.5 %collective-permute-done.15.refs_4_ = bf16[18,8,128]{2,1,0:T(8,128)(2,1)S(1)} collective-permute-done((bf16[18,8,128]{2,1,0:T(8,128)(2,1)S(1)}, bf16[18,8,128]{2,1,0:T(8,128)(2,1)S(1)}, u32[]{:S(2)}, u32[]{:S(2)}) %collective-permute-start.15) | collective-permute-done | bytes 36896 | tf_op jit(solution)/shard_map/ppermute | solution.py:24
  64.7 4.5 %shard_map.169.refs_0_ = bf16[128,1024]{1,0:T(8,128)(2,1)S(1)} custom-call(s32[3]{0:T(128)S(1)} %pad_add_fusion.refs_0_, f32[128,32]{1,0:T(8,128)S(1)} %slice.17.refs_0_.refs_1_, bf16[18,8,128]{2,1,0:T(8,128)(2,1)S(1)} %collective-permute-done.13.refs_2_, bf16[18,8,128]{2,1,0:T(8,128)(2,1)S(1)} %collective-permute-done.14.refs_3_, ...), custom_call_target="tpu_custom_call" | custom-call | tf_op jit(solution)/shard_map/pallas_call | solution.py:58
  69.2 1.4 collective-permute-start.19
  70.7 1.5 collective-permute-start.20
  72.8 4.3 %collective-permute-done.19.refs_1_ = bf16[128,1024]{1,0:T(8,128)(2,1)S(1)} collective-permute-done((bf16[128,1024]{1,0:T(8,128)(2,1)S(1)}, bf16[128,1024]{1,0:T(8,128)(2,1)S(1)}, u32[]{:S(2)}, u32[]{:S(2)}) %collective-permute-start.19) | collective-permute-done | bytes 262176 | tf_op jit(solution)/shard_map/ppermute | solution.py:24
  77.1 3.9 %collective-permute-done.20.refs_2_ = bf16[128,1024]{1,0:T(8,128)(2,1)S(1)} collective-permute-done((bf16[128,1024]{1,0:T(8,128)(2,1)S(1)}, bf16[128,1024]{1,0:T(8,128)(2,1)S(1)}, u32[]{:S(2)}, u32[]{:S(2)}) %collective-permute-start.20) | collective-permute-done | bytes 262176 | tf_op jit(solution)/shard_map/ppermute | solution.py:24
  81.0 1.3 shard_map.170
  82.3 1.9 %collective-permute-done.22.refs_1_ = bf16[4,64,1024]{2,1,0:T(8,128)(2,1)S(1)} collective-permute-done((bf16[4,64,1024]{2,1,0:T(8,128)(2,1)S(1)}, bf16[4,64,1024]{2,1,0:T(8,128)(2,1)S(1)}, u32[]{:S(2)}, u32[]{:S(2)}) %collective-permute-start.22) | collective-permute-done | bytes 524320 | tf_op jit(solution)/shard_map/ppermute | solution.py:24
  84.4 2.0 %collective-permute-start.23 = (bf16[64,1024]{1,0:T(8,128)(2,1)S(1)}, bf16[64,1024]{1,0:T(8,128)(2,1)S(1)}, u32[]{:S(2)}, u32[]{:S(2)}) collective-permute-start(bf16[64,1024]{1,0:T(8,128)(2,1)S(1)} %get-tuple-element.97), channel_id=1, source_target_pairs={{0,2},{1,3},{2,0},{3,1},{4,6},{5,7},{6,4},{7,5},{8,10},{9,11},{10,... | collective-permute-start | bytes 393224 | tf_op jit(solution)/shard_map/ppermute | solution.py:24
  86.3 1.0 collective-permute-start.24
  87.3 1.5 collective-permute-start.25
  89.6 7.9 %shard_map.173 = (bf16[1024,1792]{1,0:T(8,128)(2,1)S(1)}, bf16[1024,1792]{1,0:T(8,128)(2,1)S(1)}, bf16[1024,1792]{1,0:T(8,128)(2,1)S(1)}, bf16[1024,1792]{1,0:T(...) custom-call(s32[3]{0:T(128)S(1)} %pad_add_fusion.refs_0_, ...), custom_call_target="tpu_custom_call" | custom-call | bytes 22020096 | tf_op jit(solution)/shard_map/pallas_call | solution.py:58
  97.5 1.7 collective-permute-done.24.refs_3_
  100.1 2.4 %collective-permute-start.26 = (bf16[48,1024]{1,0:T(8,128)(2,1)S(1)}, bf16[48,1024]{1,0:T(8,128)(2,1)S(1)}, u32[]{:S(2)}, u32[]{:S(2)}) collective-permute-start(bf16[48,1024]{1,0:T(8,128)(2,1)S(1)} %get-tuple-element.108), channel_id=1, source_target_pairs={{0,2},{1,3},{2,0},{3,1},{4,6},{5,7},{6,4},{7,5},{8,10},{9,11},{10,... | collective-permute-start | bytes 294920 | tf_op jit(solution)/shard_map/ppermute | solution.py:24
  103.4 1.5 collective-permute-start.28
  104.9 1.2 collective-permute-start.29
  107.0 1.8 %collective-permute-done.29.refs_4_.refs_5_ = bf16[16,1024]{1,0:T(8,128)(2,1)S(1)} collective-permute-done((bf16[16,1024]{1,0:T(8,128)(2,1)S(1)}, bf16[16,1024]{1,0:T(8,128)(2,1)S(1)}, u32[]{:S(2)}, u32[]{:S(2)}) %collective-permute-start.29) | collective-permute-done | bytes 32800 | tf_op jit(solution)/shard_map/ppermute | solution.py:24
  108.8 1.5 collective-permute-start.31
  110.3 3.7 %shard_map.175 = (bf16[1024,1792]{1,0:T(8,128)(2,1)S(1)}, bf16[1024,1792]{1,0:T(8,128)(2,1)S(1)}) custom-call(s32[3]{0:T(128)S(1)} %pad_add_fusion.refs_0_, bf16[1,4096,1792]{2,1,0:T(8,128)(2,1)} %refs_5_.1, bf16[1,4096,1792]{2,1,0:T(8,128)(2,1)} %refs_6_.1, bf16[48,1024]{1,0:T(8,128)(2,1)S(1)} %get-tuple-element.107.refs_3_.refs_0_), custom_call_target="tpu_custom_call" | custom-call | bytes 7340032 | tf_op jit(solution)/shard_map/pallas_call | solution.py:58
  114.2 1.4 collective-permute-done.32.refs_4_
  116.0 1.5 collective-permute-start.33
  118.0 6.1 %shard_map.178 = (f32[192,1792]{1,0:T(8,128)S(1)}, f32[192,1792]{1,0:T(8,128)S(1)}, f32[192,128]{1,0:T(8,128)S(1)}, bf16[1792,1024]{1,0:T(8,128)(2,1)S(1)}, bf16...) custom-call(s32[3]{0:T(128)S(1)} %pad_add_fusion.refs_0_, ...), custom_call_target="tpu_custom_call" | custom-call | flops 1409286144 | bytes 7340032 | tf_op jit(solution)/shard_map/pallas_call | solution.py:58
  124.2 3.0 %collective-permute-done.33.refs_1_ = bf16[192,1024]{1,0:T(8,128)(2,1)S(1)} collective-permute-done((bf16[192,1024]{1,0:T(8,128)(2,1)S(1)}, bf16[192,1024]{1,0:T(8,128)(2,1)S(1)}, u32[]{:S(2)}, u32[]{:S(2)}) %collective-permute-start.33) | collective-permute-done | bytes 393248 | tf_op jit(solution)/shard_map/ppermute | solution.py:24
  127.2 1.2 collective-permute-start.34
  128.4 0.9 collective-permute-start.36
  129.3 2.2 %shard_map.179 = (f32[192,1792]{1,0:T(8,128)S(1)}, f32[192,1792]{1,0:T(8,128)S(1)}, f32[192,128]{1,0:T(8,128)S(1)}) custom-call(s32[3]{0:T(128)S(1)} %pad_add_fusion.refs_0_, bf16[192,1024]{1,0:T(8,128)(2,1)S(1)} %collective-permute-done.33.refs_1_, f32[1,4096]{1,0:T(1,128)S(1)} %bitcast.30, bf16[1024,1792]{1,0:T(8,128)(2,1)S(1)} %get-tuple-element.103.refs_12_.refs_3_, ...), custom_call_target="tpu_custom_call" | custom-call | flops 1409286144 | bytes 7340032 | tf_op jit(solution)/shard_map/pallas_call | solution.py:58
  131.6 2.2 %shard_map.180 = (f32[192,1792]{1,0:T(8,128)S(1)}, f32[192,1792]{1,0:T(8,128)S(1)}, f32[192,128]{1,0:T(8,128)S(1)}) custom-call(s32[3]{0:T(128)S(1)} %pad_add_fusion.refs_0_, bf16[192,1024]{1,0:T(8,128)(2,1)S(1)} %collective-permute-done.35.refs_1_, f32[1,4096]{1,0:T(1,128)S(1)} %bitcast.31, bf16[1024,1792]{1,0:T(8,128)(2,1)S(1)} %get-tuple-element.105.refs_14_.refs_3_, ...), custom_call_target="tpu_custom_call" | custom-call | flops 1409286144 | bytes 7340032 | tf_op jit(solution)/shard_map/pallas_call | solution.py:58
  134.3 2.3 %shard_map.181.refs_1_ = bf16[192,1792]{1,0:T(8,128)(2,1)S(1)} custom-call(s32[3]{0:T(128)S(1)} %pad_add_fusion.refs_0_, bf16[96,1024]{1,0:T(8,128)(2,1)S(1)} %collective-permute-done.34.refs_1_, bf16[96,1024]{1,0:T(8,128)(2,1)S(1)} %collective-permute-done.36.refs_2_, f32[1,4096]{1,0:T(1,128)S(1)} %bitcast.32, ...), custom_call_target="tpu_custom_call" | custom-call | flops 1409286144 | bytes 7340032 | tf_op jit(solution)/shard_map/pallas_call | solution.py:58
  136.7 3.7 %shard_map.182 = (bf16[48,4096]{1,0:T(8,128)(2,1)S(1)}, bf16[48,4096]{1,0:T(8,128)(2,1)S(1)}, bf16[48,4096]{1,0:T(8,128)(2,1)S(1)}, bf16[48,4096]{1,0:T(8,128)(2,1)S(1)}) custom-call(s32[3]{0:T(128)S(1)} %pad_add_fusion.refs_0_, bf16[192,1792]{1,0:T(8,128)(2,1)S(1)} %shard_map.181.refs_1_, bf16[1792,1024]{1,0:T(8,128)(2,1)S(1)} %get-tuple-element.119.refs_8_.refs_9_.refs_2_, ...), custom_call_target="tpu_custom_call" | custom-call | flops 2818572288 | bytes 14680064 | tf_op jit(solution)/shard_map/pallas_call | solution.py:58
  141.2 1.5 collective-permute-start.38
  142.8 1.1 collective-permute-start.39
  143.9 1.0 shard_map.183
  144.9 7.6 %collective-permute-done.37.refs_1_ = bf16[48,4096]{1,0:T(8,128)(2,1)S(1)} collective-permute-done((bf16[48,4096]{1,0:T(8,128)(2,1)S(1)}, bf16[48,4096]{1,0:T(8,128)(2,1)S(1)}, u32[]{:S(2)}, u32[]{:S(2)}) %collective-permute-start.37) | collective-permute-done | bytes 393248 | tf_op jit(solution)/shard_map/ppermute | solution.py:24
  152.4 5.2 %collective-permute-done.38.refs_2_ = bf16[48,4096]{1,0:T(8,128)(2,1)S(1)} collective-permute-done((bf16[48,4096]{1,0:T(8,128)(2,1)S(1)}, bf16[48,4096]{1,0:T(8,128)(2,1)S(1)}, u32[]{:S(2)}, u32[]{:S(2)}) %collective-permute-start.38) | collective-permute-done | bytes 393248 | tf_op jit(solution)/shard_map/ppermute | solution.py:24
  157.6 1.5 collective-permute-done.39.refs_3_
  159.6 1.1 collective-permute-start.40
  160.6 1.8 %collective-permute-start.41 = (bf16[48,1024]{1,0:T(8,128)(2,1)S(1)}, bf16[48,1024]{1,0:T(8,128)(2,1)S(1)}, u32[]{:S(2)}, u32[]{:S(2)}) collective-permute-start(bf16[48,1024]{1,0:T(8,128)(2,1)S(1)} %get-tuple-element.138), channel_id=1, source_target_pairs={{0,4},{1,5},{2,6},{3,7},{4,0},{5,1},{6,2},{7,3},{8,12},{9,13},{10,... | collective-permute-start | bytes 294920 | tf_op jit(solution)/shard_map/ppermute | solution.py:24
  162.4 1.6 collective-permute-start.42
  164.0 1.3 collective-permute-done.40.refs_1_
  165.3 3.8 %collective-permute-done.41.refs_2_ = bf16[48,1024]{1,0:T(8,128)(2,1)S(1)} collective-permute-done((bf16[48,1024]{1,0:T(8,128)(2,1)S(1)}, bf16[48,1024]{1,0:T(8,128)(2,1)S(1)}, u32[]{:S(2)}, u32[]{:S(2)}) %collective-permute-start.41) | collective-permute-done | bytes 98336 | tf_op jit(solution)/shard_map/ppermute | solution.py:24
  169.2 1.4 collective-permute-done.43.refs_4_
  170.6 1.3 shard_map.186
  (92 shorter events, 13.9 us)
Async XLA Ops:
  0.1 1.2 copy-start.2
  1.3 0.7 copy-start.7
  3.0 10.2 %collective-permute-start = (bf16[128,512]{1,0:T(8,128)(2,1)S(1)}, bf16[128,512]{1,0:T(8,128)(2,1)S(1)}, u32[]{:S(2)}, u32[]{:S(2)}) collective-permute-start(bf16[128,512]{1,0:T(8,128)(2,1)S(1)} %get-tuple-element.75), channel_id=1, source_target_pairs={{0,8},{8,0},{16,24},{24,16},{1,9},{9,1},{17,25},{25,17},{2,10},{10... | collective-permute-start | bytes 393224 | tf_op jit(solution)/shard_map/ppermute | solution.py:24
  6.0 7.8 %collective-permute-start.1 = (bf16[128,512]{1,0:T(8,128)(2,1)S(1)}, bf16[128,512]{1,0:T(8,128)(2,1)S(1)}, u32[]{:S(2)}, u32[]{:S(2)}) collective-permute-start(bf16[128,512]{1,0:T(8,128)(2,1)S(1)} %get-tuple-element.76), channel_id=1, source_target_pairs={{0,16},{8,24},{16,0},{24,8},{1,17},{9,25},{17,1},{25,9},{2,18},{10... | collective-permute-start | bytes 393224 | tf_op jit(solution)/shard_map/ppermute | solution.py:24
  7.5 6.3 %collective-permute-start.2 = (bf16[128,512]{1,0:T(8,128)(2,1)S(1)}, bf16[128,512]{1,0:T(8,128)(2,1)S(1)}, u32[]{:S(2)}, u32[]{:S(2)}) collective-permute-start(bf16[128,512]{1,0:T(8,128)(2,1)S(1)} %get-tuple-element.77), channel_id=1, source_target_pairs={{0,24},{8,16},{16,8},{24,0},{1,25},{9,17},{17,9},{25,1},{2,26},{10... | collective-permute-start | bytes 393224 | tf_op jit(solution)/shard_map/ppermute | solution.py:24
  7.5 5.6 %copy-start.14 = (s32[16,2]{0,1:T(2,128)S(1)}, s32[16,2]{0,1:T(2,128)}, u32[]{:S(2)}) copy-start(s32[16,2]{0,1:T(2,128)} %param.30) | copy-start | bytes 388
  13.8 1.4 collective-permute-start.3
  13.9 1.5 collective-permute-start.4
  14.4 1.3 collective-permute-start.5
  18.9 16.7 %copy-start.3 = (bf16[1024,288]{0,1:T(8,128)(2,1)S(1)}, bf16[1024,288]{0,1:T(8,128)(2,1)}, u32[]{:S(2)}) copy-start(bf16[1024,288]{0,1:T(8,128)(2,1)} %param.22) | copy-start | bytes 1769476
  18.9 16.7 %copy-start.8 = (f32[4,1024]{1,0:T(4,128)S(1)}, f32[4,1024]{1,0:T(4,128)}, u32[]{:S(2)}) copy-start(f32[4,1024]{1,0:T(4,128)} %refs_4_.2) | copy-start | bytes 49156
  19.0 16.7 %copy-start.9 = (f32[1024]{0:T(1024)S(1)}, f32[1024]{0:T(1024)}, u32[]{:S(2)}) copy-start(f32[1024]{0:T(1024)} %param.21) | copy-start | bytes 12292
  19.0 9.2 %collective-permute-start.7 = (bf16[144,1024]{1,0:T(8,128)(2,1)S(1)}, bf16[144,1024]{1,0:T(8,128)(2,1)S(1)}, u32[]{:S(2)}, u32[]{:S(2)}) collective-permute-start(bf16[144,1024]{1,0:T(8,128)(2,1)S(1)} %get-tuple-element.83), channel_id=1, source_target_pairs={{0,16},{8,24},{16,0},{24,8},{1,17},{9,25},{17,1},{25,9},{2,18},{10... | collective-permute-start | bytes 884744 | tf_op jit(solution)/shard_map/ppermute | solution.py:24
  20.5 10.8 %collective-permute-start.6 = (bf16[144,1024]{1,0:T(8,128)(2,1)S(1)}, bf16[144,1024]{1,0:T(8,128)(2,1)S(1)}, u32[]{:S(2)}, u32[]{:S(2)}) collective-permute-start(bf16[144,1024]{1,0:T(8,128)(2,1)S(1)} %get-tuple-element.82), channel_id=1, source_target_pairs={{0,8},{8,0},{16,24},{24,16},{1,9},{9,1},{17,25},{25,17},{2,10},{10... | collective-permute-start | bytes 884744 | tf_op jit(solution)/shard_map/ppermute | solution.py:24
  21.9 13.7 %collective-permute-start.8 = (bf16[144,1024]{1,0:T(8,128)(2,1)S(1)}, bf16[144,1024]{1,0:T(8,128)(2,1)S(1)}, u32[]{:S(2)}, u32[]{:S(2)}) collective-permute-start(bf16[144,1024]{1,0:T(8,128)(2,1)S(1)} %get-tuple-element.84), channel_id=1, source_target_pairs={{0,24},{8,16},{16,8},{24,0},{1,25},{9,17},{17,9},{25,1},{2,26},{10... | collective-permute-start | bytes 884744 | tf_op jit(solution)/shard_map/ppermute | solution.py:24
  23.4 19.0 %copy-start.13 = (f32[1024,16]{0,1:T(8,128)S(1)}, f32[1024,16]{0,1:T(8,128)}, u32[]{:S(2)}) copy-start(f32[1024,16]{0,1:T(8,128)} %param.25) | copy-start | bytes 196612
  31.3 19.1 %copy-start.4 = (bf16[256,1024]{1,0:T(8,128)(2,1)S(1)}, bf16[256,1024]{1,0:T(8,128)(2,1)}, u32[]{:S(2)}) copy-start(bf16[256,1024]{1,0:T(8,128)(2,1)} %refs_3_.1) | copy-start | bytes 1572868
  31.3 19.1 %copy-start.10 = (f32[1024]{0:T(1024)S(1)}, f32[1024]{0:T(1024)}, u32[]{:S(2)}) copy-start(f32[1024]{0:T(1024)} %param.24) | copy-start | bytes 12292
  31.3 33.4 %copy-start.11 = (f32[1024]{0:T(1024)S(1)}, f32[1024]{0:T(1024)}, u32[]{:S(2)}) copy-start(f32[1024]{0:T(1024)} %param.26) | copy-start | bytes 12292
  36.5 44.5 %copy-start.12 = (bf16[1024,1024]{1,0:T(8,128)(2,1)S(1)}, bf16[1024,1024]{1,0:T(8,128)(2,1)}, u32[]{:S(2)}) copy-start(bf16[1024,1024]{1,0:T(8,128)(2,1)} %refs_4_.3) | copy-start | bytes 6291460
  36.5 1.5 collective-permute-start.9
  38.0 7.5 %collective-permute-start.10 = (bf16[128,288]{1,0:T(8,128)(2,1)S(1)}, bf16[128,288]{1,0:T(8,128)(2,1)S(1)}, u32[]{:S(2)}, u32[]{:S(2)}) collective-permute-start(bf16[128,288]{1,0:T(8,128)(2,1)S(1)} %get-tuple-element.143), channel_id=1, source_target_pairs={{0,2},{1,3},{2,0},{3,1},{4,6},{5,7},{6,4},{7,5},{8,10},{9,11},{10,... | collective-permute-start | bytes 221192 | tf_op jit(solution)/shard_map/ppermute | solution.py:24
  39.7 10.7 %collective-permute-start.11 = (bf16[128,288]{1,0:T(8,128)(2,1)S(1)}, bf16[128,288]{1,0:T(8,128)(2,1)S(1)}, u32[]{:S(2)}, u32[]{:S(2)}) collective-permute-start(bf16[128,288]{1,0:T(8,128)(2,1)S(1)} %get-tuple-element.143), channel_id=1, source_target_pairs={{0,4},{1,5},{2,6},{3,7},{4,0},{5,1},{6,2},{7,3},{8,12},{9,13},{10,... | collective-permute-start | bytes 221192 | tf_op jit(solution)/shard_map/ppermute | solution.py:24
  42.3 8.1 %collective-permute-start.12 = (bf16[128,288]{1,0:T(8,128)(2,1)S(1)}, bf16[128,288]{1,0:T(8,128)(2,1)S(1)}, u32[]{:S(2)}, u32[]{:S(2)}) collective-permute-start(bf16[128,288]{1,0:T(8,128)(2,1)S(1)} %get-tuple-element.143), channel_id=1, source_target_pairs={{0,6},{1,7},{2,4},{3,5},{4,2},{5,3},{6,0},{7,1},{8,14},{9,15},{10,... | collective-permute-start | bytes 221192 | tf_op jit(solution)/shard_map/ppermute | solution.py:24
  42.5 22.2 %collective-permute-start.16 = (bf16[144,1024]{1,0:T(8,128)(2,1)S(1)}, bf16[144,1024]{1,0:T(8,128)(2,1)S(1)}, u32[]{:S(2)}, u32[]{:S(2)}) collective-permute-start(bf16[144,1024]{1,0:T(8,128)(2,1)S(1)} %get-tuple-element.91), channel_id=1, source_target_pairs={{0,8},{8,0},{16,24},{24,16},{1,9},{9,1},{17,25},{25,17},{2,10},{10... | collective-permute-start | bytes 884744 | tf_op jit(solution)/shard_map/ppermute | solution.py:24
  44.0 20.8 %collective-permute-start.17 = (bf16[144,1024]{1,0:T(8,128)(2,1)S(1)}, bf16[144,1024]{1,0:T(8,128)(2,1)S(1)}, u32[]{:S(2)}, u32[]{:S(2)}) collective-permute-start(bf16[144,1024]{1,0:T(8,128)(2,1)S(1)} %get-tuple-element.92), channel_id=1, source_target_pairs={{0,16},{8,24},{16,0},{24,8},{1,17},{9,25},{17,1},{25,9},{2,18},{10... | collective-permute-start | bytes 884744 | tf_op jit(solution)/shard_map/ppermute | solution.py:24
  45.5 19.2 %collective-permute-start.18 = (bf16[144,1024]{1,0:T(8,128)(2,1)S(1)}, bf16[144,1024]{1,0:T(8,128)(2,1)S(1)}, u32[]{:S(2)}, u32[]{:S(2)}) collective-permute-start(bf16[144,1024]{1,0:T(8,128)(2,1)S(1)} %get-tuple-element.93), channel_id=1, source_target_pairs={{0,24},{8,16},{16,8},{24,0},{1,25},{9,17},{17,9},{25,1},{2,26},{10... | collective-permute-start | bytes 884744 | tf_op jit(solution)/shard_map/ppermute | solution.py:24
  55.8 4.0 %collective-permute-start.13 = (bf16[18,8,128]{2,1,0:T(8,128)(2,1)S(1)}, bf16[18,8,128]{2,1,0:T(8,128)(2,1)S(1)}, u32[]{:S(2)}, u32[]{:S(2)}) collective-permute-start(bf16[18,8,128]{2,1,0:T(8,128)(2,1)S(1)} %get-tuple-element.88), channel_id=1, source_target_pairs={{0,8},{8,0},{16,24},{24,16},{1,9},{9,1},{17,25},{25,17},{2,10},{10... | collective-permute-start | bytes 110600 | tf_op jit(solution)/shard_map/ppermute | solution.py:24
  57.3 4.9 %collective-permute-start.14 = (bf16[18,8,128]{2,1,0:T(8,128)(2,1)S(1)}, bf16[18,8,128]{2,1,0:T(8,128)(2,1)S(1)}, u32[]{:S(2)}, u32[]{:S(2)}) collective-permute-start(bf16[18,8,128]{2,1,0:T(8,128)(2,1)S(1)} %get-tuple-element.88), channel_id=1, source_target_pairs={{0,16},{8,24},{16,0},{24,8},{1,17},{9,25},{17,1},{25,9},{2,18},{10... | collective-permute-start | bytes 110600 | tf_op jit(solution)/shard_map/ppermute | solution.py:24
  59.9 4.9 %collective-permute-start.15 = (bf16[18,8,128]{2,1,0:T(8,128)(2,1)S(1)}, bf16[18,8,128]{2,1,0:T(8,128)(2,1)S(1)}, u32[]{:S(2)}, u32[]{:S(2)}) collective-permute-start(bf16[18,8,128]{2,1,0:T(8,128)(2,1)S(1)} %get-tuple-element.88), channel_id=1, source_target_pairs={{0,24},{8,16},{16,8},{24,0},{1,25},{9,17},{17,9},{25,1},{2,26},{10... | collective-permute-start | bytes 110600 | tf_op jit(solution)/shard_map/ppermute | solution.py:24
  69.2 7.9 %collective-permute-start.19 = (bf16[128,1024]{1,0:T(8,128)(2,1)S(1)}, bf16[128,1024]{1,0:T(8,128)(2,1)S(1)}, u32[]{:S(2)}, u32[]{:S(2)}) collective-permute-start(bf16[128,1024]{1,0:T(8,128)(2,1)S(1)} %shard_map.169.refs_0_), channel_id=1, source_target_pairs={{0,8},{8,0},{16,24},{24,16},{1,9},{9,1},{17,25},{25,17},{2,10},{10... | collective-permute-start | bytes 786440 | tf_op jit(solution)/shard_map/ppermute | solution.py:24
  70.7 10.3 %collective-permute-start.20 = (bf16[128,1024]{1,0:T(8,128)(2,1)S(1)}, bf16[128,1024]{1,0:T(8,128)(2,1)S(1)}, u32[]{:S(2)}, u32[]{:S(2)}) collective-permute-start(bf16[128,1024]{1,0:T(8,128)(2,1)S(1)} %shard_map.169.refs_0_), channel_id=1, source_target_pairs={{0,16},{8,24},{16,0},{24,8},{1,17},{9,25},{17,1},{25,9},{2,18},{10... | collective-permute-start | bytes 786440 | tf_op jit(solution)/shard_map/ppermute | solution.py:24
  72.2 8.8 %collective-permute-start.21 = (bf16[128,1024]{1,0:T(8,128)(2,1)S(1)}, bf16[128,1024]{1,0:T(8,128)(2,1)S(1)}, u32[]{:S(2)}, u32[]{:S(2)}) collective-permute-start(bf16[128,1024]{1,0:T(8,128)(2,1)S(1)} %shard_map.169.refs_0_), channel_id=1, source_target_pairs={{0,24},{8,16},{16,8},{24,0},{1,25},{9,17},{17,9},{25,1},{2,26},{10... | collective-permute-start | bytes 786440 | tf_op jit(solution)/shard_map/ppermute | solution.py:24
  82.3 2.0 %collective-permute-start.22 = (bf16[4,64,1024]{2,1,0:T(8,128)(2,1)S(1)}, bf16[4,64,1024]{2,1,0:T(8,128)(2,1)S(1)}, u32[]{:S(2)}, u32[]{:S(2)}) collective-permute-start(bf16[4,64,1024]{2,1,0:T(8,128)(2,1)S(1)} %get-tuple-element.95), channel_id=1, source_target_pairs={{0,1},{1,0},{2,3},{3,2},{4,5},{5,4},{6,7},{7,6},{8,9},{9,8},{10,11... | collective-permute-start | bytes 1572872 | tf_op jit(solution)/shard_map/ppermute | solution.py:24
  84.4 13.1 %collective-permute-start.23 = (bf16[64,1024]{1,0:T(8,128)(2,1)S(1)}, bf16[64,1024]{1,0:T(8,128)(2,1)S(1)}, u32[]{:S(2)}, u32[]{:S(2)}) collective-permute-start(bf16[64,1024]{1,0:T(8,128)(2,1)S(1)} %get-tuple-element.97), channel_id=1, source_target_pairs={{0,2},{1,3},{2,0},{3,1},{4,6},{5,7},{6,4},{7,5},{8,10},{9,11},{10,... | collective-permute-start | bytes 393224 | tf_op jit(solution)/shard_map/ppermute | solution.py:24
  86.3 12.9 %collective-permute-start.24 = (bf16[64,1024]{1,0:T(8,128)(2,1)S(1)}, bf16[64,1024]{1,0:T(8,128)(2,1)S(1)}, u32[]{:S(2)}, u32[]{:S(2)}) collective-permute-start(bf16[64,1024]{1,0:T(8,128)(2,1)S(1)} %get-tuple-element.98), channel_id=1, source_target_pairs={{0,4},{1,5},{2,6},{3,7},{4,0},{5,1},{6,2},{7,3},{8,12},{9,13},{10,... | collective-permute-start | bytes 393224 | tf_op jit(solution)/shard_map/ppermute | solution.py:24
  87.3 11.9 %collective-permute-start.25 = (bf16[64,1024]{1,0:T(8,128)(2,1)S(1)}, bf16[64,1024]{1,0:T(8,128)(2,1)S(1)}, u32[]{:S(2)}, u32[]{:S(2)}) collective-permute-start(bf16[64,1024]{1,0:T(8,128)(2,1)S(1)} %get-tuple-element.99), channel_id=1, source_target_pairs={{0,6},{1,7},{2,4},{3,5},{4,2},{5,3},{6,0},{7,1},{8,14},{9,15},{10,... | collective-permute-start | bytes 393224 | tf_op jit(solution)/shard_map/ppermute | solution.py:24
  97.5 2.6 %copy-start = (bf16[1024,1792]{1,0:T(8,128)(2,1)}, bf16[1024,1792]{1,0:T(8,128)(2,1)S(1)}, u32[]{:S(2)}) copy-start(bf16[1024,1792]{1,0:T(8,128)(2,1)S(1)} %get-tuple-element.104.refs_13_.refs_4_) | copy-start | bytes 11010052
  100.1 14.0 %collective-permute-start.26 = (bf16[48,1024]{1,0:T(8,128)(2,1)S(1)}, bf16[48,1024]{1,0:T(8,128)(2,1)S(1)}, u32[]{:S(2)}, u32[]{:S(2)}) collective-permute-start(bf16[48,1024]{1,0:T(8,128)(2,1)S(1)} %get-tuple-element.108), channel_id=1, source_target_pairs={{0,2},{1,3},{2,0},{3,1},{4,6},{5,7},{6,4},{7,5},{8,10},{9,11},{10,... | collective-permute-start | bytes 294920 | tf_op jit(solution)/shard_map/ppermute | solution.py:24
  102.4 11.6 %collective-permute-start.27 = (bf16[48,1024]{1,0:T(8,128)(2,1)S(1)}, bf16[48,1024]{1,0:T(8,128)(2,1)S(1)}, u32[]{:S(2)}, u32[]{:S(2)}) collective-permute-start(bf16[48,1024]{1,0:T(8,128)(2,1)S(1)} %get-tuple-element.109), channel_id=1, source_target_pairs={{0,4},{1,5},{2,6},{3,7},{4,0},{5,1},{6,2},{7,3},{8,12},{9,13},{10,... | collective-permute-start | bytes 294920 | tf_op jit(solution)/shard_map/ppermute | solution.py:24
  103.4 10.7 %collective-permute-start.28 = (bf16[48,1024]{1,0:T(8,128)(2,1)S(1)}, bf16[48,1024]{1,0:T(8,128)(2,1)S(1)}, u32[]{:S(2)}, u32[]{:S(2)}) collective-permute-start(bf16[48,1024]{1,0:T(8,128)(2,1)S(1)} %get-tuple-element.110), channel_id=1, source_target_pairs={{0,6},{1,7},{2,4},{3,5},{4,2},{5,3},{6,0},{7,1},{8,14},{9,15},{10,... | collective-permute-start | bytes 294920 | tf_op jit(solution)/shard_map/ppermute | solution.py:24
  104.9 3.9 %collective-permute-start.29 = (bf16[16,1024]{1,0:T(8,128)(2,1)S(1)}, bf16[16,1024]{1,0:T(8,128)(2,1)S(1)}, u32[]{:S(2)}, u32[]{:S(2)}) collective-permute-start(bf16[16,1024]{1,0:T(8,128)(2,1)S(1)} %get-tuple-element.111), channel_id=1, source_target_pairs={{0,8},{8,0},{16,24},{24,16},{1,9},{9,1},{17,25},{25,17},{2,10},{10... | collective-permute-start | bytes 98312 | tf_op jit(solution)/shard_map/ppermute | solution.py:24
  106.0 8.0 %collective-permute-start.30 = (bf16[16,1024]{1,0:T(8,128)(2,1)S(1)}, bf16[16,1024]{1,0:T(8,128)(2,1)S(1)}, u32[]{:S(2)}, u32[]{:S(2)}) collective-permute-start(bf16[16,1024]{1,0:T(8,128)(2,1)S(1)} %get-tuple-element.112), channel_id=1, source_target_pairs={{0,16},{8,24},{16,0},{24,8},{1,17},{9,25},{17,1},{25,9},{2,18},{10... | collective-permute-start | bytes 98312 | tf_op jit(solution)/shard_map/ppermute | solution.py:24
  108.8 5.3 %collective-permute-start.31 = (bf16[16,1024]{1,0:T(8,128)(2,1)S(1)}, bf16[16,1024]{1,0:T(8,128)(2,1)S(1)}, u32[]{:S(2)}, u32[]{:S(2)}) collective-permute-start(bf16[16,1024]{1,0:T(8,128)(2,1)S(1)} %get-tuple-element.113), channel_id=1, source_target_pairs={{0,24},{8,16},{16,8},{24,0},{1,25},{9,17},{17,9},{25,1},{2,26},{10... | collective-permute-start | bytes 98312 | tf_op jit(solution)/shard_map/ppermute | solution.py:24
  114.1 3.9 %copy-start.5 = (f32[4096]{0:T(1024)S(1)}, f32[4096]{0:T(1024)}, u32[]{:S(2)}) copy-start(f32[4096]{0:T(1024)} %param.28) | copy-start | bytes 49156
  114.1 1.5 collective-permute-start.32
  116.0 11.2 %collective-permute-start.33 = (bf16[192,1024]{1,0:T(8,128)(2,1)S(1)}, bf16[192,1024]{1,0:T(8,128)(2,1)S(1)}, u32[]{:S(2)}, u32[]{:S(2)}) collective-permute-start(bf16[192,1024]{1,0:T(8,128)(2,1)S(1)} %shard_map.177.refs_1_), channel_id=1, source_target_pairs={{0,8},{8,0},{16,24},{24,16},{1,9},{9,1},{17,25},{25,17},{2,10},{10... | collective-permute-start | bytes 1179656 | tf_op jit(solution)/shard_map/ppermute | solution.py:24
  117.5 10.9 %collective-permute-start.35 = (bf16[192,1024]{1,0:T(8,128)(2,1)S(1)}, bf16[192,1024]{1,0:T(8,128)(2,1)S(1)}, u32[]{:S(2)}, u32[]{:S(2)}) collective-permute-start(bf16[192,1024]{1,0:T(8,128)(2,1)S(1)} %shard_map.177.refs_1_), channel_id=1, source_target_pairs={{0,16},{8,24},{16,0},{24,8},{1,17},{9,25},{17,1},{25,9},{2,18},{10... | collective-permute-start | bytes 1179656 | tf_op jit(solution)/shard_map/ppermute | solution.py:24
  118.0 11.3 %copy-start.1 = (bf16[1024,1792]{1,0:T(8,128)(2,1)S(1)}, bf16[1024,1792]{1,0:T(8,128)(2,1)}, u32[]{:S(2)}) copy-start(bf16[1024,1792]{1,0:T(8,128)(2,1)} %copy-done) | copy-start | bytes 11010052
  127.2 6.6 %collective-permute-start.34 = (bf16[96,1024]{1,0:T(8,128)(2,1)S(1)}, bf16[96,1024]{1,0:T(8,128)(2,1)S(1)}, u32[]{:S(2)}, u32[]{:S(2)}) collective-permute-start(bf16[96,1024]{1,0:T(8,128)(2,1)S(1)} %slice.19), channel_id=1, source_target_pairs={{0,16},{8,24},{16,0},{24,8},{1,17},{9,25},{17,1},{25,9},{2,18},{10... | collective-permute-start | bytes 589832 | tf_op jit(solution)/shard_map/ppermute | solution.py:24
  128.4 5.9 %collective-permute-start.36 = (bf16[96,1024]{1,0:T(8,128)(2,1)S(1)}, bf16[96,1024]{1,0:T(8,128)(2,1)S(1)}, u32[]{:S(2)}, u32[]{:S(2)}) collective-permute-start(bf16[96,1024]{1,0:T(8,128)(2,1)S(1)} %slice.20), channel_id=1, source_target_pairs={{0,8},{8,0},{16,24},{24,16},{1,9},{9,1},{17,25},{25,17},{2,10},{10... | collective-permute-start | bytes 589832 | tf_op jit(solution)/shard_map/ppermute | solution.py:24
  136.6 7.2 %copy-start.6 = (bf16[4096,8]{0,1:T(8,128)(2,1)S(1)}, bf16[4096,8]{0,1:T(8,128)(2,1)}, u32[]{:S(2)}) copy-start(bf16[4096,8]{0,1:T(8,128)(2,1)} %param.29) | copy-start | bytes 196612
  140.3 12.1 %collective-permute-start.37 = (bf16[48,4096]{1,0:T(8,128)(2,1)S(1)}, bf16[48,4096]{1,0:T(8,128)(2,1)S(1)}, u32[]{:S(2)}, u32[]{:S(2)}) collective-permute-start(bf16[48,4096]{1,0:T(8,128)(2,1)S(1)} %get-tuple-element.130), channel_id=1, source_target_pairs={{0,8},{8,0},{16,24},{24,16},{1,9},{9,1},{17,25},{25,17},{2,10},{10... | collective-permute-start | bytes 1179656 | tf_op jit(solution)/shard_map/ppermute | solution.py:24
  141.2 16.3 %collective-permute-start.38 = (bf16[48,4096]{1,0:T(8,128)(2,1)S(1)}, bf16[48,4096]{1,0:T(8,128)(2,1)S(1)}, u32[]{:S(2)}, u32[]{:S(2)}) collective-permute-start(bf16[48,4096]{1,0:T(8,128)(2,1)S(1)} %get-tuple-element.131), channel_id=1, source_target_pairs={{0,16},{8,24},{16,0},{24,8},{1,17},{9,25},{17,1},{25,9},{2,18},{10... | collective-permute-start | bytes 1179656 | tf_op jit(solution)/shard_map/ppermute | solution.py:24
  142.8 16.3 %collective-permute-start.39 = (bf16[48,4096]{1,0:T(8,128)(2,1)S(1)}, bf16[48,4096]{1,0:T(8,128)(2,1)S(1)}, u32[]{:S(2)}, u32[]{:S(2)}) collective-permute-start(bf16[48,4096]{1,0:T(8,128)(2,1)S(1)} %get-tuple-element.132), channel_id=1, source_target_pairs={{0,24},{8,16},{16,8},{24,0},{1,25},{9,17},{17,9},{25,1},{2,26},{10... | collective-permute-start | bytes 1179656 | tf_op jit(solution)/shard_map/ppermute | solution.py:24
  159.6 5.7 %collective-permute-start.40 = (bf16[48,1024]{1,0:T(8,128)(2,1)S(1)}, bf16[48,1024]{1,0:T(8,128)(2,1)S(1)}, u32[]{:S(2)}, u32[]{:S(2)}) collective-permute-start(bf16[48,1024]{1,0:T(8,128)(2,1)S(1)} %get-tuple-element.137), channel_id=1, source_target_pairs={{0,2},{1,3},{2,0},{3,1},{4,6},{5,7},{6,4},{7,5},{8,10},{9,11},{10,... | collective-permute-start | bytes 294920 | tf_op jit(solution)/shard_map/ppermute | solution.py:24
  160.6 8.4 %collective-permute-start.41 = (bf16[48,1024]{1,0:T(8,128)(2,1)S(1)}, bf16[48,1024]{1,0:T(8,128)(2,1)S(1)}, u32[]{:S(2)}, u32[]{:S(2)}) collective-permute-start(bf16[48,1024]{1,0:T(8,128)(2,1)S(1)} %get-tuple-element.138), channel_id=1, source_target_pairs={{0,4},{1,5},{2,6},{3,7},{4,0},{5,1},{6,2},{7,3},{8,12},{9,13},{10,... | collective-permute-start | bytes 294920 | tf_op jit(solution)/shard_map/ppermute | solution.py:24
  162.4 6.7 %collective-permute-start.42 = (bf16[48,1024]{1,0:T(8,128)(2,1)S(1)}, bf16[48,1024]{1,0:T(8,128)(2,1)S(1)}, u32[]{:S(2)}, u32[]{:S(2)}) collective-permute-start(bf16[48,1024]{1,0:T(8,128)(2,1)S(1)} %get-tuple-element.139), channel_id=1, source_target_pairs={{0,6},{1,7},{2,4},{3,5},{4,2},{5,3},{6,0},{7,1},{8,14},{9,15},{10,... | collective-permute-start | bytes 294920 | tf_op jit(solution)/shard_map/ppermute | solution.py:24
  169.1 1.5 collective-permute-start.43

commit v5 on v4

--- a/solution.py
+++ b/solution.py
@@ -109,22 +109,28 @@
         yield dot(left[...], near) + dot(right[...], far)
 
 
-def mixer_project_body(seq, place, *refs):
+def mixer_project_body(seq, cuts, place, *refs):
     own, mine, other = refs[0], refs[1:seq], refs[seq : 2 * seq - 1]
     refs = refs[2 * seq - 1 :]
-    (weight, routes), outs, (tails, held, sems) = refs[:2], refs[2 : seq + 2], refs[seq + 2 :]
+    (weight, routes), outs, (tails, held, sems) = refs[:2], refs[2:-3], refs[-3:]
     me = place[0]
     length = own.shape[0]
-    for index, product in enumerate(project(place[1], own, mine, other, weight, 0, held, sems)):
-        outs[index][HALO:, :] = product.astype(outs[index].dtype)
-        tails[index] = product[length - HALO :, :]
+
+    def store(mask, rows, values):
+        for (number, index), out in zip(cuts, outs):
+            if number == mask:
+                columns = out.shape[1]
+                out[rows, :] = values[:, index * columns : (index + 1) * columns].astype(out.dtype)
+
+    for mask, product in enumerate(project(place[1], own, mine, other, weight, 0, held, sems)):
+        store(mask, slice(HALO, HALO + length), product)
+        tails[mask] = product[length - HALO :, :]
     for mask in range(seq):
         shard = me ^ mask
         source = me ^ jnp.maximum(shard - 1, 0)
         before = jnp.where(shard > 0, tails[source], 0.0)
         row = lax.broadcasted_iota(jnp.int32, before.shape, 0)
-        before = jnp.where(row < ROUTE_ROWS, routes[mask], before)
-        outs[mask][:HALO, :] = before.astype(outs[mask].dtype)
+        store(mask, slice(0, HALO), jnp.where(row < ROUTE_ROWS, routes[mask], before))
 
 
 def gate_project_body(seq, place, *refs):
@@ -143,12 +149,13 @@
             outs[index][length:, :] = rows
 
 
-def conv_body(seq, *refs):
-    terms = refs[:seq]
-    taps, bias, proj, activated, features = refs[seq:]
-    total = terms[0][...]
-    for term in terms[1:]:
-        total = total + term[...].astype(F32)
+def conv_body(places, *refs):
+    own, terms = refs[0], refs[1 : 1 + len(places)]
+    taps, bias, proj, activated, features = refs[1 + len(places) :]
+    columns = [own[:, i * terms[0].shape[1] : (i + 1) * terms[0].shape[1]] for i in range(max(places) + 1)]
+    for index, term in zip(places, terms):
+        columns[index] = columns[index] + term[...].astype(F32)
+    total = jnp.concatenate(columns, axis=1)
     padded = total.astype(BF16).astype(F32)
     length = activated.shape[0]
     count = taps.shape[0]
@@ -158,9 +165,18 @@
         convolved = convolved + taps[tap : tap + 1, :] * padded[start : start + length]
     rounded = silu(convolved).astype(BF16)
     activated[...] = rounded
-    features[...] = lax.dot_general(
-        rounded, proj[...], (((1,), (1,)), ((), ())), preferred_element_type=F32
-    )
+    rank = features.shape[1]
+    states = (proj.shape[0] - rank) // 2
+
+    def both_last(one, other):
+        return lax.dot_general(one, other, (((1,), (1,)), ((), ())), preferred_element_type=F32)
+
+    features[:length, :] = both_last(rounded, proj[:rank, :])
+    maps = both_last(proj[rank:, :], rounded)
+    below = jnp.zeros((features.shape[0] - length, rank), F32)
+    features[length:, :] = below
+    for i in range(2):
+        features[length:, i * length : (i + 1) * length] = maps[i * states : (i + 1) * states]
 
 
 def scan_body(maps, low_rank, activated, step_weight, step_bias, rate, y, cumulated, final, steps, drive):
@@ -182,8 +198,8 @@
         fresh = []
         out = jnp.zeros_like(step)
         for n in range(states):
-            value = jnp.exp2(step * rates[n]) * state[n] + push * maps[t, n]
-            out = out + value * maps[t, states + n]
+            value = jnp.exp2(step * rates[n]) * state[n] + push * maps[n, t]
+            out = out + value * maps[n, length + t]
             fresh.append(value)
         y[t] = out
         cumulated[t] = running
@@ -225,7 +241,7 @@
         steps = cumulated[t]
         out = y[t]
         for n in range(states):
-            out = out + (jnp.exp2(steps * rates[n]) * incoming[n]) * maps[t, states + n]
+            out = out + (jnp.exp2(steps * rates[n]) * incoming[n]) * maps[n, length + t]
         scanned[t] = out
         return carry
 
@@ -267,8 +283,7 @@
 
 
 def tables_body(seq, own_rows, most_slots, place, routes, *refs):
-    terms, outs = refs[: seq - 1], refs[seq - 1 :]
-    choose, first, second, named = outs
+    terms, (choose, first, second, named) = refs[:-4], refs[-4:]
     slots, window = choose.shape
     near = routes[:8, :window]
     for term in terms:
@@ -426,7 +441,7 @@
     return results[: len(outs)], results[len(outs) :]
 
 
-def down_body(seq, place, hidden, *refs):
+def down_body(seq, cuts, place, hidden, *refs):
     downs, outs, product = refs[:seq], refs[seq:-1], refs[-1]
     width = downs[0].shape[1]
     tile = tile_of(width, 512)
@@ -435,20 +450,30 @@
             part = slice(step * tile, (step + 1) * tile)
             to = slice(block * width + step * tile, block * width + (step + 1) * tile)
             product[:, to] = dot(hidden[...], down[:, part]).astype(BF16)
-    for mask, out in enumerate(outs):
-        rows = out.shape[0]
-        out[...] = product[pl.ds(pl.multiple_of((place[0] ^ mask) * rows, 16), rows), :]
-
-
-def expert_sum_body(seq, groups, most_slots, *refs):
-    terms, outs = refs[:seq], refs[seq:]
-    total = terms[0][...].astype(F32)
-    for term in terms[1:]:
-        total = total + term[...].astype(F32)
-    rounded = total.astype(BF16)
+    for (mask, index), out in zip(cuts, outs):
+        rows, columns = out.shape
+        start = pl.multiple_of((place[0] ^ mask) * rows, 16)
+        out[...] = product[pl.ds(start, rows), index * columns : (index + 1) * columns]
+
+
+def pair_sum_body(*refs):
+    count = len(refs) // 3
+    for one, other, out in zip(refs[:count], refs[count : 2 * count], refs[2 * count :]):
+        out[...] = (one[...].astype(F32) + other[...].astype(F32)).astype(BF16)
+
+
+def expert_sum_body(seq, groups, most_slots, places, *refs):
+    own, terms, outs = refs[0], refs[1 : 1 + len(places)], refs[1 + len(places) :]
     width = outs[0].shape[1]
-    pieces = jnp.concatenate([rounded[:, q * width : (q + 1) * width] for q in range(seq)], axis=0)
-    pieces = reordered(pieces, groups, seq, most_slots)
+    pieces = []
+    for q in range(seq):
+        total = own[:, q * width : (q + 1) * width].astype(F32)
+        for index, term in zip(places, terms):
+            start = q * width - index * term.shape[1]
+            if 0 <= start < term.shape[1]:
+                total = total + term[:, start : start + width].astype(F32)
+        pieces.append(total.astype(BF16))
+    pieces = reordered(jnp.concatenate(pieces, axis=0), groups, seq, most_slots)
     rows = pieces.shape[0] // len(outs)
     for w, out in enumerate(outs):
         out[...] = pieces[w * rows : (w + 1) * rows]
@@ -523,6 +548,28 @@
         part = slice(q * width, (q + 1) * width)
         sent = first_share * rows_of(first) + (1.0 - first_share) * rows_of(second)
         out[:, part] = (rows[:, part] + sent).astype(BF16)
+
+
+halved = [(0, 0), (1, 0), (1, 1), (2, 0), (2, 1), (3, 0), (3, 1)]
+
+
+def scattered(sends, masks, deps=()):
+    if len(masks) != 3:
+        terms = [partner(block, "seq", mask) for mask, block in zip(masks, sends)]
+        return terms, [0] * len(terms)
+    left, right, lower, upper, far_left, far_right = sends
+    over = [partner(far_left, "seq", 1), partner(far_right, "seq", 2)]
+    terms = [partner(left, "seq", 1), partner(upper, "seq", 2)]
+    rows, columns = left.shape
+    lower, right = kernel_call(
+        pair_sum_body,
+        [shape(left.shape, BF16)] * 2,
+        [VMEM] * 4,
+        flops=4 * rows * columns,
+        moved=12 * rows * columns,
+        deps=deps,
+    )(lower, right, *over)
+    return terms + [partner(right, "seq", 1), partner(lower, "seq", 2)], [0, 1, 1, 0]
 
 
 def tile_of(total, most):
@@ -597,39 +644,40 @@
     in_specs = [SMEM] + [VMEM] * (2 * seq - 1) + [pl.BlockSpec(memory_space=pltpu.HBM), VMEM]
     scratch = [pltpu.VMEM((width, channels), BF16), pltpu.SemaphoreType.DMA((4,))]
     cost = dict(flops=2 * seq * length * width * channels, moved=2 * width * channels, limit=24)
+    cuts = halved if seq == 4 else [(mask, 0) for mask in range(seq)]
     mixer_own, *mixer_send = kernel_call(
-        functools.partial(mixer_project_body, seq),
-        [shape((HALO + length, channels), F32)] + [shape((HALO + length, channels), BF16)] * (seq - 1),
+        functools.partial(mixer_project_body, seq, cuts),
+        [shape((HALO + length, channels), F32)]
+        + [shape((HALO + length, channels // (2 if seq == 4 else 1)), BF16)] * (len(cuts) - 1),
         in_specs,
         [pltpu.VMEM((seq, HALO, channels), F32)] + scratch,
         **cost,
     )(place, *x, weight, spread_routes)
-    mixer_terms = [partner(block, "seq", mask) for mask, block in zip(masks, mixer_send)]
-    assert width <= channels and window <= channels
+    assert width <= channels and window <= channels and 2 * length <= rank_width
     own_tokens = lax.dynamic_slice_in_dim(tokens, expert * own_rows, own_rows, 0)
     side_own, *side_send = kernel_call(
         functools.partial(gate_project_body, seq),
         [shape((length, channels), F32)] + [shape((length + own_rows, channels), BF16)] * (seq - 1),
         in_specs,
         scratch,
-        deps=[mixer_terms[seq // 2 - 1]],
         **cost,
     )(place, *x, weight, own_tokens)
 
+    mixer_terms, places = scattered(mixer_send, masks, [side_own])
+
     side_terms = [partner(block, "seq", mask) for mask, block in zip(masks, side_send)]
     activated, features = kernel_call(
-        functools.partial(conv_body, seq),
-        [shape((length, channels), BF16), shape((length, proj_weight.shape[1]), F32)],
-        [VMEM] * (seq + 3),
+        functools.partial(conv_body, places),
+        [shape((length, channels), BF16), shape((length + state_width, rank_width), F32)],
+        [VMEM] * (len(mixer_terms) + 4),
         limit=16,
-        deps=[side_own],
     )(mixer_own, *mixer_terms, conv_weight, conv_bias[None], jnp.transpose(proj_weight))
     features = features + partner(features, "expert", 1)
     sent = features.astype(BF16)
     features_came = [partner(sent, "expert", 2 * w) for w in range(1, chips)]
     for term in features_came:
         features = features + term.astype(F32)
-    low_rank, maps = features[:, :rank_width].astype(BF16), features[:, rank_width:]
+    low_rank, maps = features[:length].astype(BF16), features[length:]
 
     rate = -LOG2_E * jnp.exp(jnp.transpose(decay_log)).reshape(state_width, tiles, lanes)
     tiled = shape((length, tiles, lanes), F32)
@@ -654,13 +702,14 @@
     slots = groups * seq * most_slots
     per_chip = slots // chips
     per_group = slots // groups
+    route_terms = [term for term, index in zip(mixer_terms, places) if index == 0]
     choose, first, second, named = kernel_call(
         functools.partial(tables_body, seq, own_rows, most_slots),
         [shape((slots, window), BF16)] + [shape((slots, own_rows), F32)] * 2 + [shape((own_rows, 8), F32)],
-        [SMEM, VMEM] + [VMEM] * (seq - 1),
+        [SMEM, VMEM] + [VMEM] * len(route_terms),
         flops=2 * slots * window * window,
         moved=8 * slots * window,
-    )(place, spread_routes[0], *mixer_terms)
+    )(place, spread_routes[0], *route_terms)
 
     keep, send = kernel_call(
         functools.partial(out_project_body, seq, own_rows),
@@ -698,8 +747,7 @@
         partner(block, "expert", 2 * w) for w, block in zip(range(1, chips), outgoing[1:])
     ]
     whole = [near_hidden[0]] + [partner(near_hidden[mask], "seq", mask) for mask in masks]
-    more = list(fetch(place, both(early), width, sources[:2], [outgoing[0]])) if early < seq else []
-    crossed = partner(second_halves(came, whole[1:] + more), "expert", 1)
+    crossed = partner(second_halves(came, whole[1:]), "expert", 1)
     rows = kernel_call(
         functools.partial(rows_body, chips, seq, groups, most_slots),
         shape((slots, width), BF16),
@@ -715,31 +763,29 @@
     else:
         pieces = [[rows]] + [[partner(rows, "seq", mask)] for mask in masks]
 
-    before, waiting, downs = [], current + more, []
+    before, waiting, downs = [], current, []
     for mask in range(seq):
-        jobs = both(mask + 4) if mask + 4 < seq else []
+        jobs = both(mask + early) if mask + early < seq else []
+        gates = len(jobs)
         if mask == max(0, seq - 4):
-            jobs = [(2, block, 1) for block in range(seq)]
+            jobs = jobs + [(2, block, 1) for block in range(seq)]
         before, came_in = expert_chunk(
             mask, mask == 0, mask == seq - 1, place, pieces[mask], moe_gain[None], *waiting[:2], before, jobs, sources, downs
         )
-        waiting = waiting[2:]
-        if mask == max(0, seq - 4):
-            downs = list(came_in)
-        else:
-            waiting = waiting + list(came_in)
+        waiting = waiting[2:] + list(came_in[:gates])
+        downs = downs + list(came_in[gates:])
     hidden = before[0]
     back = groups * most_slots
     sums = kernel_call(
-        functools.partial(down_body, seq),
-        [shape((back, model_width), BF16)] * seq,
+        functools.partial(down_body, seq, cuts),
+        [shape((back, model_width // (2 if seq == 4 and mask else 1)), BF16) for mask, _ in cuts],
         [SMEM] + [VMEM] * (seq + 1),
         [pltpu.VMEM((slots, model_width), BF16)],
         flops=2 * slots * model_width * gate_weight.shape[2],
         moved=2 * model_width * gate_weight.shape[2],
         limit=16,
     )(place, hidden, *downs)
-    terms = [sums[0]] + [partner(sums[mask], "seq", mask) for mask in masks]
+    terms, places = scattered(sums[1:], masks)
 
     own_hidden, shares = kernel_call(
         functools.partial(shares_body, seq),
@@ -750,13 +796,13 @@
         deps=[sums[0]],
     )(place, moe_gain[None], jnp.transpose(router_weight), named, *whole)
     answers = kernel_call(
-        functools.partial(expert_sum_body, seq, groups, most_slots),
+        functools.partial(expert_sum_body, seq, groups, most_slots, places),
         [shape((per_chip, width), BF16)] * chips,
-        [VMEM] * seq,
+        [VMEM] * (1 + len(terms)),
         flops=seq * slots * width,
         moved=10 * slots * width,
         deps=[shares],
-    )(*terms)
+    )(sums[0], *terms)
     answers = [answers[0]] + [
         partner(block, "expert", 2 * w) for w, block in zip(range(1, chips), answers[1:])
     ]

time: 172 us -> 165 us (0.959)
  waiting for transfers between devices: 59.3 us -> 48.5 us
  starting transfers between devices: 50.9 us -> 54.3 us
    ppermute x44 -> x50, waiting for transfers between devices: 59.3 us -> 48.5 us  [partner(): return lax.ppermute(block, axis, [(i, i ^ mask) for i in range(size)])]
    ppermute x44 -> x50, starting transfers between devices: 50.9 us -> 54.3 us  [partner(): return lax.ppermute(block, axis, [(i, i ^ mask) for i in range(size)])]
    unnamed x32 -> x36, local copies, waits for them, and re-layouts: 7.66 us -> 9.2 us
    pallas_call x24 -> x25, Pallas kernels: 52.3 us -> 51.1 us  [kernel_call(): return lambda *operands: call(*operands, *deps)]
  transfers between devices with their start and end apart: 44 -> 50, of which waited for: 24 -> 28; matrix products, arithmetic and copies ran while one was open for 4% -> 4% of each run, Pallas kernels for 19% -> 20%
where the time goes in v5:
time: 165 us
  starting transfers between devices  54.3 us (33%)
  Pallas kernels  51.1 us (31%)
  waiting for transfers between devices  48.5 us (29%)
  local copies, waits for them, and re-layouts  10.2 us (6%)
    ppermute x50, starting transfers between devices, partner(): return lax.ppermute(block, axis, [(i, i ^ mask) for i in range(size)])  54.3 us
    pallas_call x25, Pallas kernels, kernel_call(): return lambda *operands: call(*operands, *deps)  51.1 us
    ppermute x50, waiting for transfers between devices, partner(): return lax.ppermute(block, axis, [(i, i ^ mask) for i in range(size)])  48.5 us
    unnamed x36, local copies, waits for them, and re-layouts  9.2 us
  transfers between devices with their start and end apart: 50, of which 28 were waited for; matrix products, arithmetic and copies ran while one was open for 4% of the time, Pallas kernels for 20%

profile of v5, /device:TPU:0, one launch (start us, length us, event | category | flops | bytes accessed | tf_op | source)
XLA Modules:
  0.0 164.7 jit_solution(226403429165238091)
XLA Ops:
  0.1 1.2 copy-done.4
  2.0 1.0 shard_map.163
  3.0 3.0 %collective-permute-start = (bf16[128,512]{1,0:T(8,128)(2,1)S(1)}, bf16[128,512]{1,0:T(8,128)(2,1)S(1)}, u32[]{:S(2)}, u32[]{:S(2)}) collective-permute-start(bf16[128,512]{1,0:T(8,128)(2,1)S(1)} %get-tuple-element.85), channel_id=1, source_target_pairs={{0,8},{8,0},{16,24},{24,16},{1,9},{9,1},{17,25},{25,17},{2,10},{10... | collective-permute-start | bytes 393224 | tf_op jit(solution)/shard_map/ppermute | solution.py:24
  6.0 1.5 collective-permute-start.1
  7.5 5.6 %copy.18 = bf16[128,8,2,1024]{3,1,2,0:T(8,128)(2,1)} copy(bf16[128,8,2,1024]{3,2,1,0:T(2,128)(2,1)} %bitcast.42) | data formatting | bytes 8388608
  15.7 3.2 %shard_map.165 = (f32[144,1024]{1,0:T(8,128)S(1)}, bf16[144,512]{1,0:T(8,128)(2,1)S(1)}, bf16[144,512]{1,0:T(8,128)(2,1)S(1)}, bf16[144,512]{1,0:T(8,128)(2,1)S(...) custom-call(s32[3]{0:T(128)S(1)} %pad_add_fusion.refs_0_, ...), custom_call_target="tpu_custom_call" | custom-call | flops 1073741824 | bytes 2097152 | tf_op jit(solution)/shard_map/pallas_call | solution.py:58
  19.0 1.5 collective-permute-start.8
  20.4 1.5 collective-permute-start.9
  24.1 3.2 %shard_map.166 = (f32[128,1024]{1,0:T(8,128)S(1)}, bf16[144,1024]{1,0:T(8,128)(2,1)S(1)}, bf16[144,1024]{1,0:T(8,128)(2,1)S(1)}, bf16[144,1024]{1,0:T(8,128)(2,1)S(1)}) custom-call(s32[3]{0:T(128)S(1)} %pad_add_fusion.refs_0_, bf16[128,1024]{1,0:T(8,128)(2,1)S(1)} %get-tuple-element.84.refs_1_, bf16[128,512]{1,0:T(8,128)(2,1)S(1)} %collective-permute-done.refs_0_.refs_2_, ...), custom_call_target="tpu_custom_call" | custom-call | flops 1073741824 | bytes 2097152 | tf_op jit(solution)/shard_map/pallas_call | solution.py:58
  27.4 1.5 collective-permute-start.10
  28.8 1.5 collective-permute-start.11
  30.3 2.2 %collective-permute-done.10.refs_3_ = bf16[144,512]{1,0:T(8,128)(2,1)S(1)} collective-permute-done((bf16[144,512]{1,0:T(8,128)(2,1)S(1)}, bf16[144,512]{1,0:T(8,128)(2,1)S(1)}, u32[]{:S(2)}, u32[]{:S(2)}) %collective-permute-start.10) | collective-permute-done | bytes 147488 | tf_op jit(solution)/shard_map/ppermute | solution.py:24
  32.6 1.4 collective-permute-done.11.refs_4_.refs_3_
  34.9 1.4 collective-permute-done.12
  36.2 1.6 collective-permute-start.13
  38.5 1.5 collective-permute-start.20
  40.0 1.4 collective-permute-start.21
  41.4 2.6 %collective-permute-start.14 = (bf16[144,256]{1,0:T(8,128)(2,1)S(1)}, bf16[144,256]{1,0:T(8,128)(2,1)S(1)}, u32[]{:S(2)}, u32[]{:S(2)}) collective-permute-start(bf16[144,256]{1,0:T(8,128)(2,1)S(1)} %get-tuple-element.163), channel_id=1, source_target_pairs={{0,4},{1,5},{2,6},{3,7},{4,0},{5,1},{6,2},{7,3},{8,12},{9,13},{10,... | collective-permute-start | bytes 221192 | tf_op jit(solution)/shard_map/ppermute | solution.py:24
  44.3 4.2 %collective-permute-done.14 = bf16[144,256]{1,0:T(8,128)(2,1)S(1)} collective-permute-done((bf16[144,256]{1,0:T(8,128)(2,1)S(1)}, bf16[144,256]{1,0:T(8,128)(2,1)S(1)}, u32[]{:S(2)}, u32[]{:S(2)}) %collective-permute-start.14) | collective-permute-done | bytes 73760 | tf_op jit(solution)/shard_map/ppermute | solution.py:24
  48.5 1.6 collective-permute-done.15
  50.2 5.2 %shard_map.169 = (f32[128,8,128]{2,1,0:T(8,128)S(1)}, f32[128,8,128]{2,1,0:T(8,128)S(1)}, bf16[18,8,128]{2,1,0:T(8,128)(2,1)S(1)}) custom-call(f32[16,256]{1,0:T(8,128)S(1)} %slice.17.refs_0_.refs_1_, bf16[128,256]{1,0:T(8,128)(2,1)S(1)} %slice.22.refs_1_, bf16[128,1024]{1,0:T(8,128)(2,1)S(1)} %get-tuple-element.102.refs_2_.refs_8_, ...), custom_call_target="tpu_custom_call" | custom-call | tf_op jit(solution)/shard_map/pallas_call | solution.py:58
  56.1 1.5 collective-permute-start.17
  57.6 1.4 collective-permute-start.18
  60.1 2.4 %collective-permute-done.18.refs_4_ = bf16[18,8,128]{2,1,0:T(8,128)(2,1)S(1)} collective-permute-done((bf16[18,8,128]{2,1,0:T(8,128)(2,1)S(1)}, bf16[18,8,128]{2,1,0:T(8,128)(2,1)S(1)}, u32[]{:S(2)}, u32[]{:S(2)}) %collective-permute-start.18) | collective-permute-done | bytes 36896 | tf_op jit(solution)/shard_map/ppermute | solution.py:24
  62.5 3.7 %shard_map.170.refs_0_ = bf16[128,1024]{1,0:T(8,128)(2,1)S(1)} custom-call(s32[3]{0:T(128)S(1)} %pad_add_fusion.refs_0_, f32[16,256]{1,0:T(8,128)S(1)} %slice.17.refs_0_.refs_1_, bf16[18,8,128]{2,1,0:T(8,128)(2,1)S(1)} %collective-permute-done.16.refs_2_, bf16[18,8,128]{2,1,0:T(8,128)(2,1)S(1)} %collective-permute-done.17.refs_3_, ...), custom_call_target="tpu_custom_call" | custom-call | tf_op jit(solution)/shard_map/pallas_call | solution.py:58
  66.2 1.5 collective-permute-start.22
  68.2 1.6 collective-permute-start.24
  69.8 3.6 %collective-permute-done.22.refs_1_ = bf16[128,1024]{1,0:T(8,128)(2,1)S(1)} collective-permute-done((bf16[128,1024]{1,0:T(8,128)(2,1)S(1)}, bf16[128,1024]{1,0:T(8,128)(2,1)S(1)}, u32[]{:S(2)}, u32[]{:S(2)}) %collective-permute-start.22) | collective-permute-done | bytes 262176 | tf_op jit(solution)/shard_map/ppermute | solution.py:24
  73.3 3.9 %collective-permute-done.23.refs_2_ = bf16[128,1024]{1,0:T(8,128)(2,1)S(1)} collective-permute-done((bf16[128,1024]{1,0:T(8,128)(2,1)S(1)}, bf16[128,1024]{1,0:T(8,128)(2,1)S(1)}, u32[]{:S(2)}, u32[]{:S(2)}) %collective-permute-start.23) | collective-permute-done | bytes 262176 | tf_op jit(solution)/shard_map/ppermute | solution.py:24
  77.2 1.3 shard_map.171
  78.6 1.9 %collective-permute-done.25.refs_1_ = bf16[4,64,1024]{2,1,0:T(8,128)(2,1)S(1)} collective-permute-done((bf16[4,64,1024]{2,1,0:T(8,128)(2,1)S(1)}, bf16[4,64,1024]{2,1,0:T(8,128)(2,1)S(1)}, u32[]{:S(2)}, u32[]{:S(2)}) %collective-permute-start.25) | collective-permute-done | bytes 524320 | tf_op jit(solution)/shard_map/ppermute | solution.py:24
  80.6 1.3 collective-permute-start.26
  81.9 2.0 %collective-permute-start.27 = (bf16[64,1024]{1,0:T(8,128)(2,1)S(1)}, bf16[64,1024]{1,0:T(8,128)(2,1)S(1)}, u32[]{:S(2)}, u32[]{:S(2)}) collective-permute-start(bf16[64,1024]{1,0:T(8,128)(2,1)S(1)} %get-tuple-element.113), channel_id=1, source_target_pairs={{0,4},{1,5},{2,6},{3,7},{4,0},{5,1},{6,2},{7,3},{8,12},{9,13},{10,... | collective-permute-start | bytes 393224 | tf_op jit(solution)/shard_map/ppermute | solution.py:24
  83.9 1.4 collective-permute-start.28
  86.0 7.9 %shard_map.174 = (bf16[1024,1792]{1,0:T(8,128)(2,1)S(1)}, bf16[1024,1792]{1,0:T(8,128)(2,1)S(1)}, bf16[1024,1792]{1,0:T(8,128)(2,1)S(1)}, bf16[1024,1792]{1,0:T(...) custom-call(s32[3]{0:T(128)S(1)} %pad_add_fusion.refs_0_, ...), custom_call_target="tpu_custom_call" | custom-call | bytes 22020096 | tf_op jit(solution)/shard_map/pallas_call | solution.py:58
  95.8 1.1 copy-done.2
  96.9 1.1 collective-permute-start.29
  98.0 1.9 %collective-permute-start.30 = (bf16[48,1024]{1,0:T(8,128)(2,1)S(1)}, bf16[48,1024]{1,0:T(8,128)(2,1)S(1)}, u32[]{:S(2)}, u32[]{:S(2)}) collective-permute-start(bf16[48,1024]{1,0:T(8,128)(2,1)S(1)} %get-tuple-element.124), channel_id=1, source_target_pairs={{0,4},{1,5},{2,6},{3,7},{4,0},{5,1},{6,2},{7,3},{8,12},{9,13},{10,... | collective-permute-start | bytes 294920 | tf_op jit(solution)/shard_map/ppermute | solution.py:24
  99.9 1.4 collective-permute-start.31
  101.7 1.3 collective-permute-start.33
  103.0 2.2 %collective-permute-done.32.refs_4_.refs_5_ = bf16[16,1024]{1,0:T(8,128)(2,1)S(1)} collective-permute-done((bf16[16,1024]{1,0:T(8,128)(2,1)S(1)}, bf16[16,1024]{1,0:T(8,128)(2,1)S(1)}, u32[]{:S(2)}, u32[]{:S(2)}) %collective-permute-start.32) | collective-permute-done | bytes 32800 | tf_op jit(solution)/shard_map/ppermute | solution.py:24
  105.2 1.2 collective-permute-start.34
  106.3 3.6 %collective-permute-done.34.refs_6_.refs_7_ = bf16[16,1024]{1,0:T(8,128)(2,1)S(1)} collective-permute-done((bf16[16,1024]{1,0:T(8,128)(2,1)S(1)}, bf16[16,1024]{1,0:T(8,128)(2,1)S(1)}, u32[]{:S(2)}, u32[]{:S(2)}) %collective-permute-start.34) | collective-permute-done | bytes 32800 | tf_op jit(solution)/shard_map/ppermute | solution.py:24
  110.1 1.4 collective-permute-done.35.refs_4_
  112.4 1.3 collective-permute-start.38
  113.7 9.6 %shard_map.178 = (f32[192,1792]{1,0:T(8,128)S(1)}, f32[192,1792]{1,0:T(8,128)S(1)}, f32[192,128]{1,0:T(8,128)S(1)}, bf16[1024,1792]{1,0:T(8,128)(2,1)S(1)}, bf16...) custom-call(s32[3]{0:T(128)S(1)} %pad_add_fusion.refs_0_, ...), custom_call_target="tpu_custom_call" | custom-call | flops 1409286144 | bytes 7340032 | tf_op jit(solution)/shard_map/pallas_call | solution.py:58
  124.1 1.7 %collective-permute-start.39 = (bf16[96,1024]{1,0:T(8,128)(2,1)S(1)}, bf16[96,1024]{1,0:T(8,128)(2,1)S(1)}, u32[]{:S(2)}, u32[]{:S(2)}) collective-permute-start(bf16[96,1024]{1,0:T(8,128)(2,1)S(1)} %slice.20), channel_id=1, source_target_pairs={{0,8},{8,0},{16,24},{24,16},{1,9},{9,1},{17,25},{25,17},{2,10},{10... | collective-permute-start | bytes 589832 | tf_op jit(solution)/shard_map/ppermute | solution.py:24
  125.7 2.2 %shard_map.179 = (f32[192,1792]{1,0:T(8,128)S(1)}, f32[192,1792]{1,0:T(8,128)S(1)}, f32[192,128]{1,0:T(8,128)S(1)}) custom-call(s32[3]{0:T(128)S(1)} %pad_add_fusion.refs_0_, bf16[192,1024]{1,0:T(8,128)(2,1)S(1)} %collective-permute-done.36.refs_1_, f32[1,4096]{1,0:T(1,128)S(1)} %bitcast.30, bf16[1024,1792]{1,0:T(8,128)(2,1)S(1)} %copy-done.1, ...), custom_call_target="tpu_custom_call" | custom-call | flops 1409286144 | bytes 7340032 | tf_op jit(solution)/shard_map/pallas_call | solution.py:58
  128.0 2.2 %shard_map.180 = (f32[192,1792]{1,0:T(8,128)S(1)}, f32[192,1792]{1,0:T(8,128)S(1)}, f32[192,128]{1,0:T(8,128)S(1)}) custom-call(s32[3]{0:T(128)S(1)} %pad_add_fusion.refs_0_, bf16[192,1024]{1,0:T(8,128)(2,1)S(1)} %collective-permute-done.38.refs_1_, f32[1,4096]{1,0:T(1,128)S(1)} %bitcast.31, bf16[1024,1792]{1,0:T(8,128)(2,1)S(1)} %get-tuple-element.120.refs_14_.refs_3_, ...), custom_call_target="tpu_custom_call" | custom-call | flops 1409286144 | bytes 7340032 | tf_op jit(solution)/shard_map/pallas_call | solution.py:58
  130.3 2.3 %shard_map.181.refs_1_ = bf16[192,1792]{1,0:T(8,128)(2,1)S(1)} custom-call(s32[3]{0:T(128)S(1)} %pad_add_fusion.refs_0_, bf16[96,1024]{1,0:T(8,128)(2,1)S(1)} %collective-permute-done.37.refs_1_, bf16[96,1024]{1,0:T(8,128)(2,1)S(1)} %collective-permute-done.39.refs_2_, f32[1,4096]{1,0:T(1,128)S(1)} %bitcast.32, ...), custom_call_target="tpu_custom_call" | custom-call | flops 1409286144 | bytes 7340032 | tf_op jit(solution)/shard_map/pallas_call | solution.py:58
  132.6 3.7 %shard_map.182 = (bf16[48,4096]{1,0:T(8,128)(2,1)S(1)}, bf16[48,2048]{1,0:T(8,128)(2,1)S(1)}, bf16[48,2048]{1,0:T(8,128)(2,1)S(1)}, bf16[48,2048]{1,0:T(8,128)(2...) custom-call(s32[3]{0:T(128)S(1)} %pad_add_fusion.refs_0_, ...), custom_call_target="tpu_custom_call" | custom-call | flops 2818572288 | bytes 14680064 | tf_op jit(solution)/shard_map/pallas_call | solution.py:58
  136.3 1.7 %collective-permute-start.42 = (bf16[48,2048]{1,0:T(8,128)(2,1)S(1)}, bf16[48,2048]{1,0:T(8,128)(2,1)S(1)}, u32[]{:S(2)}, u32[]{:S(2)}) collective-permute-start(bf16[48,2048]{1,0:T(8,128)(2,1)S(1)} %get-tuple-element.149), channel_id=1, source_target_pairs={{0,8},{8,0},{16,24},{24,16},{1,9},{9,1},{17,25},{25,17},{2,10},{10... | collective-permute-start | bytes 589832 | tf_op jit(solution)/shard_map/ppermute | solution.py:24
  138.3 1.3 collective-permute-start.40
  140.4 3.8 %collective-permute-done.42.refs_2_ = bf16[48,2048]{1,0:T(8,128)(2,1)S(1)} collective-permute-done((bf16[48,2048]{1,0:T(8,128)(2,1)S(1)}, bf16[48,2048]{1,0:T(8,128)(2,1)S(1)}, u32[]{:S(2)}, u32[]{:S(2)}) %collective-permute-start.42) | collective-permute-done | bytes 196640 | tf_op jit(solution)/shard_map/ppermute | solution.py:24
  144.2 1.2 collective-permute-done.43.refs_3_
  146.4 0.9 collective-permute-start.45
  147.3 1.0 shard_map.184
  149.1 2.1 %collective-permute-done.44.refs_3_ = bf16[48,2048]{1,0:T(8,128)(2,1)S(1)} collective-permute-done((bf16[48,2048]{1,0:T(8,128)(2,1)S(1)}, bf16[48,2048]{1,0:T(8,128)(2,1)S(1)}, u32[]{:S(2)}, u32[]{:S(2)}) %collective-permute-start.44) | collective-permute-done | bytes 196640 | tf_op jit(solution)/shard_map/ppermute | solution.py:24
  153.1 2.4 %collective-permute-start.47 = (bf16[48,1024]{1,0:T(8,128)(2,1)S(1)}, bf16[48,1024]{1,0:T(8,128)(2,1)S(1)}, u32[]{:S(2)}, u32[]{:S(2)}) collective-permute-start(bf16[48,1024]{1,0:T(8,128)(2,1)S(1)} %get-tuple-element.158), channel_id=1, source_target_pairs={{0,4},{1,5},{2,6},{3,7},{4,0},{5,1},{6,2},{7,3},{8,12},{9,13},{10,... | collective-permute-start | bytes 294920 | tf_op jit(solution)/shard_map/ppermute | solution.py:24
  155.5 1.4 collective-permute-start.48
  156.9 2.3 %collective-permute-done.46.refs_1_ = bf16[48,1024]{1,0:T(8,128)(2,1)S(1)} collective-permute-done((bf16[48,1024]{1,0:T(8,128)(2,1)S(1)}, bf16[48,1024]{1,0:T(8,128)(2,1)S(1)}, u32[]{:S(2)}, u32[]{:S(2)}) %collective-permute-start.46) | collective-permute-done | bytes 98336 | tf_op jit(solution)/shard_map/ppermute | solution.py:24
  159.3 2.7 %collective-permute-done.48.refs_3_ = bf16[48,1024]{1,0:T(8,128)(2,1)S(1)} collective-permute-done((bf16[48,1024]{1,0:T(8,128)(2,1)S(1)}, bf16[48,1024]{1,0:T(8,128)(2,1)S(1)}, u32[]{:S(2)}, u32[]{:S(2)}) %collective-permute-start.48) | collective-permute-done | bytes 98336 | tf_op jit(solution)/shard_map/ppermute | solution.py:24
  162.0 1.4 collective-permute-done.49.refs_4_
  163.5 1.3 shard_map.187
  (109 shorter events, 19.5 us)
Async XLA Ops:
  3.0 10.2 %collective-permute-start = (bf16[128,512]{1,0:T(8,128)(2,1)S(1)}, bf16[128,512]{1,0:T(8,128)(2,1)S(1)}, u32[]{:S(2)}, u32[]{:S(2)}) collective-permute-start(bf16[128,512]{1,0:T(8,128)(2,1)S(1)} %get-tuple-element.85), channel_id=1, source_target_pairs={{0,8},{8,0},{16,24},{24,16},{1,9},{9,1},{17,25},{25,17},{2,10},{10... | collective-permute-start | bytes 393224 | tf_op jit(solution)/shard_map/ppermute | solution.py:24
  6.0 7.8 %collective-permute-start.1 = (bf16[128,512]{1,0:T(8,128)(2,1)S(1)}, bf16[128,512]{1,0:T(8,128)(2,1)S(1)}, u32[]{:S(2)}, u32[]{:S(2)}) collective-permute-start(bf16[128,512]{1,0:T(8,128)(2,1)S(1)} %get-tuple-element.86), channel_id=1, source_target_pairs={{0,16},{8,24},{16,0},{24,8},{1,17},{9,25},{17,1},{25,9},{2,18},{10... | collective-permute-start | bytes 393224 | tf_op jit(solution)/shard_map/ppermute | solution.py:24
  7.5 6.3 %collective-permute-start.2 = (bf16[128,512]{1,0:T(8,128)(2,1)S(1)}, bf16[128,512]{1,0:T(8,128)(2,1)S(1)}, u32[]{:S(2)}, u32[]{:S(2)}) collective-permute-start(bf16[128,512]{1,0:T(8,128)(2,1)S(1)} %get-tuple-element.87), channel_id=1, source_target_pairs={{0,24},{8,16},{16,8},{24,0},{1,25},{9,17},{17,9},{25,1},{2,26},{10... | collective-permute-start | bytes 393224 | tf_op jit(solution)/shard_map/ppermute | solution.py:24
  7.5 5.6 %copy-start.16 = (s32[16,2]{0,1:T(2,128)S(1)}, s32[16,2]{0,1:T(2,128)}, u32[]{:S(2)}) copy-start(s32[16,2]{0,1:T(2,128)} %param.30) | copy-start | bytes 388
  13.8 1.4 collective-permute-start.3
  13.9 1.5 collective-permute-start.4
  14.4 1.3 collective-permute-start.5
  18.9 15.0 %copy-start.5 = (bf16[1024,288]{0,1:T(8,128)(2,1)S(1)}, bf16[1024,288]{0,1:T(8,128)(2,1)}, u32[]{:S(2)}) copy-start(bf16[1024,288]{0,1:T(8,128)(2,1)} %param.22) | copy-start | bytes 1769476
  18.9 15.0 %copy-start.10 = (f32[4,1024]{1,0:T(4,128)S(1)}, f32[4,1024]{1,0:T(4,128)}, u32[]{:S(2)}) copy-start(f32[4,1024]{1,0:T(4,128)} %refs_5_.2) | copy-start | bytes 49156
  19.0 15.0 %copy-start.11 = (f32[1024]{0:T(1024)S(1)}, f32[1024]{0:T(1024)}, u32[]{:S(2)}) copy-start(f32[1024]{0:T(1024)} %param.21) | copy-start | bytes 12292
  19.0 8.3 %collective-permute-start.8 = (bf16[144,512]{1,0:T(8,128)(2,1)S(1)}, bf16[144,512]{1,0:T(8,128)(2,1)S(1)}, u32[]{:S(2)}, u32[]{:S(2)}) collective-permute-start(bf16[144,512]{1,0:T(8,128)(2,1)S(1)} %get-tuple-element.96), channel_id=1, source_target_pairs={{0,8},{8,0},{16,24},{24,16},{1,9},{9,1},{17,25},{25,17},{2,10},{10... | collective-permute-start | bytes 442376 | tf_op jit(solution)/shard_map/ppermute | solution.py:24
  20.4 6.8 %collective-permute-start.9 = (bf16[144,512]{1,0:T(8,128)(2,1)S(1)}, bf16[144,512]{1,0:T(8,128)(2,1)S(1)}, u32[]{:S(2)}, u32[]{:S(2)}) collective-permute-start(bf16[144,512]{1,0:T(8,128)(2,1)S(1)} %get-tuple-element.97), channel_id=1, source_target_pairs={{0,16},{8,24},{16,0},{24,8},{1,17},{9,25},{17,1},{25,9},{2,18},{10... | collective-permute-start | bytes 442376 | tf_op jit(solution)/shard_map/ppermute | solution.py:24
  22.9 7.5 %collective-permute-start.6 = (bf16[144,512]{1,0:T(8,128)(2,1)S(1)}, bf16[144,512]{1,0:T(8,128)(2,1)S(1)}, u32[]{:S(2)}, u32[]{:S(2)}) collective-permute-start(bf16[144,512]{1,0:T(8,128)(2,1)S(1)} %get-tuple-element.92), channel_id=1, source_target_pairs={{0,8},{8,0},{16,24},{24,16},{1,9},{9,1},{17,25},{25,17},{2,10},{10... | collective-permute-start | bytes 442376 | tf_op jit(solution)/shard_map/ppermute | solution.py:24
  23.6 20.7 %copy-start.15 = (f32[1024,16]{0,1:T(8,128)S(1)}, f32[1024,16]{0,1:T(8,128)}, u32[]{:S(2)}) copy-start(f32[1024,16]{0,1:T(8,128)} %param.25) | copy-start | bytes 196612
  23.6 26.6 %copy-start.6 = (bf16[256,1024]{1,0:T(8,128)(2,1)S(1)}, bf16[256,1024]{1,0:T(8,128)(2,1)}, u32[]{:S(2)}) copy-start(bf16[256,1024]{1,0:T(8,128)(2,1)} %refs_3_.1) | copy-start | bytes 1572868
  23.6 26.6 %copy-start.12 = (f32[1024]{0:T(1024)S(1)}, f32[1024]{0:T(1024)}, u32[]{:S(2)}) copy-start(f32[1024]{0:T(1024)} %param.24) | copy-start | bytes 12292
  23.6 6.8 %collective-permute-start.7 = (bf16[144,512]{1,0:T(8,128)(2,1)S(1)}, bf16[144,512]{1,0:T(8,128)(2,1)S(1)}, u32[]{:S(2)}, u32[]{:S(2)}) collective-permute-start(bf16[144,512]{1,0:T(8,128)(2,1)S(1)} %get-tuple-element.93), channel_id=1, source_target_pairs={{0,16},{8,24},{16,0},{24,8},{1,17},{9,25},{17,1},{25,9},{2,18},{10... | collective-permute-start | bytes 442376 | tf_op jit(solution)/shard_map/ppermute | solution.py:24
  27.2 35.2 %copy-start.13 = (f32[1024]{0:T(1024)S(1)}, f32[1024]{0:T(1024)}, u32[]{:S(2)}) copy-start(f32[1024]{0:T(1024)} %param.26) | copy-start | bytes 12292
  27.4 5.2 %collective-permute-start.10 = (bf16[144,512]{1,0:T(8,128)(2,1)S(1)}, bf16[144,512]{1,0:T(8,128)(2,1)S(1)}, u32[]{:S(2)}, u32[]{:S(2)}) collective-permute-start(bf16[144,512]{1,0:T(8,128)(2,1)S(1)} %get-tuple-element.99), channel_id=1, source_target_pairs={{0,8},{8,0},{16,24},{24,16},{1,9},{9,1},{17,25},{25,17},{2,10},{10... | collective-permute-start | bytes 442376 | tf_op jit(solution)/shard_map/ppermute | solution.py:24
  28.8 5.1 %collective-permute-start.11 = (bf16[144,512]{1,0:T(8,128)(2,1)S(1)}, bf16[144,512]{1,0:T(8,128)(2,1)S(1)}, u32[]{:S(2)}, u32[]{:S(2)}) collective-permute-start(bf16[144,512]{1,0:T(8,128)(2,1)S(1)} %get-tuple-element.100), channel_id=1, source_target_pairs={{0,16},{8,24},{16,0},{24,8},{1,17},{9,25},{17,1},{25,9},{2,18},{10... | collective-permute-start | bytes 442376 | tf_op jit(solution)/shard_map/ppermute | solution.py:24
  34.0 43.3 %copy-start.14 = (bf16[1024,1024]{1,0:T(8,128)(2,1)S(1)}, bf16[1024,1024]{1,0:T(8,128)(2,1)}, u32[]{:S(2)}) copy-start(bf16[1024,1024]{1,0:T(8,128)(2,1)} %refs_4_.1) | copy-start | bytes 6291460
  34.8 1.4 collective-permute-start.12
  36.2 7.7 %collective-permute-start.13 = (bf16[144,256]{1,0:T(8,128)(2,1)S(1)}, bf16[144,256]{1,0:T(8,128)(2,1)S(1)}, u32[]{:S(2)}, u32[]{:S(2)}) collective-permute-start(bf16[144,256]{1,0:T(8,128)(2,1)S(1)} %get-tuple-element.163), channel_id=1, source_target_pairs={{0,2},{1,3},{2,0},{3,1},{4,6},{5,7},{6,4},{7,5},{8,10},{9,11},{10,... | collective-permute-start | bytes 221192 | tf_op jit(solution)/shard_map/ppermute | solution.py:24
  37.9 19.7 %collective-permute-start.19 = (bf16[144,1024]{1,0:T(8,128)(2,1)S(1)}, bf16[144,1024]{1,0:T(8,128)(2,1)S(1)}, u32[]{:S(2)}, u32[]{:S(2)}) collective-permute-start(bf16[144,1024]{1,0:T(8,128)(2,1)S(1)} %get-tuple-element.106), channel_id=1, source_target_pairs={{0,8},{8,0},{16,24},{24,16},{1,9},{9,1},{17,25},{25,17},{2,10},{10... | collective-permute-start | bytes 884744 | tf_op jit(solution)/shard_map/ppermute | solution.py:24
  38.5 20.4 %collective-permute-start.20 = (bf16[144,1024]{1,0:T(8,128)(2,1)S(1)}, bf16[144,1024]{1,0:T(8,128)(2,1)S(1)}, u32[]{:S(2)}, u32[]{:S(2)}) collective-permute-start(bf16[144,1024]{1,0:T(8,128)(2,1)S(1)} %get-tuple-element.107), channel_id=1, source_target_pairs={{0,16},{8,24},{16,0},{24,8},{1,17},{9,25},{17,1},{25,9},{2,18},{10... | collective-permute-start | bytes 884744 | tf_op jit(solution)/shard_map/ppermute | solution.py:24
  40.0 18.9 %collective-permute-start.21 = (bf16[144,1024]{1,0:T(8,128)(2,1)S(1)}, bf16[144,1024]{1,0:T(8,128)(2,1)S(1)}, u32[]{:S(2)}, u32[]{:S(2)}) collective-permute-start(bf16[144,1024]{1,0:T(8,128)(2,1)S(1)} %get-tuple-element.108), channel_id=1, source_target_pairs={{0,24},{8,16},{16,8},{24,0},{1,25},{9,17},{17,9},{25,1},{2,26},{10... | collective-permute-start | bytes 884744 | tf_op jit(solution)/shard_map/ppermute | solution.py:24
  41.4 7.1 %collective-permute-start.14 = (bf16[144,256]{1,0:T(8,128)(2,1)S(1)}, bf16[144,256]{1,0:T(8,128)(2,1)S(1)}, u32[]{:S(2)}, u32[]{:S(2)}) collective-permute-start(bf16[144,256]{1,0:T(8,128)(2,1)S(1)} %get-tuple-element.163), channel_id=1, source_target_pairs={{0,4},{1,5},{2,6},{3,7},{4,0},{5,1},{6,2},{7,3},{8,12},{9,13},{10,... | collective-permute-start | bytes 221192 | tf_op jit(solution)/shard_map/ppermute | solution.py:24
  44.0 6.2 %collective-permute-start.15 = (bf16[144,256]{1,0:T(8,128)(2,1)S(1)}, bf16[144,256]{1,0:T(8,128)(2,1)S(1)}, u32[]{:S(2)}, u32[]{:S(2)}) collective-permute-start(bf16[144,256]{1,0:T(8,128)(2,1)S(1)} %get-tuple-element.163), channel_id=1, source_target_pairs={{0,6},{1,7},{2,4},{3,5},{4,2},{5,3},{6,0},{7,1},{8,14},{9,15},{10,... | collective-permute-start | bytes 221192 | tf_op jit(solution)/shard_map/ppermute | solution.py:24
  55.4 4.0 %collective-permute-start.16 = (bf16[18,8,128]{2,1,0:T(8,128)(2,1)S(1)}, bf16[18,8,128]{2,1,0:T(8,128)(2,1)S(1)}, u32[]{:S(2)}, u32[]{:S(2)}) collective-permute-start(bf16[18,8,128]{2,1,0:T(8,128)(2,1)S(1)} %get-tuple-element.103), channel_id=1, source_target_pairs={{0,8},{8,0},{16,24},{24,16},{1,9},{9,1},{17,25},{25,17},{2,10},{10... | collective-permute-start | bytes 110600 | tf_op jit(solution)/shard_map/ppermute | solution.py:24
  56.1 4.0 %collective-permute-start.17 = (bf16[18,8,128]{2,1,0:T(8,128)(2,1)S(1)}, bf16[18,8,128]{2,1,0:T(8,128)(2,1)S(1)}, u32[]{:S(2)}, u32[]{:S(2)}) collective-permute-start(bf16[18,8,128]{2,1,0:T(8,128)(2,1)S(1)} %get-tuple-element.103), channel_id=1, source_target_pairs={{0,16},{8,24},{16,0},{24,8},{1,17},{9,25},{17,1},{25,9},{2,18},{10... | collective-permute-start | bytes 110600 | tf_op jit(solution)/shard_map/ppermute | solution.py:24
  57.6 4.9 %collective-permute-start.18 = (bf16[18,8,128]{2,1,0:T(8,128)(2,1)S(1)}, bf16[18,8,128]{2,1,0:T(8,128)(2,1)S(1)}, u32[]{:S(2)}, u32[]{:S(2)}) collective-permute-start(bf16[18,8,128]{2,1,0:T(8,128)(2,1)S(1)} %get-tuple-element.103), channel_id=1, source_target_pairs={{0,24},{8,16},{16,8},{24,0},{1,25},{9,17},{17,9},{25,1},{2,26},{10... | collective-permute-start | bytes 110600 | tf_op jit(solution)/shard_map/ppermute | solution.py:24
  66.2 7.1 %collective-permute-start.22 = (bf16[128,1024]{1,0:T(8,128)(2,1)S(1)}, bf16[128,1024]{1,0:T(8,128)(2,1)S(1)}, u32[]{:S(2)}, u32[]{:S(2)}) collective-permute-start(bf16[128,1024]{1,0:T(8,128)(2,1)S(1)} %shard_map.170.refs_0_), channel_id=1, source_target_pairs={{0,8},{8,0},{16,24},{24,16},{1,9},{9,1},{17,25},{25,17},{2,10},{10... | collective-permute-start | bytes 786440 | tf_op jit(solution)/shard_map/ppermute | solution.py:24
  67.7 9.5 %collective-permute-start.23 = (bf16[128,1024]{1,0:T(8,128)(2,1)S(1)}, bf16[128,1024]{1,0:T(8,128)(2,1)S(1)}, u32[]{:S(2)}, u32[]{:S(2)}) collective-permute-start(bf16[128,1024]{1,0:T(8,128)(2,1)S(1)} %shard_map.170.refs_0_), channel_id=1, source_target_pairs={{0,16},{8,24},{16,0},{24,8},{1,17},{9,25},{17,1},{25,9},{2,18},{10... | collective-permute-start | bytes 786440 | tf_op jit(solution)/shard_map/ppermute | solution.py:24
  68.2 9.0 %collective-permute-start.24 = (bf16[128,1024]{1,0:T(8,128)(2,1)S(1)}, bf16[128,1024]{1,0:T(8,128)(2,1)S(1)}, u32[]{:S(2)}, u32[]{:S(2)}) collective-permute-start(bf16[128,1024]{1,0:T(8,128)(2,1)S(1)} %shard_map.170.refs_0_), channel_id=1, source_target_pairs={{0,24},{8,16},{16,8},{24,0},{1,25},{9,17},{17,9},{25,1},{2,26},{10... | collective-permute-start | bytes 786440 | tf_op jit(solution)/shard_map/ppermute | solution.py:24
  78.5 2.0 %collective-permute-start.25 = (bf16[4,64,1024]{2,1,0:T(8,128)(2,1)S(1)}, bf16[4,64,1024]{2,1,0:T(8,128)(2,1)S(1)}, u32[]{:S(2)}, u32[]{:S(2)}) collective-permute-start(bf16[4,64,1024]{2,1,0:T(8,128)(2,1)S(1)} %get-tuple-element.110), channel_id=1, source_target_pairs={{0,1},{1,0},{2,3},{3,2},{4,5},{5,4},{6,7},{7,6},{8,9},{9,8},{10,11... | collective-permute-start | bytes 1572872 | tf_op jit(solution)/shard_map/ppermute | solution.py:24
  80.6 13.3 %collective-permute-start.26 = (bf16[64,1024]{1,0:T(8,128)(2,1)S(1)}, bf16[64,1024]{1,0:T(8,128)(2,1)S(1)}, u32[]{:S(2)}, u32[]{:S(2)}) collective-permute-start(bf16[64,1024]{1,0:T(8,128)(2,1)S(1)} %get-tuple-element.112), channel_id=1, source_target_pairs={{0,2},{1,3},{2,0},{3,1},{4,6},{5,7},{6,4},{7,5},{8,10},{9,11},{10,... | collective-permute-start | bytes 393224 | tf_op jit(solution)/shard_map/ppermute | solution.py:24
  81.9 12.1 %collective-permute-start.27 = (bf16[64,1024]{1,0:T(8,128)(2,1)S(1)}, bf16[64,1024]{1,0:T(8,128)(2,1)S(1)}, u32[]{:S(2)}, u32[]{:S(2)}) collective-permute-start(bf16[64,1024]{1,0:T(8,128)(2,1)S(1)} %get-tuple-element.113), channel_id=1, source_target_pairs={{0,4},{1,5},{2,6},{3,7},{4,0},{5,1},{6,2},{7,3},{8,12},{9,13},{10,... | collective-permute-start | bytes 393224 | tf_op jit(solution)/shard_map/ppermute | solution.py:24
  83.9 10.6 %collective-permute-start.28 = (bf16[64,1024]{1,0:T(8,128)(2,1)S(1)}, bf16[64,1024]{1,0:T(8,128)(2,1)S(1)}, u32[]{:S(2)}, u32[]{:S(2)}) collective-permute-start(bf16[64,1024]{1,0:T(8,128)(2,1)S(1)} %get-tuple-element.114), channel_id=1, source_target_pairs={{0,6},{1,7},{2,4},{3,5},{4,2},{5,3},{6,0},{7,1},{8,14},{9,15},{10,... | collective-permute-start | bytes 393224 | tf_op jit(solution)/shard_map/ppermute | solution.py:24
  93.9 2.9 %copy-start.2 = (bf16[1024,1792]{1,0:T(8,128)(2,1)}, bf16[1024,1792]{1,0:T(8,128)(2,1)S(1)}, u32[]{:S(2)}) copy-start(bf16[1024,1792]{1,0:T(8,128)(2,1)S(1)} %get-tuple-element.119.refs_13_.refs_4_) | copy-start | bytes 11010052
  94.5 19.2 %copy-start.7 = (f32[4096]{0:T(1024)S(1)}, f32[4096]{0:T(1024)}, u32[]{:S(2)}) copy-start(f32[4096]{0:T(1024)} %param.28) | copy-start | bytes 49156
  96.9 13.1 %collective-permute-start.29 = (bf16[48,1024]{1,0:T(8,128)(2,1)S(1)}, bf16[48,1024]{1,0:T(8,128)(2,1)S(1)}, u32[]{:S(2)}, u32[]{:S(2)}) collective-permute-start(bf16[48,1024]{1,0:T(8,128)(2,1)S(1)} %get-tuple-element.123), channel_id=1, source_target_pairs={{0,2},{1,3},{2,0},{3,1},{4,6},{5,7},{6,4},{7,5},{8,10},{9,11},{10,... | collective-permute-start | bytes 294920 | tf_op jit(solution)/shard_map/ppermute | solution.py:24
  98.0 12.0 %collective-permute-start.30 = (bf16[48,1024]{1,0:T(8,128)(2,1)S(1)}, bf16[48,1024]{1,0:T(8,128)(2,1)S(1)}, u32[]{:S(2)}, u32[]{:S(2)}) collective-permute-start(bf16[48,1024]{1,0:T(8,128)(2,1)S(1)} %get-tuple-element.124), channel_id=1, source_target_pairs={{0,4},{1,5},{2,6},{3,7},{4,0},{5,1},{6,2},{7,3},{8,12},{9,13},{10,... | collective-permute-start | bytes 294920 | tf_op jit(solution)/shard_map/ppermute | solution.py:24
  99.9 10.1 %collective-permute-start.31 = (bf16[48,1024]{1,0:T(8,128)(2,1)S(1)}, bf16[48,1024]{1,0:T(8,128)(2,1)S(1)}, u32[]{:S(2)}, u32[]{:S(2)}) collective-permute-start(bf16[48,1024]{1,0:T(8,128)(2,1)S(1)} %get-tuple-element.125), channel_id=1, source_target_pairs={{0,6},{1,7},{2,4},{3,5},{4,2},{5,3},{6,0},{7,1},{8,14},{9,15},{10,... | collective-permute-start | bytes 294920 | tf_op jit(solution)/shard_map/ppermute | solution.py:24
  101.3 3.9 %collective-permute-start.32 = (bf16[16,1024]{1,0:T(8,128)(2,1)S(1)}, bf16[16,1024]{1,0:T(8,128)(2,1)S(1)}, u32[]{:S(2)}, u32[]{:S(2)}) collective-permute-start(bf16[16,1024]{1,0:T(8,128)(2,1)S(1)} %get-tuple-element.126), channel_id=1, source_target_pairs={{0,8},{8,0},{16,24},{24,16},{1,9},{9,1},{17,25},{25,17},{2,10},{10... | collective-permute-start | bytes 98312 | tf_op jit(solution)/shard_map/ppermute | solution.py:24
  101.7 4.6 %collective-permute-start.33 = (bf16[16,1024]{1,0:T(8,128)(2,1)S(1)}, bf16[16,1024]{1,0:T(8,128)(2,1)S(1)}, u32[]{:S(2)}, u32[]{:S(2)}) collective-permute-start(bf16[16,1024]{1,0:T(8,128)(2,1)S(1)} %get-tuple-element.127), channel_id=1, source_target_pairs={{0,16},{8,24},{16,0},{24,8},{1,17},{9,25},{17,1},{25,9},{2,18},{10... | collective-permute-start | bytes 98312 | tf_op jit(solution)/shard_map/ppermute | solution.py:24
  105.2 4.8 %collective-permute-start.34 = (bf16[16,1024]{1,0:T(8,128)(2,1)S(1)}, bf16[16,1024]{1,0:T(8,128)(2,1)S(1)}, u32[]{:S(2)}, u32[]{:S(2)}) collective-permute-start(bf16[16,1024]{1,0:T(8,128)(2,1)S(1)} %get-tuple-element.128), channel_id=1, source_target_pairs={{0,24},{8,16},{16,8},{24,0},{1,25},{9,17},{17,9},{25,1},{2,26},{10... | collective-permute-start | bytes 98312 | tf_op jit(solution)/shard_map/ppermute | solution.py:24
  110.0 1.5 collective-permute-start.35
  111.9 11.4 %collective-permute-start.36 = (bf16[192,1024]{1,0:T(8,128)(2,1)S(1)}, bf16[192,1024]{1,0:T(8,128)(2,1)S(1)}, u32[]{:S(2)}, u32[]{:S(2)}) collective-permute-start(bf16[192,1024]{1,0:T(8,128)(2,1)S(1)} %shard_map.177.refs_1_), channel_id=1, source_target_pairs={{0,8},{8,0},{16,24},{24,16},{1,9},{9,1},{17,25},{25,17},{2,10},{10... | collective-permute-start | bytes 1179656 | tf_op jit(solution)/shard_map/ppermute | solution.py:24
  112.4 11.7 %collective-permute-start.38 = (bf16[192,1024]{1,0:T(8,128)(2,1)S(1)}, bf16[192,1024]{1,0:T(8,128)(2,1)S(1)}, u32[]{:S(2)}, u32[]{:S(2)}) collective-permute-start(bf16[192,1024]{1,0:T(8,128)(2,1)S(1)} %shard_map.177.refs_1_), channel_id=1, source_target_pairs={{0,16},{8,24},{16,0},{24,8},{1,17},{9,25},{17,1},{25,9},{2,18},{10... | collective-permute-start | bytes 1179656 | tf_op jit(solution)/shard_map/ppermute | solution.py:24
  113.7 12.1 %copy-start.1 = (bf16[1024,1792]{1,0:T(8,128)(2,1)S(1)}, bf16[1024,1792]{1,0:T(8,128)(2,1)}, u32[]{:S(2)}) copy-start(bf16[1024,1792]{1,0:T(8,128)(2,1)} %copy-done) | copy-start | bytes 11010052
  113.7 12.1 %copy-start.3 = (bf16[1024,1792]{1,0:T(8,128)(2,1)S(1)}, bf16[1024,1792]{1,0:T(8,128)(2,1)}, u32[]{:S(2)}) copy-start(bf16[1024,1792]{1,0:T(8,128)(2,1)} %copy-done.2) | copy-start | bytes 11010052
  123.3 7.0 %collective-permute-start.37 = (bf16[96,1024]{1,0:T(8,128)(2,1)S(1)}, bf16[96,1024]{1,0:T(8,128)(2,1)S(1)}, u32[]{:S(2)}, u32[]{:S(2)}) collective-permute-start(bf16[96,1024]{1,0:T(8,128)(2,1)S(1)} %slice.19), channel_id=1, source_target_pairs={{0,16},{8,24},{16,0},{24,8},{1,17},{9,25},{17,1},{25,9},{2,18},{10... | collective-permute-start | bytes 589832 | tf_op jit(solution)/shard_map/ppermute | solution.py:24
  124.1 6.2 %collective-permute-start.39 = (bf16[96,1024]{1,0:T(8,128)(2,1)S(1)}, bf16[96,1024]{1,0:T(8,128)(2,1)S(1)}, u32[]{:S(2)}, u32[]{:S(2)}) collective-permute-start(bf16[96,1024]{1,0:T(8,128)(2,1)S(1)} %slice.20), channel_id=1, source_target_pairs={{0,8},{8,0},{16,24},{24,16},{1,9},{9,1},{17,25},{25,17},{2,10},{10... | collective-permute-start | bytes 589832 | tf_op jit(solution)/shard_map/ppermute | solution.py:24
  132.6 14.7 %copy-start.8 = (bf16[4096,8]{0,1:T(8,128)(2,1)S(1)}, bf16[4096,8]{0,1:T(8,128)(2,1)}, u32[]{:S(2)}) copy-start(bf16[4096,8]{0,1:T(8,128)(2,1)} %param.29) | copy-start | bytes 196612
  136.3 7.9 %collective-permute-start.42 = (bf16[48,2048]{1,0:T(8,128)(2,1)S(1)}, bf16[48,2048]{1,0:T(8,128)(2,1)S(1)}, u32[]{:S(2)}, u32[]{:S(2)}) collective-permute-start(bf16[48,2048]{1,0:T(8,128)(2,1)S(1)} %get-tuple-element.149), channel_id=1, source_target_pairs={{0,8},{8,0},{16,24},{24,16},{1,9},{9,1},{17,25},{25,17},{2,10},{10... | collective-permute-start | bytes 589832 | tf_op jit(solution)/shard_map/ppermute | solution.py:24
  137.9 7.5 %collective-permute-start.43 = (bf16[48,2048]{1,0:T(8,128)(2,1)S(1)}, bf16[48,2048]{1,0:T(8,128)(2,1)S(1)}, u32[]{:S(2)}, u32[]{:S(2)}) collective-permute-start(bf16[48,2048]{1,0:T(8,128)(2,1)S(1)} %get-tuple-element.150), channel_id=1, source_target_pairs={{0,16},{8,24},{16,0},{24,8},{1,17},{9,25},{17,1},{25,9},{2,18},{10... | collective-permute-start | bytes 589832 | tf_op jit(solution)/shard_map/ppermute | solution.py:24
  138.3 10.1 %collective-permute-start.40 = (bf16[48,2048]{1,0:T(8,128)(2,1)S(1)}, bf16[48,2048]{1,0:T(8,128)(2,1)S(1)}, u32[]{:S(2)}, u32[]{:S(2)}) collective-permute-start(bf16[48,2048]{1,0:T(8,128)(2,1)S(1)} %get-tuple-element.145), channel_id=1, source_target_pairs={{0,8},{8,0},{16,24},{24,16},{1,9},{9,1},{17,25},{25,17},{2,10},{10... | collective-permute-start | bytes 589832 | tf_op jit(solution)/shard_map/ppermute | solution.py:24
  139.7 9.5 %collective-permute-start.41 = (bf16[48,2048]{1,0:T(8,128)(2,1)S(1)}, bf16[48,2048]{1,0:T(8,128)(2,1)S(1)}, u32[]{:S(2)}, u32[]{:S(2)}) collective-permute-start(bf16[48,2048]{1,0:T(8,128)(2,1)S(1)} %get-tuple-element.146), channel_id=1, source_target_pairs={{0,16},{8,24},{16,0},{24,8},{1,17},{9,25},{17,1},{25,9},{2,18},{10... | collective-permute-start | bytes 589832 | tf_op jit(solution)/shard_map/ppermute | solution.py:24
  145.5 5.7 %collective-permute-start.44 = (bf16[48,2048]{1,0:T(8,128)(2,1)S(1)}, bf16[48,2048]{1,0:T(8,128)(2,1)S(1)}, u32[]{:S(2)}, u32[]{:S(2)}) collective-permute-start(bf16[48,2048]{1,0:T(8,128)(2,1)S(1)} %get-tuple-element.151), channel_id=1, source_target_pairs={{0,8},{8,0},{16,24},{24,16},{1,9},{9,1},{17,25},{25,17},{2,10},{10... | collective-permute-start | bytes 589832 | tf_op jit(solution)/shard_map/ppermute | solution.py:24
  146.4 5.7 %collective-permute-start.45 = (bf16[48,2048]{1,0:T(8,128)(2,1)S(1)}, bf16[48,2048]{1,0:T(8,128)(2,1)S(1)}, u32[]{:S(2)}, u32[]{:S(2)}) collective-permute-start(bf16[48,2048]{1,0:T(8,128)(2,1)S(1)} %get-tuple-element.152), channel_id=1, source_target_pairs={{0,16},{8,24},{16,0},{24,8},{1,17},{9,25},{17,1},{25,9},{2,18},{10... | collective-permute-start | bytes 589832 | tf_op jit(solution)/shard_map/ppermute | solution.py:24
  152.5 6.8 %collective-permute-start.46 = (bf16[48,1024]{1,0:T(8,128)(2,1)S(1)}, bf16[48,1024]{1,0:T(8,128)(2,1)S(1)}, u32[]{:S(2)}, u32[]{:S(2)}) collective-permute-start(bf16[48,1024]{1,0:T(8,128)(2,1)S(1)} %get-tuple-element.157), channel_id=1, source_target_pairs={{0,2},{1,3},{2,0},{3,1},{4,6},{5,7},{6,4},{7,5},{8,10},{9,11},{10,... | collective-permute-start | bytes 294920 | tf_op jit(solution)/shard_map/ppermute | solution.py:24
  153.1 6.2 %collective-permute-start.47 = (bf16[48,1024]{1,0:T(8,128)(2,1)S(1)}, bf16[48,1024]{1,0:T(8,128)(2,1)S(1)}, u32[]{:S(2)}, u32[]{:S(2)}) collective-permute-start(bf16[48,1024]{1,0:T(8,128)(2,1)S(1)} %get-tuple-element.158), channel_id=1, source_target_pairs={{0,4},{1,5},{2,6},{3,7},{4,0},{5,1},{6,2},{7,3},{8,12},{9,13},{10,... | collective-permute-start | bytes 294920 | tf_op jit(solution)/shard_map/ppermute | solution.py:24
  155.5 6.4 %collective-permute-start.48 = (bf16[48,1024]{1,0:T(8,128)(2,1)S(1)}, bf16[48,1024]{1,0:T(8,128)(2,1)S(1)}, u32[]{:S(2)}, u32[]{:S(2)}) collective-permute-start(bf16[48,1024]{1,0:T(8,128)(2,1)S(1)} %get-tuple-element.159), channel_id=1, source_target_pairs={{0,6},{1,7},{2,4},{3,5},{4,2},{5,3},{6,0},{7,1},{8,14},{9,15},{10,... | collective-permute-start | bytes 294920 | tf_op jit(solution)/shard_map/ppermute | solution.py:24
  162.0 1.5 collective-permute-start.49
  (3 other events, 3.8 us)

commit v6 on v5

--- a/solution.py
+++ b/solution.py
@@ -66,20 +66,33 @@
     return v / (1.0 + jnp.exp(-v))
 
 
-def norm_body(seq, place, tokens, gain, own, *sends):
-    values = tokens[...].astype(F32)
-    inverse = lax.rsqrt(jnp.mean(values * values, axis=-1, keepdims=True) + EPSILON)
-    own_width = own.shape[1]
+def norm_body(seq, place, tokens, gain, own, *refs):
+    sends, (held, factors, sems) = refs[: seq - 1], refs[seq - 1 :]
+    length, own_width = own.shape
     half = own_width // 2
     me, core = place[0], place[1]
-
-    def columns(start, width):
-        part = pl.ds(pl.multiple_of(start, 128), width)
-        return (tokens[:, part].astype(F32) * inverse * gain[:, part]).astype(BF16)
-
-    own[...] = columns(me * own_width, own_width)
-    for mask in range(1, seq):
-        sends[mask - 1][...] = columns((me ^ mask) * own_width + core * half, half)
+    parts = sems.shape[0] - 1
+    size = length // parts
+    copies = [pltpu.make_async_copy(gain, factors, sems.at[parts])]
+    for i in range(parts):
+        rows = pl.ds(i * size, size)
+        copies.append(pltpu.make_async_copy(tokens.at[rows], held.at[rows], sems.at[i]))
+    for copy in copies:
+        copy.start()
+    copies[0].wait()
+    for i in range(parts):
+        copies[1 + i].wait()
+        rows = slice(i * size, (i + 1) * size)
+        values = held[rows, :].astype(F32)
+        inverse = lax.rsqrt(jnp.mean(values * values, axis=-1, keepdims=True) + EPSILON)
+
+        def columns(start, width):
+            part = pl.ds(pl.multiple_of(start, 128), width)
+            return (held[rows, part].astype(F32) * inverse * factors[:, part]).astype(BF16)
+
+        own[rows, :] = columns(me * own_width, own_width)
+        for mask in range(1, seq):
+            sends[mask - 1][rows, :] = columns((me ^ mask) * own_width + core * half, half)
 
 
 def pass_body(*refs):
@@ -87,9 +100,15 @@
         out[...] = block[...]
 
 
+def weight_body(source, out, sem):
+    copy = pltpu.make_async_copy(source.at[:, pl.ds(0, out.shape[1])], out, sem)
+    copy.start()
+    copy.wait()
+
+
 def project(core, own, mine, other, source, branch, weight, sems):
     depth, channels = weight.shape
-    parts = sems.shape[0]
+    parts = sems.shape[0] if sems is not None else 0
     copies = []
     for i in range(parts):
         rows = pl.ds(i * (depth // parts), depth // parts)
@@ -101,7 +120,7 @@
     for rows, copy in copies:
         copy.wait()
         first = first + dot(own[:, rows], weight[rows, :])
-    yield first
+    yield first if copies else dot(own[...], weight[...])
     half = depth // 2
     near = weight[pl.ds(pl.multiple_of(core * half, half), half), :]
     far = weight[pl.ds(pl.multiple_of((1 - core) * half, half), half), :]
@@ -112,7 +131,7 @@
 def mixer_project_body(seq, cuts, place, *refs):
     own, mine, other = refs[0], refs[1:seq], refs[seq : 2 * seq - 1]
     refs = refs[2 * seq - 1 :]
-    (weight, routes), outs, (tails, held, sems) = refs[:2], refs[2:-3], refs[-3:]
+    (weight, routes), outs, tails = refs[:2], refs[2:-1], refs[-1]
     me = place[0]
     length = own.shape[0]
 
@@ -122,7 +141,7 @@
                 columns = out.shape[1]
                 out[rows, :] = values[:, index * columns : (index + 1) * columns].astype(out.dtype)
 
-    for mask, product in enumerate(project(place[1], own, mine, other, weight, 0, held, sems)):
+    for mask, product in enumerate(project(place[1], own, mine, other, None, 0, weight, None)):
         store(mask, slice(HALO, HALO + length), product)
         tails[mask] = product[length - HALO :, :]
     for mask in range(seq):
@@ -206,7 +225,7 @@
         return tuple(fresh), running
 
     zero = jnp.zeros((groups, lanes), F32)
-    state, running = lax.fori_loop(0, length, advance, ((zero,) * states, zero), unroll=4)
+    state, running = lax.fori_loop(0, length, advance, ((zero,) * states, zero), unroll=8)
     for n in range(states):
         final[n] = state[n].astype(BF16)
     upper = running.astype(BF16)
@@ -245,7 +264,7 @@
         scanned[t] = out
         return carry
 
-    lax.fori_loop(0, length, correct, 0, unroll=4)
+    lax.fori_loop(0, length, correct, 0, unroll=8)
     for group in range(groups):
         part = slice(group * lanes, (group + 1) * lanes)
         gate = gates[0][:, part]
@@ -619,11 +638,16 @@
     x_own, *x_send = kernel_call(
         functools.partial(norm_body, seq),
         [shape((length, width), BF16)] + [shape((length, width // 2), BF16)] * (seq - 1),
-        [SMEM, VMEM, VMEM],
+        [SMEM] + [pl.BlockSpec(memory_space=pltpu.HBM)] * 2,
+        [
+            pltpu.VMEM(tokens.shape, BF16),
+            pltpu.VMEM((1, model_width), F32),
+            pltpu.SemaphoreType.DMA((5,)),
+        ],
         flops=8 * length * model_width,
         moved=4 * length * model_width,
         limit=24,
-    )(place, tokens, norm_gain[None])
+    )(place, *in_hbm([tokens, norm_gain[None]]))
     x_mine = [partner(block, "seq", mask) for mask, block in zip(masks, x_send)]
     weight = in_hbm([in_weight.reshape(width, 2 * channels)])[0]
     x_passed = kernel_call(
@@ -634,6 +658,14 @@
     )(*x_mine)
     x_other = [partner(block, "expert", 1) for block in x_passed]
     x = [x_own, *x_mine, *x_other]
+    mixer_weight = kernel_call(
+        weight_body,
+        pltpu.VMEM((width, channels), BF16),
+        [pl.BlockSpec(memory_space=pltpu.HBM)],
+        [pltpu.SemaphoreType.DMA],
+        moved=4 * width * channels,
+        deps=x_passed[:1],
+    )(weight)
     lane_routes = jnp.transpose(routes).astype(F32)
     spread_routes = jnp.stack(
         [
@@ -649,10 +681,10 @@
         functools.partial(mixer_project_body, seq, cuts),
         [shape((HALO + length, channels), F32)]
         + [shape((HALO + length, channels // (2 if seq == 4 else 1)), BF16)] * (len(cuts) - 1),
-        in_specs,
-        [pltpu.VMEM((seq, HALO, channels), F32)] + scratch,
+        [SMEM] + [VMEM] * (2 * seq + 1),
+        [pltpu.VMEM((seq, HALO, channels), F32)],
         **cost,
-    )(place, *x, weight, spread_routes)
+    )(place, *x, mixer_weight, spread_routes)
     assert width <= channels and window <= channels and 2 * length <= rank_width
     own_tokens = lax.dynamic_slice_in_dim(tokens, expert * own_rows, own_rows, 0)
     side_own, *side_send = kernel_call(

time: 165 us -> 163 us (0.988)
  local copies, waits for them, and re-layouts: 10.2 us -> 8.27 us
    unnamed x36 -> x32, local copies, waits for them, and re-layouts: 9.2 us -> 7.24 us
    pallas_call x25 -> x26, Pallas kernels: 51.1 us -> 52.3 us  [kernel_call(): return lambda *operands: call(*operands, *deps)]
  transfers between devices with their start and end apart: 50 -> 50, of which waited for: 28 -> 25; matrix products, arithmetic and copies ran while one was open for 4% -> 4% of each run, Pallas kernels for 20% -> 21%
where the time goes in v6:
time: 163 us
  starting transfers between devices  54.3 us (33%)
  Pallas kernels  52.3 us (32%)
  waiting for transfers between devices  47.3 us (29%)
  local copies, waits for them, and re-layouts  8.27 us (5%)
    ppermute x50, starting transfers between devices, partner(): return lax.ppermute(block, axis, [(i, i ^ mask) for i in range(size)])  54.3 us
    pallas_call x26, Pallas kernels, kernel_call(): return lambda *operands: call(*operands, *deps)  52.3 us
    ppermute x50, waiting for transfers between devices, partner(): return lax.ppermute(block, axis, [(i, i ^ mask) for i in range(size)])  47.3 us
    unnamed x32, local copies, waits for them, and re-layouts  7.24 us
  transfers between devices with their start and end apart: 50, of which 25 were waited for; matrix products, arithmetic and copies ran while one was open for 4% of the time, Pallas kernels for 21%

profile of v6, /device:TPU:0, one launch (start us, length us, event | category | flops | bytes accessed | tf_op | source)
XLA Modules:
  0.0 162.9 jit_solution(17483390090105314822)
XLA Ops:
  0.1 2.2 %shard_map.163 = (bf16[128,1024]{1,0:T(8,128)(2,1)S(1)}, bf16[128,512]{1,0:T(8,128)(2,1)S(1)}, bf16[128,512]{1,0:T(8,128)(2,1)S(1)}, bf16[128,512]{1,0:T(8,128)(2,1)S(1)}) custom-call(s32[3]{0:T(128)S(1)} %pad_add_fusion.refs_0_, bf16[128,4096]{1,0:T(8,128)(2,1)} %refs_1_.2, f32[1,4096]{1,0:T(1,128)} %bitcast.42), custom_call_target="tpu_custom_call" | custom-call | flops 4194304 | bytes 2097152 | tf_op jit(solution)/shard_map/pallas_call | solution.py:58
  2.3 3.0 %collective-permute-start = (bf16[128,512]{1,0:T(8,128)(2,1)S(1)}, bf16[128,512]{1,0:T(8,128)(2,1)S(1)}, u32[]{:S(2)}, u32[]{:S(2)}) collective-permute-start(bf16[128,512]{1,0:T(8,128)(2,1)S(1)} %get-tuple-element.85), channel_id=1, source_target_pairs={{0,8},{8,0},{16,24},{24,16},{1,9},{9,1},{17,25},{25,17},{2,10},{10... | collective-permute-start | bytes 393224 | tf_op jit(solution)/shard_map/ppermute | solution.py:24
  5.3 1.5 collective-permute-start.1
  6.8 5.6 %copy.18 = bf16[128,8,2,1024]{3,1,2,0:T(8,128)(2,1)} copy(bf16[128,8,2,1024]{3,2,1,0:T(2,128)(2,1)} %bitcast.41) | data formatting | bytes 8388608
  13.9 1.6 shard_map.165.refs_8_
  15.5 1.9 %shard_map.166 = (f32[144,1024]{1,0:T(8,128)S(1)}, bf16[144,512]{1,0:T(8,128)(2,1)S(1)}, bf16[144,512]{1,0:T(8,128)(2,1)S(1)}, bf16[144,512]{1,0:T(8,128)(2,1)S(...) custom-call(s32[3]{0:T(128)S(1)} %pad_add_fusion.refs_0_, ...), custom_call_target="tpu_custom_call" | custom-call | flops 1073741824 | bytes 2097152 | tf_op jit(solution)/shard_map/pallas_call | solution.py:58
  17.4 1.4 collective-permute-start.8
  18.8 1.5 collective-permute-start.9
  22.5 3.2 %shard_map.167 = (f32[128,1024]{1,0:T(8,128)S(1)}, bf16[144,1024]{1,0:T(8,128)(2,1)S(1)}, bf16[144,1024]{1,0:T(8,128)(2,1)S(1)}, bf16[144,1024]{1,0:T(8,128)(2,1)S(1)}) custom-call(s32[3]{0:T(128)S(1)} %pad_add_fusion.refs_0_, bf16[128,1024]{1,0:T(8,128)(2,1)S(1)} %get-tuple-element.84.refs_1_, bf16[128,512]{1,0:T(8,128)(2,1)S(1)} %collective-permute-done.refs_0_.refs_2_, ...), custom_call_target="tpu_custom_call" | custom-call | flops 1073741824 | bytes 2097152 | tf_op jit(solution)/shard_map/pallas_call | solution.py:58
  25.8 1.4 collective-permute-start.10
  27.2 1.5 collective-permute-start.11
  28.8 2.3 %collective-permute-done.10.refs_3_ = bf16[144,512]{1,0:T(8,128)(2,1)S(1)} collective-permute-done((bf16[144,512]{1,0:T(8,128)(2,1)S(1)}, bf16[144,512]{1,0:T(8,128)(2,1)S(1)}, u32[]{:S(2)}, u32[]{:S(2)}) %collective-permute-start.10) | collective-permute-done | bytes 147488 | tf_op jit(solution)/shard_map/ppermute | solution.py:24
  31.0 1.4 collective-permute-done.11.refs_4_.refs_3_
  33.3 1.4 collective-permute-done.12
  34.7 1.6 %collective-permute-start.13 = (bf16[144,256]{1,0:T(8,128)(2,1)S(1)}, bf16[144,256]{1,0:T(8,128)(2,1)S(1)}, u32[]{:S(2)}, u32[]{:S(2)}) collective-permute-start(bf16[144,256]{1,0:T(8,128)(2,1)S(1)} %get-tuple-element.163), channel_id=1, source_target_pairs={{0,2},{1,3},{2,0},{3,1},{4,6},{5,7},{6,4},{7,5},{8,10},{9,11},{10,... | collective-permute-start | bytes 221192 | tf_op jit(solution)/shard_map/ppermute | solution.py:24
  36.9 1.5 collective-permute-start.20
  38.5 1.3 collective-permute-start.21
  39.8 2.6 %collective-permute-start.14 = (bf16[144,256]{1,0:T(8,128)(2,1)S(1)}, bf16[144,256]{1,0:T(8,128)(2,1)S(1)}, u32[]{:S(2)}, u32[]{:S(2)}) collective-permute-start(bf16[144,256]{1,0:T(8,128)(2,1)S(1)} %get-tuple-element.163), channel_id=1, source_target_pairs={{0,4},{1,5},{2,6},{3,7},{4,0},{5,1},{6,2},{7,3},{8,12},{9,13},{10,... | collective-permute-start | bytes 221192 | tf_op jit(solution)/shard_map/ppermute | solution.py:24
  42.7 4.2 %collective-permute-done.14 = bf16[144,256]{1,0:T(8,128)(2,1)S(1)} collective-permute-done((bf16[144,256]{1,0:T(8,128)(2,1)S(1)}, bf16[144,256]{1,0:T(8,128)(2,1)S(1)}, u32[]{:S(2)}, u32[]{:S(2)}) %collective-permute-start.14) | collective-permute-done | bytes 73760 | tf_op jit(solution)/shard_map/ppermute | solution.py:24
  46.9 1.6 collective-permute-done.15
  48.6 5.0 %shard_map.170 = (f32[128,8,128]{2,1,0:T(8,128)S(1)}, f32[128,8,128]{2,1,0:T(8,128)S(1)}, bf16[18,8,128]{2,1,0:T(8,128)(2,1)S(1)}) custom-call(f32[16,256]{1,0:T(8,128)S(1)} %slice.17.refs_0_.refs_1_, bf16[128,256]{1,0:T(8,128)(2,1)S(1)} %slice.22.refs_1_, bf16[128,1024]{1,0:T(8,128)(2,1)S(1)} %get-tuple-element.102.refs_2_.refs_8_, ...), custom_call_target="tpu_custom_call" | custom-call | tf_op jit(solution)/shard_map/pallas_call | solution.py:58
  54.4 1.5 collective-permute-start.17
  55.9 1.3 collective-permute-start.18
  58.4 2.4 %collective-permute-done.18.refs_4_ = bf16[18,8,128]{2,1,0:T(8,128)(2,1)S(1)} collective-permute-done((bf16[18,8,128]{2,1,0:T(8,128)(2,1)S(1)}, bf16[18,8,128]{2,1,0:T(8,128)(2,1)S(1)}, u32[]{:S(2)}, u32[]{:S(2)}) %collective-permute-start.18) | collective-permute-done | bytes 36896 | tf_op jit(solution)/shard_map/ppermute | solution.py:24
  60.8 3.6 %shard_map.171.refs_0_ = bf16[128,1024]{1,0:T(8,128)(2,1)S(1)} custom-call(s32[3]{0:T(128)S(1)} %pad_add_fusion.refs_0_, f32[16,256]{1,0:T(8,128)S(1)} %slice.17.refs_0_.refs_1_, bf16[18,8,128]{2,1,0:T(8,128)(2,1)S(1)} %collective-permute-done.16.refs_2_, bf16[18,8,128]{2,1,0:T(8,128)(2,1)S(1)} %collective-permute-done.17.refs_3_, ...), custom_call_target="tpu_custom_call" | custom-call | tf_op jit(solution)/shard_map/pallas_call | solution.py:58
  64.3 1.4 collective-permute-start.22
  66.3 1.6 collective-permute-start.24
  67.9 3.6 %collective-permute-done.22.refs_1_ = bf16[128,1024]{1,0:T(8,128)(2,1)S(1)} collective-permute-done((bf16[128,1024]{1,0:T(8,128)(2,1)S(1)}, bf16[128,1024]{1,0:T(8,128)(2,1)S(1)}, u32[]{:S(2)}, u32[]{:S(2)}) %collective-permute-start.22) | collective-permute-done | bytes 262176 | tf_op jit(solution)/shard_map/ppermute | solution.py:24
  71.5 3.9 %collective-permute-done.23.refs_2_ = bf16[128,1024]{1,0:T(8,128)(2,1)S(1)} collective-permute-done((bf16[128,1024]{1,0:T(8,128)(2,1)S(1)}, bf16[128,1024]{1,0:T(8,128)(2,1)S(1)}, u32[]{:S(2)}, u32[]{:S(2)}) %collective-permute-start.23) | collective-permute-done | bytes 262176 | tf_op jit(solution)/shard_map/ppermute | solution.py:24
  75.3 1.3 shard_map.172
  76.7 1.9 %collective-permute-done.25.refs_1_ = bf16[4,64,1024]{2,1,0:T(8,128)(2,1)S(1)} collective-permute-done((bf16[4,64,1024]{2,1,0:T(8,128)(2,1)S(1)}, bf16[4,64,1024]{2,1,0:T(8,128)(2,1)S(1)}, u32[]{:S(2)}, u32[]{:S(2)}) %collective-permute-start.25) | collective-permute-done | bytes 524320 | tf_op jit(solution)/shard_map/ppermute | solution.py:24
  78.7 1.3 collective-permute-start.26
  80.0 2.0 %collective-permute-start.27 = (bf16[64,1024]{1,0:T(8,128)(2,1)S(1)}, bf16[64,1024]{1,0:T(8,128)(2,1)S(1)}, u32[]{:S(2)}, u32[]{:S(2)}) collective-permute-start(bf16[64,1024]{1,0:T(8,128)(2,1)S(1)} %get-tuple-element.113), channel_id=1, source_target_pairs={{0,4},{1,5},{2,6},{3,7},{4,0},{5,1},{6,2},{7,3},{8,12},{9,13},{10,... | collective-permute-start | bytes 393224 | tf_op jit(solution)/shard_map/ppermute | solution.py:24
  82.0 1.4 collective-permute-start.28
  84.1 7.9 %shard_map.175 = (bf16[1024,1792]{1,0:T(8,128)(2,1)S(1)}, bf16[1024,1792]{1,0:T(8,128)(2,1)S(1)}, bf16[1024,1792]{1,0:T(8,128)(2,1)S(1)}, bf16[1024,1792]{1,0:T(...) custom-call(s32[3]{0:T(128)S(1)} %pad_add_fusion.refs_0_, ...), custom_call_target="tpu_custom_call" | custom-call | bytes 22020096 | tf_op jit(solution)/shard_map/pallas_call | solution.py:58
  93.9 1.1 copy-done.2
  95.0 1.1 collective-permute-start.29
  96.1 1.9 %collective-permute-start.30 = (bf16[48,1024]{1,0:T(8,128)(2,1)S(1)}, bf16[48,1024]{1,0:T(8,128)(2,1)S(1)}, u32[]{:S(2)}, u32[]{:S(2)}) collective-permute-start(bf16[48,1024]{1,0:T(8,128)(2,1)S(1)} %get-tuple-element.124), channel_id=1, source_target_pairs={{0,4},{1,5},{2,6},{3,7},{4,0},{5,1},{6,2},{7,3},{8,12},{9,13},{10,... | collective-permute-start | bytes 294920 | tf_op jit(solution)/shard_map/ppermute | solution.py:24
  98.0 1.4 collective-permute-start.31
  99.8 1.3 collective-permute-start.33
  101.1 2.2 %collective-permute-done.32.refs_4_.refs_5_ = bf16[16,1024]{1,0:T(8,128)(2,1)S(1)} collective-permute-done((bf16[16,1024]{1,0:T(8,128)(2,1)S(1)}, bf16[16,1024]{1,0:T(8,128)(2,1)S(1)}, u32[]{:S(2)}, u32[]{:S(2)}) %collective-permute-start.32) | collective-permute-done | bytes 32800 | tf_op jit(solution)/shard_map/ppermute | solution.py:24
  103.3 1.2 collective-permute-start.34
  104.5 3.6 %collective-permute-done.34.refs_6_.refs_7_ = bf16[16,1024]{1,0:T(8,128)(2,1)S(1)} collective-permute-done((bf16[16,1024]{1,0:T(8,128)(2,1)S(1)}, bf16[16,1024]{1,0:T(8,128)(2,1)S(1)}, u32[]{:S(2)}, u32[]{:S(2)}) %collective-permute-start.34) | collective-permute-done | bytes 32800 | tf_op jit(solution)/shard_map/ppermute | solution.py:24
  108.2 1.4 collective-permute-done.35.refs_4_
  110.5 1.3 collective-permute-start.38
  111.8 9.6 %shard_map.179 = (f32[192,1792]{1,0:T(8,128)S(1)}, f32[192,1792]{1,0:T(8,128)S(1)}, f32[192,128]{1,0:T(8,128)S(1)}, bf16[1024,1792]{1,0:T(8,128)(2,1)S(1)}, bf16...) custom-call(s32[3]{0:T(128)S(1)} %pad_add_fusion.refs_0_, ...), custom_call_target="tpu_custom_call" | custom-call | flops 1409286144 | bytes 7340032 | tf_op jit(solution)/shard_map/pallas_call | solution.py:58
  122.2 1.7 %collective-permute-start.39 = (bf16[96,1024]{1,0:T(8,128)(2,1)S(1)}, bf16[96,1024]{1,0:T(8,128)(2,1)S(1)}, u32[]{:S(2)}, u32[]{:S(2)}) collective-permute-start(bf16[96,1024]{1,0:T(8,128)(2,1)S(1)} %slice.20), channel_id=1, source_target_pairs={{0,8},{8,0},{16,24},{24,16},{1,9},{9,1},{17,25},{25,17},{2,10},{10... | collective-permute-start | bytes 589832 | tf_op jit(solution)/shard_map/ppermute | solution.py:24
  123.9 2.2 %shard_map.180 = (f32[192,1792]{1,0:T(8,128)S(1)}, f32[192,1792]{1,0:T(8,128)S(1)}, f32[192,128]{1,0:T(8,128)S(1)}) custom-call(s32[3]{0:T(128)S(1)} %pad_add_fusion.refs_0_, bf16[192,1024]{1,0:T(8,128)(2,1)S(1)} %collective-permute-done.36.refs_1_, f32[1,4096]{1,0:T(1,128)S(1)} %bitcast.30, bf16[1024,1792]{1,0:T(8,128)(2,1)S(1)} %copy-done.1, ...), custom_call_target="tpu_custom_call" | custom-call | flops 1409286144 | bytes 7340032 | tf_op jit(solution)/shard_map/pallas_call | solution.py:58
  126.1 2.2 %shard_map.181 = (f32[192,1792]{1,0:T(8,128)S(1)}, f32[192,1792]{1,0:T(8,128)S(1)}, f32[192,128]{1,0:T(8,128)S(1)}) custom-call(s32[3]{0:T(128)S(1)} %pad_add_fusion.refs_0_, bf16[192,1024]{1,0:T(8,128)(2,1)S(1)} %collective-permute-done.38.refs_1_, f32[1,4096]{1,0:T(1,128)S(1)} %bitcast.31, bf16[1024,1792]{1,0:T(8,128)(2,1)S(1)} %get-tuple-element.120.refs_14_.refs_3_, ...), custom_call_target="tpu_custom_call" | custom-call | flops 1409286144 | bytes 7340032 | tf_op jit(solution)/shard_map/pallas_call | solution.py:58
  128.4 2.3 %shard_map.182.refs_1_ = bf16[192,1792]{1,0:T(8,128)(2,1)S(1)} custom-call(s32[3]{0:T(128)S(1)} %pad_add_fusion.refs_0_, bf16[96,1024]{1,0:T(8,128)(2,1)S(1)} %collective-permute-done.37.refs_1_, bf16[96,1024]{1,0:T(8,128)(2,1)S(1)} %collective-permute-done.39.refs_2_, f32[1,4096]{1,0:T(1,128)S(1)} %bitcast.32, ...), custom_call_target="tpu_custom_call" | custom-call | flops 1409286144 | bytes 7340032 | tf_op jit(solution)/shard_map/pallas_call | solution.py:58
  130.7 3.7 %shard_map.183 = (bf16[48,4096]{1,0:T(8,128)(2,1)S(1)}, bf16[48,2048]{1,0:T(8,128)(2,1)S(1)}, bf16[48,2048]{1,0:T(8,128)(2,1)S(1)}, bf16[48,2048]{1,0:T(8,128)(2...) custom-call(s32[3]{0:T(128)S(1)} %pad_add_fusion.refs_0_, ...), custom_call_target="tpu_custom_call" | custom-call | flops 2818572288 | bytes 14680064 | tf_op jit(solution)/shard_map/pallas_call | solution.py:58
  134.4 1.7 %collective-permute-start.42 = (bf16[48,2048]{1,0:T(8,128)(2,1)S(1)}, bf16[48,2048]{1,0:T(8,128)(2,1)S(1)}, u32[]{:S(2)}, u32[]{:S(2)}) collective-permute-start(bf16[48,2048]{1,0:T(8,128)(2,1)S(1)} %get-tuple-element.149), channel_id=1, source_target_pairs={{0,8},{8,0},{16,24},{24,16},{1,9},{9,1},{17,25},{25,17},{2,10},{10... | collective-permute-start | bytes 589832 | tf_op jit(solution)/shard_map/ppermute | solution.py:24
  136.4 1.3 collective-permute-start.40
  138.5 3.8 %collective-permute-done.42.refs_2_ = bf16[48,2048]{1,0:T(8,128)(2,1)S(1)} collective-permute-done((bf16[48,2048]{1,0:T(8,128)(2,1)S(1)}, bf16[48,2048]{1,0:T(8,128)(2,1)S(1)}, u32[]{:S(2)}, u32[]{:S(2)}) %collective-permute-start.42) | collective-permute-done | bytes 196640 | tf_op jit(solution)/shard_map/ppermute | solution.py:24
  142.3 1.2 collective-permute-done.43.refs_3_
  144.5 0.9 collective-permute-start.45
  145.4 1.0 shard_map.185
  147.3 2.1 %collective-permute-done.44.refs_3_ = bf16[48,2048]{1,0:T(8,128)(2,1)S(1)} collective-permute-done((bf16[48,2048]{1,0:T(8,128)(2,1)S(1)}, bf16[48,2048]{1,0:T(8,128)(2,1)S(1)}, u32[]{:S(2)}, u32[]{:S(2)}) %collective-permute-start.44) | collective-permute-done | bytes 196640 | tf_op jit(solution)/shard_map/ppermute | solution.py:24
  151.2 2.4 %collective-permute-start.47 = (bf16[48,1024]{1,0:T(8,128)(2,1)S(1)}, bf16[48,1024]{1,0:T(8,128)(2,1)S(1)}, u32[]{:S(2)}, u32[]{:S(2)}) collective-permute-start(bf16[48,1024]{1,0:T(8,128)(2,1)S(1)} %get-tuple-element.158), channel_id=1, source_target_pairs={{0,4},{1,5},{2,6},{3,7},{4,0},{5,1},{6,2},{7,3},{8,12},{9,13},{10,... | collective-permute-start | bytes 294920 | tf_op jit(solution)/shard_map/ppermute | solution.py:24
  153.7 1.4 collective-permute-start.48
  155.0 2.3 %collective-permute-done.46.refs_1_ = bf16[48,1024]{1,0:T(8,128)(2,1)S(1)} collective-permute-done((bf16[48,1024]{1,0:T(8,128)(2,1)S(1)}, bf16[48,1024]{1,0:T(8,128)(2,1)S(1)}, u32[]{:S(2)}, u32[]{:S(2)}) %collective-permute-start.46) | collective-permute-done | bytes 98336 | tf_op jit(solution)/shard_map/ppermute | solution.py:24
  157.4 2.7 %collective-permute-done.48.refs_3_ = bf16[48,1024]{1,0:T(8,128)(2,1)S(1)} collective-permute-done((bf16[48,1024]{1,0:T(8,128)(2,1)S(1)}, bf16[48,1024]{1,0:T(8,128)(2,1)S(1)}, u32[]{:S(2)}, u32[]{:S(2)}) %collective-permute-start.48) | collective-permute-done | bytes 98336 | tf_op jit(solution)/shard_map/ppermute | solution.py:24
  160.2 1.4 collective-permute-done.49.refs_4_
  161.6 1.3 shard_map.188
  (106 shorter events, 17.7 us)
Async XLA Ops:
  2.3 10.2 %collective-permute-start = (bf16[128,512]{1,0:T(8,128)(2,1)S(1)}, bf16[128,512]{1,0:T(8,128)(2,1)S(1)}, u32[]{:S(2)}, u32[]{:S(2)}) collective-permute-start(bf16[128,512]{1,0:T(8,128)(2,1)S(1)} %get-tuple-element.85), channel_id=1, source_target_pairs={{0,8},{8,0},{16,24},{24,16},{1,9},{9,1},{17,25},{25,17},{2,10},{10... | collective-permute-start | bytes 393224 | tf_op jit(solution)/shard_map/ppermute | solution.py:24
  5.3 7.8 %collective-permute-start.1 = (bf16[128,512]{1,0:T(8,128)(2,1)S(1)}, bf16[128,512]{1,0:T(8,128)(2,1)S(1)}, u32[]{:S(2)}, u32[]{:S(2)}) collective-permute-start(bf16[128,512]{1,0:T(8,128)(2,1)S(1)} %get-tuple-element.86), channel_id=1, source_target_pairs={{0,16},{8,24},{16,0},{24,8},{1,17},{9,25},{17,1},{25,9},{2,18},{10... | collective-permute-start | bytes 393224 | tf_op jit(solution)/shard_map/ppermute | solution.py:24
  6.8 6.3 %collective-permute-start.2 = (bf16[128,512]{1,0:T(8,128)(2,1)S(1)}, bf16[128,512]{1,0:T(8,128)(2,1)S(1)}, u32[]{:S(2)}, u32[]{:S(2)}) collective-permute-start(bf16[128,512]{1,0:T(8,128)(2,1)S(1)} %get-tuple-element.87), channel_id=1, source_target_pairs={{0,24},{8,16},{16,8},{24,0},{1,25},{9,17},{17,9},{25,1},{2,26},{10... | collective-permute-start | bytes 393224 | tf_op jit(solution)/shard_map/ppermute | solution.py:24
  6.8 5.6 %copy-start.14 = (s32[16,2]{0,1:T(2,128)S(1)}, s32[16,2]{0,1:T(2,128)}, u32[]{:S(2)}) copy-start(s32[16,2]{0,1:T(2,128)} %param.30) | copy-start | bytes 388
  13.1 2.4 %collective-permute-start.3 = (bf16[128,512]{1,0:T(8,128)(2,1)S(1)}, bf16[128,512]{1,0:T(8,128)(2,1)S(1)}, u32[]{:S(2)}, u32[]{:S(2)}) collective-permute-start(bf16[128,512]{1,0:T(8,128)(2,1)S(1)} %get-tuple-element.88.refs_1_), channel_id=1, source_target_pairs={{0,1},{1,0},{2,3},{3,2},{4,5},{5,4},{6,7},{7,6},{8,9},{9,8},{10,11... | collective-permute-start | bytes 393224 | tf_op jit(solution)/shard_map/ppermute | solution.py:24
  13.2 2.3 %collective-permute-start.4 = (bf16[128,512]{1,0:T(8,128)(2,1)S(1)}, bf16[128,512]{1,0:T(8,128)(2,1)S(1)}, u32[]{:S(2)}, u32[]{:S(2)}) collective-permute-start(bf16[128,512]{1,0:T(8,128)(2,1)S(1)} %get-tuple-element.89), channel_id=1, source_target_pairs={{0,1},{1,0},{2,3},{3,2},{4,5},{5,4},{6,7},{7,6},{8,9},{9,8},{10,11... | collective-permute-start | bytes 393224 | tf_op jit(solution)/shard_map/ppermute | solution.py:24
  13.7 1.8 %collective-permute-start.5 = (bf16[128,512]{1,0:T(8,128)(2,1)S(1)}, bf16[128,512]{1,0:T(8,128)(2,1)S(1)}, u32[]{:S(2)}, u32[]{:S(2)}) collective-permute-start(bf16[128,512]{1,0:T(8,128)(2,1)S(1)} %get-tuple-element.90), channel_id=1, source_target_pairs={{0,1},{1,0},{2,3},{3,2},{4,5},{5,4},{6,7},{7,6},{8,9},{9,8},{10,11... | collective-permute-start | bytes 393224 | tf_op jit(solution)/shard_map/ppermute | solution.py:24
  17.4 15.0 %copy-start.4 = (bf16[1024,288]{0,1:T(8,128)(2,1)S(1)}, bf16[1024,288]{0,1:T(8,128)(2,1)}, u32[]{:S(2)}) copy-start(bf16[1024,288]{0,1:T(8,128)(2,1)} %param.22) | copy-start | bytes 1769476
  17.4 15.0 %copy-start.8 = (f32[4,1024]{1,0:T(4,128)S(1)}, f32[4,1024]{1,0:T(4,128)}, u32[]{:S(2)}) copy-start(f32[4,1024]{1,0:T(4,128)} %refs_5_.2) | copy-start | bytes 49156
  17.4 15.0 %copy-start.9 = (f32[1024]{0:T(1024)S(1)}, f32[1024]{0:T(1024)}, u32[]{:S(2)}) copy-start(f32[1024]{0:T(1024)} %param.21) | copy-start | bytes 12292
  17.4 8.3 %collective-permute-start.8 = (bf16[144,512]{1,0:T(8,128)(2,1)S(1)}, bf16[144,512]{1,0:T(8,128)(2,1)S(1)}, u32[]{:S(2)}, u32[]{:S(2)}) collective-permute-start(bf16[144,512]{1,0:T(8,128)(2,1)S(1)} %get-tuple-element.96), channel_id=1, source_target_pairs={{0,8},{8,0},{16,24},{24,16},{1,9},{9,1},{17,25},{25,17},{2,10},{10... | collective-permute-start | bytes 442376 | tf_op jit(solution)/shard_map/ppermute | solution.py:24
  18.8 6.9 %collective-permute-start.9 = (bf16[144,512]{1,0:T(8,128)(2,1)S(1)}, bf16[144,512]{1,0:T(8,128)(2,1)S(1)}, u32[]{:S(2)}, u32[]{:S(2)}) collective-permute-start(bf16[144,512]{1,0:T(8,128)(2,1)S(1)} %get-tuple-element.97), channel_id=1, source_target_pairs={{0,16},{8,24},{16,0},{24,8},{1,17},{9,25},{17,1},{25,9},{2,18},{10... | collective-permute-start | bytes 442376 | tf_op jit(solution)/shard_map/ppermute | solution.py:24
  21.3 7.5 %collective-permute-start.6 = (bf16[144,512]{1,0:T(8,128)(2,1)S(1)}, bf16[144,512]{1,0:T(8,128)(2,1)S(1)}, u32[]{:S(2)}, u32[]{:S(2)}) collective-permute-start(bf16[144,512]{1,0:T(8,128)(2,1)S(1)} %get-tuple-element.92), channel_id=1, source_target_pairs={{0,8},{8,0},{16,24},{24,16},{1,9},{9,1},{17,25},{25,17},{2,10},{10... | collective-permute-start | bytes 442376 | tf_op jit(solution)/shard_map/ppermute | solution.py:24
  22.0 20.7 %copy-start.13 = (f32[1024,16]{0,1:T(8,128)S(1)}, f32[1024,16]{0,1:T(8,128)}, u32[]{:S(2)}) copy-start(f32[1024,16]{0,1:T(8,128)} %param.25) | copy-start | bytes 196612
  22.0 26.6 %copy-start.5 = (bf16[256,1024]{1,0:T(8,128)(2,1)S(1)}, bf16[256,1024]{1,0:T(8,128)(2,1)}, u32[]{:S(2)}) copy-start(bf16[256,1024]{1,0:T(8,128)(2,1)} %refs_3_.1) | copy-start | bytes 1572868
  22.0 26.6 %copy-start.10 = (f32[1024]{0:T(1024)S(1)}, f32[1024]{0:T(1024)}, u32[]{:S(2)}) copy-start(f32[1024]{0:T(1024)} %param.24) | copy-start | bytes 12292
  22.0 6.8 %collective-permute-start.7 = (bf16[144,512]{1,0:T(8,128)(2,1)S(1)}, bf16[144,512]{1,0:T(8,128)(2,1)S(1)}, u32[]{:S(2)}, u32[]{:S(2)}) collective-permute-start(bf16[144,512]{1,0:T(8,128)(2,1)S(1)} %get-tuple-element.93), channel_id=1, source_target_pairs={{0,16},{8,24},{16,0},{24,8},{1,17},{9,25},{17,1},{25,9},{2,18},{10... | collective-permute-start | bytes 442376 | tf_op jit(solution)/shard_map/ppermute | solution.py:24
  25.7 35.1 %copy-start.11 = (f32[1024]{0:T(1024)S(1)}, f32[1024]{0:T(1024)}, u32[]{:S(2)}) copy-start(f32[1024]{0:T(1024)} %param.26) | copy-start | bytes 12292
  25.8 5.2 %collective-permute-start.10 = (bf16[144,512]{1,0:T(8,128)(2,1)S(1)}, bf16[144,512]{1,0:T(8,128)(2,1)S(1)}, u32[]{:S(2)}, u32[]{:S(2)}) collective-permute-start(bf16[144,512]{1,0:T(8,128)(2,1)S(1)} %get-tuple-element.99), channel_id=1, source_target_pairs={{0,8},{8,0},{16,24},{24,16},{1,9},{9,1},{17,25},{25,17},{2,10},{10... | collective-permute-start | bytes 442376 | tf_op jit(solution)/shard_map/ppermute | solution.py:24
  27.2 5.1 %collective-permute-start.11 = (bf16[144,512]{1,0:T(8,128)(2,1)S(1)}, bf16[144,512]{1,0:T(8,128)(2,1)S(1)}, u32[]{:S(2)}, u32[]{:S(2)}) collective-permute-start(bf16[144,512]{1,0:T(8,128)(2,1)S(1)} %get-tuple-element.100), channel_id=1, source_target_pairs={{0,16},{8,24},{16,0},{24,8},{1,17},{9,25},{17,1},{25,9},{2,18},{10... | collective-permute-start | bytes 442376 | tf_op jit(solution)/shard_map/ppermute | solution.py:24
  32.4 42.9 %copy-start.12 = (bf16[1024,1024]{1,0:T(8,128)(2,1)S(1)}, bf16[1024,1024]{1,0:T(8,128)(2,1)}, u32[]{:S(2)}) copy-start(bf16[1024,1024]{1,0:T(8,128)(2,1)} %refs_4_.1) | copy-start | bytes 6291460
  33.2 1.4 collective-permute-start.12
  34.7 7.7 %collective-permute-start.13 = (bf16[144,256]{1,0:T(8,128)(2,1)S(1)}, bf16[144,256]{1,0:T(8,128)(2,1)S(1)}, u32[]{:S(2)}, u32[]{:S(2)}) collective-permute-start(bf16[144,256]{1,0:T(8,128)(2,1)S(1)} %get-tuple-element.163), channel_id=1, source_target_pairs={{0,2},{1,3},{2,0},{3,1},{4,6},{5,7},{6,4},{7,5},{8,10},{9,11},{10,... | collective-permute-start | bytes 221192 | tf_op jit(solution)/shard_map/ppermute | solution.py:24
  36.3 19.6 %collective-permute-start.19 = (bf16[144,1024]{1,0:T(8,128)(2,1)S(1)}, bf16[144,1024]{1,0:T(8,128)(2,1)S(1)}, u32[]{:S(2)}, u32[]{:S(2)}) collective-permute-start(bf16[144,1024]{1,0:T(8,128)(2,1)S(1)} %get-tuple-element.106), channel_id=1, source_target_pairs={{0,8},{8,0},{16,24},{24,16},{1,9},{9,1},{17,25},{25,17},{2,10},{10... | collective-permute-start | bytes 884744 | tf_op jit(solution)/shard_map/ppermute | solution.py:24
  36.9 20.3 %collective-permute-start.20 = (bf16[144,1024]{1,0:T(8,128)(2,1)S(1)}, bf16[144,1024]{1,0:T(8,128)(2,1)S(1)}, u32[]{:S(2)}, u32[]{:S(2)}) collective-permute-start(bf16[144,1024]{1,0:T(8,128)(2,1)S(1)} %get-tuple-element.107), channel_id=1, source_target_pairs={{0,16},{8,24},{16,0},{24,8},{1,17},{9,25},{17,1},{25,9},{2,18},{10... | collective-permute-start | bytes 884744 | tf_op jit(solution)/shard_map/ppermute | solution.py:24
  38.5 18.8 %collective-permute-start.21 = (bf16[144,1024]{1,0:T(8,128)(2,1)S(1)}, bf16[144,1024]{1,0:T(8,128)(2,1)S(1)}, u32[]{:S(2)}, u32[]{:S(2)}) collective-permute-start(bf16[144,1024]{1,0:T(8,128)(2,1)S(1)} %get-tuple-element.108), channel_id=1, source_target_pairs={{0,24},{8,16},{16,8},{24,0},{1,25},{9,17},{17,9},{25,1},{2,26},{10... | collective-permute-start | bytes 884744 | tf_op jit(solution)/shard_map/ppermute | solution.py:24
  39.8 7.1 %collective-permute-start.14 = (bf16[144,256]{1,0:T(8,128)(2,1)S(1)}, bf16[144,256]{1,0:T(8,128)(2,1)S(1)}, u32[]{:S(2)}, u32[]{:S(2)}) collective-permute-start(bf16[144,256]{1,0:T(8,128)(2,1)S(1)} %get-tuple-element.163), channel_id=1, source_target_pairs={{0,4},{1,5},{2,6},{3,7},{4,0},{5,1},{6,2},{7,3},{8,12},{9,13},{10,... | collective-permute-start | bytes 221192 | tf_op jit(solution)/shard_map/ppermute | solution.py:24
  42.4 6.2 %collective-permute-start.15 = (bf16[144,256]{1,0:T(8,128)(2,1)S(1)}, bf16[144,256]{1,0:T(8,128)(2,1)S(1)}, u32[]{:S(2)}, u32[]{:S(2)}) collective-permute-start(bf16[144,256]{1,0:T(8,128)(2,1)S(1)} %get-tuple-element.163), channel_id=1, source_target_pairs={{0,6},{1,7},{2,4},{3,5},{4,2},{5,3},{6,0},{7,1},{8,14},{9,15},{10,... | collective-permute-start | bytes 221192 | tf_op jit(solution)/shard_map/ppermute | solution.py:24
  53.7 4.0 %collective-permute-start.16 = (bf16[18,8,128]{2,1,0:T(8,128)(2,1)S(1)}, bf16[18,8,128]{2,1,0:T(8,128)(2,1)S(1)}, u32[]{:S(2)}, u32[]{:S(2)}) collective-permute-start(bf16[18,8,128]{2,1,0:T(8,128)(2,1)S(1)} %get-tuple-element.103), channel_id=1, source_target_pairs={{0,8},{8,0},{16,24},{24,16},{1,9},{9,1},{17,25},{25,17},{2,10},{10... | collective-permute-start | bytes 110600 | tf_op jit(solution)/shard_map/ppermute | solution.py:24
  54.4 4.0 %collective-permute-start.17 = (bf16[18,8,128]{2,1,0:T(8,128)(2,1)S(1)}, bf16[18,8,128]{2,1,0:T(8,128)(2,1)S(1)}, u32[]{:S(2)}, u32[]{:S(2)}) collective-permute-start(bf16[18,8,128]{2,1,0:T(8,128)(2,1)S(1)} %get-tuple-element.103), channel_id=1, source_target_pairs={{0,16},{8,24},{16,0},{24,8},{1,17},{9,25},{17,1},{25,9},{2,18},{10... | collective-permute-start | bytes 110600 | tf_op jit(solution)/shard_map/ppermute | solution.py:24
  55.9 4.9 %collective-permute-start.18 = (bf16[18,8,128]{2,1,0:T(8,128)(2,1)S(1)}, bf16[18,8,128]{2,1,0:T(8,128)(2,1)S(1)}, u32[]{:S(2)}, u32[]{:S(2)}) collective-permute-start(bf16[18,8,128]{2,1,0:T(8,128)(2,1)S(1)} %get-tuple-element.103), channel_id=1, source_target_pairs={{0,24},{8,16},{16,8},{24,0},{1,25},{9,17},{17,9},{25,1},{2,26},{10... | collective-permute-start | bytes 110600 | tf_op jit(solution)/shard_map/ppermute | solution.py:24
  64.3 7.1 %collective-permute-start.22 = (bf16[128,1024]{1,0:T(8,128)(2,1)S(1)}, bf16[128,1024]{1,0:T(8,128)(2,1)S(1)}, u32[]{:S(2)}, u32[]{:S(2)}) collective-permute-start(bf16[128,1024]{1,0:T(8,128)(2,1)S(1)} %shard_map.171.refs_0_), channel_id=1, source_target_pairs={{0,8},{8,0},{16,24},{24,16},{1,9},{9,1},{17,25},{25,17},{2,10},{10... | collective-permute-start | bytes 786440 | tf_op jit(solution)/shard_map/ppermute | solution.py:24
  65.8 9.5 %collective-permute-start.23 = (bf16[128,1024]{1,0:T(8,128)(2,1)S(1)}, bf16[128,1024]{1,0:T(8,128)(2,1)S(1)}, u32[]{:S(2)}, u32[]{:S(2)}) collective-permute-start(bf16[128,1024]{1,0:T(8,128)(2,1)S(1)} %shard_map.171.refs_0_), channel_id=1, source_target_pairs={{0,16},{8,24},{16,0},{24,8},{1,17},{9,25},{17,1},{25,9},{2,18},{10... | collective-permute-start | bytes 786440 | tf_op jit(solution)/shard_map/ppermute | solution.py:24
  66.3 9.0 %collective-permute-start.24 = (bf16[128,1024]{1,0:T(8,128)(2,1)S(1)}, bf16[128,1024]{1,0:T(8,128)(2,1)S(1)}, u32[]{:S(2)}, u32[]{:S(2)}) collective-permute-start(bf16[128,1024]{1,0:T(8,128)(2,1)S(1)} %shard_map.171.refs_0_), channel_id=1, source_target_pairs={{0,24},{8,16},{16,8},{24,0},{1,25},{9,17},{17,9},{25,1},{2,26},{10... | collective-permute-start | bytes 786440 | tf_op jit(solution)/shard_map/ppermute | solution.py:24
  76.6 2.0 %collective-permute-start.25 = (bf16[4,64,1024]{2,1,0:T(8,128)(2,1)S(1)}, bf16[4,64,1024]{2,1,0:T(8,128)(2,1)S(1)}, u32[]{:S(2)}, u32[]{:S(2)}) collective-permute-start(bf16[4,64,1024]{2,1,0:T(8,128)(2,1)S(1)} %get-tuple-element.110), channel_id=1, source_target_pairs={{0,1},{1,0},{2,3},{3,2},{4,5},{5,4},{6,7},{7,6},{8,9},{9,8},{10,11... | collective-permute-start | bytes 1572872 | tf_op jit(solution)/shard_map/ppermute | solution.py:24
  78.7 13.4 %collective-permute-start.26 = (bf16[64,1024]{1,0:T(8,128)(2,1)S(1)}, bf16[64,1024]{1,0:T(8,128)(2,1)S(1)}, u32[]{:S(2)}, u32[]{:S(2)}) collective-permute-start(bf16[64,1024]{1,0:T(8,128)(2,1)S(1)} %get-tuple-element.112), channel_id=1, source_target_pairs={{0,2},{1,3},{2,0},{3,1},{4,6},{5,7},{6,4},{7,5},{8,10},{9,11},{10,... | collective-permute-start | bytes 393224 | tf_op jit(solution)/shard_map/ppermute | solution.py:24
  80.0 12.1 %collective-permute-start.27 = (bf16[64,1024]{1,0:T(8,128)(2,1)S(1)}, bf16[64,1024]{1,0:T(8,128)(2,1)S(1)}, u32[]{:S(2)}, u32[]{:S(2)}) collective-permute-start(bf16[64,1024]{1,0:T(8,128)(2,1)S(1)} %get-tuple-element.113), channel_id=1, source_target_pairs={{0,4},{1,5},{2,6},{3,7},{4,0},{5,1},{6,2},{7,3},{8,12},{9,13},{10,... | collective-permute-start | bytes 393224 | tf_op jit(solution)/shard_map/ppermute | solution.py:24
  82.0 10.6 %collective-permute-start.28 = (bf16[64,1024]{1,0:T(8,128)(2,1)S(1)}, bf16[64,1024]{1,0:T(8,128)(2,1)S(1)}, u32[]{:S(2)}, u32[]{:S(2)}) collective-permute-start(bf16[64,1024]{1,0:T(8,128)(2,1)S(1)} %get-tuple-element.114), channel_id=1, source_target_pairs={{0,6},{1,7},{2,4},{3,5},{4,2},{5,3},{6,0},{7,1},{8,14},{9,15},{10,... | collective-permute-start | bytes 393224 | tf_op jit(solution)/shard_map/ppermute | solution.py:24
  92.1 2.9 %copy-start.2 = (bf16[1024,1792]{1,0:T(8,128)(2,1)}, bf16[1024,1792]{1,0:T(8,128)(2,1)S(1)}, u32[]{:S(2)}) copy-start(bf16[1024,1792]{1,0:T(8,128)(2,1)S(1)} %get-tuple-element.119.refs_13_.refs_4_) | copy-start | bytes 11010052
  92.6 19.2 %copy-start.6 = (f32[4096]{0:T(1024)S(1)}, f32[4096]{0:T(1024)}, u32[]{:S(2)}) copy-start(f32[4096]{0:T(1024)} %param.28) | copy-start | bytes 49156
  95.0 13.1 %collective-permute-start.29 = (bf16[48,1024]{1,0:T(8,128)(2,1)S(1)}, bf16[48,1024]{1,0:T(8,128)(2,1)S(1)}, u32[]{:S(2)}, u32[]{:S(2)}) collective-permute-start(bf16[48,1024]{1,0:T(8,128)(2,1)S(1)} %get-tuple-element.123), channel_id=1, source_target_pairs={{0,2},{1,3},{2,0},{3,1},{4,6},{5,7},{6,4},{7,5},{8,10},{9,11},{10,... | collective-permute-start | bytes 294920 | tf_op jit(solution)/shard_map/ppermute | solution.py:24
  96.1 12.0 %collective-permute-start.30 = (bf16[48,1024]{1,0:T(8,128)(2,1)S(1)}, bf16[48,1024]{1,0:T(8,128)(2,1)S(1)}, u32[]{:S(2)}, u32[]{:S(2)}) collective-permute-start(bf16[48,1024]{1,0:T(8,128)(2,1)S(1)} %get-tuple-element.124), channel_id=1, source_target_pairs={{0,4},{1,5},{2,6},{3,7},{4,0},{5,1},{6,2},{7,3},{8,12},{9,13},{10,... | collective-permute-start | bytes 294920 | tf_op jit(solution)/shard_map/ppermute | solution.py:24
  98.0 10.1 %collective-permute-start.31 = (bf16[48,1024]{1,0:T(8,128)(2,1)S(1)}, bf16[48,1024]{1,0:T(8,128)(2,1)S(1)}, u32[]{:S(2)}, u32[]{:S(2)}) collective-permute-start(bf16[48,1024]{1,0:T(8,128)(2,1)S(1)} %get-tuple-element.125), channel_id=1, source_target_pairs={{0,6},{1,7},{2,4},{3,5},{4,2},{5,3},{6,0},{7,1},{8,14},{9,15},{10,... | collective-permute-start | bytes 294920 | tf_op jit(solution)/shard_map/ppermute | solution.py:24
  99.4 3.9 %collective-permute-start.32 = (bf16[16,1024]{1,0:T(8,128)(2,1)S(1)}, bf16[16,1024]{1,0:T(8,128)(2,1)S(1)}, u32[]{:S(2)}, u32[]{:S(2)}) collective-permute-start(bf16[16,1024]{1,0:T(8,128)(2,1)S(1)} %get-tuple-element.126), channel_id=1, source_target_pairs={{0,8},{8,0},{16,24},{24,16},{1,9},{9,1},{17,25},{25,17},{2,10},{10... | collective-permute-start | bytes 98312 | tf_op jit(solution)/shard_map/ppermute | solution.py:24
  99.8 4.7 %collective-permute-start.33 = (bf16[16,1024]{1,0:T(8,128)(2,1)S(1)}, bf16[16,1024]{1,0:T(8,128)(2,1)S(1)}, u32[]{:S(2)}, u32[]{:S(2)}) collective-permute-start(bf16[16,1024]{1,0:T(8,128)(2,1)S(1)} %get-tuple-element.127), channel_id=1, source_target_pairs={{0,16},{8,24},{16,0},{24,8},{1,17},{9,25},{17,1},{25,9},{2,18},{10... | collective-permute-start | bytes 98312 | tf_op jit(solution)/shard_map/ppermute | solution.py:24
  103.3 4.8 %collective-permute-start.34 = (bf16[16,1024]{1,0:T(8,128)(2,1)S(1)}, bf16[16,1024]{1,0:T(8,128)(2,1)S(1)}, u32[]{:S(2)}, u32[]{:S(2)}) collective-permute-start(bf16[16,1024]{1,0:T(8,128)(2,1)S(1)} %get-tuple-element.128), channel_id=1, source_target_pairs={{0,24},{8,16},{16,8},{24,0},{1,25},{9,17},{17,9},{25,1},{2,26},{10... | collective-permute-start | bytes 98312 | tf_op jit(solution)/shard_map/ppermute | solution.py:24
  108.1 1.5 collective-permute-start.35
  110.0 11.4 %collective-permute-start.36 = (bf16[192,1024]{1,0:T(8,128)(2,1)S(1)}, bf16[192,1024]{1,0:T(8,128)(2,1)S(1)}, u32[]{:S(2)}, u32[]{:S(2)}) collective-permute-start(bf16[192,1024]{1,0:T(8,128)(2,1)S(1)} %shard_map.178.refs_1_), channel_id=1, source_target_pairs={{0,8},{8,0},{16,24},{24,16},{1,9},{9,1},{17,25},{25,17},{2,10},{10... | collective-permute-start | bytes 1179656 | tf_op jit(solution)/shard_map/ppermute | solution.py:24
  110.5 11.7 %collective-permute-start.38 = (bf16[192,1024]{1,0:T(8,128)(2,1)S(1)}, bf16[192,1024]{1,0:T(8,128)(2,1)S(1)}, u32[]{:S(2)}, u32[]{:S(2)}) collective-permute-start(bf16[192,1024]{1,0:T(8,128)(2,1)S(1)} %shard_map.178.refs_1_), channel_id=1, source_target_pairs={{0,16},{8,24},{16,0},{24,8},{1,17},{9,25},{17,1},{25,9},{2,18},{10... | collective-permute-start | bytes 1179656 | tf_op jit(solution)/shard_map/ppermute | solution.py:24
  111.8 12.1 %copy-start.1 = (bf16[1024,1792]{1,0:T(8,128)(2,1)S(1)}, bf16[1024,1792]{1,0:T(8,128)(2,1)}, u32[]{:S(2)}) copy-start(bf16[1024,1792]{1,0:T(8,128)(2,1)} %copy-done) | copy-start | bytes 11010052
  111.8 12.1 %copy-start.3 = (bf16[1024,1792]{1,0:T(8,128)(2,1)S(1)}, bf16[1024,1792]{1,0:T(8,128)(2,1)}, u32[]{:S(2)}) copy-start(bf16[1024,1792]{1,0:T(8,128)(2,1)} %copy-done.2) | copy-start | bytes 11010052
  121.4 7.0 %collective-permute-start.37 = (bf16[96,1024]{1,0:T(8,128)(2,1)S(1)}, bf16[96,1024]{1,0:T(8,128)(2,1)S(1)}, u32[]{:S(2)}, u32[]{:S(2)}) collective-permute-start(bf16[96,1024]{1,0:T(8,128)(2,1)S(1)} %slice.19), channel_id=1, source_target_pairs={{0,16},{8,24},{16,0},{24,8},{1,17},{9,25},{17,1},{25,9},{2,18},{10... | collective-permute-start | bytes 589832 | tf_op jit(solution)/shard_map/ppermute | solution.py:24
  122.2 6.2 %collective-permute-start.39 = (bf16[96,1024]{1,0:T(8,128)(2,1)S(1)}, bf16[96,1024]{1,0:T(8,128)(2,1)S(1)}, u32[]{:S(2)}, u32[]{:S(2)}) collective-permute-start(bf16[96,1024]{1,0:T(8,128)(2,1)S(1)} %slice.20), channel_id=1, source_target_pairs={{0,8},{8,0},{16,24},{24,16},{1,9},{9,1},{17,25},{25,17},{2,10},{10... | collective-permute-start | bytes 589832 | tf_op jit(solution)/shard_map/ppermute | solution.py:24
  130.7 14.7 %copy-start.7 = (bf16[4096,8]{0,1:T(8,128)(2,1)S(1)}, bf16[4096,8]{0,1:T(8,128)(2,1)}, u32[]{:S(2)}) copy-start(bf16[4096,8]{0,1:T(8,128)(2,1)} %param.29) | copy-start | bytes 196612
  134.4 7.9 %collective-permute-start.42 = (bf16[48,2048]{1,0:T(8,128)(2,1)S(1)}, bf16[48,2048]{1,0:T(8,128)(2,1)S(1)}, u32[]{:S(2)}, u32[]{:S(2)}) collective-permute-start(bf16[48,2048]{1,0:T(8,128)(2,1)S(1)} %get-tuple-element.149), channel_id=1, source_target_pairs={{0,8},{8,0},{16,24},{24,16},{1,9},{9,1},{17,25},{25,17},{2,10},{10... | collective-permute-start | bytes 589832 | tf_op jit(solution)/shard_map/ppermute | solution.py:24
  136.0 7.5 %collective-permute-start.43 = (bf16[48,2048]{1,0:T(8,128)(2,1)S(1)}, bf16[48,2048]{1,0:T(8,128)(2,1)S(1)}, u32[]{:S(2)}, u32[]{:S(2)}) collective-permute-start(bf16[48,2048]{1,0:T(8,128)(2,1)S(1)} %get-tuple-element.150), channel_id=1, source_target_pairs={{0,16},{8,24},{16,0},{24,8},{1,17},{9,25},{17,1},{25,9},{2,18},{10... | collective-permute-start | bytes 589832 | tf_op jit(solution)/shard_map/ppermute | solution.py:24
  136.4 10.1 %collective-permute-start.40 = (bf16[48,2048]{1,0:T(8,128)(2,1)S(1)}, bf16[48,2048]{1,0:T(8,128)(2,1)S(1)}, u32[]{:S(2)}, u32[]{:S(2)}) collective-permute-start(bf16[48,2048]{1,0:T(8,128)(2,1)S(1)} %get-tuple-element.145), channel_id=1, source_target_pairs={{0,8},{8,0},{16,24},{24,16},{1,9},{9,1},{17,25},{25,17},{2,10},{10... | collective-permute-start | bytes 589832 | tf_op jit(solution)/shard_map/ppermute | solution.py:24
  137.8 9.5 %collective-permute-start.41 = (bf16[48,2048]{1,0:T(8,128)(2,1)S(1)}, bf16[48,2048]{1,0:T(8,128)(2,1)S(1)}, u32[]{:S(2)}, u32[]{:S(2)}) collective-permute-start(bf16[48,2048]{1,0:T(8,128)(2,1)S(1)} %get-tuple-element.146), channel_id=1, source_target_pairs={{0,16},{8,24},{16,0},{24,8},{1,17},{9,25},{17,1},{25,9},{2,18},{10... | collective-permute-start | bytes 589832 | tf_op jit(solution)/shard_map/ppermute | solution.py:24
  143.6 5.7 %collective-permute-start.44 = (bf16[48,2048]{1,0:T(8,128)(2,1)S(1)}, bf16[48,2048]{1,0:T(8,128)(2,1)S(1)}, u32[]{:S(2)}, u32[]{:S(2)}) collective-permute-start(bf16[48,2048]{1,0:T(8,128)(2,1)S(1)} %get-tuple-element.151), channel_id=1, source_target_pairs={{0,8},{8,0},{16,24},{24,16},{1,9},{9,1},{17,25},{25,17},{2,10},{10... | collective-permute-start | bytes 589832 | tf_op jit(solution)/shard_map/ppermute | solution.py:24
  144.5 5.7 %collective-permute-start.45 = (bf16[48,2048]{1,0:T(8,128)(2,1)S(1)}, bf16[48,2048]{1,0:T(8,128)(2,1)S(1)}, u32[]{:S(2)}, u32[]{:S(2)}) collective-permute-start(bf16[48,2048]{1,0:T(8,128)(2,1)S(1)} %get-tuple-element.152), channel_id=1, source_target_pairs={{0,16},{8,24},{16,0},{24,8},{1,17},{9,25},{17,1},{25,9},{2,18},{10... | collective-permute-start | bytes 589832 | tf_op jit(solution)/shard_map/ppermute | solution.py:24
  150.6 6.8 %collective-permute-start.46 = (bf16[48,1024]{1,0:T(8,128)(2,1)S(1)}, bf16[48,1024]{1,0:T(8,128)(2,1)S(1)}, u32[]{:S(2)}, u32[]{:S(2)}) collective-permute-start(bf16[48,1024]{1,0:T(8,128)(2,1)S(1)} %get-tuple-element.157), channel_id=1, source_target_pairs={{0,2},{1,3},{2,0},{3,1},{4,6},{5,7},{6,4},{7,5},{8,10},{9,11},{10,... | collective-permute-start | bytes 294920 | tf_op jit(solution)/shard_map/ppermute | solution.py:24
  151.2 6.2 %collective-permute-start.47 = (bf16[48,1024]{1,0:T(8,128)(2,1)S(1)}, bf16[48,1024]{1,0:T(8,128)(2,1)S(1)}, u32[]{:S(2)}, u32[]{:S(2)}) collective-permute-start(bf16[48,1024]{1,0:T(8,128)(2,1)S(1)} %get-tuple-element.158), channel_id=1, source_target_pairs={{0,4},{1,5},{2,6},{3,7},{4,0},{5,1},{6,2},{7,3},{8,12},{9,13},{10,... | collective-permute-start | bytes 294920 | tf_op jit(solution)/shard_map/ppermute | solution.py:24
  153.7 6.4 %collective-permute-start.48 = (bf16[48,1024]{1,0:T(8,128)(2,1)S(1)}, bf16[48,1024]{1,0:T(8,128)(2,1)S(1)}, u32[]{:S(2)}, u32[]{:S(2)}) collective-permute-start(bf16[48,1024]{1,0:T(8,128)(2,1)S(1)} %get-tuple-element.159), channel_id=1, source_target_pairs={{0,6},{1,7},{2,4},{3,5},{4,2},{5,3},{6,0},{7,1},{8,14},{9,15},{10,... | collective-permute-start | bytes 294920 | tf_op jit(solution)/shard_map/ppermute | solution.py:24
  160.1 1.5 collective-permute-start.49
  (1 other events, 1.8 us)

commit v7 on v6

--- a/solution.py
+++ b/solution.py
@@ -697,7 +697,6 @@
 
     mixer_terms, places = scattered(mixer_send, masks, [side_own])
 
-    side_terms = [partner(block, "seq", mask) for mask, block in zip(masks, side_send)]
     activated, features = kernel_call(
         functools.partial(conv_body, places),
         [shape((length, channels), BF16), shape((length + state_width, rank_width), F32)],
@@ -707,6 +706,8 @@
     features = features + partner(features, "expert", 1)
     sent = features.astype(BF16)
     features_came = [partner(sent, "expert", 2 * w) for w in range(1, chips)]
+    side_send = after(side_send, features_came[0])
+    side_terms = [partner(block, "seq", mask) for mask, block in zip(masks, side_send)]
     for term in features_came:
         features = features + term.astype(F32)
     low_rank, maps = features[:length].astype(BF16), features[length:]
@@ -779,12 +780,13 @@
         partner(block, "expert", 2 * w) for w, block in zip(range(1, chips), outgoing[1:])
     ]
     whole = [near_hidden[0]] + [partner(near_hidden[mask], "seq", mask) for mask in masks]
-    crossed = partner(second_halves(came, whole[1:]), "expert", 1)
+    crossed = partner(second_halves(came, whole[1:] + current), "expert", 1)
     rows = kernel_call(
         functools.partial(rows_body, chips, seq, groups, most_slots),
         shape((slots, width), BF16),
         [VMEM] * (chips + 1),
         moved=4 * slots * width,
+        deps=current,
     )(*came, crossed)
     if seq == 4:
         pieces = [rows, partner(rows, "seq", 1), partner(rows, "seq", 2)]

time: 163 us -> 163 us (level)
  starting transfers between devices: 54.3 us -> 56.7 us
    ppermute x50, starting transfers between devices: 54.3 us -> 56.7 us  [partner(): return lax.ppermute(block, axis, [(i, i ^ mask) for i in range(size)])]
  transfers between devices with their start and end apart: 50 -> 50, of which waited for: 25 -> 27; matrix products, arithmetic and copies ran while one was open for 4% -> 4% of each run, Pallas kernels for 21% -> 21%
where the time goes in v7:
time: 163 us
  starting transfers between devices  56.7 us (35%)
  Pallas kernels  52.4 us (32%)
  waiting for transfers between devices  46 us (28%)
  local copies, waits for them, and re-layouts  6.75 us (4%)
    ppermute x50, starting transfers between devices, partner(): return lax.ppermute(block, axis, [(i, i ^ mask) for i in range(size)])  56.7 us
    pallas_call x26, Pallas kernels, kernel_call(): return lambda *operands: call(*operands, *deps)  52.4 us
    ppermute x50, waiting for transfers between devices, partner(): return lax.ppermute(block, axis, [(i, i ^ mask) for i in range(size)])  46 us
    unnamed x32, local copies, waits for them, and re-layouts  5.72 us
  transfers between devices with their start and end apart: 50, of which 27 were waited for; matrix products, arithmetic and copies ran while one was open for 4% of the time, Pallas kernels for 21%

profile of v7, /device:TPU:0, one launch (start us, length us, event | category | flops | bytes accessed | tf_op | source)
XLA Modules:
  0.0 162.5 jit_solution(12234611379283401489)
XLA Ops:
  0.1 2.2 %shard_map.163 = (bf16[128,1024]{1,0:T(8,128)(2,1)S(1)}, bf16[128,512]{1,0:T(8,128)(2,1)S(1)}, bf16[128,512]{1,0:T(8,128)(2,1)S(1)}, bf16[128,512]{1,0:T(8,128)(2,1)S(1)}) custom-call(s32[3]{0:T(128)S(1)} %pad_add_fusion.refs_0_, bf16[128,4096]{1,0:T(8,128)(2,1)} %refs_1_.2, f32[1,4096]{1,0:T(1,128)} %bitcast.42), custom_call_target="tpu_custom_call" | custom-call | flops 4194304 | bytes 2097152 | tf_op jit(solution)/shard_map/pallas_call | solution.py:58
  2.3 3.0 %collective-permute-start = (bf16[128,512]{1,0:T(8,128)(2,1)S(1)}, bf16[128,512]{1,0:T(8,128)(2,1)S(1)}, u32[]{:S(2)}, u32[]{:S(2)}) collective-permute-start(bf16[128,512]{1,0:T(8,128)(2,1)S(1)} %get-tuple-element.88), channel_id=1, source_target_pairs={{0,8},{8,0},{16,24},{24,16},{1,9},{9,1},{17,25},{25,17},{2,10},{10... | collective-permute-start | bytes 393224 | tf_op jit(solution)/shard_map/ppermute | solution.py:24
  5.3 1.5 collective-permute-start.1
  6.8 5.6 %copy.18 = bf16[128,8,2,1024]{3,1,2,0:T(8,128)(2,1)} copy(bf16[128,8,2,1024]{3,2,1,0:T(2,128)(2,1)} %bitcast.41) | data formatting | bytes 8388608
  13.9 1.6 shard_map.165.refs_8_
  15.5 1.9 %shard_map.166 = (f32[144,1024]{1,0:T(8,128)S(1)}, bf16[144,512]{1,0:T(8,128)(2,1)S(1)}, bf16[144,512]{1,0:T(8,128)(2,1)S(1)}, bf16[144,512]{1,0:T(8,128)(2,1)S(...) custom-call(s32[3]{0:T(128)S(1)} %pad_add_fusion.refs_0_, ...), custom_call_target="tpu_custom_call" | custom-call | flops 1073741824 | bytes 2097152 | tf_op jit(solution)/shard_map/pallas_call | solution.py:58
  17.4 1.4 collective-permute-start.8
  18.8 1.5 collective-permute-start.9
  22.5 3.2 %shard_map.167 = (f32[128,1024]{1,0:T(8,128)S(1)}, bf16[144,1024]{1,0:T(8,128)(2,1)S(1)}, bf16[144,1024]{1,0:T(8,128)(2,1)S(1)}, bf16[144,1024]{1,0:T(8,128)(2,1)S(1)}) custom-call(s32[3]{0:T(128)S(1)} %pad_add_fusion.refs_0_, bf16[128,1024]{1,0:T(8,128)(2,1)S(1)} %get-tuple-element.87.refs_1_, bf16[128,512]{1,0:T(8,128)(2,1)S(1)} %collective-permute-done.refs_0_.refs_2_, ...), custom_call_target="tpu_custom_call" | custom-call | flops 1073741824 | bytes 2097152 | tf_op jit(solution)/shard_map/pallas_call | solution.py:58
  25.8 1.4 collective-permute-start.10
  27.2 1.5 collective-permute-start.11
  28.8 2.3 %collective-permute-done.10.refs_3_ = bf16[144,512]{1,0:T(8,128)(2,1)S(1)} collective-permute-done((bf16[144,512]{1,0:T(8,128)(2,1)S(1)}, bf16[144,512]{1,0:T(8,128)(2,1)S(1)}, u32[]{:S(2)}, u32[]{:S(2)}) %collective-permute-start.10) | collective-permute-done | bytes 147488 | tf_op jit(solution)/shard_map/ppermute | solution.py:24
  31.0 1.4 collective-permute-done.11.refs_4_.refs_3_
  33.3 1.4 collective-permute-done.12
  34.7 1.6 %collective-permute-start.13 = (bf16[144,256]{1,0:T(8,128)(2,1)S(1)}, bf16[144,256]{1,0:T(8,128)(2,1)S(1)}, u32[]{:S(2)}, u32[]{:S(2)}) collective-permute-start(bf16[144,256]{1,0:T(8,128)(2,1)S(1)} %get-tuple-element.169), channel_id=1, source_target_pairs={{0,2},{1,3},{2,0},{3,1},{4,6},{5,7},{6,4},{7,5},{8,10},{9,11},{10,... | collective-permute-start | bytes 221192 | tf_op jit(solution)/shard_map/ppermute | solution.py:24
  36.3 2.6 %collective-permute-start.14 = (bf16[144,256]{1,0:T(8,128)(2,1)S(1)}, bf16[144,256]{1,0:T(8,128)(2,1)S(1)}, u32[]{:S(2)}, u32[]{:S(2)}) collective-permute-start(bf16[144,256]{1,0:T(8,128)(2,1)S(1)} %get-tuple-element.169), channel_id=1, source_target_pairs={{0,4},{1,5},{2,6},{3,7},{4,0},{5,1},{6,2},{7,3},{8,12},{9,13},{10,... | collective-permute-start | bytes 221192 | tf_op jit(solution)/shard_map/ppermute | solution.py:24
  39.9 1.5 collective-permute-start.20
  41.4 1.3 collective-permute-start.21
  42.7 1.7 %collective-permute-done.14 = bf16[144,256]{1,0:T(8,128)(2,1)S(1)} collective-permute-done((bf16[144,256]{1,0:T(8,128)(2,1)S(1)}, bf16[144,256]{1,0:T(8,128)(2,1)S(1)}, u32[]{:S(2)}, u32[]{:S(2)}) %collective-permute-start.14) | collective-permute-done | bytes 73760 | tf_op jit(solution)/shard_map/ppermute | solution.py:24
  45.3 5.0 %shard_map.170 = (f32[128,8,128]{2,1,0:T(8,128)S(1)}, f32[128,8,128]{2,1,0:T(8,128)S(1)}, bf16[18,8,128]{2,1,0:T(8,128)(2,1)S(1)}) custom-call(f32[16,256]{1,0:T(8,128)S(1)} %slice.17.refs_0_.refs_1_, bf16[128,256]{1,0:T(8,128)(2,1)S(1)} %slice.22.refs_1_, bf16[128,1024]{1,0:T(8,128)(2,1)S(1)} %get-tuple-element.105.refs_2_.refs_8_, ...), custom_call_target="tpu_custom_call" | custom-call | tf_op jit(solution)/shard_map/pallas_call | solution.py:58
  51.0 1.5 collective-permute-start.17
  52.5 2.2 %collective-permute-done.16.refs_2_ = bf16[18,8,128]{2,1,0:T(8,128)(2,1)S(1)} collective-permute-done((bf16[18,8,128]{2,1,0:T(8,128)(2,1)S(1)}, bf16[18,8,128]{2,1,0:T(8,128)(2,1)S(1)}, u32[]{:S(2)}, u32[]{:S(2)}) %collective-permute-start.16) | collective-permute-done | bytes 36896 | tf_op jit(solution)/shard_map/ppermute | solution.py:24
  54.7 1.6 collective-permute-start.18
  56.3 3.3 %collective-permute-done.18.refs_4_ = bf16[18,8,128]{2,1,0:T(8,128)(2,1)S(1)} collective-permute-done((bf16[18,8,128]{2,1,0:T(8,128)(2,1)S(1)}, bf16[18,8,128]{2,1,0:T(8,128)(2,1)S(1)}, u32[]{:S(2)}, u32[]{:S(2)}) %collective-permute-start.18) | collective-permute-done | bytes 36896 | tf_op jit(solution)/shard_map/ppermute | solution.py:24
  59.6 3.6 %shard_map.171.refs_0_ = bf16[128,1024]{1,0:T(8,128)(2,1)S(1)} custom-call(s32[3]{0:T(128)S(1)} %pad_add_fusion.refs_0_, f32[16,256]{1,0:T(8,128)S(1)} %slice.17.refs_0_.refs_1_, bf16[18,8,128]{2,1,0:T(8,128)(2,1)S(1)} %collective-permute-done.16.refs_2_, bf16[18,8,128]{2,1,0:T(8,128)(2,1)S(1)} %collective-permute-done.17.refs_3_, ...), custom_call_target="tpu_custom_call" | custom-call | tf_op jit(solution)/shard_map/pallas_call | solution.py:58
  63.8 1.5 collective-permute-start.23
  65.4 1.3 collective-permute-start.24
  66.7 4.8 %collective-permute-done.22.refs_1_ = bf16[128,1024]{1,0:T(8,128)(2,1)S(1)} collective-permute-done((bf16[128,1024]{1,0:T(8,128)(2,1)S(1)}, bf16[128,1024]{1,0:T(8,128)(2,1)S(1)}, u32[]{:S(2)}, u32[]{:S(2)}) %collective-permute-start.22) | collective-permute-done | bytes 262176 | tf_op jit(solution)/shard_map/ppermute | solution.py:24
  71.5 2.2 %collective-permute-done.23.refs_2_ = bf16[128,1024]{1,0:T(8,128)(2,1)S(1)} collective-permute-done((bf16[128,1024]{1,0:T(8,128)(2,1)S(1)}, bf16[128,1024]{1,0:T(8,128)(2,1)S(1)}, u32[]{:S(2)}, u32[]{:S(2)}) %collective-permute-start.23) | collective-permute-done | bytes 262176 | tf_op jit(solution)/shard_map/ppermute | solution.py:24
  73.8 1.5 collective-permute-done.24.refs_3_
  75.2 1.3 shard_map.172
  76.6 1.9 %collective-permute-done.25.refs_1_ = bf16[4,64,1024]{2,1,0:T(8,128)(2,1)S(1)} collective-permute-done((bf16[4,64,1024]{2,1,0:T(8,128)(2,1)S(1)}, bf16[4,64,1024]{2,1,0:T(8,128)(2,1)S(1)}, u32[]{:S(2)}, u32[]{:S(2)}) %collective-permute-start.25) | collective-permute-done | bytes 524320 | tf_op jit(solution)/shard_map/ppermute | solution.py:24
  78.6 1.8 %collective-permute-start.26 = (bf16[64,1024]{1,0:T(8,128)(2,1)S(1)}, bf16[64,1024]{1,0:T(8,128)(2,1)S(1)}, u32[]{:S(2)}, u32[]{:S(2)}) collective-permute-start(bf16[64,1024]{1,0:T(8,128)(2,1)S(1)} %get-tuple-element.118), channel_id=1, source_target_pairs={{0,2},{1,3},{2,0},{3,1},{4,6},{5,7},{6,4},{7,5},{8,10},{9,11},{10,... | collective-permute-start | bytes 393224 | tf_op jit(solution)/shard_map/ppermute | solution.py:24
  80.5 1.7 %collective-permute-start.27 = (bf16[64,1024]{1,0:T(8,128)(2,1)S(1)}, bf16[64,1024]{1,0:T(8,128)(2,1)S(1)}, u32[]{:S(2)}, u32[]{:S(2)}) collective-permute-start(bf16[64,1024]{1,0:T(8,128)(2,1)S(1)} %get-tuple-element.119), channel_id=1, source_target_pairs={{0,4},{1,5},{2,6},{3,7},{4,0},{5,1},{6,2},{7,3},{8,12},{9,13},{10,... | collective-permute-start | bytes 393224 | tf_op jit(solution)/shard_map/ppermute | solution.py:24
  83.8 7.9 %shard_map.175 = (bf16[1024,1792]{1,0:T(8,128)(2,1)S(1)}, bf16[1024,1792]{1,0:T(8,128)(2,1)S(1)}, bf16[1024,1792]{1,0:T(8,128)(2,1)S(1)}, bf16[1024,1792]{1,0:T(...) custom-call(s32[3]{0:T(128)S(1)} %pad_add_fusion.refs_0_, ...), custom_call_target="tpu_custom_call" | custom-call | bytes 22020096 | tf_op jit(solution)/shard_map/pallas_call | solution.py:58
  91.8 1.6 collective-permute-done.27.refs_3_
  94.2 2.4 %collective-permute-start.29 = (bf16[48,1024]{1,0:T(8,128)(2,1)S(1)}, bf16[48,1024]{1,0:T(8,128)(2,1)S(1)}, u32[]{:S(2)}, u32[]{:S(2)}) collective-permute-start(bf16[48,1024]{1,0:T(8,128)(2,1)S(1)} %get-tuple-element.129), channel_id=1, source_target_pairs={{0,2},{1,3},{2,0},{3,1},{4,6},{5,7},{6,4},{7,5},{8,10},{9,11},{10,... | collective-permute-start | bytes 294920 | tf_op jit(solution)/shard_map/ppermute | solution.py:24
  97.2 1.8 %collective-permute-start.31 = (bf16[48,1024]{1,0:T(8,128)(2,1)S(1)}, bf16[48,1024]{1,0:T(8,128)(2,1)S(1)}, u32[]{:S(2)}, u32[]{:S(2)}) collective-permute-start(bf16[48,1024]{1,0:T(8,128)(2,1)S(1)} %get-tuple-element.131), channel_id=1, source_target_pairs={{0,6},{1,7},{2,4},{3,5},{4,2},{5,3},{6,0},{7,1},{8,14},{9,15},{10,... | collective-permute-start | bytes 294920 | tf_op jit(solution)/shard_map/ppermute | solution.py:24
  99.8 1.5 collective-permute-start.33
  101.3 1.6 collective-permute-done.32.refs_4_.refs_5_
  102.9 1.9 %collective-permute-start.34 = (bf16[16,1024]{1,0:T(8,128)(2,1)S(1)}, bf16[16,1024]{1,0:T(8,128)(2,1)S(1)}, u32[]{:S(2)}, u32[]{:S(2)}) collective-permute-start(bf16[16,1024]{1,0:T(8,128)(2,1)S(1)} %get-tuple-element.134), channel_id=1, source_target_pairs={{0,24},{8,16},{16,8},{24,0},{1,25},{9,17},{17,9},{25,1},{2,26},{10... | collective-permute-start | bytes 98312 | tf_op jit(solution)/shard_map/ppermute | solution.py:24
  104.8 3.0 %collective-permute-done.34.refs_6_.refs_7_ = bf16[16,1024]{1,0:T(8,128)(2,1)S(1)} collective-permute-done((bf16[16,1024]{1,0:T(8,128)(2,1)S(1)}, bf16[16,1024]{1,0:T(8,128)(2,1)S(1)}, u32[]{:S(2)}, u32[]{:S(2)}) %collective-permute-start.34) | collective-permute-done | bytes 32800 | tf_op jit(solution)/shard_map/ppermute | solution.py:24
  107.8 1.4 collective-permute-done.35.refs_4_
  110.5 1.6 collective-permute-start.38
  112.1 9.6 %shard_map.179 = (f32[192,1792]{1,0:T(8,128)S(1)}, f32[192,1792]{1,0:T(8,128)S(1)}, f32[192,128]{1,0:T(8,128)S(1)}, bf16[1024,1792]{1,0:T(8,128)(2,1)S(1)}, bf16...) custom-call(s32[3]{0:T(128)S(1)} %pad_add_fusion.refs_0_, ...), custom_call_target="tpu_custom_call" | custom-call | flops 1409286144 | bytes 7340032 | tf_op jit(solution)/shard_map/pallas_call | solution.py:58
  122.2 1.3 collective-permute-start.39
  123.5 2.2 %shard_map.180 = (f32[192,1792]{1,0:T(8,128)S(1)}, f32[192,1792]{1,0:T(8,128)S(1)}, f32[192,128]{1,0:T(8,128)S(1)}) custom-call(s32[3]{0:T(128)S(1)} %pad_add_fusion.refs_0_, bf16[192,1024]{1,0:T(8,128)(2,1)S(1)} %collective-permute-done.36.refs_1_, f32[1,4096]{1,0:T(1,128)S(1)} %bitcast.30, bf16[1024,1792]{1,0:T(8,128)(2,1)S(1)} %copy-done.1, ...), custom_call_target="tpu_custom_call" | custom-call | flops 1409286144 | bytes 7340032 | tf_op jit(solution)/shard_map/pallas_call | solution.py:58
  125.7 2.2 %shard_map.181 = (f32[192,1792]{1,0:T(8,128)S(1)}, f32[192,1792]{1,0:T(8,128)S(1)}, f32[192,128]{1,0:T(8,128)S(1)}) custom-call(s32[3]{0:T(128)S(1)} %pad_add_fusion.refs_0_, bf16[192,1024]{1,0:T(8,128)(2,1)S(1)} %collective-permute-done.38.refs_1_, f32[1,4096]{1,0:T(1,128)S(1)} %bitcast.31, ...), custom_call_target="tpu_custom_call" | custom-call | flops 1409286144 | bytes 7340032 | tf_op jit(solution)/shard_map/pallas_call | solution.py:58
  128.4 2.3 %shard_map.182.refs_1_ = bf16[192,1792]{1,0:T(8,128)(2,1)S(1)} custom-call(s32[3]{0:T(128)S(1)} %pad_add_fusion.refs_0_, bf16[96,1024]{1,0:T(8,128)(2,1)S(1)} %collective-permute-done.37.refs_1_, bf16[96,1024]{1,0:T(8,128)(2,1)S(1)} %collective-permute-done.39.refs_2_, f32[1,4096]{1,0:T(1,128)S(1)} %bitcast.32, ...), custom_call_target="tpu_custom_call" | custom-call | flops 1409286144 | bytes 7340032 | tf_op jit(solution)/shard_map/pallas_call | solution.py:58
  130.7 3.7 %shard_map.183 = (bf16[48,4096]{1,0:T(8,128)(2,1)S(1)}, bf16[48,2048]{1,0:T(8,128)(2,1)S(1)}, bf16[48,2048]{1,0:T(8,128)(2,1)S(1)}, bf16[48,2048]{1,0:T(8,128)(2...) custom-call(s32[3]{0:T(128)S(1)} %pad_add_fusion.refs_0_, ...), custom_call_target="tpu_custom_call" | custom-call | flops 2818572288 | bytes 14680064 | tf_op jit(solution)/shard_map/pallas_call | solution.py:58
  134.4 1.3 collective-permute-start.42
  136.6 1.5 collective-permute-start.40
  138.5 3.8 %collective-permute-done.42.refs_2_ = bf16[48,2048]{1,0:T(8,128)(2,1)S(1)} collective-permute-done((bf16[48,2048]{1,0:T(8,128)(2,1)S(1)}, bf16[48,2048]{1,0:T(8,128)(2,1)S(1)}, u32[]{:S(2)}, u32[]{:S(2)}) %collective-permute-start.42) | collective-permute-done | bytes 196640 | tf_op jit(solution)/shard_map/ppermute | solution.py:24
  143.3 1.2 collective-permute-start.44
  144.5 1.3 collective-permute-start.45
  146.9 2.1 %collective-permute-done.44.refs_3_ = bf16[48,2048]{1,0:T(8,128)(2,1)S(1)} collective-permute-done((bf16[48,2048]{1,0:T(8,128)(2,1)S(1)}, bf16[48,2048]{1,0:T(8,128)(2,1)S(1)}, u32[]{:S(2)}, u32[]{:S(2)}) %collective-permute-start.44) | collective-permute-done | bytes 196640 | tf_op jit(solution)/shard_map/ppermute | solution.py:24
  149.0 1.2 collective-permute-done.45.refs_4_
  150.6 1.1 collective-permute-start.46
  151.7 1.5 collective-permute-start.47
  153.2 1.8 %collective-permute-start.48 = (bf16[48,1024]{1,0:T(8,128)(2,1)S(1)}, bf16[48,1024]{1,0:T(8,128)(2,1)S(1)}, u32[]{:S(2)}, u32[]{:S(2)}) collective-permute-start(bf16[48,1024]{1,0:T(8,128)(2,1)S(1)} %get-tuple-element.165), channel_id=1, source_target_pairs={{0,6},{1,7},{2,4},{3,5},{4,2},{5,3},{6,0},{7,1},{8,14},{9,15},{10,... | collective-permute-start | bytes 294920 | tf_op jit(solution)/shard_map/ppermute | solution.py:24
  155.6 2.7 %collective-permute-done.47.refs_2_ = bf16[48,1024]{1,0:T(8,128)(2,1)S(1)} collective-permute-done((bf16[48,1024]{1,0:T(8,128)(2,1)S(1)}, bf16[48,1024]{1,0:T(8,128)(2,1)S(1)}, u32[]{:S(2)}, u32[]{:S(2)}) %collective-permute-start.47) | collective-permute-done | bytes 98336 | tf_op jit(solution)/shard_map/ppermute | solution.py:24
  158.3 1.4 collective-permute-done.48.refs_3_
  159.8 1.4 collective-permute-done.49.refs_4_
  161.3 1.3 shard_map.188
  (106 shorter events, 18.8 us)
Async XLA Ops:
  2.3 10.2 %collective-permute-start = (bf16[128,512]{1,0:T(8,128)(2,1)S(1)}, bf16[128,512]{1,0:T(8,128)(2,1)S(1)}, u32[]{:S(2)}, u32[]{:S(2)}) collective-permute-start(bf16[128,512]{1,0:T(8,128)(2,1)S(1)} %get-tuple-element.88), channel_id=1, source_target_pairs={{0,8},{8,0},{16,24},{24,16},{1,9},{9,1},{17,25},{25,17},{2,10},{10... | collective-permute-start | bytes 393224 | tf_op jit(solution)/shard_map/ppermute | solution.py:24
  5.3 7.8 %collective-permute-start.1 = (bf16[128,512]{1,0:T(8,128)(2,1)S(1)}, bf16[128,512]{1,0:T(8,128)(2,1)S(1)}, u32[]{:S(2)}, u32[]{:S(2)}) collective-permute-start(bf16[128,512]{1,0:T(8,128)(2,1)S(1)} %get-tuple-element.89), channel_id=1, source_target_pairs={{0,16},{8,24},{16,0},{24,8},{1,17},{9,25},{17,1},{25,9},{2,18},{10... | collective-permute-start | bytes 393224 | tf_op jit(solution)/shard_map/ppermute | solution.py:24
  6.8 6.3 %collective-permute-start.2 = (bf16[128,512]{1,0:T(8,128)(2,1)S(1)}, bf16[128,512]{1,0:T(8,128)(2,1)S(1)}, u32[]{:S(2)}, u32[]{:S(2)}) collective-permute-start(bf16[128,512]{1,0:T(8,128)(2,1)S(1)} %get-tuple-element.90), channel_id=1, source_target_pairs={{0,24},{8,16},{16,8},{24,0},{1,25},{9,17},{17,9},{25,1},{2,26},{10... | collective-permute-start | bytes 393224 | tf_op jit(solution)/shard_map/ppermute | solution.py:24
  6.8 5.6 %copy-start.14 = (s32[16,2]{0,1:T(2,128)S(1)}, s32[16,2]{0,1:T(2,128)}, u32[]{:S(2)}) copy-start(s32[16,2]{0,1:T(2,128)} %param.30) | copy-start | bytes 388
  13.1 2.4 %collective-permute-start.3 = (bf16[128,512]{1,0:T(8,128)(2,1)S(1)}, bf16[128,512]{1,0:T(8,128)(2,1)S(1)}, u32[]{:S(2)}, u32[]{:S(2)}) collective-permute-start(bf16[128,512]{1,0:T(8,128)(2,1)S(1)} %get-tuple-element.91.refs_1_), channel_id=1, source_target_pairs={{0,1},{1,0},{2,3},{3,2},{4,5},{5,4},{6,7},{7,6},{8,9},{9,8},{10,11... | collective-permute-start | bytes 393224 | tf_op jit(solution)/shard_map/ppermute | solution.py:24
  13.2 2.3 %collective-permute-start.4 = (bf16[128,512]{1,0:T(8,128)(2,1)S(1)}, bf16[128,512]{1,0:T(8,128)(2,1)S(1)}, u32[]{:S(2)}, u32[]{:S(2)}) collective-permute-start(bf16[128,512]{1,0:T(8,128)(2,1)S(1)} %get-tuple-element.92), channel_id=1, source_target_pairs={{0,1},{1,0},{2,3},{3,2},{4,5},{5,4},{6,7},{7,6},{8,9},{9,8},{10,11... | collective-permute-start | bytes 393224 | tf_op jit(solution)/shard_map/ppermute | solution.py:24
  13.7 1.8 %collective-permute-start.5 = (bf16[128,512]{1,0:T(8,128)(2,1)S(1)}, bf16[128,512]{1,0:T(8,128)(2,1)S(1)}, u32[]{:S(2)}, u32[]{:S(2)}) collective-permute-start(bf16[128,512]{1,0:T(8,128)(2,1)S(1)} %get-tuple-element.93), channel_id=1, source_target_pairs={{0,1},{1,0},{2,3},{3,2},{4,5},{5,4},{6,7},{7,6},{8,9},{9,8},{10,11... | collective-permute-start | bytes 393224 | tf_op jit(solution)/shard_map/ppermute | solution.py:24
  17.4 15.0 %copy-start.4 = (bf16[1024,288]{0,1:T(8,128)(2,1)S(1)}, bf16[1024,288]{0,1:T(8,128)(2,1)}, u32[]{:S(2)}) copy-start(bf16[1024,288]{0,1:T(8,128)(2,1)} %param.22) | copy-start | bytes 1769476
  17.4 15.0 %copy-start.8 = (f32[4,1024]{1,0:T(4,128)S(1)}, f32[4,1024]{1,0:T(4,128)}, u32[]{:S(2)}) copy-start(f32[4,1024]{1,0:T(4,128)} %refs_5_.2) | copy-start | bytes 49156
  17.4 15.0 %copy-start.9 = (f32[1024]{0:T(1024)S(1)}, f32[1024]{0:T(1024)}, u32[]{:S(2)}) copy-start(f32[1024]{0:T(1024)} %param.21) | copy-start | bytes 12292
  17.4 8.3 %collective-permute-start.8 = (bf16[144,512]{1,0:T(8,128)(2,1)S(1)}, bf16[144,512]{1,0:T(8,128)(2,1)S(1)}, u32[]{:S(2)}, u32[]{:S(2)}) collective-permute-start(bf16[144,512]{1,0:T(8,128)(2,1)S(1)} %get-tuple-element.99), channel_id=1, source_target_pairs={{0,8},{8,0},{16,24},{24,16},{1,9},{9,1},{17,25},{25,17},{2,10},{10... | collective-permute-start | bytes 442376 | tf_op jit(solution)/shard_map/ppermute | solution.py:24
  18.8 6.9 %collective-permute-start.9 = (bf16[144,512]{1,0:T(8,128)(2,1)S(1)}, bf16[144,512]{1,0:T(8,128)(2,1)S(1)}, u32[]{:S(2)}, u32[]{:S(2)}) collective-permute-start(bf16[144,512]{1,0:T(8,128)(2,1)S(1)} %get-tuple-element.100), channel_id=1, source_target_pairs={{0,16},{8,24},{16,0},{24,8},{1,17},{9,25},{17,1},{25,9},{2,18},{10... | collective-permute-start | bytes 442376 | tf_op jit(solution)/shard_map/ppermute | solution.py:24
  21.3 7.5 %collective-permute-start.6 = (bf16[144,512]{1,0:T(8,128)(2,1)S(1)}, bf16[144,512]{1,0:T(8,128)(2,1)S(1)}, u32[]{:S(2)}, u32[]{:S(2)}) collective-permute-start(bf16[144,512]{1,0:T(8,128)(2,1)S(1)} %get-tuple-element.95), channel_id=1, source_target_pairs={{0,8},{8,0},{16,24},{24,16},{1,9},{9,1},{17,25},{25,17},{2,10},{10... | collective-permute-start | bytes 442376 | tf_op jit(solution)/shard_map/ppermute | solution.py:24
  22.0 17.1 %copy-start.13 = (f32[1024,16]{0,1:T(8,128)S(1)}, f32[1024,16]{0,1:T(8,128)}, u32[]{:S(2)}) copy-start(f32[1024,16]{0,1:T(8,128)} %param.25) | copy-start | bytes 196612
  22.0 23.2 %copy-start.5 = (bf16[256,1024]{1,0:T(8,128)(2,1)S(1)}, bf16[256,1024]{1,0:T(8,128)(2,1)}, u32[]{:S(2)}) copy-start(bf16[256,1024]{1,0:T(8,128)(2,1)} %refs_3_.1) | copy-start | bytes 1572868
  22.0 23.3 %copy-start.10 = (f32[1024]{0:T(1024)S(1)}, f32[1024]{0:T(1024)}, u32[]{:S(2)}) copy-start(f32[1024]{0:T(1024)} %param.24) | copy-start | bytes 12292
  22.0 6.8 %collective-permute-start.7 = (bf16[144,512]{1,0:T(8,128)(2,1)S(1)}, bf16[144,512]{1,0:T(8,128)(2,1)S(1)}, u32[]{:S(2)}, u32[]{:S(2)}) collective-permute-start(bf16[144,512]{1,0:T(8,128)(2,1)S(1)} %get-tuple-element.96), channel_id=1, source_target_pairs={{0,16},{8,24},{16,0},{24,8},{1,17},{9,25},{17,1},{25,9},{2,18},{10... | collective-permute-start | bytes 442376 | tf_op jit(solution)/shard_map/ppermute | solution.py:24
  25.7 33.9 %copy-start.11 = (f32[1024]{0:T(1024)S(1)}, f32[1024]{0:T(1024)}, u32[]{:S(2)}) copy-start(f32[1024]{0:T(1024)} %param.26) | copy-start | bytes 12292
  25.8 5.2 %collective-permute-start.10 = (bf16[144,512]{1,0:T(8,128)(2,1)S(1)}, bf16[144,512]{1,0:T(8,128)(2,1)S(1)}, u32[]{:S(2)}, u32[]{:S(2)}) collective-permute-start(bf16[144,512]{1,0:T(8,128)(2,1)S(1)} %get-tuple-element.102), channel_id=1, source_target_pairs={{0,8},{8,0},{16,24},{24,16},{1,9},{9,1},{17,25},{25,17},{2,10},{10... | collective-permute-start | bytes 442376 | tf_op jit(solution)/shard_map/ppermute | solution.py:24
  27.2 5.1 %collective-permute-start.11 = (bf16[144,512]{1,0:T(8,128)(2,1)S(1)}, bf16[144,512]{1,0:T(8,128)(2,1)S(1)}, u32[]{:S(2)}, u32[]{:S(2)}) collective-permute-start(bf16[144,512]{1,0:T(8,128)(2,1)S(1)} %get-tuple-element.103), channel_id=1, source_target_pairs={{0,16},{8,24},{16,0},{24,8},{1,17},{9,25},{17,1},{25,9},{2,18},{10... | collective-permute-start | bytes 442376 | tf_op jit(solution)/shard_map/ppermute | solution.py:24
  32.4 42.8 %copy-start.12 = (bf16[1024,1024]{1,0:T(8,128)(2,1)S(1)}, bf16[1024,1024]{1,0:T(8,128)(2,1)}, u32[]{:S(2)}) copy-start(bf16[1024,1024]{1,0:T(8,128)(2,1)} %refs_4_.1) | copy-start | bytes 6291460
  33.2 1.4 collective-permute-start.12
  34.7 4.5 %collective-permute-start.13 = (bf16[144,256]{1,0:T(8,128)(2,1)S(1)}, bf16[144,256]{1,0:T(8,128)(2,1)S(1)}, u32[]{:S(2)}, u32[]{:S(2)}) collective-permute-start(bf16[144,256]{1,0:T(8,128)(2,1)S(1)} %get-tuple-element.169), channel_id=1, source_target_pairs={{0,2},{1,3},{2,0},{3,1},{4,6},{5,7},{6,4},{7,5},{8,10},{9,11},{10,... | collective-permute-start | bytes 221192 | tf_op jit(solution)/shard_map/ppermute | solution.py:24
  36.3 8.1 %collective-permute-start.14 = (bf16[144,256]{1,0:T(8,128)(2,1)S(1)}, bf16[144,256]{1,0:T(8,128)(2,1)S(1)}, u32[]{:S(2)}, u32[]{:S(2)}) collective-permute-start(bf16[144,256]{1,0:T(8,128)(2,1)S(1)} %get-tuple-element.169), channel_id=1, source_target_pairs={{0,4},{1,5},{2,6},{3,7},{4,0},{5,1},{6,2},{7,3},{8,12},{9,13},{10,... | collective-permute-start | bytes 221192 | tf_op jit(solution)/shard_map/ppermute | solution.py:24
  38.9 6.3 %collective-permute-start.15 = (bf16[144,256]{1,0:T(8,128)(2,1)S(1)}, bf16[144,256]{1,0:T(8,128)(2,1)S(1)}, u32[]{:S(2)}, u32[]{:S(2)}) collective-permute-start(bf16[144,256]{1,0:T(8,128)(2,1)S(1)} %get-tuple-element.169), channel_id=1, source_target_pairs={{0,6},{1,7},{2,4},{3,5},{4,2},{5,3},{6,0},{7,1},{8,14},{9,15},{10,... | collective-permute-start | bytes 221192 | tf_op jit(solution)/shard_map/ppermute | solution.py:24
  39.2 20.4 %collective-permute-start.19 = (bf16[144,1024]{1,0:T(8,128)(2,1)S(1)}, bf16[144,1024]{1,0:T(8,128)(2,1)S(1)}, u32[]{:S(2)}, u32[]{:S(2)}) collective-permute-start(bf16[144,1024]{1,0:T(8,128)(2,1)S(1)} %get-tuple-element.112), channel_id=1, source_target_pairs={{0,8},{8,0},{16,24},{24,16},{1,9},{9,1},{17,25},{25,17},{2,10},{10... | collective-permute-start | bytes 884744 | tf_op jit(solution)/shard_map/ppermute | solution.py:24
  39.9 19.7 %collective-permute-start.20 = (bf16[144,1024]{1,0:T(8,128)(2,1)S(1)}, bf16[144,1024]{1,0:T(8,128)(2,1)S(1)}, u32[]{:S(2)}, u32[]{:S(2)}) collective-permute-start(bf16[144,1024]{1,0:T(8,128)(2,1)S(1)} %get-tuple-element.113), channel_id=1, source_target_pairs={{0,16},{8,24},{16,0},{24,8},{1,17},{9,25},{17,1},{25,9},{2,18},{10... | collective-permute-start | bytes 884744 | tf_op jit(solution)/shard_map/ppermute | solution.py:24
  41.4 18.1 %collective-permute-start.21 = (bf16[144,1024]{1,0:T(8,128)(2,1)S(1)}, bf16[144,1024]{1,0:T(8,128)(2,1)S(1)}, u32[]{:S(2)}, u32[]{:S(2)}) collective-permute-start(bf16[144,1024]{1,0:T(8,128)(2,1)S(1)} %get-tuple-element.114), channel_id=1, source_target_pairs={{0,24},{8,16},{16,8},{24,0},{1,25},{9,17},{17,9},{25,1},{2,26},{10... | collective-permute-start | bytes 884744 | tf_op jit(solution)/shard_map/ppermute | solution.py:24
  50.3 4.4 %collective-permute-start.16 = (bf16[18,8,128]{2,1,0:T(8,128)(2,1)S(1)}, bf16[18,8,128]{2,1,0:T(8,128)(2,1)S(1)}, u32[]{:S(2)}, u32[]{:S(2)}) collective-permute-start(bf16[18,8,128]{2,1,0:T(8,128)(2,1)S(1)} %get-tuple-element.106), channel_id=1, source_target_pairs={{0,8},{8,0},{16,24},{24,16},{1,9},{9,1},{17,25},{25,17},{2,10},{10... | collective-permute-start | bytes 110600 | tf_op jit(solution)/shard_map/ppermute | solution.py:24
  51.0 5.3 %collective-permute-start.17 = (bf16[18,8,128]{2,1,0:T(8,128)(2,1)S(1)}, bf16[18,8,128]{2,1,0:T(8,128)(2,1)S(1)}, u32[]{:S(2)}, u32[]{:S(2)}) collective-permute-start(bf16[18,8,128]{2,1,0:T(8,128)(2,1)S(1)} %get-tuple-element.106), channel_id=1, source_target_pairs={{0,16},{8,24},{16,0},{24,8},{1,17},{9,25},{17,1},{25,9},{2,18},{10... | collective-permute-start | bytes 110600 | tf_op jit(solution)/shard_map/ppermute | solution.py:24
  54.7 4.9 %collective-permute-start.18 = (bf16[18,8,128]{2,1,0:T(8,128)(2,1)S(1)}, bf16[18,8,128]{2,1,0:T(8,128)(2,1)S(1)}, u32[]{:S(2)}, u32[]{:S(2)}) collective-permute-start(bf16[18,8,128]{2,1,0:T(8,128)(2,1)S(1)} %get-tuple-element.106), channel_id=1, source_target_pairs={{0,24},{8,16},{16,8},{24,0},{1,25},{9,17},{17,9},{25,1},{2,26},{10... | collective-permute-start | bytes 110600 | tf_op jit(solution)/shard_map/ppermute | solution.py:24
  63.1 8.4 %collective-permute-start.22 = (bf16[128,1024]{1,0:T(8,128)(2,1)S(1)}, bf16[128,1024]{1,0:T(8,128)(2,1)S(1)}, u32[]{:S(2)}, u32[]{:S(2)}) collective-permute-start(bf16[128,1024]{1,0:T(8,128)(2,1)S(1)} %shard_map.171.refs_0_), channel_id=1, source_target_pairs={{0,8},{8,0},{16,24},{24,16},{1,9},{9,1},{17,25},{25,17},{2,10},{10... | collective-permute-start | bytes 786440 | tf_op jit(solution)/shard_map/ppermute | solution.py:24
  63.8 9.9 %collective-permute-start.23 = (bf16[128,1024]{1,0:T(8,128)(2,1)S(1)}, bf16[128,1024]{1,0:T(8,128)(2,1)S(1)}, u32[]{:S(2)}, u32[]{:S(2)}) collective-permute-start(bf16[128,1024]{1,0:T(8,128)(2,1)S(1)} %shard_map.171.refs_0_), channel_id=1, source_target_pairs={{0,16},{8,24},{16,0},{24,8},{1,17},{9,25},{17,1},{25,9},{2,18},{10... | collective-permute-start | bytes 786440 | tf_op jit(solution)/shard_map/ppermute | solution.py:24
  65.4 9.9 %collective-permute-start.24 = (bf16[128,1024]{1,0:T(8,128)(2,1)S(1)}, bf16[128,1024]{1,0:T(8,128)(2,1)S(1)}, u32[]{:S(2)}, u32[]{:S(2)}) collective-permute-start(bf16[128,1024]{1,0:T(8,128)(2,1)S(1)} %shard_map.171.refs_0_), channel_id=1, source_target_pairs={{0,24},{8,16},{16,8},{24,0},{1,25},{9,17},{17,9},{25,1},{2,26},{10... | collective-permute-start | bytes 786440 | tf_op jit(solution)/shard_map/ppermute | solution.py:24
  76.5 2.0 %collective-permute-start.25 = (bf16[4,64,1024]{2,1,0:T(8,128)(2,1)S(1)}, bf16[4,64,1024]{2,1,0:T(8,128)(2,1)S(1)}, u32[]{:S(2)}, u32[]{:S(2)}) collective-permute-start(bf16[4,64,1024]{2,1,0:T(8,128)(2,1)S(1)} %get-tuple-element.116), channel_id=1, source_target_pairs={{0,1},{1,0},{2,3},{3,2},{4,5},{5,4},{6,7},{7,6},{8,9},{9,8},{10,11... | collective-permute-start | bytes 1572872 | tf_op jit(solution)/shard_map/ppermute | solution.py:24
  78.6 13.1 %collective-permute-start.26 = (bf16[64,1024]{1,0:T(8,128)(2,1)S(1)}, bf16[64,1024]{1,0:T(8,128)(2,1)S(1)}, u32[]{:S(2)}, u32[]{:S(2)}) collective-permute-start(bf16[64,1024]{1,0:T(8,128)(2,1)S(1)} %get-tuple-element.118), channel_id=1, source_target_pairs={{0,2},{1,3},{2,0},{3,1},{4,6},{5,7},{6,4},{7,5},{8,10},{9,11},{10,... | collective-permute-start | bytes 393224 | tf_op jit(solution)/shard_map/ppermute | solution.py:24
  80.5 12.9 %collective-permute-start.27 = (bf16[64,1024]{1,0:T(8,128)(2,1)S(1)}, bf16[64,1024]{1,0:T(8,128)(2,1)S(1)}, u32[]{:S(2)}, u32[]{:S(2)}) collective-permute-start(bf16[64,1024]{1,0:T(8,128)(2,1)S(1)} %get-tuple-element.119), channel_id=1, source_target_pairs={{0,4},{1,5},{2,6},{3,7},{4,0},{5,1},{6,2},{7,3},{8,12},{9,13},{10,... | collective-permute-start | bytes 393224 | tf_op jit(solution)/shard_map/ppermute | solution.py:24
  82.1 11.2 %collective-permute-start.28 = (bf16[64,1024]{1,0:T(8,128)(2,1)S(1)}, bf16[64,1024]{1,0:T(8,128)(2,1)S(1)}, u32[]{:S(2)}, u32[]{:S(2)}) collective-permute-start(bf16[64,1024]{1,0:T(8,128)(2,1)S(1)} %get-tuple-element.120), channel_id=1, source_target_pairs={{0,6},{1,7},{2,4},{3,5},{4,2},{5,3},{6,0},{7,1},{8,14},{9,15},{10,... | collective-permute-start | bytes 393224 | tf_op jit(solution)/shard_map/ppermute | solution.py:24
  91.8 17.5 %copy-start = (bf16[1024,1792]{1,0:T(8,128)(2,1)}, bf16[1024,1792]{1,0:T(8,128)(2,1)S(1)}, u32[]{:S(2)}) copy-start(bf16[1024,1792]{1,0:T(8,128)(2,1)S(1)} %get-tuple-element.124.refs_12_.refs_9_.refs_7_.refs_3_) | copy-start | bytes 11010052
  91.8 17.5 %copy-start.2 = (bf16[1024,1792]{1,0:T(8,128)(2,1)}, bf16[1024,1792]{1,0:T(8,128)(2,1)S(1)}, u32[]{:S(2)}) copy-start(bf16[1024,1792]{1,0:T(8,128)(2,1)S(1)} %get-tuple-element.125.refs_13_.refs_10_.refs_8_.refs_4_) | copy-start | bytes 11010052
  94.2 13.5 %collective-permute-start.29 = (bf16[48,1024]{1,0:T(8,128)(2,1)S(1)}, bf16[48,1024]{1,0:T(8,128)(2,1)S(1)}, u32[]{:S(2)}, u32[]{:S(2)}) collective-permute-start(bf16[48,1024]{1,0:T(8,128)(2,1)S(1)} %get-tuple-element.129), channel_id=1, source_target_pairs={{0,2},{1,3},{2,0},{3,1},{4,6},{5,7},{6,4},{7,5},{8,10},{9,11},{10,... | collective-permute-start | bytes 294920 | tf_op jit(solution)/shard_map/ppermute | solution.py:24
  96.5 11.2 %collective-permute-start.30 = (bf16[48,1024]{1,0:T(8,128)(2,1)S(1)}, bf16[48,1024]{1,0:T(8,128)(2,1)S(1)}, u32[]{:S(2)}, u32[]{:S(2)}) collective-permute-start(bf16[48,1024]{1,0:T(8,128)(2,1)S(1)} %get-tuple-element.130), channel_id=1, source_target_pairs={{0,4},{1,5},{2,6},{3,7},{4,0},{5,1},{6,2},{7,3},{8,12},{9,13},{10,... | collective-permute-start | bytes 294920 | tf_op jit(solution)/shard_map/ppermute | solution.py:24
  97.2 10.6 %collective-permute-start.31 = (bf16[48,1024]{1,0:T(8,128)(2,1)S(1)}, bf16[48,1024]{1,0:T(8,128)(2,1)S(1)}, u32[]{:S(2)}, u32[]{:S(2)}) collective-permute-start(bf16[48,1024]{1,0:T(8,128)(2,1)S(1)} %get-tuple-element.131), channel_id=1, source_target_pairs={{0,6},{1,7},{2,4},{3,5},{4,2},{5,3},{6,0},{7,1},{8,14},{9,15},{10,... | collective-permute-start | bytes 294920 | tf_op jit(solution)/shard_map/ppermute | solution.py:24
  99.0 3.9 %collective-permute-start.32 = (bf16[16,1024]{1,0:T(8,128)(2,1)S(1)}, bf16[16,1024]{1,0:T(8,128)(2,1)S(1)}, u32[]{:S(2)}, u32[]{:S(2)}) collective-permute-start(bf16[16,1024]{1,0:T(8,128)(2,1)S(1)} %get-tuple-element.132), channel_id=1, source_target_pairs={{0,8},{8,0},{16,24},{24,16},{1,9},{9,1},{17,25},{25,17},{2,10},{10... | collective-permute-start | bytes 98312 | tf_op jit(solution)/shard_map/ppermute | solution.py:24
  99.8 5.0 %collective-permute-start.33 = (bf16[16,1024]{1,0:T(8,128)(2,1)S(1)}, bf16[16,1024]{1,0:T(8,128)(2,1)S(1)}, u32[]{:S(2)}, u32[]{:S(2)}) collective-permute-start(bf16[16,1024]{1,0:T(8,128)(2,1)S(1)} %get-tuple-element.133), channel_id=1, source_target_pairs={{0,16},{8,24},{16,0},{24,8},{1,17},{9,25},{17,1},{25,9},{2,18},{10... | collective-permute-start | bytes 98312 | tf_op jit(solution)/shard_map/ppermute | solution.py:24
  102.9 4.8 %collective-permute-start.34 = (bf16[16,1024]{1,0:T(8,128)(2,1)S(1)}, bf16[16,1024]{1,0:T(8,128)(2,1)S(1)}, u32[]{:S(2)}, u32[]{:S(2)}) collective-permute-start(bf16[16,1024]{1,0:T(8,128)(2,1)S(1)} %get-tuple-element.134), channel_id=1, source_target_pairs={{0,24},{8,16},{16,8},{24,0},{1,25},{9,17},{17,9},{25,1},{2,26},{10... | collective-permute-start | bytes 98312 | tf_op jit(solution)/shard_map/ppermute | solution.py:24
  107.8 1.5 collective-permute-start.35
  109.6 12.1 %collective-permute-start.36 = (bf16[192,1024]{1,0:T(8,128)(2,1)S(1)}, bf16[192,1024]{1,0:T(8,128)(2,1)S(1)}, u32[]{:S(2)}, u32[]{:S(2)}) collective-permute-start(bf16[192,1024]{1,0:T(8,128)(2,1)S(1)} %shard_map.178.refs_1_), channel_id=1, source_target_pairs={{0,8},{8,0},{16,24},{24,16},{1,9},{9,1},{17,25},{25,17},{2,10},{10... | collective-permute-start | bytes 1179656 | tf_op jit(solution)/shard_map/ppermute | solution.py:24
  110.5 11.7 %collective-permute-start.38 = (bf16[192,1024]{1,0:T(8,128)(2,1)S(1)}, bf16[192,1024]{1,0:T(8,128)(2,1)S(1)}, u32[]{:S(2)}, u32[]{:S(2)}) collective-permute-start(bf16[192,1024]{1,0:T(8,128)(2,1)S(1)} %shard_map.178.refs_1_), channel_id=1, source_target_pairs={{0,16},{8,24},{16,0},{24,8},{1,17},{9,25},{17,1},{25,9},{2,18},{10... | collective-permute-start | bytes 1179656 | tf_op jit(solution)/shard_map/ppermute | solution.py:24
  112.1 11.4 %copy-start.1 = (bf16[1024,1792]{1,0:T(8,128)(2,1)S(1)}, bf16[1024,1792]{1,0:T(8,128)(2,1)}, u32[]{:S(2)}) copy-start(bf16[1024,1792]{1,0:T(8,128)(2,1)} %copy-done) | copy-start | bytes 11010052
  112.1 11.4 %copy-start.3 = (bf16[1024,1792]{1,0:T(8,128)(2,1)S(1)}, bf16[1024,1792]{1,0:T(8,128)(2,1)}, u32[]{:S(2)}) copy-start(bf16[1024,1792]{1,0:T(8,128)(2,1)} %copy-done.2) | copy-start | bytes 11010052
  121.7 6.5 %collective-permute-start.37 = (bf16[96,1024]{1,0:T(8,128)(2,1)S(1)}, bf16[96,1024]{1,0:T(8,128)(2,1)S(1)}, u32[]{:S(2)}, u32[]{:S(2)}) collective-permute-start(bf16[96,1024]{1,0:T(8,128)(2,1)S(1)} %slice.19), channel_id=1, source_target_pairs={{0,16},{8,24},{16,0},{24,8},{1,17},{9,25},{17,1},{25,9},{2,18},{10... | collective-permute-start | bytes 589832 | tf_op jit(solution)/shard_map/ppermute | solution.py:24
  122.2 6.2 %collective-permute-start.39 = (bf16[96,1024]{1,0:T(8,128)(2,1)S(1)}, bf16[96,1024]{1,0:T(8,128)(2,1)S(1)}, u32[]{:S(2)}, u32[]{:S(2)}) collective-permute-start(bf16[96,1024]{1,0:T(8,128)(2,1)S(1)} %slice.20), channel_id=1, source_target_pairs={{0,8},{8,0},{16,24},{24,16},{1,9},{9,1},{17,25},{25,17},{2,10},{10... | collective-permute-start | bytes 589832 | tf_op jit(solution)/shard_map/ppermute | solution.py:24
  130.7 15.0 %copy-start.7 = (bf16[4096,8]{0,1:T(8,128)(2,1)S(1)}, bf16[4096,8]{0,1:T(8,128)(2,1)}, u32[]{:S(2)}) copy-start(bf16[4096,8]{0,1:T(8,128)(2,1)} %param.29) | copy-start | bytes 196612
  134.4 7.9 %collective-permute-start.42 = (bf16[48,2048]{1,0:T(8,128)(2,1)S(1)}, bf16[48,2048]{1,0:T(8,128)(2,1)S(1)}, u32[]{:S(2)}, u32[]{:S(2)}) collective-permute-start(bf16[48,2048]{1,0:T(8,128)(2,1)S(1)} %get-tuple-element.155), channel_id=1, source_target_pairs={{0,8},{8,0},{16,24},{24,16},{1,9},{9,1},{17,25},{25,17},{2,10},{10... | collective-permute-start | bytes 589832 | tf_op jit(solution)/shard_map/ppermute | solution.py:24
  135.7 7.5 %collective-permute-start.43 = (bf16[48,2048]{1,0:T(8,128)(2,1)S(1)}, bf16[48,2048]{1,0:T(8,128)(2,1)S(1)}, u32[]{:S(2)}, u32[]{:S(2)}) collective-permute-start(bf16[48,2048]{1,0:T(8,128)(2,1)S(1)} %get-tuple-element.156), channel_id=1, source_target_pairs={{0,16},{8,24},{16,0},{24,8},{1,17},{9,25},{17,1},{25,9},{2,18},{10... | collective-permute-start | bytes 589832 | tf_op jit(solution)/shard_map/ppermute | solution.py:24
  136.6 10.1 %collective-permute-start.40 = (bf16[48,2048]{1,0:T(8,128)(2,1)S(1)}, bf16[48,2048]{1,0:T(8,128)(2,1)S(1)}, u32[]{:S(2)}, u32[]{:S(2)}) collective-permute-start(bf16[48,2048]{1,0:T(8,128)(2,1)S(1)} %get-tuple-element.151), channel_id=1, source_target_pairs={{0,8},{8,0},{16,24},{24,16},{1,9},{9,1},{17,25},{25,17},{2,10},{10... | collective-permute-start | bytes 589832 | tf_op jit(solution)/shard_map/ppermute | solution.py:24
  138.1 8.8 %collective-permute-start.41 = (bf16[48,2048]{1,0:T(8,128)(2,1)S(1)}, bf16[48,2048]{1,0:T(8,128)(2,1)S(1)}, u32[]{:S(2)}, u32[]{:S(2)}) collective-permute-start(bf16[48,2048]{1,0:T(8,128)(2,1)S(1)} %get-tuple-element.152), channel_id=1, source_target_pairs={{0,16},{8,24},{16,0},{24,8},{1,17},{9,25},{17,1},{25,9},{2,18},{10... | collective-permute-start | bytes 589832 | tf_op jit(solution)/shard_map/ppermute | solution.py:24
  143.3 5.7 %collective-permute-start.44 = (bf16[48,2048]{1,0:T(8,128)(2,1)S(1)}, bf16[48,2048]{1,0:T(8,128)(2,1)S(1)}, u32[]{:S(2)}, u32[]{:S(2)}) collective-permute-start(bf16[48,2048]{1,0:T(8,128)(2,1)S(1)} %get-tuple-element.157), channel_id=1, source_target_pairs={{0,8},{8,0},{16,24},{24,16},{1,9},{9,1},{17,25},{25,17},{2,10},{10... | collective-permute-start | bytes 589832 | tf_op jit(solution)/shard_map/ppermute | solution.py:24
  144.5 5.7 %collective-permute-start.45 = (bf16[48,2048]{1,0:T(8,128)(2,1)S(1)}, bf16[48,2048]{1,0:T(8,128)(2,1)S(1)}, u32[]{:S(2)}, u32[]{:S(2)}) collective-permute-start(bf16[48,2048]{1,0:T(8,128)(2,1)S(1)} %get-tuple-element.158), channel_id=1, source_target_pairs={{0,16},{8,24},{16,0},{24,8},{1,17},{9,25},{17,1},{25,9},{2,18},{10... | collective-permute-start | bytes 589832 | tf_op jit(solution)/shard_map/ppermute | solution.py:24
  150.6 5.0 %collective-permute-start.46 = (bf16[48,1024]{1,0:T(8,128)(2,1)S(1)}, bf16[48,1024]{1,0:T(8,128)(2,1)S(1)}, u32[]{:S(2)}, u32[]{:S(2)}) collective-permute-start(bf16[48,1024]{1,0:T(8,128)(2,1)S(1)} %get-tuple-element.163), channel_id=1, source_target_pairs={{0,2},{1,3},{2,0},{3,1},{4,6},{5,7},{6,4},{7,5},{8,10},{9,11},{10,... | collective-permute-start | bytes 294920 | tf_op jit(solution)/shard_map/ppermute | solution.py:24
  151.7 6.6 %collective-permute-start.47 = (bf16[48,1024]{1,0:T(8,128)(2,1)S(1)}, bf16[48,1024]{1,0:T(8,128)(2,1)S(1)}, u32[]{:S(2)}, u32[]{:S(2)}) collective-permute-start(bf16[48,1024]{1,0:T(8,128)(2,1)S(1)} %get-tuple-element.164), channel_id=1, source_target_pairs={{0,4},{1,5},{2,6},{3,7},{4,0},{5,1},{6,2},{7,3},{8,12},{9,13},{10,... | collective-permute-start | bytes 294920 | tf_op jit(solution)/shard_map/ppermute | solution.py:24
  153.2 6.5 %collective-permute-start.48 = (bf16[48,1024]{1,0:T(8,128)(2,1)S(1)}, bf16[48,1024]{1,0:T(8,128)(2,1)S(1)}, u32[]{:S(2)}, u32[]{:S(2)}) collective-permute-start(bf16[48,1024]{1,0:T(8,128)(2,1)S(1)} %get-tuple-element.165), channel_id=1, source_target_pairs={{0,6},{1,7},{2,4},{3,5},{4,2},{5,3},{6,0},{7,1},{8,14},{9,15},{10,... | collective-permute-start | bytes 294920 | tf_op jit(solution)/shard_map/ppermute | solution.py:24
  159.7 1.5 collective-permute-start.49
  (1 other events, 4.3 us)
